TPU v7x, 32 devices: a whole 2x2x4 slice. The times are simulated.
32 devices in a mesh: dp: 8 (over y, x, core), tensor: 4 (over z).
Axes of the slice: x: 2, y: 2, z: 4, core: 2. Of those that a mesh axis runs over, the one named last changes fastest.
Arguments:
- hidden_in: bfloat16 [24576, 1024], P(('dp', 'tensor')), may hold values from -6 to 6
- seq_lengths: int32 [8, 5], P('dp'), may hold values from 1 to 2048, as said below
- cotangent: bfloat16 [24576, 1024], P(('dp', 'tensor')), may hold values from -6 to 6
- w_qkv: float32 [1024, 3, 1024], P('dp', None, 'tensor'), may hold values from -0.1875 to 0.1875
- w_proj: float32 [1024, 1024], P('dp', 'tensor'), may hold values from -1.5 to 1.5
- w_in: float32 [1024, 2, 2624], P('dp', None, 'tensor'), may hold values from -0.1875 to 0.1875
- w_down: float32 [1024, 2624], P('dp', 'tensor'), may hold values from -0.15625 to 0.15625
- norm_gains: float32 [2, 1024], P(None, 'dp'), may hold values from 0.5 to 1.5
- qkv_first: float32 [1024, 3, 1024], P('dp', None, 'tensor'), may hold values from -112 to 112
- qkv_second: float32 [1024, 3, 1024], P('dp', None, 'tensor'), may hold values from 501.3504 to 2005.4016
- proj_first: float32 [1024, 1024], P('dp', 'tensor'), may hold values from -8 to 8
- proj_second: float32 [1024, 1024], P('dp', 'tensor'), may hold values from 3.9168 to 15.6672
- in_first: float32 [1024, 2, 2624], P('dp', None, 'tensor'), may hold values from -56 to 56
- in_second: float32 [1024, 2, 2624], P('dp', None, 'tensor'), may hold values from 125.3376 to 501.3504
- down_first: float32 [1024, 2624], P('dp', 'tensor'), may hold values from -64 to 64
- down_second: float32 [1024, 2624], P('dp', 'tensor'), may hold values from 211.3536 to 845.4144
- gain_first: float32 [2, 1024], P(None, 'dp'), may hold values from -160 to 160
- gain_second: float32 [2, 1024], P(None, 'dp'), may hold values from 1130.496 to 4521.984
Outputs:
- hidden_out: bfloat16 [24576, 1024], P(('dp', 'tensor'))
- grad_input: float32 [24576, 1024], P(('dp', 'tensor'))
- qkv_first_new: float32 [1024, 3, 1024], P('dp', None, 'tensor')
- qkv_second_new: float32 [1024, 3, 1024], P('dp', None, 'tensor')
- qkv_new: float32 [1024, 3, 1024], P('dp', None, 'tensor')
- proj_first_new: float32 [1024, 1024], P('dp', 'tensor')
- proj_second_new: float32 [1024, 1024], P('dp', 'tensor')
- proj_new: float32 [1024, 1024], P('dp', 'tensor')
- in_first_new: float32 [1024, 2, 2624], P('dp', None, 'tensor')
- in_second_new: float32 [1024, 2, 2624], P('dp', None, 'tensor')
- in_new: float32 [1024, 2, 2624], P('dp', None, 'tensor')
- down_first_new: float32 [1024, 2624], P('dp', 'tensor')
- down_second_new: float32 [1024, 2624], P('dp', 'tensor')
- down_new: float32 [1024, 2624], P('dp', 'tensor')
- gain_first_new: float32 [2, 1024], P(None, 'dp')
- gain_second_new: float32 [2, 1024], P(None, 'dp')
- gains_new: float32 [2, 1024], P(None, 'dp')
Inputs may be any that keep to these rules, and one draw needn't show every extreme that they name: `seq_lengths`: each row lists the lengths of 5 sequences that fill the 3072 tokens of its group exactly; one of them has length 2048 and starts within the group's first 768 tokens; the others are shorter.
All inputs are finite; a program needn't handle non-finite values.
Results may differ from a plain program's by a relative error of at most 0.023.
Values may be sent and summed in bfloat16 or wider, within the bound.
No kernel may reach another device: no remote copies, remote signals or barrier semaphores. Data moves between devices by JAX's collectives and lax.ppermute only.
A program may use at most 192 MiB of HBM per device.

v0:
```python
import jax
import jax.numpy as jnp
from jax import lax
from jax.sharding import PartitionSpec as P

D = 1024
HEAD_DIM = 64
FF = 2624
HALF = 64
BLOCK = 512
STEP = 10


NORM_EPS = 1e-05
THETA_BASE = 10000.0
BETA_ONE = 0.9
BETA_TWO = 0.98
ADAM_EPS = 1e-06
WEIGHT_DECAY = 0.01
GAIN_RATE = 0.5
MASKED = -1e30


def layer_norm(values, gain_row):
    mean_value = jnp.mean(values, axis=-1, keepdims=True)
    centered = values - mean_value
    variance = jnp.mean(centered * centered, axis=-1, keepdims=True)
    return centered * lax.rsqrt(variance + NORM_EPS) * gain_row


def geglu(gate_in, gate_up):
    return jax.nn.gelu(gate_in, approximate=False) * gate_up


def layout(lengths, group_rows):
    seq_ends = jnp.cumsum(lengths)
    seq_starts = seq_ends - lengths
    token_index = jnp.arange(group_rows)
    segment = jnp.sum((token_index[:, None] >= seq_ends[None, :]).astype(jnp.int32), axis=1)
    member = segment[:, None] == jnp.arange(lengths.shape[0])[None, :]
    position = token_index - jnp.sum(jnp.where(member, seq_starts[None, :], 0), axis=1)
    return (segment, position)


def rotary_tables(position):
    half_dim = HEAD_DIM // 2
    exponent = jnp.arange(half_dim).astype(jnp.float32) * (2.0 / HEAD_DIM)
    inverse = jnp.power(jnp.float32(THETA_BASE), -exponent)
    angle_table = position.astype(jnp.float32)[:, None] * inverse[None, :]
    return (jnp.cos(angle_table), jnp.sin(angle_table))


def rotate(values, cosine_table, sine_table):
    half_dim = values.shape[-1] // 2
    front_half = values[..., :half_dim]
    back_half = values[..., half_dim:]
    cos_rows = cosine_table[:, None, :]
    sin_rows = sine_table[:, None, :]
    return jnp.concatenate(
        [
            front_half * cos_rows - back_half * sin_rows,
            back_half * cos_rows + front_half * sin_rows,
        ],
        axis=-1,
    )


def block_mask(segment_pad, block_first):
    query_seg = lax.dynamic_slice_in_dim(segment_pad, block_first + HALF, BLOCK)
    key_seg = lax.dynamic_slice_in_dim(segment_pad, block_first, BLOCK + 2 * HALF)
    offset = jnp.arange(BLOCK)[:, None] + HALF - jnp.arange(BLOCK + 2 * HALF)[None, :]
    return (query_seg[:, None] == key_seg[None, :]) & (jnp.abs(offset) <= HALF)


def attend_forward(queries, key_rows, values, segment):
    group_rows = queries.shape[0]
    score_scale = HEAD_DIM ** (-0.5)
    keys_pad = jnp.pad(key_rows, ((HALF, HALF), (0, 0), (0, 0)))
    values_pad = jnp.pad(values, ((HALF, HALF), (0, 0), (0, 0)))
    segment_pad = jnp.pad(segment, HALF, constant_values=-1)

    def step_block(carried, block_number):
        block_first = block_number * BLOCK
        query_block = lax.dynamic_slice_in_dim(queries, block_first, BLOCK)
        key_block = lax.dynamic_slice_in_dim(keys_pad, block_first, BLOCK + 2 * HALF)
        value_block = lax.dynamic_slice_in_dim(values_pad, block_first, BLOCK + 2 * HALF)
        allowed = block_mask(segment_pad, block_first)
        scores = (
            jnp.einsum("qhd,khd->hqk", query_block, key_block, preferred_element_type=jnp.float32)
            * score_scale
        )
        scores = jnp.where(allowed[None], scores, MASKED)
        row_top = jnp.max(scores, axis=-1, keepdims=True)
        lifted = jnp.exp(scores - row_top)
        row_total = jnp.sum(lifted, axis=-1, keepdims=True)
        probs_low = (lifted / row_total).astype(jnp.bfloat16)
        block_out = jnp.einsum(
            "hqk,khd->qhd", probs_low, value_block, preferred_element_type=jnp.float32
        )
        return (carried, (block_out, (row_top + jnp.log(row_total))[..., 0]))

    block_count = group_rows // BLOCK
    unused, (outputs, log_totals) = lax.scan(step_block, 0, jnp.arange(block_count))
    return (outputs.reshape(queries.shape), log_totals)


def attend_backward(queries, key_rows, values, segment, log_totals, grad_output):
    group_rows = queries.shape[0]
    score_scale = HEAD_DIM ** (-0.5)
    key_span = BLOCK + 2 * HALF
    keys_pad = jnp.pad(key_rows, ((HALF, HALF), (0, 0), (0, 0)))
    values_pad = jnp.pad(values, ((HALF, HALF), (0, 0), (0, 0)))
    segment_pad = jnp.pad(segment, HALF, constant_values=-1)

    def step_block(carried, inputs):
        grad_keys_pad, grad_values_pad = carried
        block_number, log_block = inputs
        block_first = block_number * BLOCK
        query_block = lax.dynamic_slice_in_dim(queries, block_first, BLOCK)
        key_block = lax.dynamic_slice_in_dim(keys_pad, block_first, key_span)
        value_block = lax.dynamic_slice_in_dim(values_pad, block_first, key_span)
        grad_block = lax.dynamic_slice_in_dim(grad_output, block_first, BLOCK)
        allowed = block_mask(segment_pad, block_first)
        scores = (
            jnp.einsum("qhd,khd->hqk", query_block, key_block, preferred_element_type=jnp.float32)
            * score_scale
        )
        scores = jnp.where(allowed[None], scores, MASKED)
        attention_probs = jnp.exp(scores - log_block[..., None])
        grad_probs = jnp.einsum(
            "qhd,khd->hqk", grad_block, value_block, preferred_element_type=jnp.float32
        )
        row_delta = jnp.sum(attention_probs * grad_probs, axis=-1, keepdims=True)
        grad_scores = (attention_probs * (grad_probs - row_delta)).astype(jnp.bfloat16)
        grad_query = (
            jnp.einsum("hqk,khd->qhd", grad_scores, key_block, preferred_element_type=jnp.float32)
            * score_scale
        )
        grad_key = (
            jnp.einsum("hqk,qhd->khd", grad_scores, query_block, preferred_element_type=jnp.float32)
            * score_scale
        )
        grad_value = jnp.einsum(
            "hqk,qhd->khd",
            attention_probs.astype(jnp.bfloat16),
            grad_block,
            preferred_element_type=jnp.float32,
        )
        grad_keys_pad = lax.dynamic_update_slice_in_dim(
            grad_keys_pad,
            lax.dynamic_slice_in_dim(grad_keys_pad, block_first, key_span) + grad_key,
            block_first,
            0,
        )
        grad_values_pad = lax.dynamic_update_slice_in_dim(
            grad_values_pad,
            lax.dynamic_slice_in_dim(grad_values_pad, block_first, key_span) + grad_value,
            block_first,
            0,
        )
        return ((grad_keys_pad, grad_values_pad), grad_query)

    block_count = group_rows // BLOCK
    zeros_pad = jnp.zeros((group_rows + 2 * HALF,) + key_rows.shape[1:], jnp.float32)
    (grad_keys_pad, grad_values_pad), grad_queries = lax.scan(
        step_block, (zeros_pad, zeros_pad), (jnp.arange(block_count), log_totals)
    )
    return (
        grad_queries.reshape(queries.shape),
        grad_keys_pad[HALF : HALF + group_rows],
        grad_values_pad[HALF : HALF + group_rows],
    )


def gather_rows(rows_low):
    return lax.all_gather(rows_low, "tensor", axis=0, tiled=True)


def sum_rows(left_low, weight_low):
    return lax.psum_scatter(
        jnp.einsum("tj,oj->to", left_low, weight_low, preferred_element_type=jnp.float32).astype(
            jnp.bfloat16
        ),
        "tensor",
        scatter_dimension=0,
        tiled=True,
    ).astype(jnp.float32)


def adam_update(master, gradient, moment_one, moment_two, step_rate):
    one_new = BETA_ONE * moment_one + (1.0 - BETA_ONE) * gradient
    two_new = BETA_TWO * moment_two + (1.0 - BETA_TWO) * gradient * gradient
    one_hat = one_new / (1.0 - BETA_ONE**STEP)
    two_hat = two_new / (1.0 - BETA_TWO**STEP)
    master_new = master - step_rate * (
        one_hat / (jnp.sqrt(two_hat) + ADAM_EPS) + WEIGHT_DECAY * master
    )
    return (one_new, two_new, master_new)


def local(
    hidden_in,
    seq_lengths,
    cotangent,
    w_qkv,
    w_proj,
    w_in,
    w_down,
    norm_gains,
    qkv_first,
    qkv_second,
    proj_first,
    proj_second,
    in_first,
    in_second,
    down_first,
    down_second,
    gain_first,
    gain_second,
):
    row_count = hidden_in.shape[0]
    group_rows = row_count * lax.axis_size("tensor")
    local_width = w_qkv.shape[2]
    local_hidden = w_in.shape[2]
    head_shape = (group_rows, local_width // HEAD_DIM, HEAD_DIM)
    qkv_low, proj_low, gains_low = (
        lax.all_gather(w_qkv.astype(jnp.bfloat16), "dp", axis=0, tiled=True),
        lax.all_gather(w_proj.astype(jnp.bfloat16), "dp", axis=0, tiled=True),
        lax.all_gather(norm_gains.astype(jnp.bfloat16), "dp", axis=1, tiled=True),
    )
    gains_full = gains_low.astype(jnp.float32)
    segment, position = layout(seq_lengths[0], group_rows)
    cosine_table, sine_table = rotary_tables(position)
    hidden = hidden_in.astype(jnp.float32)
    normed_one, norm_pull_one = jax.vjp(layer_norm, hidden, gains_full[0])
    rows_one = gather_rows(normed_one.astype(jnp.bfloat16))
    mixed_qkv = jnp.einsum("td,dcf->tcf", rows_one, qkv_low, preferred_element_type=jnp.float32)

    def rotate_pair(query_pre, key_pre):
        return (
            rotate(query_pre.reshape(head_shape), cosine_table, sine_table),
            rotate(key_pre.reshape(head_shape), cosine_table, sine_table),
        )

    (query_turned, key_turned), turn_pull = jax.vjp(rotate_pair, mixed_qkv[:, 0], mixed_qkv[:, 1])
    queries = query_turned.astype(jnp.bfloat16)
    key_rows = key_turned.astype(jnp.bfloat16)
    values = mixed_qkv[:, 2].reshape(head_shape).astype(jnp.bfloat16)
    attended_heads, log_totals = attend_forward(queries, key_rows, values, segment)
    attended = attended_heads.reshape(group_rows, local_width).astype(jnp.bfloat16)
    middle = hidden + sum_rows(attended, proj_low)
    in_low, down_low = (
        lax.all_gather(w_in.astype(jnp.bfloat16), "dp", axis=0, tiled=True),
        lax.all_gather(w_down.astype(jnp.bfloat16), "dp", axis=0, tiled=True),
    )
    normed_two, norm_pull_two = jax.vjp(layer_norm, middle, gains_full[1])
    rows_two = gather_rows(normed_two.astype(jnp.bfloat16))
    gate_pair = jnp.einsum("td,dcf->tcf", rows_two, in_low, preferred_element_type=jnp.float32)
    active_full, geglu_pull = jax.vjp(geglu, gate_pair[:, 0], gate_pair[:, 1])
    active = active_full.astype(jnp.bfloat16)
    output = middle + sum_rows(active, down_low)
    grad_out = cotangent.astype(jnp.float32)
    in_low, down_low = (
        lax.all_gather(w_in.astype(jnp.bfloat16), "dp", axis=0, tiled=True),
        lax.all_gather(w_down.astype(jnp.bfloat16), "dp", axis=0, tiled=True),
    )
    grad_rows = gather_rows(grad_out.astype(jnp.bfloat16))
    grad_active = jnp.dot(grad_rows, down_low, preferred_element_type=jnp.float32)
    grad_down = jnp.einsum("to,tf->of", grad_rows, active, preferred_element_type=jnp.float32)
    grad_gate_in, grad_gate_up = geglu_pull(grad_active)
    grad_pair = jnp.stack([grad_gate_in, grad_gate_up], axis=1).astype(jnp.bfloat16)
    grad_in_weight = jnp.einsum(
        "td,tcf->dcf", rows_two, grad_pair, preferred_element_type=jnp.float32
    )
    grad_normed_two = sum_rows(
        grad_pair.reshape(group_rows, 2 * local_hidden),
        in_low.reshape(in_low.shape[0], 2 * local_hidden),
    )
    grad_middle_norm, grad_gain_two = norm_pull_two(grad_normed_two)
    grad_middle = grad_out + grad_middle_norm
    qkv_low, proj_low = (
        lax.all_gather(w_qkv.astype(jnp.bfloat16), "dp", axis=0, tiled=True),
        lax.all_gather(w_proj.astype(jnp.bfloat16), "dp", axis=0, tiled=True),
    )
    grad_rows_mid = gather_rows(grad_middle.astype(jnp.bfloat16))
    grad_attended = jnp.dot(grad_rows_mid, proj_low, preferred_element_type=jnp.float32).astype(
        jnp.bfloat16
    )
    grad_proj = jnp.einsum("to,tj->oj", grad_rows_mid, attended, preferred_element_type=jnp.float32)
    grad_queries, grad_keys, grad_values = attend_backward(
        queries, key_rows, values, segment, log_totals, grad_attended.reshape(head_shape)
    )
    grad_query_pre, grad_key_pre = turn_pull((grad_queries, grad_keys))
    grad_mixed = jnp.stack(
        [grad_query_pre, grad_key_pre, grad_values.reshape(group_rows, local_width)], axis=1
    ).astype(jnp.bfloat16)
    grad_qkv = jnp.einsum("td,tcf->dcf", rows_one, grad_mixed, preferred_element_type=jnp.float32)
    grad_normed_one = sum_rows(
        grad_mixed.reshape(group_rows, 3 * local_width),
        qkv_low.reshape(qkv_low.shape[0], 3 * local_width),
    )
    grad_hidden_norm, grad_gain_one = norm_pull_one(grad_normed_one)
    grad_input = grad_middle + grad_hidden_norm
    gain_total = lax.psum(jnp.stack([grad_gain_one, grad_gain_two]), "tensor")
    qkv_sum, proj_sum, in_sum, down_sum, gain_sum = (
        lax.psum_scatter(grad_qkv, "dp", scatter_dimension=0, tiled=True),
        lax.psum_scatter(grad_proj, "dp", scatter_dimension=0, tiled=True),
        lax.psum_scatter(grad_in_weight, "dp", scatter_dimension=0, tiled=True),
        lax.psum_scatter(grad_down, "dp", scatter_dimension=0, tiled=True),
        lax.psum_scatter(gain_total, "dp", scatter_dimension=1, tiled=True),
    )
    qkv_one, qkv_two, qkv_new = adam_update(w_qkv, qkv_sum, qkv_first, qkv_second, D ** (-0.5))
    proj_one, proj_two, proj_new = adam_update(
        w_proj, proj_sum, proj_first, proj_second, (D // HALF) ** (-0.5)
    )
    in_one, in_two, in_new = adam_update(w_in, in_sum, in_first, in_second, D ** (-0.5))
    down_one, down_two, down_new = adam_update(
        w_down, down_sum, down_first, down_second, (FF // 2) ** (-0.5)
    )
    gain_one, gain_two, gains_new = adam_update(
        norm_gains, gain_sum, gain_first, gain_second, GAIN_RATE
    )
    return (
        output.astype(jnp.bfloat16),
        grad_input,
        qkv_one,
        qkv_two,
        qkv_new,
        proj_one,
        proj_two,
        proj_new,
        in_one,
        in_two,
        in_new,
        down_one,
        down_two,
        down_new,
        gain_one,
        gain_two,
        gains_new,
    )


def solution(mesh):
    placed = (
        P(("dp", "tensor"), None),
        P("dp", None),
        P(("dp", "tensor"), None),
        P("dp", None, "tensor"),
        P("dp", "tensor"),
        P("dp", None, "tensor"),
        P("dp", "tensor"),
        P(None, "dp"),
        P("dp", None, "tensor"),
        P("dp", None, "tensor"),
        P("dp", "tensor"),
        P("dp", "tensor"),
        P("dp", None, "tensor"),
        P("dp", None, "tensor"),
        P("dp", "tensor"),
        P("dp", "tensor"),
        P(None, "dp"),
        P(None, "dp"),
    )
    return jax.shard_map(
        local,
        mesh=mesh,
        in_specs=placed,
        out_specs=(
            P(("dp", "tensor"), None),
            P(("dp", "tensor"), None),
            P("dp", None, "tensor"),
            P("dp", None, "tensor"),
            P("dp", None, "tensor"),
            P("dp", "tensor"),
            P("dp", "tensor"),
            P("dp", "tensor"),
            P("dp", None, "tensor"),
            P("dp", None, "tensor"),
            P("dp", None, "tensor"),
            P("dp", "tensor"),
            P("dp", "tensor"),
            P("dp", "tensor"),
            P(None, "dp"),
            P(None, "dp"),
            P(None, "dp"),
        ),
        check_vma=False,
    )
```

profile of v0, /device:TPU:0, one launch (start us, length us, event | category | flops | bytes accessed | tf_op | source)
XLA Modules:
  0.0 1562.1 jit_solution(16554840765994940521)
XLA Ops:
  9.9 10.2 all_gather.31
  26.4 12.3 all_gather.34
  40.5 117.5 %all-gather.8.cloned.1.call-done = bf16[3072,1024]{1,0:T(8,128)(2,1)} async-done(((bf16[768,1024]{1,0:T(8,128)(2,1)}), bf16[3072,1024]{1,0:T(8,128)(2,1)}) %all-gather.8.cloned.1.call-update) | async-done | bytes 6291472 | tf_op jit(solution)/shard_map/all_gather | solution.py:176
  158.0 7.7 fusion.74
  171.5 66.7 %while.30 = (s32[]{:T(128)}, bf16[6,512,4,64]{1,3,2,0:T(8,128)(2,1)}, f32[6,4,512]{2,1,0:T(4,128)}, s32[6]{0:T(128)S(1)}, bf16[3200,4,64]{0,2,1:T(8,128)(2,1)}, ...) while((s32[]{:T(128)}, ...), condition=%wide.region_8.9_spmd, body=%wide.region_5.8_spmd.sunk | while | flops 352909824 | bytes 18565920 | solution.py:103
  179.1 3.5 fusion.163
  201.3 3.5 fusion.163
  212.4 3.5 fusion.163
  223.4 3.5 fusion.163
  243.0 4.5 convolution_convert_fusion.1
  250.7 106.0 %reduce-scatter.12.cloned.1.call-done = bf16[768,1024]{1,0:T(8,128)(2,1)} async-done(((bf16[3072,1024]{1,0:T(8,128)(2,1)}), bf16[768,1024]{1,0:T(8,128)(2,1)}) %reduce-scatter.12.cloned.1.call-update) | async-done | bytes 1572880 | tf_op jit(solution)/shard_map/reduce_scatter | solution.py:180
  361.3 23.1 %all-gather.16.cloned.1.call-done = bf16[1024,656]{0,1:T(8,128)(2,1)} async-done(((bf16[128,656]{0,1:T(8,128)(2,1)}), bf16[1024,656]{0,1:T(8,128)(2,1)}) %all-gather.16.cloned.1.call-update) | async-done | bytes 1343504 | tf_op jit(solution)/shard_map/all_gather | solution.py:254
  384.4 116.8 %all-gather.18.cloned.1.call-done = bf16[3072,1024]{1,0:T(8,128)(2,1)} async-done(((bf16[768,1024]{1,0:T(8,128)(2,1)}), bf16[3072,1024]{1,0:T(8,128)(2,1)}) %all-gather.18.cloned.1.call-update) | async-done | bytes 6291472 | tf_op jit(solution)/shard_map/all_gather | solution.py:176
  501.2 10.6 fusion.121
  511.8 20.7 %all-gather.14.cloned.1.call-done = bf16[1024,2,656]{0,2,1:T(8,128)(2,1)} async-done(((bf16[128,2,656]{0,2,1:T(8,128)(2,1)}), bf16[1024,2,656]{0,2,1:T(8,128)(2,1)}) %all-gather.14.cloned.1.call-update) | async-done | bytes 2686992 | tf_op jit(solution)/shard_map/all_gather | solution.py:253
  532.6 117.5 %all-gather.12.cloned.1.call-done = bf16[3072,1024]{1,0:T(8,128)(2,1)} async-done(((bf16[768,1024]{1,0:T(8,128)(2,1)}), bf16[3072,1024]{1,0:T(8,128)(2,1)}) %all-gather.12.cloned.1.call-update) | async-done | bytes 6291472 | tf_op jit(solution)/shard_map/all_gather | solution.py:176
  650.1 12.2 fusion.70
  662.3 20.6 %fusion.81 = (bf16[3072,1,656]{0,2,1:T(8,128)(2,1)}, f32[3072,656]{0,1:T(8,128)}) fusion(f32[3072,656]{0,1:T(8,128)S(1)} %copy-done.4, f32[3072,2,656]{0,2,1:T(8,128)S(1)} %fusion.70), kind=kLoop, calls=%fused_computation.113 | loop fusion | flops 147111936 | bytes 36274176 | tf_op jit(solution)/shard_map/stack | solution.py:271
  682.9 13.0 fusion.80
  695.9 15.1 bitcast_convert_fusion.1
  711.0 8.9 convolution_convert_fusion
  720.0 100.1 %reduce-scatter.16.cloned.1.call-done = bf16[768,1024]{1,0:T(8,128)(2,1)} async-done(((bf16[3072,1024]{1,0:T(8,128)(2,1)}), bf16[768,1024]{1,0:T(8,128)(2,1)}) %reduce-scatter.16.cloned.1.call-update) | async-done | bytes 1572880 | tf_op jit(solution)/shard_map/reduce_scatter | solution.py:180
  820.1 3.5 fusion.89
  823.6 110.1 %reduce-scatter.14.cloned.1.call-done = bf16[768,1024]{1,0:T(8,128)(2,1)} async-done(((bf16[3072,1024]{1,0:T(8,128)(2,1)}), bf16[768,1024]{1,0:T(8,128)(2,1)}) %reduce-scatter.14.cloned.1.call-update) | async-done | bytes 1572880 | tf_op jit(solution)/shard_map/reduce_scatter | solution.py:180
  933.7 4.2 fusion.117
  941.5 9.9 convolution_bitcast_fusion
  951.5 14.7 fusion.68
  966.3 91.0 %all-gather.20.cloned.1.call-done = bf16[3072,1024]{1,0:T(8,128)(2,1)} async-done(((bf16[768,1024]{1,0:T(8,128)(2,1)}), bf16[3072,1024]{1,0:T(8,128)(2,1)}) %all-gather.20.cloned.1.call-update) | async-done | bytes 6291472 | tf_op jit(solution)/shard_map/all_gather | solution.py:176
  1057.3 4.6 convolution_convert_fusion.2
  1065.8 216.6 %while.31 = (s32[]{:T(128)}, f32[3200,4,64]{0,2,1:T(8,128)}, f32[3200,4,64]{0,2,1:T(8,128)}, f32[6,512,4,64]{1,0,3,2:T(8,128)}, s32[6]{0:T(128)S(1)}, /*index=5*...) while((s32[]{:T(128)}, f32[3200,4,64]{0,2,1:T(8,128)}, ...), condition=%wide.region_18.19_spmd, body=%wide.region_16.18_spmd.sunk | while | flops 860781056 | bytes 76294080 | solution.py:165
  1067.5 4.3 fusion.172
  1074.6 4.1 multiply_reduce_fusion.3
  1082.8 11.5 dynamic_update_slice.45
  1097.0 5.3 fusion.175
  1103.6 4.2 fusion.172
  1110.6 4.3 multiply_reduce_fusion.3
  1119.6 11.6 dynamic_update_slice.45
  1133.8 5.2 fusion.175
  1140.4 4.2 fusion.172
  1147.4 4.2 multiply_reduce_fusion.3
  1155.7 11.5 dynamic_update_slice.45
  1169.8 5.2 fusion.175
  1176.4 4.2 fusion.172
  1183.4 4.1 multiply_reduce_fusion.3
  1191.5 11.5 dynamic_update_slice.45
  1205.6 5.2 fusion.175
  1212.2 4.2 fusion.172
  1219.2 4.1 multiply_reduce_fusion.3
  1227.3 11.5 dynamic_update_slice.45
  1241.4 5.2 fusion.175
  1248.0 4.2 fusion.172
  1254.9 4.1 multiply_reduce_fusion.3
  1263.1 11.5 dynamic_update_slice.45
  1277.2 5.2 fusion.175
  1282.4 5.5 reshape.338
  1299.0 5.7 fusion.122
  1305.0 10.7 fusion.72
  1317.1 8.6 bitcast_convert_fusion
  1332.0 6.9 reduce-scatter.22.cloned.1.call-done
  1340.7 48.2 %reduce-scatter.20.cloned.1.call-done = f32[128,3,256]{2,0,1:T(8,128)} async-done(((f32[1024,3,256]{2,0,1:T(8,128)}), f32[128,3,256]{2,0,1:T(8,128)}) %reduce-scatter.20.cloned.1.call-update) | async-done | bytes 393232 | tf_op jit(solution)/shard_map/reduce_scatter | solution.py:306
  1391.4 110.6 %reduce-scatter.18.cloned.1.call-done = bf16[768,1024]{1,0:T(8,128)(2,1)} async-done(((bf16[3072,1024]{1,0:T(8,128)(2,1)}), bf16[768,1024]{1,0:T(8,128)(2,1)}) %reduce-scatter.18.cloned.1.call-update) | async-done | bytes 1572880 | tf_op jit(solution)/shard_map/reduce_scatter | solution.py:180
  1507.4 4.3 add_add_fusion.2
  1511.7 30.5 %reduce-scatter.28.cloned.1.call-done = f32[128,2]{1,0:T(8,128)} async-done(((f32[1024,2]{1,0:T(8,128)}), f32[128,2]{1,0:T(8,128)}) %reduce-scatter.28.cloned.1.call-update) | async-done | bytes 1040
  1543.1 11.7 psum.8
  (341 shorter events, 176.3 us)
Async XLA Ops:
  7.2 14.6 copy-start
  7.2 33.3 %all-gather.10.cloned.1.call-start = ((), (), s32[]{:S(2)}) async-start(), calls=%async_computation.10 | async-start | bytes 1769472 | tf_op jit(solution)/shard_map/all_gather | solution.py:227
  9.2 148.9 %all-gather.8.cloned.1.call-start = ((), (), s32[]{:S(2)}) async-start(), calls=%async_computation.9 | async-start | bytes 7864320 | tf_op jit(solution)/shard_map/all_gather | solution.py:176
  21.9 3.7 copy-start.26
  25.3 331.3 %reduce-scatter.12.cloned.1.call-start = ((), (), s32[]{:S(2)}) async-start(), calls=%async_computation.11 | async-start | bytes 7864320 | tf_op jit(solution)/shard_map/reduce_scatter | solution.py:180
  40.2 126.4 %copy-start.12 = (f32[3072,32]{0,1:T(8,128)}, f32[3072,32]{0,1:T(8,128)S(1)}, u32[]{:S(2)}) copy-start(f32[3072,32]{0,1:T(8,128)S(1)} %get-tuple-element.345) | copy-start | bytes 1179652
  40.2 126.4 %copy-start.13 = (f32[3072,32]{0,1:T(8,128)}, f32[3072,32]{0,1:T(8,128)S(1)}, u32[]{:S(2)}) copy-start(f32[3072,32]{0,1:T(8,128)S(1)} %get-tuple-element.346) | copy-start | bytes 1179652
  238.2 3.6 copy-start.7
  238.2 4.8 copy-start.16
  247.5 136.9 %all-gather.16.cloned.1.call-start = ((), (), s32[]{:S(2)}) async-start(), calls=%async_computation.14 | async-start | bytes 1511424 | tf_op jit(solution)/shard_map/all_gather | solution.py:254
  249.2 252.0 %all-gather.18.cloned.1.call-start = ((), (), s32[]{:S(2)}) async-start(), calls=%async_computation.16 | async-start | bytes 7864320 | tf_op jit(solution)/shard_map/all_gather | solution.py:176
  249.8 282.8 %all-gather.14.cloned.1.call-start = ((), (), s32[]{:S(2)}) async-start(), calls=%async_computation.13 | async-start | bytes 3022848 | tf_op jit(solution)/shard_map/all_gather | solution.py:253
  250.6 399.5 %all-gather.12.cloned.1.call-start = ((), (), s32[]{:S(2)}) async-start(), calls=%async_computation.12 | async-start | bytes 7864320 | tf_op jit(solution)/shard_map/all_gather | solution.py:176
  361.3 458.8 %reduce-scatter.16.cloned.1.call-start = ((), (), s32[]{:S(2)}) async-start(), calls=%async_computation.17 | async-start | bytes 7864320 | tf_op jit(solution)/shard_map/reduce_scatter | solution.py:180
  650.1 12.2 copy-start.4
  662.3 20.6 %copy-start.2 = (f32[3072,2,656]{0,2,1:T(8,128)}, f32[3072,2,656]{0,2,1:T(8,128)S(1)}, u32[]{:S(2)}) copy-start(f32[3072,2,656]{0,2,1:T(8,128)S(1)} %fusion.70) | copy-start | bytes 48365572
  711.0 222.8 %reduce-scatter.14.cloned.1.call-start = ((), (), s32[]{:S(2)}) async-start(), calls=%async_computation.15 | async-start | bytes 7864320 | tf_op jit(solution)/shard_map/reduce_scatter | solution.py:180
  720.0 337.3 %all-gather.20.cloned.1.call-start = ((), (), s32[]{:S(2)}) async-start(), calls=%async_computation.18 | async-start | bytes 7864320 | tf_op jit(solution)/shard_map/all_gather | solution.py:176
  933.7 5.9 copy-start.9
  941.3 384.6 %reduce-scatter.26.cloned.1.call-start = ((), (), s32[]{:S(2)}) async-start(), calls=%async_computation.23 | async-start | bytes 3022848 | tf_op jit(solution)/shard_map/reduce_scatter | solution.py:309
  951.4 377.5 %reduce-scatter.24.cloned.1.call-start = ((), (), s32[]{:S(2)}) async-start(), calls=%async_computation.22 | async-start | bytes 6045696 | tf_op jit(solution)/shard_map/reduce_scatter | solution.py:308
  966.2 91.1 %copy-start.17 = (bf16[1024,256]{1,0:T(8,128)(2,1)S(1)}, bf16[1024,256]{1,0:T(8,128)(2,1)}, u32[]{:S(2)}) copy-start(bf16[1024,256]{1,0:T(8,128)(2,1)} %all_gather.34) | copy-start | bytes 1572868
  966.2 372.7 %reduce-scatter.22.cloned.1.call-start = ((), (), s32[]{:S(2)}) async-start(), calls=%async_computation.21 | async-start | bytes 1179648 | tf_op jit(solution)/shard_map/reduce_scatter | solution.py:307
  1066.2 12.5 copy-start.23
  1074.6 4.1 slice-start
  1074.6 4.1 slice-start.1
  1097.0 5.3 copy-start.24
  1102.3 12.7 copy-start.23
  1110.6 4.5 slice-start
  1110.6 5.0 slice-start.1
  1133.8 5.2 copy-start.24
  1139.1 12.5 copy-start.23
  1147.4 4.2 slice-start
  1147.4 4.2 slice-start.1
  1169.8 5.2 copy-start.24
  1175.1 12.4 copy-start.23
  1183.4 4.1 slice-start
  1183.4 4.1 slice-start.1
  1205.6 5.2 copy-start.24
  1210.9 12.4 copy-start.23
  1219.2 4.1 slice-start
  1219.2 4.1 slice-start.1
  1241.4 5.2 copy-start.24
  1246.6 12.4 copy-start.23
  1254.9 4.1 slice-start
  1254.9 4.1 slice-start.1
  1277.2 5.2 copy-start.24
  1282.4 5.5 copy-start.5
  1294.9 4.2 copy-start.11
  1299.0 6.0 copy-start.18
  1304.8 84.2 %reduce-scatter.20.cloned.1.call-start = ((), (), s32[]{:S(2)}) async-start(), calls=%async_computation.20 | async-start | bytes 3538944 | tf_op jit(solution)/shard_map/reduce_scatter | solution.py:306
  1315.7 186.3 %reduce-scatter.18.cloned.1.call-start = ((), (), s32[]{:S(2)}) async-start(), calls=%async_computation.19 | async-start | bytes 7864320 | tf_op jit(solution)/shard_map/reduce_scatter | solution.py:180
  1325.7 13.1 copy-start.27
  1325.8 216.4 %reduce-scatter.28.cloned.1.call-start = ((), (), s32[]{:S(2)}) async-start(), calls=%async_computation.24 | async-start | bytes 589824
  1328.9 60.0 %copy-start.20 = (f32[128,3,256]{2,0,1:T(8,128)S(1)}, f32[128,3,256]{2,0,1:T(8,128)}, u32[]{:S(2)}) copy-start(f32[128,3,256]{2,0,1:T(8,128)} %param.25) | copy-start | bytes 1179652
  1329.0 173.0 %copy-start.1 = (bf16[768,1024]{1,0:T(8,128)(2,1)S(1)}, bf16[768,1024]{1,0:T(8,128)(2,1)}, u32[]{:S(2)}) copy-start(bf16[768,1024]{1,0:T(8,128)(2,1)} %param.22) | copy-start | bytes 4718596
  1329.0 173.0 %copy-start.31 = (f32[768]{0:T(1024)S(1)}, f32[768]{0:T(1024)}, u32[]{:S(2)}) copy-start(f32[768]{0:T(1024)} %copy-done.30) | copy-start | bytes 9220
  1329.0 173.0 %copy-start.33 = (f32[1,1024]{1,0:T(1,128)S(1)}, f32[1,1024]{1,0:T(1,128)}, u32[]{:S(2)}) copy-start(f32[1,1024]{1,0:T(1,128)} %copy-done.32) | copy-start | bytes 12292
  1340.7 163.6 %copy-start.37 = (f32[768]{0:T(1024)S(1)}, f32[768]{0:T(1024)}, u32[]{:S(2)}) copy-start(f32[768]{0:T(1024)} %copy-done.36) | copy-start | bytes 9220
  1340.7 163.6 %copy-start.35 = (f32[768]{0:T(1024)S(1)}, f32[768]{0:T(1024)}, u32[]{:S(2)}) copy-start(f32[768]{0:T(1024)} %copy-done.34) | copy-start | bytes 9220
  1391.4 114.9 %copy-start.38 = (f32[1024]{0:T(1024)S(1)}, f32[1024]{0:T(1024)}, u32[]{:S(2)}) copy-start(f32[1024]{0:T(1024)} %get-tuple-element.263) | copy-start | bytes 12292
  1507.4 47.4 %copy-start.39 = (f32[2,128]{1,0:T(2,128)S(1)}, f32[2,128]{1,0:T(2,128)}, u32[]{:S(2)}) copy-start(f32[2,128]{1,0:T(2,128)} %param.29) | copy-start | bytes 3076
  1507.4 47.3 %copy-start.40 = (f32[2,128]{1,0:T(2,128)S(1)}, f32[2,128]{1,0:T(2,128)}, u32[]{:S(2)}) copy-start(f32[2,128]{1,0:T(2,128)} %param.39) | copy-start | bytes 3076
  1507.4 47.3 %copy-start.41 = (f32[2,128]{1,0:T(2,128)S(1)}, f32[2,128]{1,0:T(2,128)}, u32[]{:S(2)}) copy-start(f32[2,128]{1,0:T(2,128)} %param.38) | copy-start | bytes 3076
  (17 other events, 28.2 us)
Sparse Core Ops, SparseCore 0:
  10.5 29.9 all-gather.9
  42.7 115.3 all-gather.7
  247.6 108.9 reduce-scatter.11
  359.0 25.3 all-gather.15
  385.8 115.3 all-gather.17
  503.5 29.0 all-gather.13
  534.7 115.3 all-gather.11
  711.1 108.9 reduce-scatter.15
  822.4 111.2 reduce-scatter.13
  941.4 115.8 all-gather.19
  1060.7 42.8 reduce-scatter.25
  1106.9 57.1 reduce-scatter.23
  1304.9 33.9 reduce-scatter.21
  1342.7 46.2 reduce-scatter.19
  1391.2 110.7 reduce-scatter.17
  1507.5 34.6 reduce-scatter.27
where the time goes:
time: 1580 us; the launch traced here: 1560 us
  waiting for transfers between devices  1000 us (63%)
  matrix products  256 us (16%)
  local copies, waits for them, and re-layouts  139 us (9%)
  other arithmetic  108 us (7%)
  blocking collectives  34.1 us (2%)
    all_gather x4, waiting for transfers between devices, gather_rows(): return lax.all_gather(rows_low, 'tensor', axis=0, tiled=True)  443 us
    reduce_scatter x4, waiting for transfers between devices, sum_rows(): lax.psum_scatter(jnp.einsum('tj,oj->to', left_low, weight_low, preferred_...  427 us
    dynamic_update_slice x12, local copies, waits for them, and re-layouts, attend_forward(): lax.scan(step_block, 0, jnp.arange(block_count))  72.4 us
    reduce_scatter x1, waiting for transfers between devices, local(): lax.psum_scatter(grad_qkv, 'dp', scatter_dimension=0, tiled=True)  48.2 us
    dot_general x12, matrix products, step_block(): jnp.einsum('qhd,khd->hqk', query_block, key_block, preferred_element_type...  38.9 us
    dot_general x4, matrix products, sum_rows(): jnp.einsum('tj,oj->to', left_low, weight_low, preferred_element_type=jnp....  37.1 us
    another operation x2, other arithmetic, local(): jnp.stack([grad_gate_in, grad_gate_up], axis=1).astype(jnp.bfloat16)  33.6 us
  transfers between devices with their start and end apart: 16, of which 14 were waited for; matrix products, arithmetic and copies ran while one was open for 21% of the time, Pallas kernels for 0%

commit v1 on v0

v1 whole, which is shorter than its diff:
```python
import jax
import jax.numpy as jnp
from jax import lax
from jax.sharding import PartitionSpec as P

D = 1024
HEADS = 16
HEAD_DIM = 64
FF = 2624
HALF = 64
BLOCK = 128
STEP = 10

NORM_EPS = 1e-05
THETA_BASE = 10000.0
BETA_ONE = 0.9
BETA_TWO = 0.98
ADAM_EPS = 1e-06
WEIGHT_DECAY = 0.01
GAIN_RATE = 0.5
MASKED = -1e30


def layer_norm(values, gain_row):
    mean_value = jnp.mean(values, axis=-1, keepdims=True)
    centered = values - mean_value
    variance = jnp.mean(centered * centered, axis=-1, keepdims=True)
    return centered * lax.rsqrt(variance + NORM_EPS) * gain_row


def geglu(gate_in, gate_up):
    return jax.nn.gelu(gate_in, approximate=False) * gate_up


def layout(lengths, token_index, group_rows):
    seq_ends = jnp.cumsum(lengths)
    seq_starts = seq_ends - lengths
    segment = jnp.sum((token_index[:, None] >= seq_ends[None, :]).astype(jnp.int32), axis=1)
    member = segment[:, None] == jnp.arange(lengths.shape[0])[None, :]
    position = token_index - jnp.sum(jnp.where(member, seq_starts[None, :], 0), axis=1)
    inside = (token_index >= 0) & (token_index < group_rows)
    return (jnp.where(inside, segment, -1), jnp.where(inside, position, 0))


def rotary_tables(position):
    half_dim = HEAD_DIM // 2
    exponent = jnp.arange(half_dim).astype(jnp.float32) * (2.0 / HEAD_DIM)
    inverse = jnp.power(jnp.float32(THETA_BASE), -exponent)
    angle_table = position.astype(jnp.float32)[:, None] * inverse[None, :]
    return (jnp.cos(angle_table), jnp.sin(angle_table))


def rotate(values, cosine_table, sine_table):
    half_dim = values.shape[-1] // 2
    front_half = values[..., :half_dim]
    back_half = values[..., half_dim:]
    cos_rows = cosine_table[:, None, :]
    sin_rows = sine_table[:, None, :]
    return jnp.concatenate(
        [
            front_half * cos_rows - back_half * sin_rows,
            back_half * cos_rows + front_half * sin_rows,
        ],
        axis=-1,
    )


def windows(rows):
    count = (rows.shape[0] - 2 * HALF) // BLOCK
    return jnp.stack([rows[n * BLOCK : n * BLOCK + BLOCK + 2 * HALF] for n in range(count)])


def unwindows(parts):
    count = parts.shape[0]
    total = jnp.zeros((count * BLOCK + 2 * HALF,) + parts.shape[2:], parts.dtype)
    for n in range(count):
        total = total.at[n * BLOCK : n * BLOCK + BLOCK + 2 * HALF].add(parts[n])
    return total


def allowed_pairs(segment):
    key_seg = windows(segment)
    query_seg = segment[HALF:-HALF].reshape(-1, BLOCK)
    offset = jnp.arange(BLOCK)[:, None] + HALF - jnp.arange(BLOCK + 2 * HALF)[None, :]
    return (query_seg[:, :, None] == key_seg[:, None, :]) & (jnp.abs(offset) <= HALF)[None]


def attend_forward(queries, key_rows, values, allowed):
    score_scale = HEAD_DIM ** (-0.5)
    query_blocks = queries.reshape(-1, BLOCK, HEADS, HEAD_DIM)
    scores = (
        jnp.einsum(
            "nqhd,nkhd->nhqk", query_blocks, windows(key_rows), preferred_element_type=jnp.float32
        )
        * score_scale
    )
    scores = jnp.where(allowed[:, None], scores, MASKED)
    row_top = jnp.max(scores, axis=-1, keepdims=True)
    lifted = jnp.exp(scores - row_top)
    row_total = jnp.sum(lifted, axis=-1, keepdims=True)
    probs_low = (lifted / row_total).astype(jnp.bfloat16)
    block_out = jnp.einsum(
        "nhqk,nkhd->nqhd", probs_low, windows(values), preferred_element_type=jnp.float32
    )
    return (block_out.reshape(queries.shape), row_top + jnp.log(row_total))


def attend_backward(queries, key_rows, values, allowed, log_totals, grad_output):
    score_scale = HEAD_DIM ** (-0.5)
    query_blocks = queries.reshape(-1, BLOCK, HEADS, HEAD_DIM)
    grad_blocks = grad_output.reshape(-1, BLOCK, HEADS, HEAD_DIM)
    key_blocks = windows(key_rows)
    scores = (
        jnp.einsum("nqhd,nkhd->nhqk", query_blocks, key_blocks, preferred_element_type=jnp.float32)
        * score_scale
    )
    scores = jnp.where(allowed[:, None], scores, MASKED)
    attention_probs = jnp.exp(scores - log_totals)
    grad_probs = jnp.einsum(
        "nqhd,nkhd->nhqk", grad_blocks, windows(values), preferred_element_type=jnp.float32
    )
    row_delta = jnp.sum(attention_probs * grad_probs, axis=-1, keepdims=True)
    grad_scores = (attention_probs * (grad_probs - row_delta)).astype(jnp.bfloat16)
    grad_query = (
        jnp.einsum("nhqk,nkhd->nqhd", grad_scores, key_blocks, preferred_element_type=jnp.float32)
        * score_scale
    )
    grad_key = (
        jnp.einsum("nhqk,nqhd->nkhd", grad_scores, query_blocks, preferred_element_type=jnp.float32)
        * score_scale
    )
    grad_value = jnp.einsum(
        "nhqk,nqhd->nkhd",
        attention_probs.astype(jnp.bfloat16),
        grad_blocks,
        preferred_element_type=jnp.float32,
    )
    return (grad_query.reshape(queries.shape), unwindows(grad_key), unwindows(grad_value))


def adam_update(master, gradient, moment_one, moment_two, step_rate):
    one_new = BETA_ONE * moment_one + (1.0 - BETA_ONE) * gradient
    two_new = BETA_TWO * moment_two + (1.0 - BETA_TWO) * gradient * gradient
    one_hat = one_new / (1.0 - BETA_ONE**STEP)
    two_hat = two_new / (1.0 - BETA_TWO**STEP)
    master_new = master - step_rate * (
        one_hat / (jnp.sqrt(two_hat) + ADAM_EPS) + WEIGHT_DECAY * master
    )
    return (one_new, two_new, master_new)


def dot(left, right, left_dims, right_dims):
    return lax.dot_general(
        left, right, ((left_dims, right_dims), ((), ())), preferred_element_type=jnp.float32
    )


def gather(slab):
    return lax.all_gather(lax.all_gather(slab, "tensor", axis=0), "dp", axis=0)


def scatter(parts):
    return lax.psum_scatter(
        lax.psum_scatter(parts, "dp", scatter_dimension=0, tiled=False),
        "tensor",
        scatter_dimension=0,
        tiled=False,
    )


def shift(rows, step):
    size = lax.axis_size("tensor")
    pairs = [(n, n + step) for n in range(size) if 0 <= n + step < size]
    return lax.ppermute(rows, "tensor", pairs)


def local(
    hidden_in,
    seq_lengths,
    cotangent,
    w_qkv,
    w_proj,
    w_in,
    w_down,
    norm_gains,
    qkv_first,
    qkv_second,
    proj_first,
    proj_second,
    in_first,
    in_second,
    down_first,
    down_second,
    gain_first,
    gain_second,
):
    row_count = hidden_in.shape[0]
    tensor_size = lax.axis_size("tensor")
    group_rows = row_count * tensor_size
    low = jnp.bfloat16

    def slab(weight):
        return weight.reshape(weight.shape[0], -1).T.astype(low)

    def whole(weight, kinds):
        gathered = gather(slab(weight))
        dp_size, tp_size, wide, chunk = gathered.shape
        full = gathered.reshape(dp_size, tp_size, kinds, wide // kinds, chunk)
        return jnp.transpose(full, (2, 1, 3, 0, 4)).reshape(
            kinds, tp_size * wide // kinds, dp_size * chunk
        )

    def split(grad):
        kinds, wide, depth = grad.shape
        dp_size = lax.axis_size("dp")
        parts = grad.astype(low).reshape(
            kinds, tensor_size, wide // tensor_size, dp_size, depth // dp_size
        )
        parts = jnp.transpose(parts, (3, 1, 0, 2, 4)).reshape(
            dp_size, tensor_size, kinds * wide // tensor_size, depth // dp_size
        )
        return scatter(parts).astype(jnp.float32).T

    gains_full = lax.all_gather(norm_gains.astype(low), "dp", axis=1, tiled=True).astype(
        jnp.float32
    )
    edges = (shift(hidden_in[-HALF:], 1), shift(hidden_in[:HALF], -1))
    qkv_full = whole(w_qkv, 3)
    proj_full = whole(w_proj, 1)[0]
    in_full = whole(w_in, 2)
    down_full = whole(w_down, 1)[0]

    first_row = lax.axis_index("tensor") * row_count
    segment, position = layout(
        seq_lengths[0], first_row - HALF + jnp.arange(row_count + 2 * HALF), group_rows
    )
    cosine_table, sine_table = rotary_tables(position)
    allowed = allowed_pairs(segment)

    hidden = hidden_in.astype(jnp.float32)
    normed_one, norm_pull_one = jax.vjp(layer_norm, hidden, gains_full[0])
    normed_edges = layer_norm(jnp.concatenate(edges).astype(jnp.float32), gains_full[0])
    rows_one = normed_one.astype(low)
    rows_edges = normed_edges.astype(low)
    rows_wide = jnp.concatenate([rows_edges[:HALF], rows_one, rows_edges[HALF:]])
    query_pre = dot(rows_one, qkv_full[0], (1,), (1,))
    key_pre = dot(rows_wide, qkv_full[1], (1,), (1,))
    values = dot(rows_wide, qkv_full[2], (1,), (1,)).astype(low).reshape(-1, HEADS, HEAD_DIM)

    def rotate_pair(query_pre, key_pre):
        return (
            rotate(
                query_pre.reshape(-1, HEADS, HEAD_DIM),
                cosine_table[HALF:-HALF],
                sine_table[HALF:-HALF],
            ),
            rotate(key_pre.reshape(-1, HEADS, HEAD_DIM), cosine_table, sine_table),
        )

    (query_turned, key_turned), turn_pull = jax.vjp(rotate_pair, query_pre, key_pre)
    queries = query_turned.astype(low)
    key_rows = key_turned.astype(low)
    attended_heads, log_totals = attend_forward(queries, key_rows, values, allowed)
    attended = attended_heads.reshape(row_count, D).astype(low)
    middle = hidden + dot(attended, proj_full, (1,), (0,))
    normed_two, norm_pull_two = jax.vjp(layer_norm, middle, gains_full[1])
    rows_two = normed_two.astype(low)
    gate_in = dot(rows_two, in_full[0], (1,), (1,))
    gate_up = dot(rows_two, in_full[1], (1,), (1,))
    active_full, geglu_pull = jax.vjp(geglu, gate_in, gate_up)
    active = active_full.astype(low)
    output = middle + dot(active, down_full, (1,), (0,))

    grad_active = dot(cotangent, down_full, (1,), (1,))
    down_sum = split(dot(active, cotangent, (0,), (0,))[None]).reshape(w_down.shape)
    grad_gate_in, grad_gate_up = geglu_pull(grad_active)
    grad_gate_in = grad_gate_in.astype(low)
    grad_gate_up = grad_gate_up.astype(low)
    in_sum = split(
        jnp.stack(
            [
                dot(grad_gate_in, rows_two, (0,), (0,)),
                dot(grad_gate_up, rows_two, (0,), (0,)),
            ]
        )
    ).reshape(w_in.shape)
    grad_normed_two = dot(grad_gate_in, in_full[0], (1,), (0,)) + dot(
        grad_gate_up, in_full[1], (1,), (0,)
    )
    grad_middle_norm, grad_gain_two = norm_pull_two(grad_normed_two)
    grad_middle = cotangent.astype(jnp.float32) + grad_middle_norm
    grad_middle_low = grad_middle.astype(low)
    grad_attended = dot(grad_middle_low, proj_full, (1,), (1,)).astype(low)
    proj_sum = split(dot(attended, grad_middle_low, (0,), (0,))[None]).reshape(w_proj.shape)
    grad_queries, grad_keys, grad_values = attend_backward(
        queries,
        key_rows,
        values,
        allowed,
        log_totals,
        grad_attended.reshape(row_count, HEADS, HEAD_DIM),
    )
    grad_query_pre, grad_key_pre = turn_pull((grad_queries, grad_keys))
    grad_pair = jnp.stack([grad_key_pre, grad_values.reshape(-1, D)])
    from_after = shift(grad_pair[:, :HALF].astype(low), -1).astype(jnp.float32)
    from_before = shift(grad_pair[:, -HALF:].astype(low), 1).astype(jnp.float32)
    grad_pair = grad_pair[:, HALF:-HALF]
    grad_pair = grad_pair.at[:, :HALF].add(from_before).at[:, -HALF:].add(from_after)
    grad_mixed = jnp.concatenate([grad_query_pre[None], grad_pair]).astype(low)
    qkv_sum = split(
        jnp.stack([dot(grad_mixed[c], rows_one, (0,), (0,)) for c in range(3)])
    ).reshape(w_qkv.shape)
    grad_normed_one = sum(dot(grad_mixed[c], qkv_full[c], (1,), (0,)) for c in range(3))
    grad_hidden_norm, grad_gain_one = norm_pull_one(grad_normed_one)
    grad_input = grad_middle + grad_hidden_norm
    gain_sum = lax.psum(
        lax.psum_scatter(
            jnp.stack([grad_gain_one, grad_gain_two]), "dp", scatter_dimension=1, tiled=True
        ),
        "tensor",
    )
    qkv_one, qkv_two, qkv_new = adam_update(w_qkv, qkv_sum, qkv_first, qkv_second, D ** (-0.5))
    proj_one, proj_two, proj_new = adam_update(
        w_proj, proj_sum, proj_first, proj_second, (D // HALF) ** (-0.5)
    )
    in_one, in_two, in_new = adam_update(w_in, in_sum, in_first, in_second, D ** (-0.5))
    down_one, down_two, down_new = adam_update(
        w_down, down_sum, down_first, down_second, (FF // 2) ** (-0.5)
    )
    gain_one, gain_two, gains_new = adam_update(
        norm_gains, gain_sum, gain_first, gain_second, GAIN_RATE
    )
    return (
        output.astype(jnp.bfloat16),
        grad_input,
        qkv_one,
        qkv_two,
        qkv_new,
        proj_one,
        proj_two,
        proj_new,
        in_one,
        in_two,
        in_new,
        down_one,
        down_two,
        down_new,
        gain_one,
        gain_two,
        gains_new,
    )


def solution(mesh):
    placed = (
        P(("dp", "tensor"), None),
        P("dp", None),
        P(("dp", "tensor"), None),
        P("dp", None, "tensor"),
        P("dp", "tensor"),
        P("dp", None, "tensor"),
        P("dp", "tensor"),
        P(None, "dp"),
        P("dp", None, "tensor"),
        P("dp", None, "tensor"),
        P("dp", "tensor"),
        P("dp", "tensor"),
        P("dp", None, "tensor"),
        P("dp", None, "tensor"),
        P("dp", "tensor"),
        P("dp", "tensor"),
        P(None, "dp"),
        P(None, "dp"),
    )
    return jax.shard_map(
        local,
        mesh=mesh,
        in_specs=placed,
        out_specs=(
            P(("dp", "tensor"), None),
            P(("dp", "tensor"), None),
            P("dp", None, "tensor"),
            P("dp", None, "tensor"),
            P("dp", None, "tensor"),
            P("dp", "tensor"),
            P("dp", "tensor"),
            P("dp", "tensor"),
            P("dp", None, "tensor"),
            P("dp", None, "tensor"),
            P("dp", None, "tensor"),
            P("dp", "tensor"),
            P("dp", "tensor"),
            P("dp", "tensor"),
            P(None, "dp"),
            P(None, "dp"),
            P(None, "dp"),
        ),
        check_vma=False,
    )
```

time: 1580 us -> 773 us (0.49)
  waiting for transfers between devices: 1000 us -> 286 us
  matrix products: 256 us -> 141 us
  blocking collectives: 34.1 us -> 82 us
  other arithmetic: 108 us -> 75.1 us
  local copies, waits for them, and re-layouts: 139 us -> 158 us
    all_gather x7 -> x5, waiting for transfers between devices: 487 us -> 64.6 us  [gather(): return lax.all_gather(lax.all_gather(slab, 'tensor', axis=0), 'dp', axis=0)]
    reduce_scatter x8, waiting for transfers between devices: 482 us -> 194 us  [the longest x4 113 us: scatter(): lax.psum_scatter(parts, 'dp', scatter_dimension=0, tiled=False)]
    dot_general x54 -> x27, matrix products: 256 us -> 141 us  [the longest x21 113 us: dot(): lax.dot_general(left, right, ((left_dims, right_dims), ((), ())), preferr...]
    dynamic_update_slice x12 -> x0, local copies, waits for them, and re-layouts: 72.4 us -> none  [attend_forward(): lax.scan(step_block, 0, jnp.arange(block_count))]
    slice x3 -> x21, local copies, waits for them, and re-layouts: 3.5 us -> 52.3 us  [the longest x2 15.7 us: local(): gate_in = dot(rows_two, in_full[0], (1,), (1,))]
    all_gather x2 -> x4, blocking collectives: 22.4 us -> 70.3 us  [the longest x3 61.7 us: gather(): return lax.all_gather(lax.all_gather(slab, 'tensor', axis=0), 'dp', axis=0)]
    unnamed x86 -> x208, local copies, waits for them, and re-layouts: 11.9 us -> 42.5 us
    dynamic_slice x36 -> x0, local copies, waits for them, and re-layouts: 26 us -> none  [the longest x12 9.29 us: block_mask(): lax.dynamic_slice_in_dim(segment_pad, block_first, BLOCK + 2 * HALF)]
  transfers between devices with their start and end apart: 16 -> 18, of which waited for: 14 -> 10; matrix products, arithmetic and copies ran while one was open for 21% -> 30% of each run, Pallas kernels for 0% -> 0%
where the time goes in v1:
time: 773 us; the launch traced here: 768 us
  waiting for transfers between devices  286 us (37%)
  local copies, waits for them, and re-layouts  158 us (20%)
  matrix products  141 us (18%)
  blocking collectives  82 us (11%)
  other arithmetic  75.1 us (10%)
  between operations  15.9 us (2%)
  starting transfers between devices  10.5 us (1%)
    dot_general x21, matrix products, dot(): lax.dot_general(left, right, ((left_dims, right_dims), ((), ())), preferr...  113 us
    reduce_scatter x4, waiting for transfers between devices, scatter(): lax.psum_scatter(parts, 'dp', scatter_dimension=0, tiled=False)  113 us
    reduce_scatter x4, waiting for transfers between devices, scatter(): lax.psum_scatter(lax.psum_scatter(parts, 'dp', scatter_dimension=0, tiled...  81.5 us
    all_gather x5, waiting for transfers between devices, gather(): return lax.all_gather(lax.all_gather(slab, 'tensor', axis=0), 'dp', axis=0)  64.6 us
    all_gather x3, blocking collectives, gather(): return lax.all_gather(lax.all_gather(slab, 'tensor', axis=0), 'dp', axis=0)  61.7 us
    unnamed x208, local copies, waits for them, and re-layouts  42.5 us
    unnamed x15, waiting for transfers between devices  26.4 us
    slice x2, local copies, waits for them, and re-layouts, local(): gate_in = dot(rows_two, in_full[0], (1,), (1,))  15.7 us
  transfers between devices with their start and end apart: 18, of which 10 were waited for; matrix products, arithmetic and copies ran while one was open for 30% of the time, Pallas kernels for 0%

profile of v1, /device:TPU:0, one launch (start us, length us, event | category | flops | bytes accessed | tf_op | source)
XLA Modules:
  0.0 768.3 jit_solution(6403718343607556176)
XLA Ops:
  10.1 16.7 %all-gather.2 = bf16[1024,128]{0,1:T(8,128)(2,1)S(1)} all-gather(bf16[256,128]{0,1:T(8,128)(2,1)S(1)} %convert_bitcast_fusion.7), channel_id=4, replica_groups=mesh['dp'=8,'tensor'=4] {'tensor'}, dimensions={0}, use_global_device_ids=true | all-gather | bytes 327680 | tf_op jit(solution)/shard_map/all_gather | solution.py:159
  28.9 26.9 %all-gather.6 = bf16[2624,128]{1,0:T(8,128)(2,1)} all-gather(bf16[656,128]{1,0:T(8,128)(2,1)S(1)} %convert_bitcast_fusion.5), channel_id=8, replica_groups=mesh['dp'=8,'tensor'=4] {'tensor'}, dimensions={0}, use_global_device_ids=true | all-gather | bytes 839680 | tf_op jit(solution)/shard_map/all_gather | solution.py:159
  56.1 18.1 %all-gather = bf16[3072,128]{1,0:T(8,128)(2,1)} all-gather(bf16[768,128]{1,0:T(8,128)(2,1)S(1)} %bitcast.469), channel_id=2, replica_groups=mesh['dp'=8,'tensor'=4] {'tensor'}, dimensions={0}, use_global_device_ids=true | all-gather | bytes 983040 | tf_op jit(solution)/shard_map/all_gather | solution.py:159
  75.6 2.9 collective-permute-start
  81.6 8.5 %all_gather.51 = bf16[2,1024]{1,0:T(2,128)(2,1)S(1)} all-gather(bf16[2,128]{1,0:T(2,128)(2,1)S(1)} %convert_element_type.154), channel_id=1, replica_groups=mesh['dp'=8,'tensor'=4] {'dp'}, dimensions={1}, use_global_device_ids=true | all-gather | bytes 4608 | tf_op jit(solution)/shard_map/all_gather | solution.py:224
  101.4 4.4 copy.174
  105.8 25.5 %all-gather.22.cloned.1.call-done = bf16[32,656,128]{2,1,0:T(8,128)(2,1)} async-done(((bf16[4,656,128]{2,1,0:T(8,128)(2,1)}), bf16[32,656,128]{2,1,0:T(8,128)(2,1)}) %all-gather.22.cloned.1.call-update) | async-done | bytes 5373968 | tf_op jit(solution)/shard_map/all_gather | solution.py:159
  131.3 8.3 %copy.177 = bf16[1,4,656,8,128]{4,3,2,1,0:T(8,128)(2,1)} copy(bf16[1,4,656,8,128]{4,2,1,3,0:T(8,128)(2,1)} %bitcast.434) | data formatting | bytes 10747904 | tf_op jit(solution)/shard_map/transpose | solution.py:209
  139.6 39.0 %all-gather.14.cloned.1.call-done = bf16[32,768,128]{2,1,0:T(8,128)(2,1)} async-done(((bf16[4,768,128]{2,1,0:T(8,128)(2,1)}), bf16[32,768,128]{2,1,0:T(8,128)(2,1)}) %all-gather.14.cloned.1.call-update) | async-done | bytes 6291472 | tf_op jit(solution)/shard_map/all_gather | solution.py:159
  178.6 5.7 fusion.177
  184.4 2.7 copy.171
  187.0 4.3 dot_general.105
  191.3 4.3 copy.168
  195.5 4.5 dot_general.103
  200.1 3.0 copy.161
  214.2 4.6 fusion.68
  226.4 3.6 fusion.36
  230.0 4.7 fusion
  234.7 5.0 fusion.94
  245.5 9.4 %fusion.176 = (bf16[1,4,656,8,128]{4,2,0,1,3:T(8,128)(2,1)}, bf16[1,4,656,8,128]{4,2,0,1,3:T(8,128)(2,1)}) fusion(bf16[2,4,656,8,128]{4,2,0,1,3:T(8,128)(2,1)} %bitcast.424), kind=kLoop, calls=%fused_computation.294 | loop fusion | bytes 21495808 | tf_op jit(solution)/shard_map/slice | solution.py:268
  255.0 8.6 %copy.176 = bf16[1,4,656,8,128]{4,3,2,1,0:T(8,128)(2,1)} copy(bf16[1,4,656,8,128]{4,2,0,1,3:T(8,128)(2,1)} %get-tuple-element.279) | data formatting | bytes 10747904 | tf_op jit(solution)/shard_map/slice | solution.py:269
  263.5 6.2 copy.175
  269.8 7.4 fusion.20
  277.2 7.4 fusion.24
  284.7 24.0 %add_convert_fusion = (bf16[768,2624]{0,1:T(8,128)(2,1)}, f32[768,2624]{0,1:T(8,128)}, f32[768,2624]{0,1:T(8,128)}) fusion(f32[768,2624]{0,1:T(8,128)S(1)} %fusion.20, f32[768,2624]{0,1:T(8,128)S(1)} %fusion.24, bf16[768,1024]{1,0:T(8,128)(2,1)S(1)} %copy-done.22, bf16[328,8,8,128]{3,2,1,0:T(8,128)(2,1)S(1)} %bitcast.433), kind=kOutput, calls=%fused_computation.17 | convolution fusion | flops 4274307072 | bytes 43220992 | tf_op jit(solution)/shard_map/dot_general | solution.py:153
  308.8 12.4 %multiply_convert_fusion.1 = (bf16[768,2624]{0,1:T(8,128)(2,1)}, bf16[768,2624]{0,1:T(8,128)(2,1)}) fusion(f32[768,2624]{0,1:T(8,128)} %get-tuple-element.319, f32[768,2624]{0,1:T(8,128)} %get-tuple-element.275, f32[768,2624]{0,1:T(8,128)} %copy-done.21, f32[768,2624]{0,1:T(8,128)S(1)} %fusion.20), kind=kLoop, calls=%fused_computation.16 | loop fusion | flops 12091392 | bytes 40304640 | tf_op jit(solution)/shard_map/convert_element_type | solution.py:278
  321.2 8.3 %fusion.18 = f32[768,1024]{1,0:T(8,128)S(1)} fusion(bf16[768,2624]{0,1:T(8,128)(2,1)} %get-tuple-element.276, bf16[328,8,8,128]{3,2,1,0:T(8,128)(2,1)} %bitcast.438), kind=kOutput, calls=%fused_computation.47 | convolution fusion | flops 4127195136 | bytes 12550144 | tf_op jit(solution)/shard_map/dot_general | solution.py:153
  329.5 8.8 %multiply_reduce_fusion.1 = (f32[1024]{0:T(1024)}, f32[768]{0:T(1024)S(1)}, f32[768,1024]{1,0:T(8,128)S(1)}) fusion(f32[768,1024]{1,0:T(8,128)S(1)} %copy-done.6, f32[768]{0:T(1024)S(1)} %fusion.155, f32[768]{0:T(1024)S(1)} %broadcast_multiply_fusion, f32[1024]{0:T(1024)S(1)} %bitcast.480, f32[768,1024]{1,0:T(8,128)S(1)} %fusion.18, ...), kind=kOutput, calls=%fused_computation.80 | convolution fusion | flops 4133484800 | bytes 18859008 | tf_op jit(solution)/shard_map/dot_general | solution.py:153
  344.0 3.1 convert_bitcast_fusion
  347.1 3.3 reshape.854
  350.4 4.0 copy.179
  354.4 3.6 copy.218
  358.0 4.2 copy.192
  362.3 9.0 %multiply_reduce_fusion = (f32[6,16,128]{2,1,0:T(8,128)S(1)}, f32[6,16,128,256]{3,2,1,0:T(8,128)S(1)}) fusion(f32[6,16,128]{2,1,0:T(8,128)S(1)} %log_add_fusion, f32[6,16,128,256]{3,2,1,0:T(8,128)} %copy-done, pred[6,128,256]{2,1,0:T(8,128)(4,1)S(1)} %compare_and_fusion, bf16[6,128,16,64]{1,3,2,0:T(8,128)(2,1)S(1)} %copy.179, ...), kind=kOutput, calls=%fused_computation.1 | convolution fusion | flops 418369536 | bytes 30179328 | tf_op jit(solution)/shard_map/nqhd,nkhd->nhqk/dot_general | solution.py:119
  371.3 9.0 %multiply_convert_fusion = bf16[6,16,128,256]{3,2,1,0:T(8,128)(2,1)S(1)} fusion(f32[6,16,128,256]{3,2,1,0:T(8,128)S(1)} %get-tuple-element.322, f32[6,16,128]{2,1,0:T(8,128)S(1)} %get-tuple-element.321, f32[6,16,128]{2,1,0:T(8,128)S(1)} %log_add_fusion, f32[6,16,128,256]{3,2,1,0:T(8,128)} %copy-done, pred[6,128,256]{2,1,0:T(8,128)(4,1)S(1)} %compare_and_fusion), kind=kLoop, calls=%fused_computation | loop fusion | flops 18874368 | bytes 31752192 | tf_op jit(solution)/shard_map/convert_element_type | solution.py:123
  380.3 2.3 multiply_bitcast_fusion.1
  386.4 6.2 fusion.48
  392.5 4.1 copy.221
  396.6 3.2 copy.304
  399.9 4.0 fusion.43
  404.0 2.6 scatter-add.56
  409.2 3.8 multiply_bitcast_fusion
  422.6 3.3 collective-permute-start.2
  432.2 4.3 fusion.11
  437.5 5.9 scatter-add.66
  445.2 6.0 scatter-add.69
  451.2 3.1 convert.61
  462.1 3.0 copy.188
  466.6 6.7 fusion.47
  477.0 4.6 fusion.46
  483.7 4.8 pad_maximum_fusion
  490.1 3.4 fusion.52
  495.7 2.7 fusion.42
  504.1 26.6 %reduce-scatter.12.cloned.1.call-done = bf16[1,4,768,128]{3,2,1,0:T(8,128)(2,1)} async-done(((bf16[8,4,768,128]{3,2,1,0:T(8,128)(2,1)}), bf16[1,4,768,128]{3,2,1,0:T(8,128)(2,1)}) %reduce-scatter.12.cloned.1.call-update) | async-done | bytes 786448 | tf_op jit(solution)/shard_map/reduce_scatter | solution.py:164
  531.1 85.9 %reduce-scatter.20.cloned.1.call-done = bf16[1,4,1312,128]{3,2,1,0:T(8,128)(2,1)} async-done(((bf16[8,4,1312,128]{3,2,1,0:T(8,128)(2,1)}), bf16[1,4,1312,128]{3,2,1,0:T(8,128)(2,1)}) %reduce-scatter.20.cloned.1.call-update) | async-done | bytes 1343504 | tf_op jit(solution)/shard_map/reduce_scatter | solution.py:164
  617.1 10.6 %add_convert_fusion.2 = bf16[768,1024]{1,0:T(8,128)(2,1)} fusion(f32[768,1024]{1,0:T(8,128)} %copy-done.5, bf16[768,2624]{0,1:T(8,128)(2,1)} %get-tuple-element.277, bf16[328,8,8,128]{3,2,1,0:T(8,128)(2,1)} %bitcast.430), kind=kOutput, calls=%fused_computation.87 | convolution fusion | flops 4128768000 | bytes 14123008 | tf_op jit(solution)/shard_map/dot_general | solution.py:153
  627.8 2.6 add_add_fusion.2
  630.5 24.5 %reduce-scatter.28.cloned.1.call-done = f32[128,2]{1,0:T(8,128)} async-done(((f32[1024,2]{1,0:T(8,128)}), f32[128,2]{1,0:T(8,128)}) %reduce-scatter.28.cloned.1.call-update) | async-done | bytes 1040
  655.9 11.7 %psum.7 = f32[2,128]{1,0:T(2,128)S(1)} all-reduce(f32[2,128]{1,0:T(2,128)S(1)} %copy.203), channel_id=1, replica_groups=mesh['dp'=8,'tensor'=4] {'tensor'}, use_global_device_ids=true, to_apply=%region_27.28 | all-reduce | flops 256 | bytes 2048 | tf_op jit(solution)/shard_map/psum | solution.py:316
  668.2 8.7 %reduce-scatter.18.cloned.1.call-done = bf16[1,256,128]{1,2,0:T(8,128)(2,1)} async-done(((bf16[4,256,128]{1,2,0:T(8,128)(2,1)}), bf16[1,256,128]{1,2,0:T(8,128)(2,1)}) %reduce-scatter.18.cloned.1.call-update) | async-done | bytes 65552 | tf_op jit(solution)/shard_map/reduce_scatter | solution.py:163
  678.7 21.2 %reduce-scatter.26.cloned.1.call-done = bf16[1,656,128]{2,1,0:T(8,128)(2,1)} async-done(((bf16[4,656,128]{2,1,0:T(8,128)(2,1)}), bf16[1,656,128]{2,1,0:T(8,128)(2,1)}) %reduce-scatter.26.cloned.1.call-update) | async-done | bytes 167952 | tf_op jit(solution)/shard_map/reduce_scatter | solution.py:163
  701.9 22.5 %reduce-scatter.14.cloned.1.call-done = bf16[1,768,128]{2,1,0:T(8,128)(2,1)} async-done(((bf16[4,768,128]{2,1,0:T(8,128)(2,1)}), bf16[1,768,128]{2,1,0:T(8,128)(2,1)}) %reduce-scatter.14.cloned.1.call-update) | async-done | bytes 196624 | tf_op jit(solution)/shard_map/reduce_scatter | solution.py:163
  728.5 29.1 %reduce-scatter.22.cloned.1.call-done = bf16[1,1312,128]{2,1,0:T(8,128)(2,1)} async-done(((bf16[4,1312,128]{2,1,0:T(8,128)(2,1)}), bf16[1,1312,128]{2,1,0:T(8,128)(2,1)}) %reduce-scatter.22.cloned.1.call-update) | async-done | bytes 335888 | tf_op jit(solution)/shard_map/reduce_scatter | solution.py:163
  758.6 2.9 multiply_subtract_fusion
  (357 shorter events, 110.3 us)
Async XLA Ops:
  7.2 48.7 %copy-start.58 = (f32[128,3,256]{2,0,1:T(8,128)S(1)}, f32[128,3,256]{2,0,1:T(8,128)}, u32[]{:S(2)}) copy-start(f32[128,3,256]{2,0,1:T(8,128)} %param.49) | copy-start | bytes 1179652
  7.2 67.1 %all-gather.18.cloned.1.call-start = ((), (), s32[]{:S(2)}) async-start(), calls=%async_computation.19 | async-start | bytes 1679360 | tf_op jit(solution)/shard_map/all_gather | solution.py:159
  9.2 92.2 %all-gather.16.cloned.1.call-start = ((), (), s32[]{:S(2)}) async-start(), calls=%async_computation.18 | async-start | bytes 2359296 | tf_op jit(solution)/shard_map/all_gather | solution.py:159
  27.7 47.2 %copy-start.3 = (bf16[768,1024]{1,0:T(8,128)(2,1)S(1)}, bf16[768,1024]{1,0:T(8,128)(2,1)}, u32[]{:S(2)}) copy-start(bf16[768,1024]{1,0:T(8,128)(2,1)} %param.46) | copy-start | bytes 4718596
  27.7 103.6 %all-gather.22.cloned.1.call-start = ((), (), s32[]{:S(2)}) async-start(), calls=%async_computation.21 | async-start | bytes 6045696 | tf_op jit(solution)/shard_map/all_gather | solution.py:159
  28.9 51.0 %copy-start.79 = (f32[2,128]{1,0:T(2,128)S(1)}, f32[2,128]{1,0:T(2,128)}, u32[]{:S(2)}) copy-start(f32[2,128]{1,0:T(2,128)} %param.53) | copy-start | bytes 3076
  28.9 51.0 %copy-start.83 = (s32[1,5]{1,0:T(1,128)S(1)}, s32[1,5]{1,0:T(1,128)}, u32[]{:S(2)}) copy-start(s32[1,5]{1,0:T(1,128)} %param.47) | copy-start | bytes 64
  55.8 122.8 %all-gather.14.cloned.1.call-start = ((), (), s32[]{:S(2)}) async-start(), calls=%async_computation.17 | async-start | bytes 7077888 | tf_op jit(solution)/shard_map/all_gather | solution.py:159
  56.0 34.4 %copy-start.26 = (f32[128,3,256]{0,2,1:T(8,128)}, f32[128,3,256]{0,2,1:T(8,128)S(1)}, u32[]{:S(2)}) copy-start(f32[128,3,256]{0,2,1:T(8,128)S(1)} %copy.160) | copy-start | bytes 1179652
  74.2 171.3 %all-gather.20.cloned.1.call-start = ((), (), s32[]{:S(2)}) async-start(), calls=%async_computation.20 | async-start | bytes 12091392 | tf_op jit(solution)/shard_map/all_gather | solution.py:159
  74.8 428.0 %reduce-scatter.16.cloned.1.call-start = ((), (), s32[]{:S(2)}) async-start(), calls=%async_computation.11 | async-start | bytes 2359296 | tf_op jit(solution)/shard_map/reduce_scatter | solution.py:164
  75.6 21.2 %collective-permute-start = (bf16[64,1024]{1,0:T(8,128)(2,1)}, bf16[64,1024]{1,0:T(8,128)(2,1)}, u32[]{:S(2)}, u32[]{:S(2)}) collective-permute-start(bf16[64,1024]{1,0:T(8,128)(2,1)} %get-tuple-element.301), channel_id=1, source_target_pairs={{0,1},{1,2},{2,3},{4,5},{5,6},{6,7},{8,9},{9,10},{10,11},{12,13},{... | collective-permute-start | bytes 393224 | tf_op jit(solution)/shard_map/ppermute | solution.py:174
  78.5 18.3 %collective-permute-start.1 = (bf16[64,1024]{1,0:T(8,128)(2,1)}, bf16[64,1024]{1,0:T(8,128)(2,1)}, u32[]{:S(2)}, u32[]{:S(2)}) collective-permute-start(bf16[64,1024]{1,0:T(8,128)(2,1)} %get-tuple-element.302), channel_id=1, source_target_pairs={{1,0},{2,1},{3,2},{5,4},{6,5},{7,6},{9,8},{10,9},{11,10},{13,12},{... | collective-permute-start | bytes 393224 | tf_op jit(solution)/shard_map/ppermute | solution.py:174
  80.7 11.5 %copy-start.42 = (f32[896,32]{0,1:T(8,128)}, f32[896,32]{0,1:T(8,128)S(1)}, u32[]{:S(2)}) copy-start(f32[896,32]{0,1:T(8,128)S(1)} %get-tuple-element.306) | copy-start | bytes 344068
  80.8 138.1 %copy-start.40 = (f32[896,32]{0,1:T(8,128)}, f32[896,32]{0,1:T(8,128)S(1)}, u32[]{:S(2)}) copy-start(f32[896,32]{0,1:T(8,128)S(1)} %get-tuple-element.305) | copy-start | bytes 344068
  80.9 144.6 %copy-start.53 = (f32[768,32]{0,1:T(8,128)}, f32[768,32]{0,1:T(8,128)S(1)}, u32[]{:S(2)}) copy-start(f32[768,32]{0,1:T(8,128)S(1)} %slice.604) | copy-start | bytes 294916
  95.2 4.3 copy-start.66
  96.6 106.5 %copy-start.47 = (bf16[768,1024]{1,0:T(8,128)(2,1)}, bf16[768,1024]{1,0:T(8,128)(2,1)S(1)}, u32[]{:S(2)}) copy-start(bf16[768,1024]{1,0:T(8,128)(2,1)S(1)} %fusion.39) | copy-start | bytes 4718596
  214.2 4.6 copy-start.43
  219.8 6.6 copy-start.10
  223.6 11.1 %copy-start.24 = (bf16[6,256,16,64]{1,3,2,0:T(8,128)(2,1)}, bf16[6,256,16,64]{1,3,2,0:T(8,128)(2,1)S(1)}, u32[]{:S(2)}) copy-start(bf16[6,256,16,64]{1,3,2,0:T(8,128)(2,1)S(1)} %constant_dynamic-update-slice_fusion) | copy-start | bytes 9437188
  230.0 4.7 copy-start
  245.5 31.7 %copy-start.49 = (bf16[768,1024]{1,0:T(8,128)(2,1)}, bf16[768,1024]{1,0:T(8,128)(2,1)S(1)}, u32[]{:S(2)}) copy-start(bf16[768,1024]{1,0:T(8,128)(2,1)S(1)} %multiply_convert_fusion.3) | copy-start | bytes 4718596
  255.0 8.6 %slice-start.5 = ((s8[5373952]{0:T(1024)(128)(4,1)}), s8[4194304]{0:T(1024)(128)(4,1)S(1)}, s32[]{:S(2)}) async-start(s8[5373952]{0:T(1024)(128)(4,1)} %bitcast.418), calls=%async_computation.28 | async-start | bytes 8388608
  255.0 8.6 %slice-start.6 = ((s8[5373952]{0:T(1024)(128)(4,1)}), s8[1179648]{0:T(1024)(128)(4,1)S(1)}, s32[]{:S(2)}) async-start(s8[5373952]{0:T(1024)(128)(4,1)} %bitcast.418), calls=%async_computation.29 | async-start | bytes 2359296
  269.8 14.9 %slice-start.7 = ((s8[5373952]{0:T(1024)(128)(4,1)}), s8[4194304]{0:T(1024)(128)(4,1)S(1)}, s32[]{:S(2)}) async-start(s8[5373952]{0:T(1024)(128)(4,1)} %bitcast.431), calls=%async_computation.30 | async-start | bytes 8388608
  277.2 7.5 copy-start.22
  277.2 7.5 slice-start.8
  284.7 24.1 %copy-start.21 = (f32[768,2624]{0,1:T(8,128)}, f32[768,2624]{0,1:T(8,128)S(1)}, u32[]{:S(2)}) copy-start(f32[768,2624]{0,1:T(8,128)S(1)} %fusion.24) | copy-start | bytes 24182788
  321.2 8.3 %copy-start.6 = (f32[768,1024]{1,0:T(8,128)S(1)}, f32[768,1024]{1,0:T(8,128)}, u32[]{:S(2)}) copy-start(f32[768,1024]{1,0:T(8,128)} %copy-done.5) | copy-start | bytes 9437188
  321.2 8.3 %copy-start.84 = (bf16[768,2624]{0,1:T(8,128)(2,1)S(1)}, bf16[768,2624]{0,1:T(8,128)(2,1)}, u32[]{:S(2)}) copy-start(bf16[768,2624]{0,1:T(8,128)(2,1)} %get-tuple-element.274) | copy-start | bytes 12091396
  362.3 141.3 %reduce-scatter.24.cloned.1.call-start = ((), (), s32[]{:S(2)}) async-start(), calls=%async_computation.15 | async-start | bytes 6045696 | tf_op jit(solution)/shard_map/reduce_scatter | solution.py:164
  371.3 9.1 %copy-start.11 = (bf16[6,256,16,64]{1,3,2,0:T(8,128)(2,1)S(1)}, bf16[6,256,16,64]{1,3,2,0:T(8,128)(2,1)}, u32[]{:S(2)}) copy-start(bf16[6,256,16,64]{1,3,2,0:T(8,128)(2,1)} %copy-done.10) | copy-start | bytes 9437188
  386.4 13.5 %slice-start = ((s8[12582912]{0:T(1024)(128)(4,1)}), s8[4194304]{0:T(1024)(128)(4,1)S(1)}, s32[]{:S(2)}) async-start(s8[12582912]{0:T(1024)(128)(4,1)} %bitcast.405), calls=%async_computation.23 | async-start | bytes 8388608
  386.4 13.5 %slice-start.1 = ((s8[12582912]{0:T(1024)(128)(4,1)}), s8[4194304]{0:T(1024)(128)(4,1)S(1)}, s32[]{:S(2)}) async-start(s8[12582912]{0:T(1024)(128)(4,1)} %bitcast.405), calls=%async_computation.24 | async-start | bytes 8388608
  392.5 7.4 slice-start.2
  407.9 122.9 %reduce-scatter.12.cloned.1.call-start = ((), (), s32[]{:S(2)}) async-start(), calls=%async_computation.9 | async-start | bytes 7077888 | tf_op jit(solution)/shard_map/reduce_scatter | solution.py:164
  421.1 6.6 copy-start.14
  421.1 6.6 copy-start.54
  421.1 6.6 copy-start.56
  422.6 14.6 %collective-permute-start.2 = (bf16[2,64,1024]{1,2,0:T(8,128)(2,1)S(1)}, bf16[2,64,1024]{1,2,0:T(8,128)(2,1)S(1)}, u32[]{:S(2)}, u32[]{:S(2)}) collective-permute-start(bf16[2,64,1024]{1,2,0:T(8,128)(2,1)S(1)} %get-tuple-element.288), channel_id=1, source_target_pairs={{0,1},{1,2},{2,3},{4,5},{5,6},{6,7},{8,9},{9,10},{10,11},{12,13},{... | collective-permute-start | bytes 786440 | tf_op jit(solution)/shard_map/ppermute | solution.py:174
  425.9 17.6 %collective-permute-start.3 = (bf16[2,64,1024]{1,2,0:T(8,128)(2,1)}, bf16[2,64,1024]{1,2,0:T(8,128)(2,1)}, u32[]{:S(2)}, u32[]{:S(2)}) collective-permute-start(bf16[2,64,1024]{1,2,0:T(8,128)(2,1)} %get-tuple-element.287), channel_id=1, source_target_pairs={{1,0},{2,1},{3,2},{5,4},{6,5},{7,6},{9,8},{10,9},{11,10},{13,12},{... | collective-permute-start | bytes 786440 | tf_op jit(solution)/shard_map/ppermute | solution.py:174
  465.2 151.9 %reduce-scatter.20.cloned.1.call-start = ((), (), s32[]{:S(2)}) async-start(), calls=%async_computation.13 | async-start | bytes 12091392 | tf_op jit(solution)/shard_map/reduce_scatter | solution.py:164
  488.6 166.5 %reduce-scatter.28.cloned.1.call-start = ((), (), s32[]{:S(2)}) async-start(), calls=%async_computation.22 | async-start | bytes 589824
  495.7 4.3 copy-start.71
  499.9 30.9 %copy-start.59 = (f32[128,3,256]{2,0,1:T(8,128)S(1)}, f32[128,3,256]{2,0,1:T(8,128)}, u32[]{:S(2)}) copy-start(f32[128,3,256]{2,0,1:T(8,128)} %param.54) | copy-start | bytes 1179652
  499.9 31.0 %copy-start.60 = (f32[128,3,256]{2,0,1:T(8,128)S(1)}, f32[128,3,256]{2,0,1:T(8,128)}, u32[]{:S(2)}) copy-start(f32[128,3,256]{2,0,1:T(8,128)} %param.55) | copy-start | bytes 1179652
  502.8 174.2 %reduce-scatter.18.cloned.1.call-start = ((), (), s32[]{:S(2)}) async-start(), calls=%async_computation.12 | async-start | bytes 327680 | tf_op jit(solution)/shard_map/reduce_scatter | solution.py:163
  503.5 196.4 %reduce-scatter.26.cloned.1.call-start = ((), (), s32[]{:S(2)}) async-start(), calls=%async_computation.16 | async-start | bytes 839680 | tf_op jit(solution)/shard_map/reduce_scatter | solution.py:163
  504.1 220.4 %reduce-scatter.14.cloned.1.call-start = ((), (), s32[]{:S(2)}) async-start(), calls=%async_computation.10 | async-start | bytes 983040 | tf_op jit(solution)/shard_map/reduce_scatter | solution.py:163
  530.7 226.9 %reduce-scatter.22.cloned.1.call-start = ((), (), s32[]{:S(2)}) async-start(), calls=%async_computation.14 | async-start | bytes 1679360 | tf_op jit(solution)/shard_map/reduce_scatter | solution.py:163
  617.1 10.7 %copy-start.8 = (f32[768,1024]{1,0:T(8,128)S(1)}, f32[768,1024]{1,0:T(8,128)}, u32[]{:S(2)}) copy-start(f32[768,1024]{1,0:T(8,128)} %copy-done.7) | copy-start | bytes 9437188
  617.1 10.7 %copy-start.16 = (f32[768,1024]{1,0:T(8,128)S(1)}, f32[768,1024]{1,0:T(8,128)}, u32[]{:S(2)}) copy-start(f32[768,1024]{1,0:T(8,128)} %copy-done.15) | copy-start | bytes 9437188
  617.1 10.6 %copy-start.23 = (bf16[768,1024]{1,0:T(8,128)(2,1)S(1)}, bf16[768,1024]{1,0:T(8,128)(2,1)}, u32[]{:S(2)}) copy-start(bf16[768,1024]{1,0:T(8,128)(2,1)} %param.48) | copy-start | bytes 4718596
  617.1 10.6 %copy-start.75 = (f32[768]{0:T(1024)S(1)}, f32[768]{0:T(1024)}, u32[]{:S(2)}) copy-start(f32[768]{0:T(1024)} %copy-done.74) | copy-start | bytes 9220
  627.8 39.9 %copy-start.80 = (f32[2,128]{1,0:T(2,128)S(1)}, f32[2,128]{1,0:T(2,128)}, u32[]{:S(2)}) copy-start(f32[2,128]{1,0:T(2,128)} %param.53) | copy-start | bytes 3076
  627.8 39.8 %copy-start.81 = (f32[2,128]{1,0:T(2,128)S(1)}, f32[2,128]{1,0:T(2,128)}, u32[]{:S(2)}) copy-start(f32[2,128]{1,0:T(2,128)} %param.63) | copy-start | bytes 3076
  627.8 39.8 %copy-start.82 = (f32[2,128]{1,0:T(2,128)S(1)}, f32[2,128]{1,0:T(2,128)}, u32[]{:S(2)}) copy-start(f32[2,128]{1,0:T(2,128)} %param.62) | copy-start | bytes 3076
  627.8 49.1 %copy-start.57 = (f32[128,256]{1,0:T(8,128)S(1)}, f32[128,256]{1,0:T(8,128)}, u32[]{:S(2)}) copy-start(f32[128,256]{1,0:T(8,128)} %param.50) | copy-start | bytes 393220
  627.8 72.1 %copy-start.52 = (f32[128,656]{0,1:T(8,128)S(1)}, f32[128,656]{0,1:T(8,128)}, u32[]{:S(2)}) copy-start(f32[128,656]{0,1:T(8,128)} %param.52) | copy-start | bytes 1007620
  627.8 72.1 %copy-start.61 = (f32[128,656]{0,1:T(8,128)S(1)}, f32[128,656]{0,1:T(8,128)}, u32[]{:S(2)}) copy-start(f32[128,656]{0,1:T(8,128)} %param.61) | copy-start | bytes 1007620
  627.8 72.1 %copy-start.62 = (f32[128,656]{0,1:T(8,128)S(1)}, f32[128,656]{0,1:T(8,128)}, u32[]{:S(2)}) copy-start(f32[128,656]{0,1:T(8,128)} %param.60) | copy-start | bytes 1007620
  630.5 95.0 %copy-start.27 = (f32[128,3,256]{0,2,1:T(8,128)S(1)}, f32[128,3,256]{0,2,1:T(8,128)}, u32[]{:S(2)}) copy-start(f32[128,3,256]{0,2,1:T(8,128)} %copy-done.26) | copy-start | bytes 1179652
  725.4 33.2 %copy-start.28 = (f32[128,2,656]{0,2,1:T(8,128)S(1)}, f32[128,2,656]{0,2,1:T(8,128)}, u32[]{:S(2)}) copy-start(f32[128,2,656]{0,2,1:T(8,128)} %param.51) | copy-start | bytes 2015236
  (49 other events, 111.0 us)
Sparse Core Ops, SparseCore 0:
  10.2 47.8 all-gather.17
  60.5 27.2 all-gather.15
  89.6 41.6 all-gather.21
  133.1 45.5 all-gather.13
  180.4 64.3 all-gather.19
  362.4 41.3 reduce-scatter.15
  408.0 57.1 reduce-scatter.23
  468.9 61.7 reduce-scatter.11
  534.3 82.7 reduce-scatter.19
  620.8 34.1 reduce-scatter.27
  657.3 19.6 reduce-scatter.17
  679.2 20.6 reduce-scatter.25
  702.2 22.2 reduce-scatter.13
  726.6 30.9 reduce-scatter.21

commit v2 on v1

--- a/solution.py
+++ b/solution.py
@@ -155,17 +155,99 @@
     )
 
 
-def gather(slab):
-    return lax.all_gather(lax.all_gather(slab, "tensor", axis=0), "dp", axis=0)
-
-
-def scatter(parts):
-    return lax.psum_scatter(
-        lax.psum_scatter(parts, "dp", scatter_dimension=0, tiled=False),
-        "tensor",
-        scatter_dimension=0,
-        tiled=False,
-    )
+def line_gather(slab):
+    size = lax.axis_size("tensor")
+    place = lax.axis_index("tensor")
+    from_before, from_after = [slab], [slab]
+    for step in range(1, size):
+        from_before.append(
+            lax.ppermute(from_before[-1], "tensor", [(n, n + 1) for n in range(step - 1, size - 1)])
+        )
+        from_after.append(
+            lax.ppermute(from_after[-1], "tensor", [(n, n - 1) for n in range(1, size - step + 1)])
+        )
+    return jnp.stack(
+        [slab]
+        + [
+            jnp.where(place >= step, from_before[step], from_after[size - step])
+            for step in range(1, size)
+        ]
+    )
+
+
+def line_scatter(parts):
+    size = lax.axis_size("tensor")
+    up, down = 0.0, 0.0
+    for step in range(size - 1, 0, -1):
+        to_after = (parts[size - step].astype(jnp.float32) + up).astype(parts.dtype)
+        to_before = (parts[step].astype(jnp.float32) + down).astype(parts.dtype)
+        up = lax.ppermute(to_after, "tensor", [(n, n + 1) for n in range(size - step)])
+        down = lax.ppermute(to_before, "tensor", [(n, n - 1) for n in range(step, size)])
+        up, down = up.astype(jnp.float32), down.astype(jnp.float32)
+    return parts[0].astype(jnp.float32) + up + down
+
+
+def flip(rows, mask):
+    return lax.ppermute(rows, "dp", [(n, n ^ mask) for n in range(lax.axis_size("dp"))])
+
+
+def far_bits():
+    size = lax.axis_size("dp")
+    return [1 << n for n in range(3, size.bit_length() - 1)]
+
+
+def gather(slab, x_first):
+    piece = line_gather(slab)
+    piece = piece.reshape(-1, piece.shape[-1])
+    for mask in far_bits():
+        piece = jnp.concatenate([piece, flip(piece, mask)], axis=1)
+    by_x, by_y = flip(piece, 2), flip(piece, 4)
+    far = flip(by_x, 4) if x_first else flip(by_y, 2)
+    mine = [piece, by_x, by_y, far]
+    return mine + [flip(part, 1) for part in mine]
+
+
+def add_low(left, right):
+    return (left.astype(jnp.float32) + right.astype(jnp.float32)).astype(left.dtype)
+
+
+def scatter(pieces, x_first):
+    own, by_x, by_y, far = [
+        add_low(mine, flip(theirs, 1)) for mine, theirs in zip(pieces[:4], pieces[4:])
+    ]
+    if x_first:
+        by_y = add_low(by_y, flip(far, 2))
+    else:
+        by_x = add_low(by_x, flip(far, 4))
+    total = (
+        own.astype(jnp.float32)
+        + flip(by_x, 2).astype(jnp.float32)
+        + flip(by_y, 4).astype(jnp.float32)
+    ).astype(own.dtype)
+    for mask in reversed(far_bits()):
+        half = total.shape[1] // 2
+        total = add_low(total[:, :half], flip(total[:, half:], mask))
+    size = lax.axis_size("tensor")
+    return line_scatter(total.reshape(size, total.shape[0] // size, total.shape[1]))
+
+
+def to_relative(rows, back=False):
+    size = lax.axis_size("dp")
+    place = lax.axis_index("dp")
+    bits = size.bit_length() - 1
+    lead = rows.shape[:-1]
+    axes = len(lead)
+    chunk = rows.shape[-1] // size
+    wanted = [bits - 1, bits - 3, bits - 2] + list(range(bits - 3))
+    order = list(range(axes)) + [axes + n for n in wanted] + [axes + bits]
+    cube = rows.reshape(lead + (2,) * bits + (chunk,))
+    if back:
+        cube = jnp.transpose(cube, [order.index(n) for n in range(len(order))])
+    for n in range(bits):
+        cube = jnp.where((place >> (bits - 1 - n)) & 1 == 1, jnp.flip(cube, axes + n), cube)
+    if not back:
+        cube = jnp.transpose(cube, order)
+    return cube.reshape(rows.shape)
 
 
 def shift(rows, step):
@@ -198,37 +280,39 @@
     tensor_size = lax.axis_size("tensor")
     group_rows = row_count * tensor_size
     low = jnp.bfloat16
+    qkv_wide, proj_wide = w_qkv.shape[1] * w_qkv.shape[2], w_proj.shape[1]
+    head_wide = w_qkv.shape[2]
+    up_wide = w_down.shape[1]
 
     def slab(weight):
         return weight.reshape(weight.shape[0], -1).T.astype(low)
 
-    def whole(weight, kinds):
-        gathered = gather(slab(weight))
-        dp_size, tp_size, wide, chunk = gathered.shape
-        full = gathered.reshape(dp_size, tp_size, kinds, wide // kinds, chunk)
-        return jnp.transpose(full, (2, 1, 3, 0, 4)).reshape(
-            kinds, tp_size * wide // kinds, dp_size * chunk
+    def whole(pieces):
+        full = jnp.concatenate(pieces, axis=1)
+        return full.reshape(tensor_size, -1, full.shape[1])
+
+    def split(grads):
+        stacked = jnp.concatenate(
+            [grad.astype(low).reshape(tensor_size, -1, grad.shape[1]) for grad in grads], axis=1
         )
-
-    def split(grad):
-        kinds, wide, depth = grad.shape
-        dp_size = lax.axis_size("dp")
-        parts = grad.astype(low).reshape(
-            kinds, tensor_size, wide // tensor_size, dp_size, depth // dp_size
-        )
-        parts = jnp.transpose(parts, (3, 1, 0, 2, 4)).reshape(
-            dp_size, tensor_size, kinds * wide // tensor_size, depth // dp_size
-        )
-        return scatter(parts).astype(jnp.float32).T
-
-    gains_full = lax.all_gather(norm_gains.astype(low), "dp", axis=1, tiled=True).astype(
-        jnp.float32
-    )
-    edges = (shift(hidden_in[-HALF:], 1), shift(hidden_in[:HALF], -1))
-    qkv_full = whole(w_qkv, 3)
-    proj_full = whole(w_proj, 1)[0]
-    in_full = whole(w_in, 2)
-    down_full = whole(w_down, 1)[0]
+        stacked = stacked.reshape(-1, stacked.shape[2])
+        return jnp.split(stacked, 8, axis=1)
+
+    hidden_low = to_relative(hidden_in)
+    cot_low = to_relative(cotangent)
+    edges = (shift(hidden_low[-HALF:], 1), shift(hidden_low[:HALF], -1))
+    gain_rows = jnp.pad(norm_gains.astype(low), ((0, 14), (0, 0)))
+    heads_full = whole(
+        gather(jnp.concatenate([slab(w_qkv), slab(w_proj), gain_rows], axis=0), True)
+    )
+    in_full = whole(gather(slab(w_in), False))
+    down_full = whole(gather(slab(w_down), True)).reshape(-1, D)
+    qkv_full = [
+        heads_full[:, c * head_wide : (c + 1) * head_wide].reshape(-1, D) for c in range(3)
+    ]
+    proj_full = heads_full[:, qkv_wide : qkv_wide + proj_wide].reshape(-1, D)
+    gains_full = heads_full[0, qkv_wide + proj_wide : qkv_wide + proj_wide + 2].astype(jnp.float32)
+    in_full = [in_full[:, c * up_wide : (c + 1) * up_wide].reshape(-1, D) for c in range(2)]
 
     first_row = lax.axis_index("tensor") * row_count
     segment, position = layout(
@@ -237,7 +321,7 @@
     cosine_table, sine_table = rotary_tables(position)
     allowed = allowed_pairs(segment)
 
-    hidden = hidden_in.astype(jnp.float32)
+    hidden = hidden_low.astype(jnp.float32)
     normed_one, norm_pull_one = jax.vjp(layer_norm, hidden, gains_full[0])
     normed_edges = layer_norm(jnp.concatenate(edges).astype(jnp.float32), gains_full[0])
     rows_one = normed_one.astype(low)
@@ -271,27 +355,28 @@
     active = active_full.astype(low)
     output = middle + dot(active, down_full, (1,), (0,))
 
-    grad_active = dot(cotangent, down_full, (1,), (1,))
-    down_sum = split(dot(active, cotangent, (0,), (0,))[None]).reshape(w_down.shape)
+    grad_active = dot(cot_low, down_full, (1,), (1,))
+    down_sum = scatter(split([dot(active, cot_low, (0,), (0,))]), True).T
     grad_gate_in, grad_gate_up = geglu_pull(grad_active)
     grad_gate_in = grad_gate_in.astype(low)
     grad_gate_up = grad_gate_up.astype(low)
-    in_sum = split(
-        jnp.stack(
+    in_sum = scatter(
+        split(
             [
                 dot(grad_gate_in, rows_two, (0,), (0,)),
                 dot(grad_gate_up, rows_two, (0,), (0,)),
             ]
-        )
-    ).reshape(w_in.shape)
+        ),
+        False,
+    ).T.reshape(w_in.shape)
     grad_normed_two = dot(grad_gate_in, in_full[0], (1,), (0,)) + dot(
         grad_gate_up, in_full[1], (1,), (0,)
     )
     grad_middle_norm, grad_gain_two = norm_pull_two(grad_normed_two)
-    grad_middle = cotangent.astype(jnp.float32) + grad_middle_norm
+    grad_middle = cot_low.astype(jnp.float32) + grad_middle_norm
     grad_middle_low = grad_middle.astype(low)
     grad_attended = dot(grad_middle_low, proj_full, (1,), (1,)).astype(low)
-    proj_sum = split(dot(attended, grad_middle_low, (0,), (0,))[None]).reshape(w_proj.shape)
+    grad_proj = dot(attended, grad_middle_low, (0,), (0,))
     grad_queries, grad_keys, grad_values = attend_backward(
         queries,
         key_rows,
@@ -304,21 +389,24 @@
     grad_pair = jnp.stack([grad_key_pre, grad_values.reshape(-1, D)])
     from_after = shift(grad_pair[:, :HALF].astype(low), -1).astype(jnp.float32)
     from_before = shift(grad_pair[:, -HALF:].astype(low), 1).astype(jnp.float32)
+    from_after = jnp.roll(from_after, -head_wide, axis=-1)
+    from_before = jnp.roll(from_before, head_wide, axis=-1)
     grad_pair = grad_pair[:, HALF:-HALF]
     grad_pair = grad_pair.at[:, :HALF].add(from_before).at[:, -HALF:].add(from_after)
     grad_mixed = jnp.concatenate([grad_query_pre[None], grad_pair]).astype(low)
-    qkv_sum = split(
-        jnp.stack([dot(grad_mixed[c], rows_one, (0,), (0,)) for c in range(3)])
-    ).reshape(w_qkv.shape)
+    heads_sum = scatter(
+        split([dot(grad_mixed[c], rows_one, (0,), (0,)) for c in range(3)] + [grad_proj]), True
+    ).T
+    qkv_sum = heads_sum[:, :qkv_wide].reshape(w_qkv.shape)
+    proj_sum = heads_sum[:, qkv_wide:]
     grad_normed_one = sum(dot(grad_mixed[c], qkv_full[c], (1,), (0,)) for c in range(3))
     grad_hidden_norm, grad_gain_one = norm_pull_one(grad_normed_one)
     grad_input = grad_middle + grad_hidden_norm
-    gain_sum = lax.psum(
-        lax.psum_scatter(
-            jnp.stack([grad_gain_one, grad_gain_two]), "dp", scatter_dimension=1, tiled=True
-        ),
-        "tensor",
-    )
+    gain_total = lax.psum(
+        to_relative(jnp.stack([grad_gain_one, grad_gain_two]), back=True), ("dp", "tensor")
+    )
+    chunk = norm_gains.shape[1]
+    gain_sum = lax.dynamic_slice_in_dim(gain_total, lax.axis_index("dp") * chunk, chunk, axis=1)
     qkv_one, qkv_two, qkv_new = adam_update(w_qkv, qkv_sum, qkv_first, qkv_second, D ** (-0.5))
     proj_one, proj_two, proj_new = adam_update(
         w_proj, proj_sum, proj_first, proj_second, (D // HALF) ** (-0.5)
@@ -331,8 +419,8 @@
         norm_gains, gain_sum, gain_first, gain_second, GAIN_RATE
     )
     return (
-        output.astype(jnp.bfloat16),
-        grad_input,
+        to_relative(output.astype(low), back=True),
+        to_relative(grad_input, back=True),
         qkv_one,
         qkv_two,
         qkv_new,

time: 773 us -> 904 us (1.17)
  starting transfers between devices: 10.5 us -> 114 us
  waiting for transfers between devices: 286 us -> 188 us
  other arithmetic: 75.1 us -> 163 us
  local copies, waits for them, and re-layouts: 158 us -> 221 us
  blocking collectives: 82 us -> 43.3 us
  matrix products: 141 us -> 158 us
  between operations: 15.9 us -> 3.94 us
    reduce_scatter x8 -> x0, waiting for transfers between devices: 194 us -> none  [the longest x4 113 us: scatter(): lax.psum_scatter(parts, 'dp', scatter_dimension=0, tiled=False)]
    ppermute x0 -> x78, waiting for transfers between devices: none -> 188 us  [the longest x42 154 us: flip(): lax.ppermute(rows, 'dp', [(n, n ^ mask) for n in range(lax.axis_size('dp'...]
    ppermute x0 -> x78, starting transfers between devices: none -> 105 us  [the longest x9 36.2 us: line_scatter(): lax.ppermute(to_after, 'tensor', [(n, n + 1) for n in range(size - step)])]
    all_gather x4 -> x0, blocking collectives: 70.3 us -> none  [the longest x3 61.7 us: gather(): return lax.all_gather(lax.all_gather(slab, 'tensor', axis=0), 'dp', axis=0)]
    all_gather x5 -> x0, waiting for transfers between devices: 64.6 us -> none  [gather(): return lax.all_gather(lax.all_gather(slab, 'tensor', axis=0), 'dp', axis=0)]
    rev x0 -> x5, local copies, waits for them, and re-layouts: none -> 53.4 us  [to_relative(): jnp.flip(cube, axes + n)]
    psum x1, blocking collectives: 11.7 us -> 43.3 us  [local(): lax.psum(to_relative(jnp.stack([grad_gain_one, grad_gain_two]), back=True...]
    select_n x0 -> x12, other arithmetic: none -> 27.3 us  [to_relative(): jnp.where(place >> bits - 1 - n & 1 == 1, jnp.flip(cube, axes + n), cube)]
  transfers between devices with their start and end apart: 18 -> 82, of which waited for: 10 -> 20; matrix products, arithmetic and copies ran while one was open for 30% -> 38% of each run, Pallas kernels for 0% -> 0%
where the time goes in v2:
time: 904 us; the launch traced here: 891 us
  local copies, waits for them, and re-layouts  221 us (24%)
  waiting for transfers between devices  188 us (21%)
  other arithmetic  163 us (18%)
  matrix products  158 us (17%)
  starting transfers between devices  114 us (13%)
  blocking collectives  43.3 us (5%)
    ppermute x42, waiting for transfers between devices, flip(): lax.ppermute(rows, 'dp', [(n, n ^ mask) for n in range(lax.axis_size('dp'...  154 us
    dot_general x21, matrix products, dot(): lax.dot_general(left, right, ((left_dims, right_dims), ((), ())), preferr...  123 us
    unnamed x287, local copies, waits for them, and re-layouts  56.8 us
    rev x5, local copies, waits for them, and re-layouts, to_relative(): jnp.flip(cube, axes + n)  53.4 us
    psum x1, blocking collectives, local(): lax.psum(to_relative(jnp.stack([grad_gain_one, grad_gain_two]), back=True...  43.3 us
    ppermute x9, starting transfers between devices, line_scatter(): lax.ppermute(to_after, 'tensor', [(n, n + 1) for n in range(size - step)])  36.2 us
    ppermute x9, waiting for transfers between devices, line_gather(): lax.ppermute(from_after[-1], 'tensor', [(n, n - 1) for n in range(1, size...  30.8 us
    select_n x12, other arithmetic, to_relative(): jnp.where(place >> bits - 1 - n & 1 == 1, jnp.flip(cube, axes + n), cube)  27.3 us
  transfers between devices with their start and end apart: 82, of which 20 were waited for; matrix products, arithmetic and copies ran while one was open for 38% of the time, Pallas kernels for 0%

profile of v2, /device:TPU:0, one launch (start us, length us, event | category | flops | bytes accessed | tf_op | source)
XLA Modules:
  0.0 891.0 jit_solution(15200156522530951247)
XLA Ops:
  6.0 6.3 collective-permute-start.2
  18.4 4.1 broadcast_select_fusion
  22.5 8.2 rev.55
  37.5 3.9 collective-permute-start
  50.1 12.8 %multiply_reduce_fusion.6 = f32[768]{0:T(1024)} fusion(bf16[768,2,2,2,128]{4,3,2,1,0:T(2,128)(2,1)} %copy-done.12, f32[768]{0:T(1024)S(1)} %broadcast_multiply_fusion.1), kind=kLoop, calls=%fused_computation.64 | loop fusion | flops 3144960 | bytes 1579008 | tf_op jit(solution)/shard_map/jvp()/reduce_sum | solution.py:27
  66.8 14.9 %rev.61 = bf16[768,2,2,2,128]{4,2,1,3,0:T(2,128)(2,1)} reverse(bf16[768,2,2,2,128]{4,2,1,3,0:T(2,128)(2,1)} %get-tuple-element.356), dimensions={2} | reverse | bytes 3145728 | tf_op jit(solution)/shard_map/jit(_flip)/rev | solution.py:247
  99.8 5.2 collective-permute-start.28
  108.6 4.6 collective-permute-start.15
  116.5 4.4 collective-permute-done.30
  126.5 7.9 collective-permute-done.31
  142.7 9.5 %collective-permute-done.5 = bf16[1040,128]{1,0:T(8,128)(2,1)S(1)} collective-permute-done((bf16[1040,128]{1,0:T(8,128)(2,1)S(1)}, bf16[1040,128]{1,0:T(8,128)(2,1)S(1)}, u32[]{:S(2)}, u32[]{:S(2)}) %collective-permute-start.5) | collective-permute-done | bytes 266272 | tf_op jit(solution)/shard_map/ppermute | solution.py:167
  154.7 9.1 %collective-permute-done.18 = bf16[1312,128]{1,0:T(8,128)(2,1)S(1)} collective-permute-done((bf16[1312,128]{1,0:T(8,128)(2,1)S(1)}, bf16[1312,128]{1,0:T(8,128)(2,1)S(1)}, u32[]{:S(2)}, u32[]{:S(2)}) %collective-permute-start.18) | collective-permute-done | bytes 335904 | tf_op jit(solution)/shard_map/ppermute | solution.py:167
  168.4 34.2 %collective-permute-done.36 = bf16[2624,128]{1,0:T(8,128)(2,1)S(1)} collective-permute-done((bf16[2624,128]{1,0:T(8,128)(2,1)S(1)}, bf16[2624,128]{1,0:T(8,128)(2,1)S(1)}, u32[]{:S(2)}, u32[]{:S(2)}) %collective-permute-start.36) | collective-permute-done | bytes 671776 | tf_op jit(solution)/shard_map/ppermute | solution.py:191
  210.0 27.0 %collective-permute-done.22 = bf16[5248,128]{1,0:T(8,128)(2,1)S(1)} collective-permute-done((bf16[5248,128]{1,0:T(8,128)(2,1)S(1)}, bf16[5248,128]{1,0:T(8,128)(2,1)S(1)}, u32[]{:S(2)}, u32[]{:S(2)}) %collective-permute-start.22) | collective-permute-done | bytes 1343520 | tf_op jit(solution)/shard_map/ppermute | solution.py:191
  239.1 20.0 %collective-permute-done.10 = bf16[4160,128]{1,0:T(8,128)(2,1)S(1)} collective-permute-done((bf16[4160,128]{1,0:T(8,128)(2,1)S(1)}, bf16[4160,128]{1,0:T(8,128)(2,1)S(1)}, u32[]{:S(2)}, u32[]{:S(2)}) %collective-permute-start.10) | collective-permute-done | bytes 1064992 | tf_op jit(solution)/shard_map/ppermute | solution.py:191
  261.8 8.6 collective-permute-done.23
  289.0 3.9 multiply_convert_fusion.4
  292.9 4.0 reshape.934
  296.9 3.9 fusion.128
  323.5 5.7 fusion.14
  329.3 4.7 fusion
  336.3 5.5 fusion.26
  347.9 4.0 convert_element_type.495
  356.6 9.5 %fusion.114 = (bf16[4,656,1024]{2,1,0:T(8,128)(2,1)}, bf16[4,656,1024]{2,1,0:T(8,128)(2,1)}) fusion(bf16[4,1312,1024]{2,1,0:T(8,128)(2,1)} %constant_dynamic-update-slice_fusion.14), kind=kLoop, calls=%fused_computation.340 | loop fusion | bytes 21495808 | tf_op jit(solution)/shard_map/slice | solution.py:315
  366.1 7.5 fusion.129
  373.6 8.6 fusion.130
  382.3 27.2 %add_convert_fusion = (bf16[768,2624]{0,1:T(8,128)(2,1)}, f32[768,2624]{0,1:T(8,128)}, f32[768,2624]{0,1:T(8,128)}) fusion(f32[768,2624]{0,1:T(8,128)S(1)} %fusion.130, f32[768,2624]{0,1:T(8,128)S(1)} %fusion.129, bf16[768,1024]{1,0:T(8,128)(2,1)S(1)} %copy-done.17, bf16[2624,1024]{1,0:T(8,128)(2,1)} %copy-done.100), kind=kOutput, calls=%fused_computation.18 | convolution fusion | flops 4274307072 | bytes 43220992 | tf_op jit(solution)/shard_map/dot_general | solution.py:153
  409.5 14.8 %multiply_convert_fusion.1 = (bf16[768,2624]{0,1:T(8,128)(2,1)}, bf16[768,2624]{0,1:T(8,128)(2,1)}) fusion(f32[768,2624]{0,1:T(8,128)} %get-tuple-element.349, f32[768,2624]{0,1:T(8,128)} %get-tuple-element.260, f32[768,2624]{0,1:T(8,128)} %copy-done.26, f32[768,2624]{0,1:T(8,128)} %copy-done.27), kind=kLoop, calls=%fused_computation.17 | loop fusion | flops 12091392 | bytes 40304640 | tf_op jit(solution)/shard_map/convert_element_type | solution.py:362
  424.3 8.2 fusion.131
  432.5 6.3 multiply_reduce_fusion.1
  445.9 5.2 reshape.937
  451.1 4.9 copy.145
  456.1 8.4 fusion.15
  464.5 12.3 %multiply_reduce_fusion = (f32[6,16,128]{2,1,0:T(8,128)S(1)}, f32[6,16,128,256]{3,2,1,0:T(8,128)}) fusion(f32[6,16,128]{2,1,0:T(8,128)S(1)} %log_add_fusion, f32[6,16,128,256]{3,2,1,0:T(8,128)} %copy-done, pred[6,128,256]{2,1,0:T(8,128)(4,1)S(1)} %compare_and_fusion, bf16[6,128,16,64]{1,3,2,0:T(8,128)(2,1)S(1)} %copy-done.16, ...), kind=kOutput, calls=%fused_computation.1 | convolution fusion | flops 418369536 | bytes 30179328 | tf_op jit(solution)/shard_map/nqhd,nkhd->nhqk/dot_general | solution.py:119
  476.8 8.8 multiply_convert_fusion
  489.8 7.6 convolution_convert_fusion.1
  497.4 6.1 convolution_convert_fusion.2
  506.7 6.3 convolution_convert_fusion
  513.1 8.3 add_convert_fusion.2
  537.0 7.9 pad_maximum_fusion
  562.7 14.3 %rev.58 = bf16[768,2,2,2,128]{4,2,1,3,0:T(2,128)(2,1)S(1)} reverse(bf16[768,2,2,2,128]{4,2,1,3,0:T(2,128)(2,1)} %broadcast_select_fusion.1), dimensions={2} | reverse | bytes 3145728 | tf_op jit(solution)/shard_map/jit(_flip)/rev | solution.py:247
  581.1 4.3 fusion.11
  592.9 5.9 scatter-add.66
  602.4 6.1 scatter-add.69
  621.5 4.1 multiply_reduce_fusion.2
  625.6 4.2 pad_maximum_fusion.2
  640.2 4.2 reshape.920
  647.7 16.0 %rev.64 = f32[768,2,2,2,128]{4,2,1,3,0:T(2,128)} reverse(f32[768,2,2,2,128]{4,2,1,3,0:T(2,128)} %reverse_select_fusion.1), dimensions={2} | reverse | bytes 6291456 | tf_op jit(solution)/shard_map/jit(_flip)/rev | solution.py:247
  667.6 43.3 %psum.7 = f32[2,1024]{1,0:T(2,128)S(1)} all-reduce(f32[2,1024]{1,0:T(2,128)S(1)} %reshape.932), channel_id=1, replica_groups=mesh['dp'=8,'tensor'=4] {'dp','tensor'}, use_global_device_ids=true, to_apply=%region_18.19 | all-reduce | flops 2048 | bytes 16384 | tf_op jit(solution)/shard_map/psum | solution.py:405
  710.9 4.6 reverse_select_fusion
  723.5 13.1 %collective-permute-done.74 = bf16[2624,128]{1,0:T(8,128)(2,1)S(1)} collective-permute-done((bf16[2624,128]{1,0:T(8,128)(2,1)S(1)}, bf16[2624,128]{1,0:T(8,128)(2,1)S(1)}, u32[]{:S(2)}, u32[]{:S(2)}) %collective-permute-start.74) | collective-permute-done | bytes 671776 | tf_op jit(solution)/shard_map/ppermute | solution.py:191
  743.5 7.5 collective-permute-done.71
  751.0 5.1 collective-permute-done.75
  760.1 13.1 %collective-permute-done.48 = bf16[4096,128]{1,0:T(8,128)(2,1)S(1)} collective-permute-done((bf16[4096,128]{1,0:T(8,128)(2,1)S(1)}, bf16[4096,128]{1,0:T(8,128)(2,1)S(1)}, u32[]{:S(2)}, u32[]{:S(2)}) %collective-permute-start.48) | collective-permute-done | bytes 1048608 | tf_op jit(solution)/shard_map/ppermute | solution.py:191
  776.7 4.0 collective-permute-start.76
  780.7 5.0 collective-permute-done.59
  787.2 4.1 add_convert_fusion.5
  792.0 8.5 collective-permute-done.45
  802.2 6.6 collective-permute-done.49
  813.0 4.0 collective-permute-start.50
  840.1 4.2 collective-permute-start.63
  847.9 4.6 collective-permute-start.52
  854.0 4.6 collective-permute-start.64
  864.7 9.0 %collective-permute-start.65 = (bf16[1312,128]{1,0:T(8,128)(2,1)}, bf16[1312,128]{1,0:T(8,128)(2,1)}, u32[]{:S(2)}, u32[]{:S(2)}) collective-permute-start(bf16[1312,128]{1,0:T(8,128)(2,1)} %get-tuple-element.307), channel_id=1, source_target_pairs={{0,1},{1,2},{2,3},{4,5},{5,6},{6,7},{8,9},{9,10},{10,11},{12,13},{... | collective-permute-start | bytes 1007624 | tf_op jit(solution)/shard_map/ppermute | solution.py:184
  (610 shorter events, 316.7 us)
Async XLA Ops:
  4.7 109.8 %collective-permute-start.3 = (bf16[1040,128]{1,0:T(8,128)(2,1)}, bf16[1040,128]{1,0:T(8,128)(2,1)}, u32[]{:S(2)}, u32[]{:S(2)}) collective-permute-start(bf16[1040,128]{1,0:T(8,128)(2,1)} %get-tuple-element.332), channel_id=1, source_target_pairs={{1,0},{2,1},{3,2},{5,4},{6,5},{7,6},{9,8},{10,9},{11,10},{13,12},{... | collective-permute-start | bytes 798728 | tf_op jit(solution)/shard_map/ppermute | solution.py:167
  6.0 109.2 %collective-permute-start.2 = (bf16[1040,128]{1,0:T(8,128)(2,1)}, bf16[1040,128]{1,0:T(8,128)(2,1)}, u32[]{:S(2)}, u32[]{:S(2)}) collective-permute-start(bf16[1040,128]{1,0:T(8,128)(2,1)} %get-tuple-element.332), channel_id=1, source_target_pairs={{0,1},{1,2},{2,3},{4,5},{5,6},{6,7},{8,9},{9,10},{10,11},{12,13},{... | collective-permute-start | bytes 798728 | tf_op jit(solution)/shard_map/ppermute | solution.py:164
  37.5 62.3 %collective-permute-start = (bf16[64,1024]{1,0:T(8,128)(2,1)}, bf16[64,1024]{1,0:T(8,128)(2,1)}, u32[]{:S(2)}, u32[]{:S(2)}) collective-permute-start(bf16[64,1024]{1,0:T(8,128)(2,1)} %slice.611), channel_id=1, source_target_pairs={{0,1},{1,2},{2,3},{4,5},{5,6},{6,7},{8,9},{9,10},{10,11},{12,13},{... | collective-permute-start | bytes 393224 | tf_op jit(solution)/shard_map/ppermute | solution.py:256
  42.1 62.9 %collective-permute-start.1 = (bf16[64,1024]{1,0:T(8,128)(2,1)}, bf16[64,1024]{1,0:T(8,128)(2,1)}, u32[]{:S(2)}, u32[]{:S(2)}) collective-permute-start(bf16[64,1024]{1,0:T(8,128)(2,1)} %slice.613), channel_id=1, source_target_pairs={{1,0},{2,1},{3,2},{5,4},{6,5},{7,6},{9,8},{10,9},{11,10},{13,12},{... | collective-permute-start | bytes 393224 | tf_op jit(solution)/shard_map/ppermute | solution.py:256
  44.2 64.4 %collective-permute-start.29 = (bf16[656,128]{1,0:T(8,128)(2,1)}, bf16[656,128]{1,0:T(8,128)(2,1)}, u32[]{:S(2)}, u32[]{:S(2)}) collective-permute-start(bf16[656,128]{1,0:T(8,128)(2,1)} %get-tuple-element.330), channel_id=1, source_target_pairs={{1,0},{2,1},{3,2},{5,4},{6,5},{7,6},{9,8},{10,9},{11,10},{13,12},{... | collective-permute-start | bytes 503816 | tf_op jit(solution)/shard_map/ppermute | solution.py:167
  99.8 13.4 %collective-permute-start.28 = (bf16[656,128]{1,0:T(8,128)(2,1)}, bf16[656,128]{1,0:T(8,128)(2,1)S(1)}, u32[]{:S(2)}, u32[]{:S(2)}) collective-permute-start(bf16[656,128]{1,0:T(8,128)(2,1)} %get-tuple-element.330), channel_id=1, source_target_pairs={{0,1},{1,2},{2,3},{4,5},{5,6},{6,7},{8,9},{9,10},{10,11},{12,13},{... | collective-permute-start | bytes 503816 | tf_op jit(solution)/shard_map/ppermute | solution.py:164
  105.0 17.3 %collective-permute-start.16 = (bf16[1312,128]{1,0:T(8,128)(2,1)}, bf16[1312,128]{1,0:T(8,128)(2,1)S(1)}, u32[]{:S(2)}, u32[]{:S(2)}) collective-permute-start(bf16[1312,128]{1,0:T(8,128)(2,1)} %bitcast.365), channel_id=1, source_target_pairs={{1,0},{2,1},{3,2},{5,4},{6,5},{7,6},{9,8},{10,9},{11,10},{13,12},{... | collective-permute-start | bytes 1007624 | tf_op jit(solution)/shard_map/ppermute | solution.py:167
  108.6 15.0 %collective-permute-start.15 = (bf16[1312,128]{1,0:T(8,128)(2,1)}, bf16[1312,128]{1,0:T(8,128)(2,1)S(1)}, u32[]{:S(2)}, u32[]{:S(2)}) collective-permute-start(bf16[1312,128]{1,0:T(8,128)(2,1)} %bitcast.366), channel_id=1, source_target_pairs={{0,1},{1,2},{2,3},{4,5},{5,6},{6,7},{8,9},{9,10},{10,11},{12,13},{... | collective-permute-start | bytes 1007624 | tf_op jit(solution)/shard_map/ppermute | solution.py:164
  115.2 22.1 %collective-permute-start.4 = (bf16[1040,128]{1,0:T(8,128)(2,1)}, bf16[1040,128]{1,0:T(8,128)(2,1)S(1)}, u32[]{:S(2)}, u32[]{:S(2)}) collective-permute-start(bf16[1040,128]{1,0:T(8,128)(2,1)} %collective-permute-done.3), channel_id=1, source_target_pairs={{1,0},{2,1},{5,4},{6,5},{9,8},{10,9},{13,12},{14,13},{17,16},{18,1... | collective-permute-start | bytes 798728 | tf_op jit(solution)/shard_map/ppermute | solution.py:167
  120.9 18.0 %collective-permute-start.6 = (bf16[1040,128]{1,0:T(8,128)(2,1)}, bf16[1040,128]{1,0:T(8,128)(2,1)S(1)}, u32[]{:S(2)}, u32[]{:S(2)}) collective-permute-start(bf16[1040,128]{1,0:T(8,128)(2,1)} %collective-permute-done.2), channel_id=1, source_target_pairs={{1,2},{2,3},{5,6},{6,7},{9,10},{10,11},{13,14},{14,15},{17,18},{18... | collective-permute-start | bytes 798728 | tf_op jit(solution)/shard_map/ppermute | solution.py:164
  123.6 15.3 %collective-permute-start.17 = (bf16[1312,128]{1,0:T(8,128)(2,1)S(1)}, bf16[1312,128]{1,0:T(8,128)(2,1)S(1)}, u32[]{:S(2)}, u32[]{:S(2)}) collective-permute-start(bf16[1312,128]{1,0:T(8,128)(2,1)S(1)} %collective-permute-done.16), channel_id=1, source_target_pairs={{1,0},{2,1},{5,4},{6,5},{9,8},{10,9},{13,12},{14,13},{17,16},{18,1... | collective-permute-start | bytes 1007624 | tf_op jit(solution)/shard_map/ppermute | solution.py:167
  124.9 14.7 %collective-permute-start.19 = (bf16[1312,128]{1,0:T(8,128)(2,1)S(1)}, bf16[1312,128]{1,0:T(8,128)(2,1)S(1)}, u32[]{:S(2)}, u32[]{:S(2)}) collective-permute-start(bf16[1312,128]{1,0:T(8,128)(2,1)S(1)} %collective-permute-done.15), channel_id=1, source_target_pairs={{1,2},{2,3},{5,6},{6,7},{9,10},{10,11},{13,14},{14,15},{17,18},{18... | collective-permute-start | bytes 1007624 | tf_op jit(solution)/shard_map/ppermute | solution.py:164
  135.5 30.2 %collective-permute-start.34 = (bf16[2624,128]{1,0:T(8,128)(2,1)S(1)}, bf16[2624,128]{1,0:T(8,128)(2,1)S(1)}, u32[]{:S(2)}, u32[]{:S(2)}) collective-permute-start(bf16[2624,128]{1,0:T(8,128)(2,1)S(1)} %bitcast.336), channel_id=1, source_target_pairs={{0,8},{4,12},{8,0},{12,4},{16,24},{20,28},{24,16},{28,20},{1,9},{5... | collective-permute-start | bytes 2015240 | tf_op jit(solution)/shard_map/ppermute | solution.py:191
  137.3 30.3 %collective-permute-start.35 = (bf16[2624,128]{1,0:T(8,128)(2,1)S(1)}, bf16[2624,128]{1,0:T(8,128)(2,1)S(1)}, u32[]{:S(2)}, u32[]{:S(2)}) collective-permute-start(bf16[2624,128]{1,0:T(8,128)(2,1)S(1)} %bitcast.338), channel_id=1, source_target_pairs={{0,16},{4,20},{8,24},{12,28},{16,0},{20,4},{24,8},{28,12},{1,17},{... | collective-permute-start | bytes 2015240 | tf_op jit(solution)/shard_map/ppermute | solution.py:191
  138.9 64.0 %collective-permute-start.37 = (bf16[2624,128]{1,0:T(8,128)(2,1)S(1)}, bf16[2624,128]{1,0:T(8,128)(2,1)S(1)}, u32[]{:S(2)}, u32[]{:S(2)}) collective-permute-start(bf16[2624,128]{1,0:T(8,128)(2,1)S(1)} %bitcast.339), channel_id=1, source_target_pairs={{0,4},{4,0},{8,12},{12,8},{16,20},{20,16},{24,28},{28,24},{1,5},{5... | collective-permute-start | bytes 2015240 | tf_op jit(solution)/shard_map/ppermute | solution.py:191
  141.0 13.0 %collective-permute-start.20 = (bf16[1312,128]{1,0:T(8,128)(2,1)S(1)}, bf16[1312,128]{1,0:T(8,128)(2,1)S(1)}, u32[]{:S(2)}, u32[]{:S(2)}) collective-permute-start(bf16[1312,128]{1,0:T(8,128)(2,1)S(1)} %collective-permute-done.19), channel_id=1, source_target_pairs={{2,3},{6,7},{10,11},{14,15},{18,19},{22,23},{26,27},{30,31}} | collective-permute-start | bytes 1007624 | tf_op jit(solution)/shard_map/ppermute | solution.py:164
  154.0 52.1 %collective-permute-start.8 = (bf16[4160,128]{1,0:T(8,128)(2,1)S(1)}, bf16[4160,128]{1,0:T(8,128)(2,1)S(1)}, u32[]{:S(2)}, u32[]{:S(2)}) collective-permute-start(bf16[4160,128]{1,0:T(8,128)(2,1)S(1)} %bitcast.368), channel_id=1, source_target_pairs={{0,8},{4,12},{8,0},{12,4},{16,24},{20,28},{24,16},{28,20},{1,9},{5... | collective-permute-start | bytes 3194888 | tf_op jit(solution)/shard_map/ppermute | solution.py:191
  163.7 43.2 %collective-permute-start.9 = (bf16[4160,128]{1,0:T(8,128)(2,1)S(1)}, bf16[4160,128]{1,0:T(8,128)(2,1)S(1)}, u32[]{:S(2)}, u32[]{:S(2)}) collective-permute-start(bf16[4160,128]{1,0:T(8,128)(2,1)S(1)} %bitcast.369), channel_id=1, source_target_pairs={{0,16},{4,20},{8,24},{12,28},{16,0},{20,4},{24,8},{28,12},{1,17},{... | collective-permute-start | bytes 3194888 | tf_op jit(solution)/shard_map/ppermute | solution.py:191
  165.7 36.9 %collective-permute-start.36 = (bf16[2624,128]{1,0:T(8,128)(2,1)S(1)}, bf16[2624,128]{1,0:T(8,128)(2,1)S(1)}, u32[]{:S(2)}, u32[]{:S(2)}) collective-permute-start(bf16[2624,128]{1,0:T(8,128)(2,1)S(1)} %collective-permute-done.34), channel_id=1, source_target_pairs={{0,16},{4,20},{8,24},{12,28},{16,0},{20,4},{24,8},{28,12},{1,17},{... | collective-permute-start | bytes 2015240 | tf_op jit(solution)/shard_map/ppermute | solution.py:191
  167.6 41.1 %collective-permute-start.21 = (bf16[5248,128]{1,0:T(8,128)(2,1)S(1)}, bf16[5248,128]{1,0:T(8,128)(2,1)S(1)}, u32[]{:S(2)}, u32[]{:S(2)}) collective-permute-start(bf16[5248,128]{1,0:T(8,128)(2,1)S(1)} %bitcast.357), channel_id=1, source_target_pairs={{0,8},{4,12},{8,0},{12,4},{16,24},{20,28},{24,16},{28,20},{1,9},{5... | collective-permute-start | bytes 4030472 | tf_op jit(solution)/shard_map/ppermute | solution.py:191
  204.7 32.3 %collective-permute-start.22 = (bf16[5248,128]{1,0:T(8,128)(2,1)S(1)}, bf16[5248,128]{1,0:T(8,128)(2,1)S(1)}, u32[]{:S(2)}, u32[]{:S(2)}) collective-permute-start(bf16[5248,128]{1,0:T(8,128)(2,1)S(1)} %bitcast.358), channel_id=1, source_target_pairs={{0,16},{4,20},{8,24},{12,28},{16,0},{20,4},{24,8},{28,12},{1,17},{... | collective-permute-start | bytes 4030472 | tf_op jit(solution)/shard_map/ppermute | solution.py:191
  205.7 53.8 %collective-permute-start.11 = (bf16[4160,128]{1,0:T(8,128)(2,1)S(1)}, bf16[4160,128]{1,0:T(8,128)(2,1)S(1)}, u32[]{:S(2)}, u32[]{:S(2)}) collective-permute-start(bf16[4160,128]{1,0:T(8,128)(2,1)S(1)} %bitcast.370), channel_id=1, source_target_pairs={{0,4},{4,0},{8,12},{12,8},{16,20},{20,16},{24,28},{28,24},{1,5},{5... | collective-permute-start | bytes 3194888 | tf_op jit(solution)/shard_map/ppermute | solution.py:191
  206.1 32.3 %collective-permute-start.40 = (bf16[2624,128]{1,0:T(8,128)(2,1)S(1)}, bf16[2624,128]{1,0:T(8,128)(2,1)S(1)}, u32[]{:S(2)}, u32[]{:S(2)}) collective-permute-start(bf16[2624,128]{1,0:T(8,128)(2,1)S(1)} %collective-permute-done.36), channel_id=1, source_target_pairs={{0,4},{4,0},{8,12},{12,8},{16,20},{20,16},{24,28},{28,24},{1,5},{5... | collective-permute-start | bytes 2015240 | tf_op jit(solution)/shard_map/ppermute | solution.py:191
  206.9 52.2 %collective-permute-start.10 = (bf16[4160,128]{1,0:T(8,128)(2,1)S(1)}, bf16[4160,128]{1,0:T(8,128)(2,1)S(1)}, u32[]{:S(2)}, u32[]{:S(2)}) collective-permute-start(bf16[4160,128]{1,0:T(8,128)(2,1)S(1)} %collective-permute-done.8), channel_id=1, source_target_pairs={{0,16},{4,20},{8,24},{12,28},{16,0},{20,4},{24,8},{28,12},{1,17},{... | collective-permute-start | bytes 3194888 | tf_op jit(solution)/shard_map/ppermute | solution.py:191
  208.7 51.7 %collective-permute-start.12 = (bf16[4160,128]{1,0:T(8,128)(2,1)S(1)}, bf16[4160,128]{1,0:T(8,128)(2,1)S(1)}, u32[]{:S(2)}, u32[]{:S(2)}) collective-permute-start(bf16[4160,128]{1,0:T(8,128)(2,1)S(1)} %collective-permute-done.8), channel_id=1, source_target_pairs={{0,4},{4,0},{8,12},{12,8},{16,20},{20,16},{24,28},{28,24},{1,5},{5... | collective-permute-start | bytes 3194888 | tf_op jit(solution)/shard_map/ppermute | solution.py:191
  237.0 23.8 %collective-permute-start.13 = (bf16[4160,128]{1,0:T(8,128)(2,1)S(1)}, bf16[4160,128]{1,0:T(8,128)(2,1)S(1)}, u32[]{:S(2)}, u32[]{:S(2)}) collective-permute-start(bf16[4160,128]{1,0:T(8,128)(2,1)S(1)} %collective-permute-done.9), channel_id=1, source_target_pairs={{0,4},{4,0},{8,12},{12,8},{16,20},{20,16},{24,28},{28,24},{1,5},{5... | collective-permute-start | bytes 3194888 | tf_op jit(solution)/shard_map/ppermute | solution.py:191
  238.4 32.0 %collective-permute-start.23 = (bf16[5248,128]{1,0:T(8,128)(2,1)S(1)}, bf16[5248,128]{1,0:T(8,128)(2,1)}, u32[]{:S(2)}, u32[]{:S(2)}) collective-permute-start(bf16[5248,128]{1,0:T(8,128)(2,1)S(1)} %collective-permute-done.22), channel_id=1, source_target_pairs={{0,8},{4,12},{8,0},{12,4},{16,24},{20,28},{24,16},{28,20},{1,9},{5... | collective-permute-start | bytes 4030472 | tf_op jit(solution)/shard_map/ppermute | solution.py:191
  259.1 13.9 %collective-permute-start.24 = (bf16[5248,128]{1,0:T(8,128)(2,1)S(1)}, bf16[5248,128]{1,0:T(8,128)(2,1)S(1)}, u32[]{:S(2)}, u32[]{:S(2)}) collective-permute-start(bf16[5248,128]{1,0:T(8,128)(2,1)S(1)} %bitcast.359), channel_id=1, source_target_pairs={{0,4},{4,0},{8,12},{12,8},{16,20},{20,16},{24,28},{28,24},{1,5},{5... | collective-permute-start | bytes 4030472 | tf_op jit(solution)/shard_map/ppermute | solution.py:191
  259.5 14.8 %collective-permute-start.25 = (bf16[5248,128]{1,0:T(8,128)(2,1)S(1)}, bf16[5248,128]{1,0:T(8,128)(2,1)S(1)}, u32[]{:S(2)}, u32[]{:S(2)}) collective-permute-start(bf16[5248,128]{1,0:T(8,128)(2,1)S(1)} %collective-permute-done.21), channel_id=1, source_target_pairs={{0,4},{4,0},{8,12},{12,8},{16,20},{20,16},{24,28},{28,24},{1,5},{5... | collective-permute-start | bytes 4030472 | tf_op jit(solution)/shard_map/ppermute | solution.py:191
  260.4 15.1 %collective-permute-start.26 = (bf16[5248,128]{1,0:T(8,128)(2,1)S(1)}, bf16[5248,128]{1,0:T(8,128)(2,1)S(1)}, u32[]{:S(2)}, u32[]{:S(2)}) collective-permute-start(bf16[5248,128]{1,0:T(8,128)(2,1)S(1)} %collective-permute-done.22), channel_id=1, source_target_pairs={{0,4},{4,0},{8,12},{12,8},{16,20},{20,16},{24,28},{28,24},{1,5},{5... | collective-permute-start | bytes 4030472 | tf_op jit(solution)/shard_map/ppermute | solution.py:191
  260.9 15.9 %collective-permute-start.14 = (bf16[4160,128]{1,0:T(8,128)(2,1)S(1)}, bf16[4160,128]{1,0:T(8,128)(2,1)S(1)}, u32[]{:S(2)}, u32[]{:S(2)}) collective-permute-start(bf16[4160,128]{1,0:T(8,128)(2,1)S(1)} %collective-permute-done.10), channel_id=1, source_target_pairs={{0,4},{4,0},{8,12},{12,8},{16,20},{20,16},{24,28},{28,24},{1,5},{5... | collective-permute-start | bytes 3194888 | tf_op jit(solution)/shard_map/ppermute | solution.py:191
  270.4 83.6 %collective-permute-start.27 = (bf16[5248,128]{1,0:T(8,128)(2,1)}, bf16[5248,128]{1,0:T(8,128)(2,1)}, u32[]{:S(2)}, u32[]{:S(2)}) collective-permute-start(bf16[5248,128]{1,0:T(8,128)(2,1)} %collective-permute-done.23), channel_id=1, source_target_pairs={{0,4},{4,0},{8,12},{12,8},{16,20},{20,16},{24,28},{28,24},{1,5},{5... | collective-permute-start | bytes 4030472 | tf_op jit(solution)/shard_map/ppermute | solution.py:191
  529.2 60.2 %collective-permute-start.41 = (bf16[2,64,1024]{1,2,0:T(8,128)(2,1)}, bf16[2,64,1024]{1,2,0:T(8,128)(2,1)}, u32[]{:S(2)}, u32[]{:S(2)}) collective-permute-start(bf16[2,64,1024]{1,2,0:T(8,128)(2,1)} %get-tuple-element.294), channel_id=1, source_target_pairs={{0,1},{1,2},{2,3},{4,5},{5,6},{6,7},{8,9},{9,10},{10,11},{12,13},{... | collective-permute-start | bytes 786440 | tf_op jit(solution)/shard_map/ppermute | solution.py:256
  531.6 67.3 %collective-permute-start.42 = (bf16[2,64,1024]{1,2,0:T(8,128)(2,1)}, bf16[2,64,1024]{1,2,0:T(8,128)(2,1)}, u32[]{:S(2)}, u32[]{:S(2)}) collective-permute-start(bf16[2,64,1024]{1,2,0:T(8,128)(2,1)} %get-tuple-element.293), channel_id=1, source_target_pairs={{1,0},{2,1},{3,2},{5,4},{6,5},{7,6},{9,8},{10,9},{11,10},{13,12},{... | collective-permute-start | bytes 786440 | tf_op jit(solution)/shard_map/ppermute | solution.py:256
  535.8 179.7 %collective-permute-start.70 = (bf16[2624,128]{1,0:T(8,128)(2,1)}, bf16[2624,128]{1,0:T(8,128)(2,1)}, u32[]{:S(2)}, u32[]{:S(2)}) collective-permute-start(bf16[2624,128]{1,0:T(8,128)(2,1)} %get-tuple-element.286), channel_id=1, source_target_pairs={{0,4},{4,0},{8,12},{12,8},{16,20},{20,16},{24,28},{28,24},{1,5},{5... | collective-permute-start | bytes 2015240 | tf_op jit(solution)/shard_map/ppermute | solution.py:191
  536.1 179.5 %collective-permute-start.73 = (bf16[2624,128]{1,0:T(8,128)(2,1)}, bf16[2624,128]{1,0:T(8,128)(2,1)}, u32[]{:S(2)}, u32[]{:S(2)}) collective-permute-start(bf16[2624,128]{1,0:T(8,128)(2,1)} %get-tuple-element.284), channel_id=1, source_target_pairs={{0,4},{4,0},{8,12},{12,8},{16,20},{20,16},{24,28},{28,24},{1,5},{5... | collective-permute-start | bytes 2015240 | tf_op jit(solution)/shard_map/ppermute | solution.py:191
  536.3 187.1 %collective-permute-start.72 = (bf16[2624,128]{1,0:T(8,128)(2,1)}, bf16[2624,128]{1,0:T(8,128)(2,1)}, u32[]{:S(2)}, u32[]{:S(2)}) collective-permute-start(bf16[2624,128]{1,0:T(8,128)(2,1)} %get-tuple-element.285), channel_id=1, source_target_pairs={{0,4},{4,0},{8,12},{12,8},{16,20},{20,16},{24,28},{28,24},{1,5},{5... | collective-permute-start | bytes 2015240 | tf_op jit(solution)/shard_map/ppermute | solution.py:191
  635.0 83.2 %collective-permute-start.44 = (bf16[4096,128]{1,0:T(8,128)(2,1)}, bf16[4096,128]{1,0:T(8,128)(2,1)}, u32[]{:S(2)}, u32[]{:S(2)}) collective-permute-start(bf16[4096,128]{1,0:T(8,128)(2,1)} %get-tuple-element.280), channel_id=1, source_target_pairs={{0,4},{4,0},{8,12},{12,8},{16,20},{20,16},{24,28},{28,24},{1,5},{5... | collective-permute-start | bytes 3145736 | tf_op jit(solution)/shard_map/ppermute | solution.py:191
  635.3 83.0 %collective-permute-start.47 = (bf16[4096,128]{1,0:T(8,128)(2,1)}, bf16[4096,128]{1,0:T(8,128)(2,1)}, u32[]{:S(2)}, u32[]{:S(2)}) collective-permute-start(bf16[4096,128]{1,0:T(8,128)(2,1)} %get-tuple-element.278), channel_id=1, source_target_pairs={{0,4},{4,0},{8,12},{12,8},{16,20},{20,16},{24,28},{28,24},{1,5},{5... | collective-permute-start | bytes 3145736 | tf_op jit(solution)/shard_map/ppermute | solution.py:191
  715.5 27.9 %collective-permute-start.69 = (bf16[2624,128]{1,0:T(8,128)(2,1)S(1)}, bf16[2624,128]{1,0:T(8,128)(2,1)S(1)}, u32[]{:S(2)}, u32[]{:S(2)}) collective-permute-start(bf16[2624,128]{1,0:T(8,128)(2,1)S(1)} %copy-done.83), channel_id=1, source_target_pairs={{0,4},{4,0},{8,12},{12,8},{16,20},{20,16},{24,28},{28,24},{1,5},{5... | collective-permute-start | bytes 2015240 | tf_op jit(solution)/shard_map/ppermute | solution.py:191
  715.6 24.5 %collective-permute-start.58 = (bf16[5248,128]{1,0:T(8,128)(2,1)S(1)}, bf16[5248,128]{1,0:T(8,128)(2,1)S(1)}, u32[]{:S(2)}, u32[]{:S(2)}) collective-permute-start(bf16[5248,128]{1,0:T(8,128)(2,1)S(1)} %copy-done.72), channel_id=1, source_target_pairs={{0,4},{4,0},{8,12},{12,8},{16,20},{20,16},{24,28},{28,24},{1,5},{5... | collective-permute-start | bytes 4030472 | tf_op jit(solution)/shard_map/ppermute | solution.py:191
  718.2 41.8 %collective-permute-start.46 = (bf16[4096,128]{1,0:T(8,128)(2,1)S(1)}, bf16[4096,128]{1,0:T(8,128)(2,1)S(1)}, u32[]{:S(2)}, u32[]{:S(2)}) collective-permute-start(bf16[4096,128]{1,0:T(8,128)(2,1)S(1)} %copy-done.77), channel_id=1, source_target_pairs={{0,4},{4,0},{8,12},{12,8},{16,20},{20,16},{24,28},{28,24},{1,5},{5... | collective-permute-start | bytes 3145736 | tf_op jit(solution)/shard_map/ppermute | solution.py:191
  718.4 18.2 %collective-permute-start.74 = (bf16[2624,128]{1,0:T(8,128)(2,1)S(1)}, bf16[2624,128]{1,0:T(8,128)(2,1)S(1)}, u32[]{:S(2)}, u32[]{:S(2)}) collective-permute-start(bf16[2624,128]{1,0:T(8,128)(2,1)S(1)} %get-tuple-element.288), channel_id=1, source_target_pairs={{0,8},{4,12},{8,0},{12,4},{16,24},{20,28},{24,16},{28,20},{1,9},{5... | collective-permute-start | bytes 2015240 | tf_op jit(solution)/shard_map/ppermute | solution.py:191
  723.4 27.6 %collective-permute-start.71 = (bf16[2624,128]{1,0:T(8,128)(2,1)S(1)}, bf16[2624,128]{1,0:T(8,128)(2,1)S(1)}, u32[]{:S(2)}, u32[]{:S(2)}) collective-permute-start(bf16[2624,128]{1,0:T(8,128)(2,1)S(1)} %get-tuple-element.287), channel_id=1, source_target_pairs={{0,8},{4,12},{8,0},{12,4},{16,24},{20,28},{24,16},{28,20},{1,9},{5... | collective-permute-start | bytes 2015240 | tf_op jit(solution)/shard_map/ppermute | solution.py:191
  736.6 36.6 %collective-permute-start.48 = (bf16[4096,128]{1,0:T(8,128)(2,1)S(1)}, bf16[4096,128]{1,0:T(8,128)(2,1)S(1)}, u32[]{:S(2)}, u32[]{:S(2)}) collective-permute-start(bf16[4096,128]{1,0:T(8,128)(2,1)S(1)} %get-tuple-element.282), channel_id=1, source_target_pairs={{0,8},{4,12},{8,0},{12,4},{16,24},{20,28},{24,16},{28,20},{1,9},{5... | collective-permute-start | bytes 3145736 | tf_op jit(solution)/shard_map/ppermute | solution.py:191
  740.1 15.9 %collective-permute-start.75 = (bf16[2624,128]{1,0:T(8,128)(2,1)S(1)}, bf16[2624,128]{1,0:T(8,128)(2,1)S(1)}, u32[]{:S(2)}, u32[]{:S(2)}) collective-permute-start(bf16[2624,128]{1,0:T(8,128)(2,1)S(1)} %add_convert_fusion.18), channel_id=1, source_target_pairs={{0,16},{4,20},{8,24},{12,28},{16,0},{20,4},{24,8},{28,12},{1,17},{... | collective-permute-start | bytes 2015240 | tf_op jit(solution)/shard_map/ppermute | solution.py:191
  743.4 31.4 %collective-permute-start.57 = (bf16[5248,128]{1,0:T(8,128)(2,1)S(1)}, bf16[5248,128]{1,0:T(8,128)(2,1)S(1)}, u32[]{:S(2)}, u32[]{:S(2)}) collective-permute-start(bf16[5248,128]{1,0:T(8,128)(2,1)S(1)} %copy-done.71), channel_id=1, source_target_pairs={{0,4},{4,0},{8,12},{12,8},{16,20},{20,16},{24,28},{28,24},{1,5},{5... | collective-permute-start | bytes 4030472 | tf_op jit(solution)/shard_map/ppermute | solution.py:191
  751.0 25.7 %collective-permute-start.61 = (bf16[5248,128]{1,0:T(8,128)(2,1)S(1)}, bf16[5248,128]{1,0:T(8,128)(2,1)S(1)}, u32[]{:S(2)}, u32[]{:S(2)}) collective-permute-start(bf16[5248,128]{1,0:T(8,128)(2,1)S(1)} %copy-done.70), channel_id=1, source_target_pairs={{0,4},{4,0},{8,12},{12,8},{16,20},{20,16},{24,28},{28,24},{1,5},{5... | collective-permute-start | bytes 4030472 | tf_op jit(solution)/shard_map/ppermute | solution.py:191
  756.1 29.6 %collective-permute-start.59 = (bf16[5248,128]{1,0:T(8,128)(2,1)S(1)}, bf16[5248,128]{1,0:T(8,128)(2,1)S(1)}, u32[]{:S(2)}, u32[]{:S(2)}) collective-permute-start(bf16[5248,128]{1,0:T(8,128)(2,1)S(1)} %add_convert_fusion.6), channel_id=1, source_target_pairs={{0,16},{4,20},{8,24},{12,28},{16,0},{20,4},{24,8},{28,12},{1,17},{... | collective-permute-start | bytes 4030472 | tf_op jit(solution)/shard_map/ppermute | solution.py:191
  760.0 69.0 %collective-permute-start.56 = (bf16[5248,128]{1,0:T(8,128)(2,1)}, bf16[5248,128]{1,0:T(8,128)(2,1)}, u32[]{:S(2)}, u32[]{:S(2)}) collective-permute-start(bf16[5248,128]{1,0:T(8,128)(2,1)} %get-tuple-element.265), channel_id=1, source_target_pairs={{0,4},{4,0},{8,12},{12,8},{16,20},{20,16},{24,28},{28,24},{1,5},{5... | collective-permute-start | bytes 4030472 | tf_op jit(solution)/shard_map/ppermute | solution.py:191
  773.2 18.2 %collective-permute-start.43 = (bf16[4096,128]{1,0:T(8,128)(2,1)S(1)}, bf16[4096,128]{1,0:T(8,128)(2,1)S(1)}, u32[]{:S(2)}, u32[]{:S(2)}) collective-permute-start(bf16[4096,128]{1,0:T(8,128)(2,1)S(1)} %copy-done.76), channel_id=1, source_target_pairs={{0,4},{4,0},{8,12},{12,8},{16,20},{20,16},{24,28},{28,24},{1,5},{5... | collective-permute-start | bytes 3145736 | tf_op jit(solution)/shard_map/ppermute | solution.py:191
  774.8 25.7 %collective-permute-start.45 = (bf16[4096,128]{1,0:T(8,128)(2,1)S(1)}, bf16[4096,128]{1,0:T(8,128)(2,1)S(1)}, u32[]{:S(2)}, u32[]{:S(2)}) collective-permute-start(bf16[4096,128]{1,0:T(8,128)(2,1)S(1)} %get-tuple-element.281), channel_id=1, source_target_pairs={{0,8},{4,12},{8,0},{12,4},{16,24},{20,28},{24,16},{28,20},{1,9},{5... | collective-permute-start | bytes 3145736 | tf_op jit(solution)/shard_map/ppermute | solution.py:191
  776.7 36.4 %collective-permute-start.76 = (bf16[656,128]{1,0:T(8,128)(2,1)S(1)}, bf16[656,128]{1,0:T(8,128)(2,1)S(1)}, u32[]{:S(2)}, u32[]{:S(2)}) collective-permute-start(bf16[656,128]{1,0:T(8,128)(2,1)S(1)} %get-tuple-element.327), channel_id=1, source_target_pairs={{0,1},{4,5},{8,9},{12,13},{16,17},{20,21},{24,25},{28,29}} | collective-permute-start | bytes 503816 | tf_op jit(solution)/shard_map/ppermute | solution.py:184
  785.7 23.1 %collective-permute-start.49 = (bf16[4096,128]{1,0:T(8,128)(2,1)S(1)}, bf16[4096,128]{1,0:T(8,128)(2,1)S(1)}, u32[]{:S(2)}, u32[]{:S(2)}) collective-permute-start(bf16[4096,128]{1,0:T(8,128)(2,1)S(1)} %add_convert_fusion.10), channel_id=1, source_target_pairs={{0,16},{4,20},{8,24},{12,28},{16,0},{20,4},{24,8},{28,12},{1,17},{... | collective-permute-start | bytes 3145736 | tf_op jit(solution)/shard_map/ppermute | solution.py:191
  791.4 25.7 %collective-permute-start.79 = (bf16[656,128]{1,0:T(8,128)(2,1)S(1)}, bf16[656,128]{1,0:T(8,128)(2,1)S(1)}, u32[]{:S(2)}, u32[]{:S(2)}) collective-permute-start(bf16[656,128]{1,0:T(8,128)(2,1)S(1)} %get-tuple-element.328), channel_id=1, source_target_pairs={{3,2},{7,6},{11,10},{15,14},{19,18},{23,22},{27,26},{31,30}} | collective-permute-start | bytes 503816 | tf_op jit(solution)/shard_map/ppermute | solution.py:185
  800.5 31.7 %collective-permute-start.60 = (bf16[5248,128]{1,0:T(8,128)(2,1)}, bf16[5248,128]{1,0:T(8,128)(2,1)}, u32[]{:S(2)}, u32[]{:S(2)}) collective-permute-start(bf16[5248,128]{1,0:T(8,128)(2,1)} %get-tuple-element.269), channel_id=1, source_target_pairs={{0,8},{4,12},{8,0},{12,4},{16,24},{20,28},{24,16},{28,20},{1,9},{5... | collective-permute-start | bytes 4030472 | tf_op jit(solution)/shard_map/ppermute | solution.py:191
  808.8 28.0 %collective-permute-start.62 = (bf16[5248,128]{1,0:T(8,128)(2,1)}, bf16[5248,128]{1,0:T(8,128)(2,1)}, u32[]{:S(2)}, u32[]{:S(2)}) collective-permute-start(bf16[5248,128]{1,0:T(8,128)(2,1)} %get-tuple-element.270), channel_id=1, source_target_pairs={{0,16},{4,20},{8,24},{12,28},{16,0},{20,4},{24,8},{28,12},{1,17},{... | collective-permute-start | bytes 4030472 | tf_op jit(solution)/shard_map/ppermute | solution.py:191
  825.8 18.5 %collective-permute-start.77 = (bf16[656,128]{1,0:T(8,128)(2,1)S(1)}, bf16[656,128]{1,0:T(8,128)(2,1)S(1)}, u32[]{:S(2)}, u32[]{:S(2)}) collective-permute-start(bf16[656,128]{1,0:T(8,128)(2,1)S(1)} %get-tuple-element.325), channel_id=1, source_target_pairs={{0,1},{1,2},{4,5},{5,6},{8,9},{9,10},{12,13},{13,14},{16,17},{17,1... | collective-permute-start | bytes 503816 | tf_op jit(solution)/shard_map/ppermute | solution.py:184
  827.1 17.9 %collective-permute-start.80 = (bf16[656,128]{1,0:T(8,128)(2,1)S(1)}, bf16[656,128]{1,0:T(8,128)(2,1)S(1)}, u32[]{:S(2)}, u32[]{:S(2)}) collective-permute-start(bf16[656,128]{1,0:T(8,128)(2,1)S(1)} %get-tuple-element.326), channel_id=1, source_target_pairs={{2,1},{3,2},{6,5},{7,6},{10,9},{11,10},{14,13},{15,14},{18,17},{19... | collective-permute-start | bytes 503816 | tf_op jit(solution)/shard_map/ppermute | solution.py:185
  829.0 17.5 %collective-permute-start.51 = (bf16[1024,128]{1,0:T(8,128)(2,1)S(1)}, bf16[1024,128]{1,0:T(8,128)(2,1)S(1)}, u32[]{:S(2)}, u32[]{:S(2)}) collective-permute-start(bf16[1024,128]{1,0:T(8,128)(2,1)S(1)} %get-tuple-element.319), channel_id=1, source_target_pairs={{0,1},{1,2},{4,5},{5,6},{8,9},{9,10},{12,13},{13,14},{16,17},{17,1... | collective-permute-start | bytes 786440 | tf_op jit(solution)/shard_map/ppermute | solution.py:184
  832.2 15.5 %collective-permute-start.54 = (bf16[1024,128]{1,0:T(8,128)(2,1)S(1)}, bf16[1024,128]{1,0:T(8,128)(2,1)S(1)}, u32[]{:S(2)}, u32[]{:S(2)}) collective-permute-start(bf16[1024,128]{1,0:T(8,128)(2,1)S(1)} %get-tuple-element.320), channel_id=1, source_target_pairs={{2,1},{3,2},{6,5},{7,6},{10,9},{11,10},{14,13},{15,14},{18,17},{19... | collective-permute-start | bytes 786440 | tf_op jit(solution)/shard_map/ppermute | solution.py:185
  845.2 13.4 %collective-permute-start.78 = (bf16[656,128]{1,0:T(8,128)(2,1)S(1)}, bf16[656,128]{1,0:T(8,128)(2,1)S(1)}, u32[]{:S(2)}, u32[]{:S(2)}) collective-permute-start(bf16[656,128]{1,0:T(8,128)(2,1)S(1)} %get-tuple-element.323), channel_id=1, source_target_pairs={{0,1},{1,2},{2,3},{4,5},{5,6},{6,7},{8,9},{9,10},{10,11},{12,13},{... | collective-permute-start | bytes 503816 | tf_op jit(solution)/shard_map/ppermute | solution.py:184
  864.7 22.0 %collective-permute-start.65 = (bf16[1312,128]{1,0:T(8,128)(2,1)}, bf16[1312,128]{1,0:T(8,128)(2,1)}, u32[]{:S(2)}, u32[]{:S(2)}) collective-permute-start(bf16[1312,128]{1,0:T(8,128)(2,1)} %get-tuple-element.307), channel_id=1, source_target_pairs={{0,1},{1,2},{2,3},{4,5},{5,6},{6,7},{8,9},{9,10},{10,11},{12,13},{... | collective-permute-start | bytes 1007624 | tf_op jit(solution)/shard_map/ppermute | solution.py:184
  873.7 13.0 %collective-permute-start.68 = (bf16[1312,128]{1,0:T(8,128)(2,1)}, bf16[1312,128]{1,0:T(8,128)(2,1)}, u32[]{:S(2)}, u32[]{:S(2)}) collective-permute-start(bf16[1312,128]{1,0:T(8,128)(2,1)} %get-tuple-element.308), channel_id=1, source_target_pairs={{1,0},{2,1},{3,2},{5,4},{6,5},{7,6},{9,8},{10,9},{11,10},{13,12},{... | collective-permute-start | bytes 1007624 | tf_op jit(solution)/shard_map/ppermute | solution.py:185
  (143 other events, 2068.5 us)

commit v3 on v2

v3 whole, which is shorter than its diff:
```python
import functools
import math

import jax
import jax.numpy as jnp
from jax import lax
from jax.experimental import pallas as pl
from jax.experimental.pallas import tpu as pltpu
from jax.sharding import PartitionSpec as P

D = 1024
HEADS = 16
HEAD_DIM = 64
FF = 2624
HALF = 64
BLOCK = 128
STEP = 10

NORM_EPS = 1e-05
THETA_BASE = 10000.0
BETA_ONE = 0.9
BETA_TWO = 0.98
ADAM_EPS = 1e-06
WEIGHT_DECAY = 0.01
GAIN_RATE = 0.5
MASKED = -1e30


LANES = 128
PIECES = 8
SLAB_PAD = 16
VMEM_BYTES = 52 * 1024 * 1024


def layout(lengths, token_index, group_rows):
    seq_ends = jnp.cumsum(lengths)
    seq_starts = seq_ends - lengths
    segment = jnp.sum((token_index[:, None] >= seq_ends[None, :]).astype(jnp.int32), axis=1)
    member = segment[:, None] == jnp.arange(lengths.shape[0])[None, :]
    position = token_index - jnp.sum(jnp.where(member, seq_starts[None, :], 0), axis=1)
    inside = (token_index >= 0) & (token_index < group_rows)
    return (jnp.where(inside, segment, -1), jnp.where(inside, position, 0))


def rotary_tables(position):
    half_dim = HEAD_DIM // 2
    exponent = jnp.arange(half_dim).astype(jnp.float32) * (2.0 / HEAD_DIM)
    inverse = jnp.power(jnp.float32(THETA_BASE), -exponent)
    angle_table = position.astype(jnp.float32)[:, None] * inverse[None, :]
    copies = LANES // half_dim
    return (jnp.tile(jnp.cos(angle_table), (1, copies)), jnp.tile(jnp.sin(angle_table), (1, copies)))


def windows(rows):
    count = (rows.shape[0] - 2 * HALF) // BLOCK
    return jnp.stack([rows[n * BLOCK : n * BLOCK + BLOCK + 2 * HALF] for n in range(count)])


def allowed_pairs(segment):
    key_seg = windows(segment)
    query_seg = segment[HALF:-HALF].reshape(-1, BLOCK)
    offset = jnp.arange(BLOCK)[:, None] + HALF - jnp.arange(BLOCK + 2 * HALF)[None, :]
    return (query_seg[:, :, None] == key_seg[:, None, :]) & (jnp.abs(offset) <= HALF)[None]


def adam_update(master, gradient, moment_one, moment_two, step_rate):
    one_new = BETA_ONE * moment_one + (1.0 - BETA_ONE) * gradient
    two_new = BETA_TWO * moment_two + (1.0 - BETA_TWO) * gradient * gradient
    one_hat = one_new / (1.0 - BETA_ONE**STEP)
    two_hat = two_new / (1.0 - BETA_TWO**STEP)
    master_new = master - step_rate * (
        one_hat / (jnp.sqrt(two_hat) + ADAM_EPS) + WEIGHT_DECAY * master
    )
    return (one_new, two_new, master_new)


def line_gather(slab):
    size = lax.axis_size("tensor")
    place = lax.axis_index("tensor")
    from_before, from_after = [slab], [slab]
    for step in range(1, size):
        from_before.append(
            lax.ppermute(from_before[-1], "tensor", [(n, n + 1) for n in range(step - 1, size - 1)])
        )
        from_after.append(
            lax.ppermute(from_after[-1], "tensor", [(n, n - 1) for n in range(1, size - step + 1)])
        )
    return jnp.stack(
        [slab]
        + [
            jnp.where(place >= step, from_before[step], from_after[size - step])
            for step in range(1, size)
        ]
    )


def line_scatter(parts):
    size = lax.axis_size("tensor")
    up, down = 0.0, 0.0
    for step in range(size - 1, 0, -1):
        to_after = (parts[size - step].astype(jnp.float32) + up).astype(parts.dtype)
        to_before = (parts[step].astype(jnp.float32) + down).astype(parts.dtype)
        up = lax.ppermute(to_after, "tensor", [(n, n + 1) for n in range(size - step)])
        down = lax.ppermute(to_before, "tensor", [(n, n - 1) for n in range(step, size)])
        up, down = up.astype(jnp.float32), down.astype(jnp.float32)
    return parts[0].astype(jnp.float32) + up + down


def flip(rows, mask):
    return lax.ppermute(rows, "dp", [(n, n ^ mask) for n in range(lax.axis_size("dp"))])


def far_bits():
    size = lax.axis_size("dp")
    return [1 << n for n in range(3, size.bit_length() - 1)]


def gather(slab, x_first):
    piece = line_gather(slab)
    piece = piece.reshape(-1, piece.shape[-1])
    for mask in far_bits():
        piece = jnp.concatenate([piece, flip(piece, mask)], axis=1)
    by_x, by_y = flip(piece, 2), flip(piece, 4)
    far = flip(by_x, 4) if x_first else flip(by_y, 2)
    mine = [piece, by_x, by_y, far]
    return (mine + [flip(part, 1) for part in mine], piece)


def add_low(left, right):
    return (left.astype(jnp.float32) + right.astype(jnp.float32)).astype(left.dtype)


def scatter(own, partner, x_first):
    received = flip(partner, 1)
    own, by_x, by_y, far = [add_low(mine, received[n]) for n, mine in enumerate(own)]
    if x_first:
        passed = flip(far, 2)
        by_y = add_low(by_y, passed)
    else:
        passed = flip(far, 4)
        by_x = add_low(by_x, passed)
    from_x, from_y = flip(by_x, 2), flip(by_y, 4)
    total = (
        own.astype(jnp.float32) + from_x.astype(jnp.float32) + from_y.astype(jnp.float32)
    ).astype(own.dtype)
    for mask in reversed(far_bits()):
        half = total.shape[1] // 2
        total = add_low(total[:, :half], flip(total[:, half:], mask))
    size = lax.axis_size("tensor")
    total = total.reshape(size, total.shape[0] // size, total.shape[1])
    return (total, (received, passed, from_x, from_y))


def to_relative(rows, back=False):
    size = lax.axis_size("dp")
    place = lax.axis_index("dp")
    bits = size.bit_length() - 1
    lead = rows.shape[:-1]
    axes = len(lead)
    chunk = rows.shape[-1] // size
    wanted = [bits - 1, bits - 3, bits - 2] + list(range(bits - 3))
    order = list(range(axes)) + [axes + n for n in wanted] + [axes + bits]
    cube = rows.reshape(lead + (2,) * bits + (chunk,))
    if back:
        cube = jnp.transpose(cube, [order.index(n) for n in range(len(order))])
    for n in range(bits):
        cube = jnp.where((place >> (bits - 1 - n)) & 1 == 1, jnp.flip(cube, axes + n), cube)
    if not back:
        cube = jnp.transpose(cube, order)
    return cube.reshape(rows.shape)


def shift(rows, step):
    size = lax.axis_size("tensor")
    pairs = [(n, n + step) for n in range(size) if 0 <= n + step < size]
    return lax.ppermute(rows, "tensor", pairs)


NN = ((1,), (0,))
NT = ((1,), (1,))
TN = ((0,), (0,))


def dot(left, right, dims):
    return lax.dot_general(left, right, (dims, ((), ())), preferred_element_type=jnp.float32)


def wide(pieces, rows):
    return jnp.concatenate([piece[0, rows, :] for piece in pieces], axis=1)


def relative(order, ref, rows):
    return jnp.concatenate(
        [
            ref[rows, pl.ds(pl.multiple_of(order[n] * LANES, LANES), LANES)]
            for n in range(PIECES)
        ],
        axis=1,
    )


def normed(values):
    centered = values - jnp.mean(values, axis=-1, keepdims=True)
    scale = lax.rsqrt(jnp.mean(centered * centered, axis=-1, keepdims=True) + NORM_EPS)
    return (centered * scale, scale)


def norm_pull(hat, scale, gain, grad):
    scaled = grad * gain
    return scale * (
        scaled
        - jnp.mean(scaled, axis=-1, keepdims=True)
        - hat * jnp.mean(scaled * hat, axis=-1, keepdims=True)
    )


def row_steps(count, size, body):
    def step(n, carried):
        body(pl.ds(pl.multiple_of(n * size, size), size))
        return carried

    lax.fori_loop(0, count // size, step, 0)


def whole_spec(array):
    return pl.BlockSpec(array.shape, lambda *_: (0,) * len(array.shape))


def run(kernel, name, operands, outs, scratch, flops, after=()):
    order, operands = operands[0], operands[1:]
    specs = [spec if spec is not None else whole_spec(array) for array, spec in operands]
    out_specs = [
        spec if spec is not None else pl.BlockSpec(shape, lambda *_, n=len(shape): (0,) * n)
        for shape, dtype, spec in outs
    ]
    moved = sum(array.size * array.dtype.itemsize for array, _ in operands)
    moved += sum(math.prod(shape) * jnp.dtype(dtype).itemsize for shape, dtype, _ in outs)
    kept = len(operands)

    def body(order_ref, *refs):
        kernel(order_ref, *refs[:kept], *refs[kept + len(after) :])

    return pl.pallas_call(
        body,
        grid_spec=pltpu.PrefetchScalarGridSpec(
            num_scalar_prefetch=1,
            grid=(lax.axis_size("tensor"),),
            in_specs=specs + [pl.BlockSpec(memory_space=pl.ANY)] * len(after),
            out_specs=out_specs,
            scratch_shapes=scratch,
        ),
        out_shape=[jax.ShapeDtypeStruct(shape, dtype) for shape, dtype, _ in outs],
        compiler_params=pltpu.CompilerParams(
            dimension_semantics=("arbitrary",), vmem_limit_bytes=VMEM_BYTES
        ),
        cost_estimate=pl.CostEstimate(flops=flops, bytes_accessed=moved, transcendentals=0),
        name=name,
    )(order, *[array for array, _ in operands], *after)


def slabs(piece, rows, first=0):
    return (piece, pl.BlockSpec((1, rows, LANES), lambda n, *_: (n, first, 0)))


def lead(array):
    shape = (1,) + array.shape[1:]
    return (array, pl.BlockSpec(shape, lambda n, *_: (n,) + (0,) * (len(shape) - 1)))


def lead_out(shape, dtype):
    return (shape, dtype, pl.BlockSpec((1,) + shape[1:], lambda n, *_: (n,) + (0,) * (len(shape) - 1)))


def piece_outs(parts, rows):
    low = jnp.bfloat16
    own = pl.BlockSpec((1, rows, LANES), lambda n, *_: (n, 0, 0))
    other = pl.BlockSpec((4, 1, rows, LANES), lambda n, *_: (0, n, 0, 0))
    return [((parts, rows, LANES), low, own)] * 4 + [((4, parts, rows, LANES), low, other)]


def store_pieces(refs, rows, values):
    values = values.astype(jnp.bfloat16)
    for n in range(4):
        refs[n][0, rows, :] = values[:, n * LANES : (n + 1) * LANES]
        refs[4][n, 0, rows, :] = values[:, (n + 4) * LANES : (n + 5) * LANES]


def heads_kernel(order, hidden, before, after, gains, cosine, sine, *refs):
    pieces, (q_out, k_out, v_out, rows_out, rows_wide) = refs[:PIECES], refs[PIECES:]
    row_count = hidden.shape[0]
    gain = gains[0:1, :]

    def norm_rows(source, rows, first):
        values = relative(order, source, rows).astype(jnp.float32)
        return (normed(values)[0] * gain).astype(jnp.bfloat16)

    @pl.when(pl.program_id(0) == 0)
    def _():
        rows_wide[0:HALF, :] = norm_rows(before, slice(0, HALF), 0)
        rows_wide[HALF + row_count :, :] = norm_rows(after, slice(0, HALF), 0)

        def one(rows):
            values = norm_rows(hidden, rows, 0)
            rows_out[rows, :] = values
            rows_wide[pl.ds(pl.multiple_of(rows.start + HALF, HALF), HALF), :] = values

        row_steps(row_count, HALF, one)

    width = 2 * LANES

    def turned(mixed, rows):
        front, back = mixed[:, :LANES], mixed[:, LANES:]
        cos, sin = cosine[rows, :], sine[rows, :]
        return (front * cos - back * sin, back * cos + front * sin)

    inner = slice(HALF, HALF + row_count)
    scale = HEAD_DIM ** (-0.5)
    front, back = turned(dot(rows_out[...], wide(pieces, slice(0, width)), NT), inner)
    q_out[0, :, :LANES] = (front.astype(jnp.bfloat16) * scale).astype(jnp.bfloat16)
    q_out[0, :, LANES:] = (back.astype(jnp.bfloat16) * scale).astype(jnp.bfloat16)
    front, back = turned(
        dot(rows_wide[...], wide(pieces, slice(width, 2 * width)), NT), slice(None)
    )
    k_out[0, :, :LANES] = front.astype(jnp.bfloat16)
    k_out[0, :, LANES:] = back.astype(jnp.bfloat16)
    v_out[0] = dot(rows_wide[...], wide(pieces, slice(2 * width, 3 * width)), NT).astype(
        jnp.bfloat16
    )


def head_masks():
    lane = lax.broadcasted_iota(jnp.int32, (1, 2 * LANES), 1)
    turned = [((lane % LANES) // 32 == n).astype(jnp.float32).astype(jnp.bfloat16) for n in range(4)]
    plain = [(lane // HEAD_DIM == n).astype(jnp.float32).astype(jnp.bfloat16) for n in range(4)]
    return (turned, plain)


def attend_kernel(order, bias, q_in, k_in, v_in, out, log_out):
    turned, plain = head_masks()
    lane = lax.broadcasted_iota(jnp.int32, (BLOCK, LANES), 1)

    def block(n, carried):
        rows = pl.ds(pl.multiple_of(n * BLOCK, BLOCK), BLOCK)
        span = pl.ds(pl.multiple_of(n * BLOCK, BLOCK), BLOCK + 2 * HALF)
        queries, keys, values = q_in[0, rows, :], k_in[0, span, :], v_in[0, span, :]
        masked = bias[n]
        total = jnp.zeros((BLOCK, 2 * LANES), jnp.float32)
        logs = jnp.zeros((BLOCK, LANES), jnp.float32)
        for h in range(4):
            scores = dot(queries * turned[h], keys, NT) + masked
            row_top = jnp.max(scores, axis=-1, keepdims=True)
            lifted = jnp.exp(scores - row_top)
            row_total = jnp.sum(lifted, axis=-1, keepdims=True)
            probs_low = (lifted * (1.0 / row_total)).astype(jnp.bfloat16)
            total = total + dot(probs_low, values * plain[h], NN)
            logs = jnp.where(lane == h, row_top + jnp.log(row_total), logs)
        out[0, rows, :] = total.astype(jnp.bfloat16)
        log_out[0, rows, :] = logs
        return carried

    lax.fori_loop(0, bias.shape[0], block, 0)


def proj_kernel(order, hidden, gains, attended, *refs):
    pieces, (middle, rows_two) = refs[:PIECES], refs[PIECES:]
    step = pl.program_id(0)

    @pl.when(step == 0)
    def _():
        def one(rows):
            middle[rows, :] = relative(order, hidden, rows).astype(jnp.float32)

        row_steps(hidden.shape[0], HALF, one)

    middle[...] += dot(attended[0], wide(pieces, slice(None)), NN)

    @pl.when(step == pl.num_programs(0) - 1)
    def _():
        def one(rows):
            rows_two[rows, :] = (normed(middle[rows, :])[0] * gains[1:2, :]).astype(jnp.bfloat16)

        row_steps(hidden.shape[0], HALF, one)


def gate_kernel(order, rows_two, *refs):
    pieces, (active, gate_side, up_side, rows_turned, gate, up) = refs[:PIECES], refs[PIECES:]

    @pl.when(pl.program_id(0) == 0)
    def _():
        rows_turned[...] = rows_two[...].T

    count = gate.shape[0]
    gate[...] = dot(wide(pieces, slice(0, count)), rows_turned[...], NN)
    up[...] = dot(wide(pieces, slice(count, 2 * count)), rows_turned[...], NN)

    def one(rows):
        x, u = gate[rows, :], up[rows, :]
        below = 0.5 * (1.0 + lax.erf(x * (0.5**0.5)))
        density = jnp.exp(-0.5 * x * x) * ((2.0 * math.pi) ** -0.5)
        lifted = x * below
        active[rows, :] = (lifted * u).astype(jnp.bfloat16)
        gate_side[rows, :] = (u * (below + x * density)).astype(jnp.bfloat16)
        up_side[rows, :] = lifted.astype(jnp.bfloat16)

    row_steps(count, 16, one)


def down_kernel(order, middle, active, *refs):
    pieces, (out, total) = refs[:PIECES], refs[PIECES:]
    step = pl.program_id(0)

    @pl.when(step == 0)
    def _():
        total[...] = middle[...]

    total[...] += dot(active[...], wide(pieces, slice(None)), TN)

    @pl.when(step == pl.num_programs(0) - 1)
    def _():
        for n in range(PIECES):
            lanes = pl.ds(pl.multiple_of(order[n] * LANES, LANES), LANES)
            out[:, lanes] = total[:, n * LANES : (n + 1) * LANES].astype(jnp.bfloat16)


def down_grad_kernel(order, cotangent, active, *refs):
    pieces, (cot_out,) = refs[:5], refs[5:]

    @pl.when(pl.program_id(0) == 0)
    def _():
        def one(rows):
            cot_out[rows, :] = relative(order, cotangent, rows)

        row_steps(cotangent.shape[0], HALF, one)

    store_pieces(pieces, slice(None), dot(active[...], cot_out[...], NN))


def in_grad_kernel(order, cot, rows_two, gate_side, up_side, *refs):
    pieces, grads = refs[:PIECES], refs[PIECES : PIECES + 5]
    gate_out, up_out, cot_turned, grad_active = refs[PIECES + 5 :]

    @pl.when(pl.program_id(0) == 0)
    def _():
        cot_turned[...] = cot[...].T

    count = grad_active.shape[0]
    grad_active[...] = dot(wide(pieces, slice(None)), cot_turned[...], NN)

    def one(rows):
        grad = grad_active[rows, :]
        gate_out[rows, :] = (grad * gate_side[rows, :].astype(jnp.float32)).astype(jnp.bfloat16)
        up_out[rows, :] = (grad * up_side[rows, :].astype(jnp.float32)).astype(jnp.bfloat16)

    row_steps(count, 16, one)
    store_pieces(grads, slice(0, count), dot(gate_out[...], rows_two[...], NN))
    store_pieces(grads, slice(count, 2 * count), dot(up_out[...], rows_two[...], NN))


def middle_grad_kernel(order, middle, cot, gains, gate_grad, up_grad, *refs):
    pieces, (grad_middle, grad_low, gain_out, total) = refs[:PIECES], refs[PIECES:]
    step = pl.program_id(0)
    count = gate_grad.shape[0]

    @pl.when(step == 0)
    def _():
        total[...] = jnp.zeros_like(total)
        gain_out[...] = jnp.zeros_like(gain_out)

    total[...] += dot(gate_grad[...], wide(pieces, slice(0, count)), TN)
    total[...] += dot(up_grad[...], wide(pieces, slice(count, 2 * count)), TN)

    @pl.when(step == pl.num_programs(0) - 1)
    def _():
        def one(rows):
            grad = total[rows, :]
            hat, scale = normed(middle[rows, :])
            result = cot[rows, :].astype(jnp.float32) + norm_pull(hat, scale, gains[1:2, :], grad)
            grad_middle[rows, :] = result
            grad_low[rows, :] = result.astype(jnp.bfloat16)
            gain_out[0:1, :] += jnp.sum(grad * hat, axis=0, keepdims=True)

        row_steps(middle.shape[0], HALF, one)


def attend_grad_kernel(order, bias, cosine, sine, grad_low, q_in, k_in, v_in, logs, *refs):
    pieces, (grads, edges, grad_keys, grad_values, grad_out) = refs[:PIECES], refs[PIECES:]
    turned, plain = head_masks()
    row_count = grad_low.shape[0]
    low = jnp.bfloat16
    grad_out[...] = dot(grad_low[...], wide(pieces, slice(None)), NT).astype(low)
    grad_keys[...] = jnp.zeros_like(grad_keys)
    grad_values[...] = jnp.zeros_like(grad_values)

    def back(values, rows):
        front, rear = values[:, :LANES], values[:, LANES:]
        cos, sin = cosine[rows, :], sine[rows, :]
        return (front * cos + rear * sin, rear * cos - front * sin)

    def block(n, carried):
        rows = pl.ds(pl.multiple_of(n * BLOCK, BLOCK), BLOCK)
        span = pl.ds(pl.multiple_of(n * BLOCK, BLOCK), BLOCK + 2 * HALF)
        queries, keys, values = q_in[0, rows, :], k_in[0, span, :], v_in[0, span, :]
        grad_rows = grad_out[rows, :]
        masked = bias[n]
        log_rows = logs[0, rows, :]
        grad_query = jnp.zeros((BLOCK, 2 * LANES), jnp.float32)
        grad_key = jnp.zeros((BLOCK + 2 * HALF, 2 * LANES), jnp.float32)
        grad_value = jnp.zeros((BLOCK + 2 * HALF, 2 * LANES), jnp.float32)
        for h in range(4):
            query_head, grad_head = queries * turned[h], grad_rows * plain[h]
            scores = dot(query_head, keys, NT) + masked
            probs = jnp.exp(scores - log_rows[:, h : h + 1])
            grad_probs = dot(grad_head, values, NT)
            row_delta = jnp.sum(probs * grad_probs, axis=-1, keepdims=True)
            grad_scores = (probs * (grad_probs - row_delta)).astype(low)
            grad_query = grad_query + dot(grad_scores, keys * turned[h], NN)
            grad_key = grad_key + dot(grad_scores, query_head, TN)
            grad_value = grad_value + dot(probs.astype(low), grad_head, TN)
        place = pl.ds(pl.multiple_of(n * BLOCK + HALF, HALF), BLOCK)
        front, rear = back(grad_query * HEAD_DIM ** (-0.5), place)
        grads[0, 0, rows, :LANES] = front.astype(low)
        grads[0, 0, rows, LANES:] = rear.astype(low)
        grad_keys[span, :] += grad_key
        grad_values[span, :] += grad_value
        return carried

    lax.fori_loop(0, bias.shape[0], block, 0)
    inner = slice(HALF, HALF + row_count)
    for rows, out in (
        (inner, lambda n: grads.at[0, 1 + n]),
        (slice(0, HALF), lambda n: edges.at[0, 0, n]),
        (slice(HALF + row_count, None), lambda n: edges.at[0, 1, n]),
    ):
        front, rear = back(grad_keys[rows, :], rows)
        out(0)[:, :LANES] = front.astype(low)
        out(0)[:, LANES:] = rear.astype(low)
        out(1)[...] = grad_values[rows, :].astype(low)


def heads_grad_kernel(
    order, hidden, gains, gain_two, grad_middle, grad_low, rows_one, attended, grads, before, after, *refs
):
    pieces, outs = refs[:PIECES], refs[PIECES : PIECES + 5]
    grad_input, mixed, total, gain_one = refs[PIECES + 5 :]
    step = pl.program_id(0)
    row_count = hidden.shape[0]
    width = 2 * LANES
    last = row_count - HALF

    @pl.when(step == 0)
    def _():
        total[...] = jnp.zeros_like(total)
        gain_one[...] = jnp.zeros_like(gain_one)

    def add_low(left, right):
        return (left.astype(jnp.float32) + right.astype(jnp.float32)).astype(jnp.bfloat16)

    mixed[...] = grads[0]
    for c in range(2):
        mixed[1 + c, 0:HALF, :] = add_low(grads[0, 1 + c, 0:HALF, :], before[0, c])
        mixed[1 + c, last:, :] = add_low(grads[0, 1 + c, last:, :], after[0, c])
    for c in range(3):
        rows = slice(c * width, (c + 1) * width)
        total[...] += dot(mixed[c], wide(pieces, rows), NN)
        store_pieces(outs, rows, dot(mixed[c], rows_one[...], TN))
    store_pieces(outs, slice(3 * width, 4 * width), dot(attended[0], grad_low[...], TN))
    tail = slice(4 * width, 4 * width + SLAB_PAD)
    store_pieces(outs, tail, jnp.zeros((SLAB_PAD, PIECES * LANES), jnp.float32))

    @pl.when(step == pl.num_programs(0) - 1)
    def _():
        def one(rows):
            grad = total[rows, :]
            hat, scale = normed(relative(order, hidden, rows).astype(jnp.float32))
            result = grad_middle[rows, :] + norm_pull(hat, scale, gains[0:1, :], grad)
            for n in range(PIECES):
                lanes = pl.ds(pl.multiple_of(order[n] * LANES, LANES), LANES)
                grad_input[rows, lanes] = result[:, n * LANES : (n + 1) * LANES]
            gain_one[0:1, :] += jnp.sum(grad * hat, axis=0, keepdims=True)

        row_steps(row_count, HALF, one)
        both = jnp.concatenate(
            [gain_one[0:1, :], gain_two[0:1, :], jnp.zeros((SLAB_PAD - 2, PIECES * LANES), jnp.float32)],
            axis=0,
        )
        store_pieces(outs, tail, both)


def local(
    hidden_in,
    seq_lengths,
    cotangent,
    w_qkv,
    w_proj,
    w_in,
    w_down,
    norm_gains,
    qkv_first,
    qkv_second,
    proj_first,
    proj_second,
    in_first,
    in_second,
    down_first,
    down_second,
    gain_first,
    gain_second,
):
    row_count = hidden_in.shape[0]
    wide_count = row_count + 2 * HALF
    size = lax.axis_size("tensor")
    dp_size = lax.axis_size("dp")
    group_rows = row_count * size
    low, full = jnp.bfloat16, jnp.float32
    chunk = norm_gains.shape[1]
    head_wide = w_proj.shape[1]
    head_rows = 4 * head_wide
    slab_rows = head_rows + SLAB_PAD
    hidden_wide = w_down.shape[1]
    head_count, half_dim = head_wide // HEAD_DIM, HEAD_DIM // 2

    def halves_first(weight):
        split = weight.reshape(chunk, 2, head_count, 2, half_dim)
        return jnp.transpose(split, (0, 1, 3, 2, 4)).reshape(chunk, 2 * head_wide)

    def heads_first(weight):
        split = weight.reshape(chunk, 2, 2, head_count, half_dim)
        return jnp.transpose(split, (0, 1, 3, 2, 4)).reshape(chunk, 2, head_wide)

    heads_slab = jnp.concatenate(
        [
            jnp.concatenate(
                [halves_first(w_qkv[:, :2].astype(low)), w_qkv[:, 2].astype(low), w_proj.astype(low)],
                axis=1,
            ).T,
            jnp.pad(norm_gains.astype(low), ((0, SLAB_PAD - 2), (0, 0))),
        ]
    )
    in_slab = w_in.astype(low).reshape(chunk, 2 * hidden_wide).T
    down_slab = w_down.astype(low).T
    if dp_size == PIECES:
        place = jnp.array([0, 2, 4, 6, 1, 3, 5, 7], jnp.int32)
        order = lax.axis_index("dp").astype(jnp.int32) ^ place
        hidden, cot_in = hidden_in, cotangent
    else:
        order = jnp.arange(PIECES, dtype=jnp.int32)
        hidden, cot_in = to_relative(hidden_in), to_relative(cotangent)

    edges = (shift(hidden[-HALF:], 1), shift(hidden[:HALF], -1))
    heads_pieces, heads_line = gather(heads_slab, True)
    in_pieces, in_line = gather(in_slab, False)
    down_pieces, down_line = gather(down_slab, True)
    heads_pieces = [piece.reshape(size, -1, LANES) for piece in heads_pieces]
    in_pieces = [piece.reshape(size, -1, LANES) for piece in in_pieces]
    down_pieces = [piece.reshape(size, -1, LANES) for piece in down_pieces]
    gains = jnp.concatenate(
        [piece[0, head_rows : head_rows + 8] for piece in heads_pieces], axis=1
    ).astype(full)

    first_row = lax.axis_index("tensor") * row_count
    segment, position = layout(
        seq_lengths[0], first_row - HALF + jnp.arange(wide_count), group_rows
    )
    cosine, sine = rotary_tables(position)
    bias = jnp.where(allowed_pairs(segment), 0.0, MASKED).astype(full)

    head_block = (size, row_count, head_wide)
    wide_block = (size, wide_count, head_wide)
    tokens = (row_count, D)
    turned = (size * hidden_wide, row_count)
    turned_spec = pl.BlockSpec((hidden_wide, row_count), lambda n, *_: (n, 0))
    matmul = 2 * row_count * D

    queries, keys, values, rows_one = run(
        heads_kernel,
        "heads",
        [order, (hidden, None), (edges[0], None), (edges[1], None), (gains, None)]
        + [(cosine, None), (sine, None)]
        + [slabs(piece, 3 * head_wide) for piece in heads_pieces],
        [lead_out(head_block, low), lead_out(wide_block, low), lead_out(wide_block, low)]
        + [(tokens, low, None)],
        [pltpu.VMEM((wide_count, D), low)],
        3 * matmul * D,
        after=(in_line, down_line),
    )
    attended, logs = run(
        attend_kernel,
        "attend",
        [order, (bias, None), lead(queries), lead(keys), lead(values)],
        [lead_out(head_block, low), lead_out((size, row_count, LANES), full)],
        [],
        2 * matmul * D,
    )
    middle, rows_two = run(
        proj_kernel,
        "proj",
        [order, (hidden, None), (gains, None), lead(attended)]
        + [slabs(piece, head_wide, 3) for piece in heads_pieces],
        [(tokens, full, None), (tokens, low, None)],
        [],
        matmul * D,
    )
    active, gate_side, up_side = run(
        gate_kernel,
        "gate",
        [order, (rows_two, None)] + [slabs(piece, 2 * hidden_wide) for piece in in_pieces],
        [(turned, low, turned_spec)] * 3,
        [
            pltpu.VMEM((D, row_count), low),
            pltpu.VMEM((hidden_wide, row_count), full),
            pltpu.VMEM((hidden_wide, row_count), full),
        ],
        2 * matmul * FF,
    )

    *down_own, down_partner, cot = run(
        down_grad_kernel,
        "down_grad",
        [order, (cot_in, None), (active, turned_spec)],
        piece_outs(size, hidden_wide) + [(tokens, low, None)],
        [],
        matmul * FF,
    )
    flat = lambda part: part.reshape(-1, LANES)
    flat_four = lambda part: part.reshape(4, -1, LANES)
    down_total, down_steps = scatter([flat(p) for p in down_own], flat_four(down_partner), True)
    *in_own, in_partner, gate_grad, up_grad = run(
        in_grad_kernel,
        "in_grad",
        [order, (cot, None), (rows_two, None), (gate_side, turned_spec), (up_side, turned_spec)]
        + [slabs(piece, hidden_wide) for piece in down_pieces],
        piece_outs(size, 2 * hidden_wide) + [(turned, low, turned_spec)] * 2,
        [pltpu.VMEM((D, row_count), low), pltpu.VMEM((hidden_wide, row_count), full)],
        3 * matmul * FF,
    )
    in_total, in_steps = scatter([flat(p) for p in in_own], flat_four(in_partner), False)
    grad_middle, grad_low, gain_two = run(
        middle_grad_kernel,
        "middle_grad",
        [order, (middle, None), (cot, None), (gains, None)]
        + [(gate_grad, turned_spec), (up_grad, turned_spec)]
        + [slabs(piece, 2 * hidden_wide) for piece in in_pieces],
        [(tokens, full, None), (tokens, low, None), ((8, D), full, None)],
        [pltpu.VMEM(tokens, full)],
        2 * matmul * FF,
        after=down_steps[:1],
    )
    grads, edge_grads = run(
        attend_grad_kernel,
        "attend_grad",
        [order, (bias, None), (cosine, None), (sine, None), (grad_low, None)]
        + [lead(queries), lead(keys), lead(values), lead(logs)]
        + [slabs(piece, head_wide, 3) for piece in heads_pieces],
        [
            lead_out((size, 3, row_count, head_wide), low),
            lead_out((size, 2, 2, HALF, head_wide), low),
        ],
        [
            pltpu.VMEM((wide_count, head_wide), full),
            pltpu.VMEM((wide_count, head_wide), full),
            pltpu.VMEM((row_count, head_wide), low),
        ],
        5 * matmul * D,
        after=(down_steps[1], in_steps[0]),
    )
    grads_before = jnp.roll(shift(edge_grads[:, 1], 1), 1, axis=0)
    grads_after = jnp.roll(shift(edge_grads[:, 0], -1), -1, axis=0)
    *heads_own, heads_partner, grad_input = run(
        heads_grad_kernel,
        "heads_grad",
        [order, (hidden, None), (gains, None), (gain_two, None), (grad_middle, None)]
        + [(grad_low, None), (rows_one, None), lead(attended), lead(grads)]
        + [lead(grads_before), lead(grads_after)]
        + [slabs(piece, 3 * head_wide) for piece in heads_pieces],
        piece_outs(size, slab_rows) + [(tokens, full, None)],
        [
            pltpu.VMEM((3, row_count, head_wide), low),
            pltpu.VMEM(tokens, full),
            pltpu.VMEM((8, D), full),
        ],
        7 * matmul * D,
        after=down_steps[2:] + in_steps[1:2],
    )
    heads_total, heads_steps = scatter([flat(p) for p in heads_own], flat_four(heads_partner), True)
    (hidden_out,) = run(
        down_kernel,
        "down",
        [order, (middle, None), (active, turned_spec)]
        + [slabs(piece, hidden_wide) for piece in down_pieces],
        [(tokens, low, None)],
        [pltpu.VMEM(tokens, full)],
        matmul * FF,
        after=heads_steps[:1],
    )
    if dp_size != PIECES:
        hidden_out, grad_input = to_relative(hidden_out, True), to_relative(grad_input, True)

    down_sum = line_scatter(down_total).T
    in_sum = line_scatter(in_total).T.reshape(w_in.shape)
    gain_sum = heads_total[size - 1, head_rows : head_rows + 2].astype(full)
    for mask in (1 << n for n in range(size.bit_length() - 1)):
        gain_sum = gain_sum + lax.ppermute(
            gain_sum, "tensor", [(n, n ^ mask) for n in range(size)]
        )
    heads_sum = line_scatter(heads_total[:, :head_rows]).T
    qkv_sum = jnp.concatenate(
        [
            heads_first(heads_sum[:, : 2 * head_wide]),
            heads_sum[:, None, 2 * head_wide : 3 * head_wide],
        ],
        axis=1,
    )
    proj_sum = heads_sum[:, 3 * head_wide :]
    qkv_one, qkv_two, qkv_new = adam_update(w_qkv, qkv_sum, qkv_first, qkv_second, D ** (-0.5))
    proj_one, proj_two, proj_new = adam_update(
        w_proj, proj_sum, proj_first, proj_second, (D // HALF) ** (-0.5)
    )
    in_one, in_two, in_new = adam_update(w_in, in_sum, in_first, in_second, D ** (-0.5))
    down_one, down_two, down_new = adam_update(
        w_down, down_sum, down_first, down_second, (FF // 2) ** (-0.5)
    )
    gain_one, gain_two, gains_new = adam_update(
        norm_gains, gain_sum, gain_first, gain_second, GAIN_RATE
    )
    return (
        hidden_out,
        grad_input,
        qkv_one,
        qkv_two,
        qkv_new,
        proj_one,
        proj_two,
        proj_new,
        in_one,
        in_two,
        in_new,
        down_one,
        down_two,
        down_new,
        gain_one,
        gain_two,
        gains_new,
    )


def solution(mesh):
    placed = (
        P(("dp", "tensor"), None),
        P("dp", None),
        P(("dp", "tensor"), None),
        P("dp", None, "tensor"),
        P("dp", "tensor"),
        P("dp", None, "tensor"),
        P("dp", "tensor"),
        P(None, "dp"),
        P("dp", None, "tensor"),
        P("dp", None, "tensor"),
        P("dp", "tensor"),
        P("dp", "tensor"),
        P("dp", None, "tensor"),
        P("dp", None, "tensor"),
        P("dp", "tensor"),
        P("dp", "tensor"),
        P(None, "dp"),
        P(None, "dp"),
    )
    return jax.shard_map(
        local,
        mesh=mesh,
        in_specs=placed,
        out_specs=(
            P(("dp", "tensor"), None),
            P(("dp", "tensor"), None),
            P("dp", None, "tensor"),
            P("dp", None, "tensor"),
            P("dp", None, "tensor"),
            P("dp", "tensor"),
            P("dp", "tensor"),
            P("dp", "tensor"),
            P("dp", None, "tensor"),
            P("dp", None, "tensor"),
            P("dp", None, "tensor"),
            P("dp", "tensor"),
            P("dp", "tensor"),
            P("dp", "tensor"),
            P(None, "dp"),
            P(None, "dp"),
            P(None, "dp"),
        ),
        check_vma=False,
    )
```

time: 904 us -> 548 us (0.61)
  local copies, waits for them, and re-layouts: 221 us -> 17 us
  Pallas kernels: 0 us -> 202 us
  matrix products: 158 us -> 0 us
  other arithmetic: 163 us -> 30.9 us
  blocking collectives: 43.3 us -> 0 us
  waiting for transfers between devices: 188 us -> 156 us
  starting transfers between devices: 114 us -> 134 us
    pallas_call x0 -> x10, Pallas kernels: none -> 202 us  [run(): pl.pallas_call(body, grid_spec=pltpu.PrefetchScalarGridSpec(num_scalar_pr...]
    dot_general x27 -> x0, matrix products: 158 us -> none  [the longest x21 123 us: dot(): lax.dot_general(left, right, ((left_dims, right_dims), ((), ())), preferr...]
    rev x5 -> x0, local copies, waits for them, and re-layouts: 53.4 us -> none  [to_relative(): jnp.flip(cube, axes + n)]
    psum x1 -> x0, blocking collectives: 43.3 us -> none  [local(): lax.psum(to_relative(jnp.stack([grad_gain_one, grad_gain_two]), back=True...]
    unnamed x287 -> x129, local copies, waits for them, and re-layouts: 56.8 us -> 14.5 us
    ppermute x42 -> x33, waiting for transfers between devices: 154 us -> 115 us  [flip(): lax.ppermute(rows, 'dp', [(n, n ^ mask) for n in range(lax.axis_size('dp'...]
    convert_element_type x15 -> x8, other arithmetic: 40.5 us -> 6.12 us  [the longest x3 6.05 us: scatter(): total = (own.astype(jnp.float32) + from_x.astype(jnp.float32) + from_y.as...]
    select_n x12 -> x1, other arithmetic: 27.3 us -> 0.2 us  [local(): bias = jnp.where(allowed_pairs(segment), 0.0, MASKED).astype(full)]
  transfers between devices with their start and end apart: 82 -> 75, of which waited for: 20 -> 19; matrix products, arithmetic and copies ran while one was open for 38% -> 7% of each run, Pallas kernels for 0% -> 28%
where the time goes in v3:
time: 548 us; the launch traced here: 543 us
  Pallas kernels  202 us (37%)
  waiting for transfers between devices  156 us (28%)
  starting transfers between devices  134 us (24%)
  other arithmetic  30.9 us (6%)
  local copies, waits for them, and re-layouts  17 us (3%)
    pallas_call x10, Pallas kernels, run(): pl.pallas_call(body, grid_spec=pltpu.PrefetchScalarGridSpec(num_scalar_pr...  202 us
    ppermute x33, waiting for transfers between devices, flip(): lax.ppermute(rows, 'dp', [(n, n ^ mask) for n in range(lax.axis_size('dp'...  115 us
    ppermute x9, starting transfers between devices, line_scatter(): lax.ppermute(to_after, 'tensor', [(n, n + 1) for n in range(size - step)])  48.2 us
    ppermute x9, waiting for transfers between devices, line_gather(): lax.ppermute(from_after[-1], 'tensor', [(n, n - 1) for n in range(1, size...  25.7 us
    ppermute x33, starting transfers between devices, flip(): lax.ppermute(rows, 'dp', [(n, n ^ mask) for n in range(lax.axis_size('dp'...  24.8 us
    ppermute x9, starting transfers between devices, line_gather(): lax.ppermute(from_before[-1], 'tensor', [(n, n + 1) for n in range(step -...  20.3 us
    ppermute x4, starting transfers between devices, shift(): return lax.ppermute(rows, 'tensor', pairs)  15.1 us
    unnamed x129, local copies, waits for them, and re-layouts  14.5 us
  transfers between devices with their start and end apart: 75, of which 19 were waited for; matrix products, arithmetic and copies ran while one was open for 7% of the time, Pallas kernels for 28%

profile of v3, /device:TPU:0, one launch (start us, length us, event | category | flops | bytes accessed | tf_op | source)
XLA Modules:
  0.0 543.0 jit_solution(10715483829214098172)
XLA Ops:
  2.2 5.8 %collective-permute-start = (bf16[1040,128]{1,0:T(8,128)(2,1)S(1)}, bf16[1040,128]{1,0:T(8,128)(2,1)}, u32[]{:S(2)}, u32[]{:S(2)}) collective-permute-start(bf16[1040,128]{1,0:T(8,128)(2,1)S(1)} %get-tuple-element.184), channel_id=1, source_target_pairs={{0,1},{1,2},{2,3},{4,5},{5,6},{6,7},{8,9},{9,10},{10,11},{12,13},{... | collective-permute-start | bytes 798728 | tf_op jit(solution)/shard_map/ppermute | solution.py:83
  9.4 4.6 collective-permute-start.21
  15.3 4.6 collective-permute-start.15
  20.3 1.7 fusion.41
  28.4 10.9 %collective-permute-start.13 = (bf16[64,1024]{1,0:T(8,128)(2,1)}, bf16[64,1024]{1,0:T(8,128)(2,1)S(1)}, u32[]{:S(2)}, u32[]{:S(2)}) collective-permute-start(bf16[64,1024]{1,0:T(8,128)(2,1)} %get-tuple-element.160), channel_id=1, source_target_pairs={{0,1},{1,2},{2,3},{4,5},{5,6},{6,7},{8,9},{9,10},{10,11},{12,13},{... | collective-permute-start | bytes 393224 | tf_op jit(solution)/shard_map/ppermute | solution.py:176
  45.0 10.2 %collective-permute-done.17 = bf16[1312,128]{1,0:T(8,128)(2,1)S(1)} collective-permute-done((bf16[1312,128]{1,0:T(8,128)(2,1)}, bf16[1312,128]{1,0:T(8,128)(2,1)S(1)}, u32[]{:S(2)}, u32[]{:S(2)}) %collective-permute-start.17) | collective-permute-done | bytes 335904 | tf_op jit(solution)/shard_map/ppermute | solution.py:86
  58.2 6.4 %collective-permute-done.3 = bf16[1040,128]{1,0:T(8,128)(2,1)S(1)} collective-permute-done((bf16[1040,128]{1,0:T(8,128)(2,1)}, bf16[1040,128]{1,0:T(8,128)(2,1)S(1)}, u32[]{:S(2)}, u32[]{:S(2)}) %collective-permute-start.3) | collective-permute-done | bytes 266272 | tf_op jit(solution)/shard_map/ppermute | solution.py:86
  66.1 1.6 collective-permute-start.6
  68.7 4.9 collective-permute-done.18
  74.9 1.9 collective-permute-start.28
  78.4 1.5 collective-permute-start.14
  79.9 4.2 collective-permute-done.24
  85.2 1.5 collective-permute-start.8
  86.9 1.6 collective-permute-start.34
  88.8 13.1 %collective-permute-done.34 = bf16[2624,128]{1,0:T(8,128)(2,1)S(1)} collective-permute-done((bf16[2624,128]{1,0:T(8,128)(2,1)S(1)}, bf16[2624,128]{1,0:T(8,128)(2,1)S(1)}, u32[]{:S(2)}, u32[]{:S(2)}) %collective-permute-start.34) | collective-permute-done | bytes 671776 | tf_op jit(solution)/shard_map/ppermute | solution.py:110
  101.9 1.5 collective-permute-start.27
  103.4 27.0 %collective-permute-done.7 = bf16[4160,128]{1,0:T(8,128)(2,1)S(1)} collective-permute-done((bf16[4160,128]{1,0:T(8,128)(2,1)S(1)}, bf16[4160,128]{1,0:T(8,128)(2,1)S(1)}, u32[]{:S(2)}, u32[]{:S(2)}) %collective-permute-start.7) | collective-permute-done | bytes 1064992 | tf_op jit(solution)/shard_map/ppermute | solution.py:110
  130.4 1.6 collective-permute-start.29
  132.2 13.5 %collective-permute-done.8 = bf16[4160,128]{1,0:T(8,128)(2,1)S(1)} collective-permute-done((bf16[4160,128]{1,0:T(8,128)(2,1)S(1)}, bf16[4160,128]{1,0:T(8,128)(2,1)S(1)}, u32[]{:S(2)}, u32[]{:S(2)}) %collective-permute-start.8) | collective-permute-done | bytes 1064992 | tf_op jit(solution)/shard_map/ppermute | solution.py:110
  145.8 1.6 collective-permute-start.35
  147.9 14.7 %collective-permute-done.29 = bf16[5248,128]{1,0:T(8,128)(2,1)} collective-permute-done((bf16[5248,128]{1,0:T(8,128)(2,1)}, bf16[5248,128]{1,0:T(8,128)(2,1)}, u32[]{:S(2)}, u32[]{:S(2)}) %collective-permute-start.29) | collective-permute-done | bytes 1343520 | tf_op jit(solution)/shard_map/ppermute | solution.py:110
  163.3 1.8 collective-permute-start.36
  165.1 13.6 %heads.1 = (bf16[4,768,256]{2,1,0:T(8,128)(2,1)}, bf16[4,896,256]{2,1,0:T(8,128)(2,1)}, bf16[4,896,256]{2,1,0:T(8,128)(2,1)}, bf16[768,1024]{1,0:T(8,128)(2,1)}) custom-call(s32[8]{0:T(128)S(1)} %broadcast_xor_fusion.order_ref, bf16[768,1024]{1,0:T(8,128)(2,1)} %refs_0_.7, bf16[64,1024]{1,0:T(8,128)(2,1)S(1)} %collective-permute-done.13.refs_1_, ...), custom_call_target="tpu_custom_call" | custom-call | flops 4831838208 | bytes 18120704 | tf_op jit(solution)/shard_map/heads/pallas_call | solution.py:243
  178.8 19.7 %attend.1 = (bf16[4,768,256]{2,1,0:T(8,128)(2,1)}, f32[4,768,128]{2,1,0:T(8,128)}) custom-call(s32[8]{0:T(128)S(1)} %broadcast_xor_fusion.order_ref, f32[6,128,256]{2,1,0:T(8,128)S(1)} %and_select_fusion.refs_0_, bf16[4,768,256]{2,1,0:T(8,128)(2,1)} %get-tuple-element.52.refs_1_.refs_4_, bf16[4,896,256]{2,1,0:T(8,128)(2,1)} %get-tuple-element.53.refs_2_.refs_5_, ...), custom_call_target="tpu_custom_call" | custom-call | flops 3221225472 | bytes 9175040 | tf_op jit(solution)/shard_map/attend/pallas_call | solution.py:243
  198.4 10.5 %proj.1 = (f32[768,1024]{1,0:T(8,128)}, bf16[768,1024]{1,0:T(8,128)(2,1)}) custom-call(s32[8]{0:T(128)S(1)} %broadcast_xor_fusion.order_ref, bf16[768,1024]{1,0:T(8,128)(2,1)} %refs_0_.7, f32[8,1024]{1,0:T(8,128)S(1)} %convert_element_type.438.refs_3_.refs_1_.refs_2_, bf16[4,768,256]{2,1,0:T(8,128)(2,1)} %get-tuple-element.55.refs_2_.refs_6_, ...), custom_call_target="tpu_custom_call" | custom-call | flops 1610612736 | bytes 16416768 | tf_op jit(solution)/shard_map/proj/pallas_call | solution.py:243
  210.1 20.5 %gate.1 = (bf16[2624,768]{1,0:T(8,128)(2,1)}, bf16[2624,768]{1,0:T(8,128)(2,1)}, bf16[2624,768]{1,0:T(8,128)(2,1)}) custom-call(s32[8]{0:T(128)S(1)} %broadcast_xor_fusion.order_ref, bf16[768,1024]{1,0:T(8,128)(2,1)} %get-tuple-element.57.refs_0_.refs_1_, bf16[4,1312,128]{2,1,0:T(8,128)(2,1)} %pad_maximum_fusion.refs_1_.refs_5_, ...), custom_call_target="tpu_custom_call" | custom-call | flops 8254390272 | bytes 24412160 | tf_op jit(solution)/shard_map/gate/pallas_call | solution.py:243
  230.5 9.3 %down_grad.1 = (bf16[4,656,128]{2,1,0:T(8,128)(2,1)S(1)}, bf16[4,656,128]{2,1,0:T(8,128)(2,1)S(1)}, bf16[4,656,128]{2,1,0:T(8,128)(2,1)S(1)}, bf16[4,656,128]{2,...) custom-call(s32[8]{0:T(128)S(1)} %broadcast_xor_fusion.order_ref, ...), custom_call_target="tpu_custom_call" | custom-call | flops 4127195136 | bytes 12550144 | tf_op jit(solution)/shard_map/down_grad/pallas_call | solution.py:243
  241.4 26.8 %in_grad.1 = (bf16[4,1312,128]{2,1,0:T(8,128)(2,1)}, bf16[4,1312,128]{2,1,0:T(8,128)(2,1)}, bf16[4,1312,128]{2,1,0:T(8,128)(2,1)}, bf16[4,1312,128]{2,1,0:T(8,12...) custom-call(s32[8]{0:T(128)S(1)} %broadcast_xor_fusion.order_ref, ...), custom_call_target="tpu_custom_call" | custom-call | flops 12381585408 | bytes 35389440 | tf_op jit(solution)/shard_map/in_grad/pallas_call | solution.py:243
  268.8 11.9 %collective-permute-done.41.refs_13_ = bf16[4,2624,128]{2,1,0:T(8,128)(2,1)S(1)} collective-permute-done((bf16[4,2624,128]{2,1,0:T(8,128)(2,1)S(1)}, bf16[4,2624,128]{2,1,0:T(8,128)(2,1)S(1)}, u32[]{:S(2)}, u32[]{:S(2)}) %collective-permute-start.41) | collective-permute-done | bytes 2687008 | tf_op jit(solution)/shard_map/ppermute | solution.py:110
  280.9 1.6 collective-permute-start.42
  282.5 22.4 %middle_grad.1 = (f32[768,1024]{1,0:T(8,128)}, bf16[768,1024]{1,0:T(8,128)(2,1)}, f32[8,1024]{1,0:T(8,128)S(1)}) custom-call(s32[8]{0:T(128)S(1)} %broadcast_xor_fusion.order_ref, f32[768,1024]{1,0:T(8,128)} %get-tuple-element.56.refs_0_, bf16[768,1024]{1,0:T(8,128)(2,1)} %get-tuple-element.59.refs_0_.refs_1_, ...), custom_call_target="tpu_custom_call" | custom-call | flops 8254390272 | bytes 28311552 | tf_op jit(solution)/shard_map/middle_grad/pallas_call | solution.py:243
  304.9 2.0 add_convert_fusion.5
  308.8 1.7 fusion.3
  311.9 44.0 %attend_grad.1 = (bf16[4,3,768,256]{3,2,1,0:T(8,128)(2,1)}, bf16[4,2,2,64,256]{4,3,2,1,0:T(8,128)(2,1)S(1)}) custom-call(s32[8]{0:T(128)S(1)} %broadcast_xor_fusion.order_ref, f32[6,128,256]{2,1,0:T(8,128)} %copy-done.2, f32[896,128]{1,0:T(8,128)S(1)} %copy.77.refs_4_.refs_1_, f32[896,128]{1,0:T(8,128)S(1)} %copy.78.refs_5_.refs_2_, ...), custom_call_target="tpu_custom_call" | custom-call | flops 8053063680 | bytes 23855104 | tf_op jit(solution)/shard_map/attend_grad/pallas_call | solution.py:243
  356.0 1.5 collective-permute-start.44
  358.8 4.0 collective-permute-done.44
  362.8 4.9 collective-permute-done.45
  369.0 24.7 %heads_grad.1 = (bf16[4,1040,128]{2,1,0:T(8,128)(2,1)}, bf16[4,1040,128]{2,1,0:T(8,128)(2,1)}, bf16[4,1040,128]{2,1,0:T(8,128)(2,1)}, bf16[4,1040,128]{2,1,0:T(8...) custom-call(s32[8]{0:T(128)S(1)} %broadcast_xor_fusion.order_ref, bf16[768,1024]{1,0:T(8,128)(2,1)} %refs_0_.7, ...), custom_call_target="tpu_custom_call" | custom-call | flops 11274289152 | bytes 34930688 | tf_op jit(solution)/shard_map/heads_grad/pallas_call | solution.py:243
  393.8 1.6 add_convert_fusion.4
  395.4 4.5 collective-permute-start.67
  400.7 3.5 collective-permute-done.67
  404.2 4.4 collective-permute-start.68
  409.4 2.8 add_convert_fusion.1
  412.1 1.6 collective-permute-start.60
  416.4 7.7 %collective-permute-start.69 = (bf16[656,128]{1,0:T(8,128)(2,1)}, bf16[656,128]{1,0:T(8,128)(2,1)}, u32[]{:S(2)}, u32[]{:S(2)}) collective-permute-start(bf16[656,128]{1,0:T(8,128)(2,1)} %get-tuple-element.173), channel_id=1, source_target_pairs={{0,1},{1,2},{2,3},{4,5},{5,6},{6,7},{8,9},{9,10},{10,11},{12,13},{... | collective-permute-start | bytes 503816 | tf_op jit(solution)/shard_map/ppermute | solution.py:103
  424.1 1.7 fusion.6
  426.3 16.7 %collective-permute-done.60 = bf16[5248,128]{1,0:T(8,128)(2,1)S(1)} collective-permute-done((bf16[5248,128]{1,0:T(8,128)(2,1)S(1)}, bf16[5248,128]{1,0:T(8,128)(2,1)S(1)}, u32[]{:S(2)}, u32[]{:S(2)}) %collective-permute-start.60) | collective-permute-done | bytes 1343520 | tf_op jit(solution)/shard_map/ppermute | solution.py:110
  443.0 3.2 collective-permute-done.59
  446.2 2.0 add_convert_fusion
  448.3 5.1 collective-permute-start.61
  454.0 13.0 %collective-permute-done.51 = bf16[4160,128]{1,0:T(8,128)(2,1)S(1)} collective-permute-done((bf16[4160,128]{1,0:T(8,128)(2,1)S(1)}, bf16[4160,128]{1,0:T(8,128)(2,1)S(1)}, u32[]{:S(2)}, u32[]{:S(2)}) %collective-permute-start.51) | collective-permute-done | bytes 1064992 | tf_op jit(solution)/shard_map/ppermute | solution.py:110
  467.6 1.5 add_convert_fusion.3
  470.6 5.6 %collective-permute-start.62 = (bf16[1312,128]{1,0:T(8,128)(2,1)}, bf16[1312,128]{1,0:T(8,128)(2,1)}, u32[]{:S(2)}, u32[]{:S(2)}) collective-permute-start(bf16[1312,128]{1,0:T(8,128)(2,1)} %get-tuple-element.163), channel_id=1, source_target_pairs={{0,1},{1,2},{4,5},{5,6},{8,9},{9,10},{12,13},{13,14},{16,17},{17,1... | collective-permute-start | bytes 1007624 | tf_op jit(solution)/shard_map/ppermute | solution.py:103
  480.3 1.9 copy.83
  482.2 2.6 multiply_subtract_fusion.2
  487.5 4.9 collective-permute-start.63
  492.8 2.4 add_convert_fusion.2
  495.3 4.9 collective-permute-start.53
  501.3 2.8 collective-permute-done.53
  504.2 4.4 collective-permute-start.54
  509.3 1.6 multiply_subtract_fusion
  510.9 5.6 %collective-permute-start.74 = (f32[2,128]{1,0:T(2,128)S(1)}, f32[2,128]{1,0:T(2,128)S(1)}, u32[]{:S(2)}, u32[]{:S(2)}) collective-permute-start(f32[2,128]{1,0:T(2,128)S(1)} %fusion.33), channel_id=1, source_target_pairs={{0,2},{1,3},{2,0},{3,1},{4,6},{5,7},{6,4},{7,5},{8,10},{9,11},{10,... | collective-permute-start | bytes 3080 | tf_op jit(solution)/shard_map/ppermute | solution.py:802
  518.0 6.6 %collective-permute-start.55 = (bf16[1024,128]{1,0:T(8,128)(2,1)S(1)}, bf16[1024,128]{1,0:T(8,128)(2,1)S(1)}, u32[]{:S(2)}, u32[]{:S(2)}) collective-permute-start(bf16[1024,128]{1,0:T(8,128)(2,1)S(1)} %get-tuple-element.167), channel_id=1, source_target_pairs={{0,1},{1,2},{2,3},{4,5},{5,6},{6,7},{8,9},{9,10},{10,11},{12,13},{... | collective-permute-start | bytes 786440 | tf_op jit(solution)/shard_map/ppermute | solution.py:103
  524.7 10.7 %down.1 = bf16[768,1024]{1,0:T(8,128)(2,1)} custom-call(s32[8]{0:T(128)S(1)} %broadcast_xor_fusion.order_ref, f32[768,1024]{1,0:T(8,128)} %get-tuple-element.56.refs_0_, bf16[2624,768]{1,0:T(8,128)(2,1)} %get-tuple-element.58.refs_1_, bf16[4,656,128]{2,1,0:T(8,128)(2,1)S(1)} %pad_maximum_fusion.2.refs_4_.refs_2_, bf16[4,656,128]{2,1,0:T(8,128)(2,1)S(1)} %bitcast.269, ...), custom_call_target="tpu_custom_call" | custom-call | flops 4127195136 | bytes 14123008 | tf_op jit(solution)/shard_map/down/pallas_call | solution.py:243
  (305 shorter events, 62.1 us)
Async XLA Ops:
  2.2 22.9 %collective-permute-start = (bf16[1040,128]{1,0:T(8,128)(2,1)S(1)}, bf16[1040,128]{1,0:T(8,128)(2,1)}, u32[]{:S(2)}, u32[]{:S(2)}) collective-permute-start(bf16[1040,128]{1,0:T(8,128)(2,1)S(1)} %get-tuple-element.184), channel_id=1, source_target_pairs={{0,1},{1,2},{2,3},{4,5},{5,6},{6,7},{8,9},{9,10},{10,11},{12,13},{... | collective-permute-start | bytes 798728 | tf_op jit(solution)/shard_map/ppermute | solution.py:83
  8.0 18.5 %collective-permute-start.1 = (bf16[1040,128]{1,0:T(8,128)(2,1)S(1)}, bf16[1040,128]{1,0:T(8,128)(2,1)}, u32[]{:S(2)}, u32[]{:S(2)}) collective-permute-start(bf16[1040,128]{1,0:T(8,128)(2,1)S(1)} %get-tuple-element.184), channel_id=1, source_target_pairs={{1,0},{2,1},{3,2},{5,4},{6,5},{7,6},{9,8},{10,9},{11,10},{13,12},{... | collective-permute-start | bytes 798728 | tf_op jit(solution)/shard_map/ppermute | solution.py:86
  9.4 13.1 %collective-permute-start.21 = (bf16[656,128]{1,0:T(8,128)(2,1)S(1)}, bf16[656,128]{1,0:T(8,128)(2,1)S(1)}, u32[]{:S(2)}, u32[]{:S(2)}) collective-permute-start(bf16[656,128]{1,0:T(8,128)(2,1)S(1)} %get-tuple-element.183), channel_id=1, source_target_pairs={{0,1},{1,2},{2,3},{4,5},{5,6},{6,7},{8,9},{9,10},{10,11},{12,13},{... | collective-permute-start | bytes 503816 | tf_op jit(solution)/shard_map/ppermute | solution.py:83
  13.9 9.9 %collective-permute-start.22 = (bf16[656,128]{1,0:T(8,128)(2,1)S(1)}, bf16[656,128]{1,0:T(8,128)(2,1)S(1)}, u32[]{:S(2)}, u32[]{:S(2)}) collective-permute-start(bf16[656,128]{1,0:T(8,128)(2,1)S(1)} %get-tuple-element.183), channel_id=1, source_target_pairs={{1,0},{2,1},{3,2},{5,4},{6,5},{7,6},{9,8},{10,9},{11,10},{13,12},{... | collective-permute-start | bytes 503816 | tf_op jit(solution)/shard_map/ppermute | solution.py:86
  15.3 13.1 %collective-permute-start.15 = (bf16[1312,128]{1,0:T(8,128)(2,1)S(1)}, bf16[1312,128]{1,0:T(8,128)(2,1)S(1)}, u32[]{:S(2)}, u32[]{:S(2)}) collective-permute-start(bf16[1312,128]{1,0:T(8,128)(2,1)S(1)} %bitcast.281), channel_id=1, source_target_pairs={{0,1},{1,2},{2,3},{4,5},{5,6},{6,7},{8,9},{9,10},{10,11},{12,13},{... | collective-permute-start | bytes 1007624 | tf_op jit(solution)/shard_map/ppermute | solution.py:83
  22.5 16.8 %collective-permute-start.16 = (bf16[1312,128]{1,0:T(8,128)(2,1)S(1)}, bf16[1312,128]{1,0:T(8,128)(2,1)}, u32[]{:S(2)}, u32[]{:S(2)}) collective-permute-start(bf16[1312,128]{1,0:T(8,128)(2,1)S(1)} %bitcast.282), channel_id=1, source_target_pairs={{1,0},{2,1},{3,2},{5,4},{6,5},{7,6},{9,8},{10,9},{11,10},{13,12},{... | collective-permute-start | bytes 1007624 | tf_op jit(solution)/shard_map/ppermute | solution.py:86
  23.8 16.8 %collective-permute-start.25 = (bf16[656,128]{1,0:T(8,128)(2,1)S(1)}, bf16[656,128]{1,0:T(8,128)(2,1)}, u32[]{:S(2)}, u32[]{:S(2)}) collective-permute-start(bf16[656,128]{1,0:T(8,128)(2,1)S(1)} %collective-permute-done.21), channel_id=1, source_target_pairs={{1,2},{2,3},{5,6},{6,7},{9,10},{10,11},{13,14},{14,15},{17,18},{18... | collective-permute-start | bytes 503816 | tf_op jit(solution)/shard_map/ppermute | solution.py:83
  25.1 16.2 %collective-permute-start.4 = (bf16[1040,128]{1,0:T(8,128)(2,1)}, bf16[1040,128]{1,0:T(8,128)(2,1)}, u32[]{:S(2)}, u32[]{:S(2)}) collective-permute-start(bf16[1040,128]{1,0:T(8,128)(2,1)} %collective-permute-done), channel_id=1, source_target_pairs={{1,2},{2,3},{5,6},{6,7},{9,10},{10,11},{13,14},{14,15},{17,18},{18... | collective-permute-start | bytes 798728 | tf_op jit(solution)/shard_map/ppermute | solution.py:83
  26.5 16.1 %collective-permute-start.2 = (bf16[1040,128]{1,0:T(8,128)(2,1)}, bf16[1040,128]{1,0:T(8,128)(2,1)}, u32[]{:S(2)}, u32[]{:S(2)}) collective-permute-start(bf16[1040,128]{1,0:T(8,128)(2,1)} %collective-permute-done.1), channel_id=1, source_target_pairs={{1,0},{2,1},{5,4},{6,5},{9,8},{10,9},{13,12},{14,13},{17,16},{18,1... | collective-permute-start | bytes 798728 | tf_op jit(solution)/shard_map/ppermute | solution.py:86
  28.4 50.0 %collective-permute-start.13 = (bf16[64,1024]{1,0:T(8,128)(2,1)}, bf16[64,1024]{1,0:T(8,128)(2,1)S(1)}, u32[]{:S(2)}, u32[]{:S(2)}) collective-permute-start(bf16[64,1024]{1,0:T(8,128)(2,1)} %get-tuple-element.160), channel_id=1, source_target_pairs={{0,1},{1,2},{2,3},{4,5},{5,6},{6,7},{8,9},{9,10},{10,11},{12,13},{... | collective-permute-start | bytes 393224 | tf_op jit(solution)/shard_map/ppermute | solution.py:176
  39.3 37.5 %collective-permute-start.23 = (bf16[656,128]{1,0:T(8,128)(2,1)}, bf16[656,128]{1,0:T(8,128)(2,1)S(1)}, u32[]{:S(2)}, u32[]{:S(2)}) collective-permute-start(bf16[656,128]{1,0:T(8,128)(2,1)} %copy-done.43), channel_id=1, source_target_pairs={{1,0},{2,1},{5,4},{6,5},{9,8},{10,9},{13,12},{14,13},{17,16},{18,1... | collective-permute-start | bytes 503816 | tf_op jit(solution)/shard_map/ppermute | solution.py:86
  41.3 13.9 %collective-permute-start.17 = (bf16[1312,128]{1,0:T(8,128)(2,1)}, bf16[1312,128]{1,0:T(8,128)(2,1)S(1)}, u32[]{:S(2)}, u32[]{:S(2)}) collective-permute-start(bf16[1312,128]{1,0:T(8,128)(2,1)} %collective-permute-done.16), channel_id=1, source_target_pairs={{1,0},{2,1},{5,4},{6,5},{9,8},{10,9},{13,12},{14,13},{17,16},{18,1... | collective-permute-start | bytes 1007624 | tf_op jit(solution)/shard_map/ppermute | solution.py:86
  42.6 35.5 %collective-permute-start.26 = (bf16[656,128]{1,0:T(8,128)(2,1)}, bf16[656,128]{1,0:T(8,128)(2,1)S(1)}, u32[]{:S(2)}, u32[]{:S(2)}) collective-permute-start(bf16[656,128]{1,0:T(8,128)(2,1)} %collective-permute-done.25), channel_id=1, source_target_pairs={{2,3},{6,7},{10,11},{14,15},{18,19},{22,23},{26,27},{30,31}} | collective-permute-start | bytes 503816 | tf_op jit(solution)/shard_map/ppermute | solution.py:83
  44.3 12.2 %collective-permute-start.5 = (bf16[1040,128]{1,0:T(8,128)(2,1)}, bf16[1040,128]{1,0:T(8,128)(2,1)S(1)}, u32[]{:S(2)}, u32[]{:S(2)}) collective-permute-start(bf16[1040,128]{1,0:T(8,128)(2,1)} %collective-permute-done.4), channel_id=1, source_target_pairs={{2,3},{6,7},{10,11},{14,15},{18,19},{22,23},{26,27},{30,31}} | collective-permute-start | bytes 798728 | tf_op jit(solution)/shard_map/ppermute | solution.py:83
  55.2 9.4 %collective-permute-start.3 = (bf16[1040,128]{1,0:T(8,128)(2,1)}, bf16[1040,128]{1,0:T(8,128)(2,1)S(1)}, u32[]{:S(2)}, u32[]{:S(2)}) collective-permute-start(bf16[1040,128]{1,0:T(8,128)(2,1)} %collective-permute-done.2), channel_id=1, source_target_pairs={{1,0},{5,4},{9,8},{13,12},{17,16},{21,20},{25,24},{29,28}} | collective-permute-start | bytes 798728 | tf_op jit(solution)/shard_map/ppermute | solution.py:86
  56.5 9.5 %collective-permute-start.20 = (bf16[1312,128]{1,0:T(8,128)(2,1)S(1)}, bf16[1312,128]{1,0:T(8,128)(2,1)S(1)}, u32[]{:S(2)}, u32[]{:S(2)}) collective-permute-start(bf16[1312,128]{1,0:T(8,128)(2,1)S(1)} %collective-permute-done.19), channel_id=1, source_target_pairs={{2,3},{6,7},{10,11},{14,15},{18,19},{22,23},{26,27},{30,31}} | collective-permute-start | bytes 1007624 | tf_op jit(solution)/shard_map/ppermute | solution.py:83
  64.6 9.0 %collective-permute-start.18 = (bf16[1312,128]{1,0:T(8,128)(2,1)S(1)}, bf16[1312,128]{1,0:T(8,128)(2,1)S(1)}, u32[]{:S(2)}, u32[]{:S(2)}) collective-permute-start(bf16[1312,128]{1,0:T(8,128)(2,1)S(1)} %collective-permute-done.17), channel_id=1, source_target_pairs={{1,0},{5,4},{9,8},{13,12},{17,16},{21,20},{25,24},{29,28}} | collective-permute-start | bytes 1007624 | tf_op jit(solution)/shard_map/ppermute | solution.py:86
  66.1 19.2 %collective-permute-start.6 = (bf16[4160,128]{1,0:T(8,128)(2,1)S(1)}, bf16[4160,128]{1,0:T(8,128)(2,1)S(1)}, u32[]{:S(2)}, u32[]{:S(2)}) collective-permute-start(bf16[4160,128]{1,0:T(8,128)(2,1)S(1)} %bitcast.261), channel_id=1, source_target_pairs={{0,8},{4,12},{8,0},{12,4},{16,24},{20,28},{24,16},{28,20},{1,9},{5... | collective-permute-start | bytes 3194888 | tf_op jit(solution)/shard_map/ppermute | solution.py:110
  74.9 55.5 %collective-permute-start.28 = (bf16[5248,128]{1,0:T(8,128)(2,1)}, bf16[5248,128]{1,0:T(8,128)(2,1)}, u32[]{:S(2)}, u32[]{:S(2)}) collective-permute-start(bf16[5248,128]{1,0:T(8,128)(2,1)} %bitcast.45.refs_14_), channel_id=1, source_target_pairs={{0,16},{4,20},{8,24},{12,28},{16,0},{20,4},{24,8},{28,12},{1,17},{... | collective-permute-start | bytes 4030472 | tf_op jit(solution)/shard_map/ppermute | solution.py:110
  78.2 52.2 %collective-permute-start.7 = (bf16[4160,128]{1,0:T(8,128)(2,1)S(1)}, bf16[4160,128]{1,0:T(8,128)(2,1)S(1)}, u32[]{:S(2)}, u32[]{:S(2)}) collective-permute-start(bf16[4160,128]{1,0:T(8,128)(2,1)S(1)} %bitcast.262), channel_id=1, source_target_pairs={{0,16},{4,20},{8,24},{12,28},{16,0},{20,4},{24,8},{28,12},{1,17},{... | collective-permute-start | bytes 3194888 | tf_op jit(solution)/shard_map/ppermute | solution.py:110
  84.1 47.9 %collective-permute-start.9 = (bf16[4160,128]{1,0:T(8,128)(2,1)S(1)}, bf16[4160,128]{1,0:T(8,128)(2,1)S(1)}, u32[]{:S(2)}, u32[]{:S(2)}) collective-permute-start(bf16[4160,128]{1,0:T(8,128)(2,1)S(1)} %bitcast.263), channel_id=1, source_target_pairs={{0,4},{4,0},{8,12},{12,8},{16,20},{20,16},{24,28},{28,24},{1,5},{5... | collective-permute-start | bytes 3194888 | tf_op jit(solution)/shard_map/ppermute | solution.py:110
  85.2 60.4 %collective-permute-start.8 = (bf16[4160,128]{1,0:T(8,128)(2,1)S(1)}, bf16[4160,128]{1,0:T(8,128)(2,1)S(1)}, u32[]{:S(2)}, u32[]{:S(2)}) collective-permute-start(bf16[4160,128]{1,0:T(8,128)(2,1)S(1)} %collective-permute-done.6), channel_id=1, source_target_pairs={{0,16},{4,20},{8,24},{12,28},{16,0},{20,4},{24,8},{28,12},{1,17},{... | collective-permute-start | bytes 3194888 | tf_op jit(solution)/shard_map/ppermute | solution.py:110
  86.9 15.0 %collective-permute-start.34 = (bf16[2624,128]{1,0:T(8,128)(2,1)S(1)}, bf16[2624,128]{1,0:T(8,128)(2,1)S(1)}, u32[]{:S(2)}, u32[]{:S(2)}) collective-permute-start(bf16[2624,128]{1,0:T(8,128)(2,1)S(1)} %bitcast.264), channel_id=1, source_target_pairs={{0,8},{4,12},{8,0},{12,4},{16,24},{20,28},{24,16},{28,20},{1,9},{5... | collective-permute-start | bytes 2015240 | tf_op jit(solution)/shard_map/ppermute | solution.py:110
  101.9 45.5 %collective-permute-start.27 = (bf16[5248,128]{1,0:T(8,128)(2,1)}, bf16[5248,128]{1,0:T(8,128)(2,1)}, u32[]{:S(2)}, u32[]{:S(2)}) collective-permute-start(bf16[5248,128]{1,0:T(8,128)(2,1)} %bitcast.45.refs_14_), channel_id=1, source_target_pairs={{0,8},{4,12},{8,0},{12,4},{16,24},{20,28},{24,16},{28,20},{1,9},{5... | collective-permute-start | bytes 4030472 | tf_op jit(solution)/shard_map/ppermute | solution.py:110
  130.4 15.3 %collective-permute-start.10 = (bf16[4160,128]{1,0:T(8,128)(2,1)S(1)}, bf16[4160,128]{1,0:T(8,128)(2,1)S(1)}, u32[]{:S(2)}, u32[]{:S(2)}) collective-permute-start(bf16[4160,128]{1,0:T(8,128)(2,1)S(1)} %collective-permute-done.6), channel_id=1, source_target_pairs={{0,4},{4,0},{8,12},{12,8},{16,20},{20,16},{24,28},{28,24},{1,5},{5... | collective-permute-start | bytes 3194888 | tf_op jit(solution)/shard_map/ppermute | solution.py:110
  130.4 32.2 %collective-permute-start.29 = (bf16[5248,128]{1,0:T(8,128)(2,1)}, bf16[5248,128]{1,0:T(8,128)(2,1)}, u32[]{:S(2)}, u32[]{:S(2)}) collective-permute-start(bf16[5248,128]{1,0:T(8,128)(2,1)} %collective-permute-done.28), channel_id=1, source_target_pairs={{0,8},{4,12},{8,0},{12,4},{16,24},{20,28},{24,16},{28,20},{1,9},{5... | collective-permute-start | bytes 4030472 | tf_op jit(solution)/shard_map/ppermute | solution.py:110
  132.0 15.6 %collective-permute-start.11 = (bf16[4160,128]{1,0:T(8,128)(2,1)S(1)}, bf16[4160,128]{1,0:T(8,128)(2,1)S(1)}, u32[]{:S(2)}, u32[]{:S(2)}) collective-permute-start(bf16[4160,128]{1,0:T(8,128)(2,1)S(1)} %collective-permute-done.7), channel_id=1, source_target_pairs={{0,4},{4,0},{8,12},{12,8},{16,20},{20,16},{24,28},{28,24},{1,5},{5... | collective-permute-start | bytes 3194888 | tf_op jit(solution)/shard_map/ppermute | solution.py:110
  145.7 16.9 %collective-permute-start.12 = (bf16[4160,128]{1,0:T(8,128)(2,1)S(1)}, bf16[4160,128]{1,0:T(8,128)(2,1)S(1)}, u32[]{:S(2)}, u32[]{:S(2)}) collective-permute-start(bf16[4160,128]{1,0:T(8,128)(2,1)S(1)} %collective-permute-done.8), channel_id=1, source_target_pairs={{0,4},{4,0},{8,12},{12,8},{16,20},{20,16},{24,28},{28,24},{1,5},{5... | collective-permute-start | bytes 3194888 | tf_op jit(solution)/shard_map/ppermute | solution.py:110
  145.8 17.5 %collective-permute-start.35 = (bf16[2624,128]{1,0:T(8,128)(2,1)S(1)}, bf16[2624,128]{1,0:T(8,128)(2,1)S(1)}, u32[]{:S(2)}, u32[]{:S(2)}) collective-permute-start(bf16[2624,128]{1,0:T(8,128)(2,1)S(1)} %bitcast.265), channel_id=1, source_target_pairs={{0,16},{4,20},{8,24},{12,28},{16,0},{20,4},{24,8},{28,12},{1,17},{... | collective-permute-start | bytes 2015240 | tf_op jit(solution)/shard_map/ppermute | solution.py:110
  147.3 61.7 %collective-permute-start.30 = (bf16[5248,128]{1,0:T(8,128)(2,1)}, bf16[5248,128]{1,0:T(8,128)(2,1)}, u32[]{:S(2)}, u32[]{:S(2)}) collective-permute-start(bf16[5248,128]{1,0:T(8,128)(2,1)} %bitcast.45.refs_14_), channel_id=1, source_target_pairs={{0,4},{4,0},{8,12},{12,8},{16,20},{20,16},{24,28},{28,24},{1,5},{5... | collective-permute-start | bytes 4030472 | tf_op jit(solution)/shard_map/ppermute | solution.py:110
  147.6 62.1 %collective-permute-start.32 = (bf16[5248,128]{1,0:T(8,128)(2,1)}, bf16[5248,128]{1,0:T(8,128)(2,1)}, u32[]{:S(2)}, u32[]{:S(2)}) collective-permute-start(bf16[5248,128]{1,0:T(8,128)(2,1)} %collective-permute-done.28), channel_id=1, source_target_pairs={{0,4},{4,0},{8,12},{12,8},{16,20},{20,16},{24,28},{28,24},{1,5},{5... | collective-permute-start | bytes 4030472 | tf_op jit(solution)/shard_map/ppermute | solution.py:110
  162.6 46.9 %collective-permute-start.31 = (bf16[5248,128]{1,0:T(8,128)(2,1)}, bf16[5248,128]{1,0:T(8,128)(2,1)}, u32[]{:S(2)}, u32[]{:S(2)}) collective-permute-start(bf16[5248,128]{1,0:T(8,128)(2,1)} %collective-permute-done.27), channel_id=1, source_target_pairs={{0,4},{4,0},{8,12},{12,8},{16,20},{20,16},{24,28},{28,24},{1,5},{5... | collective-permute-start | bytes 4030472 | tf_op jit(solution)/shard_map/ppermute | solution.py:110
  162.6 47.4 %collective-permute-start.33 = (bf16[5248,128]{1,0:T(8,128)(2,1)}, bf16[5248,128]{1,0:T(8,128)(2,1)}, u32[]{:S(2)}, u32[]{:S(2)}) collective-permute-start(bf16[5248,128]{1,0:T(8,128)(2,1)} %collective-permute-done.29), channel_id=1, source_target_pairs={{0,4},{4,0},{8,12},{12,8},{16,20},{20,16},{24,28},{28,24},{1,5},{5... | collective-permute-start | bytes 4030472 | tf_op jit(solution)/shard_map/ppermute | solution.py:110
  163.3 45.6 %collective-permute-start.36 = (bf16[2624,128]{1,0:T(8,128)(2,1)S(1)}, bf16[2624,128]{1,0:T(8,128)(2,1)S(1)}, u32[]{:S(2)}, u32[]{:S(2)}) collective-permute-start(bf16[2624,128]{1,0:T(8,128)(2,1)S(1)} %collective-permute-done.34), channel_id=1, source_target_pairs={{0,16},{4,20},{8,24},{12,28},{16,0},{20,4},{24,8},{28,12},{1,17},{... | collective-permute-start | bytes 2015240 | tf_op jit(solution)/shard_map/ppermute | solution.py:110
  209.0 30.9 %collective-permute-start.37 = (bf16[2624,128]{1,0:T(8,128)(2,1)S(1)}, bf16[2624,128]{1,0:T(8,128)(2,1)S(1)}, u32[]{:S(2)}, u32[]{:S(2)}) collective-permute-start(bf16[2624,128]{1,0:T(8,128)(2,1)S(1)} %bitcast.267), channel_id=1, source_target_pairs={{0,4},{4,0},{8,12},{12,8},{16,20},{20,16},{24,28},{28,24},{1,5},{5... | collective-permute-start | bytes 2015240 | tf_op jit(solution)/shard_map/ppermute | solution.py:110
  209.0 30.9 %collective-permute-start.38 = (bf16[2624,128]{1,0:T(8,128)(2,1)S(1)}, bf16[2624,128]{1,0:T(8,128)(2,1)S(1)}, u32[]{:S(2)}, u32[]{:S(2)}) collective-permute-start(bf16[2624,128]{1,0:T(8,128)(2,1)S(1)} %collective-permute-done.34), channel_id=1, source_target_pairs={{0,4},{4,0},{8,12},{12,8},{16,20},{20,16},{24,28},{28,24},{1,5},{5... | collective-permute-start | bytes 2015240 | tf_op jit(solution)/shard_map/ppermute | solution.py:110
  209.5 30.4 %collective-permute-start.39 = (bf16[2624,128]{1,0:T(8,128)(2,1)S(1)}, bf16[2624,128]{1,0:T(8,128)(2,1)S(1)}, u32[]{:S(2)}, u32[]{:S(2)}) collective-permute-start(bf16[2624,128]{1,0:T(8,128)(2,1)S(1)} %collective-permute-done.35), channel_id=1, source_target_pairs={{0,4},{4,0},{8,12},{12,8},{16,20},{20,16},{24,28},{28,24},{1,5},{5... | collective-permute-start | bytes 2015240 | tf_op jit(solution)/shard_map/ppermute | solution.py:110
  209.6 30.3 %collective-permute-start.40 = (bf16[2624,128]{1,0:T(8,128)(2,1)S(1)}, bf16[2624,128]{1,0:T(8,128)(2,1)S(1)}, u32[]{:S(2)}, u32[]{:S(2)}) collective-permute-start(bf16[2624,128]{1,0:T(8,128)(2,1)S(1)} %collective-permute-done.36), channel_id=1, source_target_pairs={{0,4},{4,0},{8,12},{12,8},{16,20},{20,16},{24,28},{28,24},{1,5},{5... | collective-permute-start | bytes 2015240 | tf_op jit(solution)/shard_map/ppermute | solution.py:110
  268.2 40.6 %collective-permute-start.43 = (bf16[4,5248,128]{2,1,0:T(8,128)(2,1)}, bf16[4,5248,128]{2,1,0:T(8,128)(2,1)}, u32[]{:S(2)}, u32[]{:S(2)}) collective-permute-start(bf16[4,5248,128]{2,1,0:T(8,128)(2,1)} %bitcast.340), channel_id=1, source_target_pairs={{0,4},{4,0},{8,12},{12,8},{16,20},{20,16},{24,28},{28,24},{1,5},{5... | collective-permute-start | bytes 16121864 | tf_op jit(solution)/shard_map/ppermute | solution.py:110
  268.3 12.3 %collective-permute-start.41 = (bf16[4,2624,128]{2,1,0:T(8,128)(2,1)S(1)}, bf16[4,2624,128]{2,1,0:T(8,128)(2,1)S(1)}, u32[]{:S(2)}, u32[]{:S(2)}) collective-permute-start(bf16[4,2624,128]{2,1,0:T(8,128)(2,1)S(1)} %bitcast.342), channel_id=1, source_target_pairs={{0,4},{4,0},{8,12},{12,8},{16,20},{20,16},{24,28},{28,24},{1,5},{5... | collective-permute-start | bytes 8060936 | tf_op jit(solution)/shard_map/ppermute | solution.py:110
  280.9 23.9 %collective-permute-start.42 = (bf16[2624,128]{1,0:T(8,128)(2,1)S(1)}, bf16[2624,128]{1,0:T(8,128)(2,1)S(1)}, u32[]{:S(2)}, u32[]{:S(2)}) collective-permute-start(bf16[2624,128]{1,0:T(8,128)(2,1)S(1)} %fusion.11), channel_id=1, source_target_pairs={{0,8},{4,12},{8,0},{12,4},{16,24},{20,28},{24,16},{28,20},{1,9},{5... | collective-permute-start | bytes 2015240 | tf_op jit(solution)/shard_map/ppermute | solution.py:110
  306.9 61.0 %collective-permute-start.46 = (bf16[2624,128]{1,0:T(8,128)(2,1)S(1)}, bf16[2624,128]{1,0:T(8,128)(2,1)S(1)}, u32[]{:S(2)}, u32[]{:S(2)}) collective-permute-start(bf16[2624,128]{1,0:T(8,128)(2,1)S(1)} %get-tuple-element.158), channel_id=1, source_target_pairs={{0,8},{4,12},{8,0},{12,4},{16,24},{20,28},{24,16},{28,20},{1,9},{5... | collective-permute-start | bytes 2015240 | tf_op jit(solution)/shard_map/ppermute | solution.py:110
  308.1 59.8 %collective-permute-start.47 = (bf16[2624,128]{1,0:T(8,128)(2,1)S(1)}, bf16[2624,128]{1,0:T(8,128)(2,1)S(1)}, u32[]{:S(2)}, u32[]{:S(2)}) collective-permute-start(bf16[2624,128]{1,0:T(8,128)(2,1)S(1)} %get-tuple-element.157), channel_id=1, source_target_pairs={{0,16},{4,20},{8,24},{12,28},{16,0},{20,4},{24,8},{28,12},{1,17},{... | collective-permute-start | bytes 2015240 | tf_op jit(solution)/shard_map/ppermute | solution.py:110
  310.5 57.4 %collective-permute-start.48 = (bf16[5248,128]{1,0:T(8,128)(2,1)S(1)}, bf16[5248,128]{1,0:T(8,128)(2,1)S(1)}, u32[]{:S(2)}, u32[]{:S(2)}) collective-permute-start(bf16[5248,128]{1,0:T(8,128)(2,1)S(1)} %fusion.3), channel_id=1, source_target_pairs={{0,16},{4,20},{8,24},{12,28},{16,0},{20,4},{24,8},{28,12},{1,17},{... | collective-permute-start | bytes 4030472 | tf_op jit(solution)/shard_map/ppermute | solution.py:110
  357.5 10.3 %collective-permute-start.45 = (bf16[4,2,64,256]{3,2,1,0:T(8,128)(2,1)S(1)}, bf16[4,2,64,256]{3,2,1,0:T(8,128)(2,1)S(1)}, u32[]{:S(2)}, u32[]{:S(2)}) collective-permute-start(bf16[4,2,64,256]{3,2,1,0:T(8,128)(2,1)S(1)} %get-tuple-element.180), channel_id=1, source_target_pairs={{1,0},{2,1},{3,2},{5,4},{6,5},{7,6},{9,8},{10,9},{11,10},{13,12},{... | collective-permute-start | bytes 786440 | tf_op jit(solution)/shard_map/ppermute | solution.py:176
  393.7 30.3 %collective-permute-start.49 = (bf16[4,4160,128]{2,1,0:T(8,128)(2,1)}, bf16[4,4160,128]{2,1,0:T(8,128)(2,1)S(1)}, u32[]{:S(2)}, u32[]{:S(2)}) collective-permute-start(bf16[4,4160,128]{2,1,0:T(8,128)(2,1)} %bitcast.341), channel_id=1, source_target_pairs={{0,4},{4,0},{8,12},{12,8},{16,20},{20,16},{24,28},{28,24},{1,5},{5... | collective-permute-start | bytes 12779528 | tf_op jit(solution)/shard_map/ppermute | solution.py:110
  404.2 10.1 %collective-permute-start.68 = (bf16[656,128]{1,0:T(8,128)(2,1)S(1)}, bf16[656,128]{1,0:T(8,128)(2,1)S(1)}, u32[]{:S(2)}, u32[]{:S(2)}) collective-permute-start(bf16[656,128]{1,0:T(8,128)(2,1)S(1)} %get-tuple-element.175), channel_id=1, source_target_pairs={{0,1},{1,2},{4,5},{5,6},{8,9},{9,10},{12,13},{13,14},{16,17},{17,1... | collective-permute-start | bytes 503816 | tf_op jit(solution)/shard_map/ppermute | solution.py:103
  412.1 30.9 %collective-permute-start.60 = (bf16[5248,128]{1,0:T(8,128)(2,1)S(1)}, bf16[5248,128]{1,0:T(8,128)(2,1)S(1)}, u32[]{:S(2)}, u32[]{:S(2)}) collective-permute-start(bf16[5248,128]{1,0:T(8,128)(2,1)S(1)} %get-tuple-element.154), channel_id=1, source_target_pairs={{0,16},{4,20},{8,24},{12,28},{16,0},{20,4},{24,8},{28,12},{1,17},{... | collective-permute-start | bytes 4030472 | tf_op jit(solution)/shard_map/ppermute | solution.py:110
  413.7 32.4 %collective-permute-start.59 = (bf16[5248,128]{1,0:T(8,128)(2,1)S(1)}, bf16[5248,128]{1,0:T(8,128)(2,1)S(1)}, u32[]{:S(2)}, u32[]{:S(2)}) collective-permute-start(bf16[5248,128]{1,0:T(8,128)(2,1)S(1)} %get-tuple-element.153), channel_id=1, source_target_pairs={{0,8},{4,12},{8,0},{12,4},{16,24},{20,28},{24,16},{28,20},{1,9},{5... | collective-permute-start | bytes 4030472 | tf_op jit(solution)/shard_map/ppermute | solution.py:110
  415.1 61.2 %collective-permute-start.72 = (bf16[656,128]{1,0:T(8,128)(2,1)S(1)}, bf16[656,128]{1,0:T(8,128)(2,1)}, u32[]{:S(2)}, u32[]{:S(2)}) collective-permute-start(bf16[656,128]{1,0:T(8,128)(2,1)S(1)} %get-tuple-element.174), channel_id=1, source_target_pairs={{1,0},{2,1},{3,2},{5,4},{6,5},{7,6},{9,8},{10,9},{11,10},{13,12},{... | collective-permute-start | bytes 503816 | tf_op jit(solution)/shard_map/ppermute | solution.py:104
  416.4 65.9 %collective-permute-start.69 = (bf16[656,128]{1,0:T(8,128)(2,1)}, bf16[656,128]{1,0:T(8,128)(2,1)}, u32[]{:S(2)}, u32[]{:S(2)}) collective-permute-start(bf16[656,128]{1,0:T(8,128)(2,1)} %get-tuple-element.173), channel_id=1, source_target_pairs={{0,1},{1,2},{2,3},{4,5},{5,6},{6,7},{8,9},{9,10},{10,11},{12,13},{... | collective-permute-start | bytes 503816 | tf_op jit(solution)/shard_map/ppermute | solution.py:103
  425.8 41.3 %collective-permute-start.51 = (bf16[4160,128]{1,0:T(8,128)(2,1)S(1)}, bf16[4160,128]{1,0:T(8,128)(2,1)S(1)}, u32[]{:S(2)}, u32[]{:S(2)}) collective-permute-start(bf16[4160,128]{1,0:T(8,128)(2,1)S(1)} %get-tuple-element.156), channel_id=1, source_target_pairs={{0,8},{4,12},{8,0},{12,4},{16,24},{20,28},{24,16},{28,20},{1,9},{5... | collective-permute-start | bytes 3194888 | tf_op jit(solution)/shard_map/ppermute | solution.py:110
  448.3 20.9 %collective-permute-start.61 = (bf16[1312,128]{1,0:T(8,128)(2,1)S(1)}, bf16[1312,128]{1,0:T(8,128)(2,1)S(1)}, u32[]{:S(2)}, u32[]{:S(2)}) collective-permute-start(bf16[1312,128]{1,0:T(8,128)(2,1)S(1)} %get-tuple-element.165), channel_id=1, source_target_pairs={{0,1},{4,5},{8,9},{12,13},{16,17},{20,21},{24,25},{28,29}} | collective-permute-start | bytes 1007624 | tf_op jit(solution)/shard_map/ppermute | solution.py:103
  453.4 16.3 %collective-permute-start.64 = (bf16[1312,128]{1,0:T(8,128)(2,1)S(1)}, bf16[1312,128]{1,0:T(8,128)(2,1)S(1)}, u32[]{:S(2)}, u32[]{:S(2)}) collective-permute-start(bf16[1312,128]{1,0:T(8,128)(2,1)S(1)} %get-tuple-element.166), channel_id=1, source_target_pairs={{3,2},{7,6},{11,10},{15,14},{19,18},{23,22},{27,26},{31,30}} | collective-permute-start | bytes 1007624 | tf_op jit(solution)/shard_map/ppermute | solution.py:104
  467.1 25.3 %collective-permute-start.50 = (bf16[4160,128]{1,0:T(8,128)(2,1)}, bf16[4160,128]{1,0:T(8,128)(2,1)}, u32[]{:S(2)}, u32[]{:S(2)}) collective-permute-start(bf16[4160,128]{1,0:T(8,128)(2,1)} %get-tuple-element.155), channel_id=1, source_target_pairs={{0,8},{4,12},{8,0},{12,4},{16,24},{20,28},{24,16},{28,20},{1,9},{5... | collective-permute-start | bytes 3194888 | tf_op jit(solution)/shard_map/ppermute | solution.py:110
  469.1 23.7 %collective-permute-start.52 = (bf16[4160,128]{1,0:T(8,128)(2,1)}, bf16[4160,128]{1,0:T(8,128)(2,1)}, u32[]{:S(2)}, u32[]{:S(2)}) collective-permute-start(bf16[4160,128]{1,0:T(8,128)(2,1)} %add_convert_fusion.3), channel_id=1, source_target_pairs={{0,16},{4,20},{8,24},{12,28},{16,0},{20,4},{24,8},{28,12},{1,17},{... | collective-permute-start | bytes 3194888 | tf_op jit(solution)/shard_map/ppermute | solution.py:110
  470.6 14.2 %collective-permute-start.62 = (bf16[1312,128]{1,0:T(8,128)(2,1)}, bf16[1312,128]{1,0:T(8,128)(2,1)}, u32[]{:S(2)}, u32[]{:S(2)}) collective-permute-start(bf16[1312,128]{1,0:T(8,128)(2,1)} %get-tuple-element.163), channel_id=1, source_target_pairs={{0,1},{1,2},{4,5},{5,6},{8,9},{9,10},{12,13},{13,14},{16,17},{17,1... | collective-permute-start | bytes 1007624 | tf_op jit(solution)/shard_map/ppermute | solution.py:103
  486.2 14.9 %collective-permute-start.66 = (bf16[1312,128]{1,0:T(8,128)(2,1)S(1)}, bf16[1312,128]{1,0:T(8,128)(2,1)S(1)}, u32[]{:S(2)}, u32[]{:S(2)}) collective-permute-start(bf16[1312,128]{1,0:T(8,128)(2,1)S(1)} %get-tuple-element.162), channel_id=1, source_target_pairs={{1,0},{2,1},{3,2},{5,4},{6,5},{7,6},{9,8},{10,9},{11,10},{13,12},{... | collective-permute-start | bytes 1007624 | tf_op jit(solution)/shard_map/ppermute | solution.py:104
  487.5 13.6 %collective-permute-start.63 = (bf16[1312,128]{1,0:T(8,128)(2,1)S(1)}, bf16[1312,128]{1,0:T(8,128)(2,1)S(1)}, u32[]{:S(2)}, u32[]{:S(2)}) collective-permute-start(bf16[1312,128]{1,0:T(8,128)(2,1)S(1)} %get-tuple-element.161), channel_id=1, source_target_pairs={{0,1},{1,2},{2,3},{4,5},{5,6},{6,7},{8,9},{9,10},{10,11},{12,13},{... | collective-permute-start | bytes 1007624 | tf_op jit(solution)/shard_map/ppermute | solution.py:103
  501.2 9.7 %collective-permute-start.73 = (f32[2,128]{1,0:T(2,128)S(1)}, f32[2,128]{1,0:T(2,128)S(1)}, u32[]{:S(2)}, u32[]{:S(2)}) collective-permute-start(f32[2,128]{1,0:T(2,128)S(1)} %fusion.31), channel_id=1, source_target_pairs={{0,1},{1,0},{2,3},{3,2},{4,5},{5,4},{6,7},{7,6},{8,9},{9,8},{10,11... | collective-permute-start | bytes 3080 | tf_op jit(solution)/shard_map/ppermute | solution.py:802
  504.2 12.4 %collective-permute-start.54 = (bf16[1024,128]{1,0:T(8,128)(2,1)S(1)}, bf16[1024,128]{1,0:T(8,128)(2,1)S(1)}, u32[]{:S(2)}, u32[]{:S(2)}) collective-permute-start(bf16[1024,128]{1,0:T(8,128)(2,1)S(1)} %get-tuple-element.169), channel_id=1, source_target_pairs={{0,1},{1,2},{4,5},{5,6},{8,9},{9,10},{12,13},{13,14},{16,17},{17,1... | collective-permute-start | bytes 786440 | tf_op jit(solution)/shard_map/ppermute | solution.py:103
  510.9 24.5 %collective-permute-start.74 = (f32[2,128]{1,0:T(2,128)S(1)}, f32[2,128]{1,0:T(2,128)S(1)}, u32[]{:S(2)}, u32[]{:S(2)}) collective-permute-start(f32[2,128]{1,0:T(2,128)S(1)} %fusion.33), channel_id=1, source_target_pairs={{0,2},{1,3},{2,0},{3,1},{4,6},{5,7},{6,4},{7,5},{8,10},{9,11},{10,... | collective-permute-start | bytes 3080 | tf_op jit(solution)/shard_map/ppermute | solution.py:802
  516.7 19.4 %collective-permute-start.58 = (bf16[1024,128]{1,0:T(8,128)(2,1)S(1)}, bf16[1024,128]{1,0:T(8,128)(2,1)S(1)}, u32[]{:S(2)}, u32[]{:S(2)}) collective-permute-start(bf16[1024,128]{1,0:T(8,128)(2,1)S(1)} %get-tuple-element.168), channel_id=1, source_target_pairs={{1,0},{2,1},{3,2},{5,4},{6,5},{7,6},{9,8},{10,9},{11,10},{13,12},{... | collective-permute-start | bytes 786440 | tf_op jit(solution)/shard_map/ppermute | solution.py:104
  518.0 18.0 %collective-permute-start.55 = (bf16[1024,128]{1,0:T(8,128)(2,1)S(1)}, bf16[1024,128]{1,0:T(8,128)(2,1)S(1)}, u32[]{:S(2)}, u32[]{:S(2)}) collective-permute-start(bf16[1024,128]{1,0:T(8,128)(2,1)S(1)} %get-tuple-element.167), channel_id=1, source_target_pairs={{0,1},{1,2},{2,3},{4,5},{5,6},{6,7},{8,9},{9,10},{10,11},{12,13},{... | collective-permute-start | bytes 786440 | tf_op jit(solution)/shard_map/ppermute | solution.py:103
  (66 other events, 922.4 us)

commit v4 on v3

--- a/solution.py
+++ b/solution.py
@@ -30,6 +30,7 @@
 PIECES = 8
 SLAB_PAD = 16
 VMEM_BYTES = 52 * 1024 * 1024
+COST_FACTOR = 100
 
 
 def layout(lengths, token_index, group_rows):
@@ -74,9 +75,8 @@
     return (one_new, two_new, master_new)
 
 
-def line_gather(slab):
+def line_gather(slab, place):
     size = lax.axis_size("tensor")
-    place = lax.axis_index("tensor")
     from_before, from_after = [slab], [slab]
     for step in range(1, size):
         from_before.append(
@@ -94,16 +94,30 @@
     )
 
 
-def line_scatter(parts):
+def tied(values, token):
+    return values if token is None else jnp.where(token[0, 0] == 0, values, 0.0 * values)
+
+
+def line_hop(to_after, to_before, step):
     size = lax.axis_size("tensor")
-    up, down = 0.0, 0.0
-    for step in range(size - 1, 0, -1):
-        to_after = (parts[size - step].astype(jnp.float32) + up).astype(parts.dtype)
-        to_before = (parts[step].astype(jnp.float32) + down).astype(parts.dtype)
-        up = lax.ppermute(to_after, "tensor", [(n, n + 1) for n in range(size - step)])
-        down = lax.ppermute(to_before, "tensor", [(n, n - 1) for n in range(step, size)])
-        up, down = up.astype(jnp.float32), down.astype(jnp.float32)
-    return parts[0].astype(jnp.float32) + up + down
+    return (
+        lax.ppermute(to_after, "tensor", [(n, n + 1) for n in range(size - step)]),
+        lax.ppermute(to_before, "tensor", [(n, n - 1) for n in range(step, size)]),
+    )
+
+
+def line_end(own, arrived):
+    return sum((part.astype(jnp.float32) for part in arrived), own.astype(jnp.float32))
+
+
+def gain_scatter(gains):
+    for mask in [1, 4, 2] + far_bits()[::-1]:
+        half = gains.shape[1] // 2
+        gains = gains[:, :half] + flip(gains[:, half:], mask)
+    size = lax.axis_size("tensor")
+    for mask in (1 << n for n in range(size.bit_length() - 1)):
+        gains = gains + lax.ppermute(gains, "tensor", [(n, n ^ mask) for n in range(size)])
+    return gains
 
 
 def flip(rows, mask):
@@ -115,40 +129,30 @@
     return [1 << n for n in range(3, size.bit_length() - 1)]
 
 
-def gather(slab, x_first):
-    piece = line_gather(slab)
+def gather_near(slab, place):
+    piece = line_gather(slab, place)
     piece = piece.reshape(-1, piece.shape[-1])
     for mask in far_bits():
         piece = jnp.concatenate([piece, flip(piece, mask)], axis=1)
-    by_x, by_y = flip(piece, 2), flip(piece, 4)
-    far = flip(by_x, 4) if x_first else flip(by_y, 2)
-    mine = [piece, by_x, by_y, far]
-    return (mine + [flip(part, 1) for part in mine], piece)
+    return (piece, flip(piece, 2), flip(piece, 4))
+
+
+def gather_far(near, x_first, token=None, core_token=None):
+    piece, by_x, by_y = near
+    far = flip(tied(by_x, token), 4) if x_first else flip(tied(by_y, token), 2)
+    mine = [piece, by_x, by_y, tied(far, core_token)]
+    return mine + [flip(part, 1) for part in mine]
 
 
 def add_low(left, right):
     return (left.astype(jnp.float32) + right.astype(jnp.float32)).astype(left.dtype)
 
 
-def scatter(own, partner, x_first):
-    received = flip(partner, 1)
-    own, by_x, by_y, far = [add_low(mine, received[n]) for n, mine in enumerate(own)]
-    if x_first:
-        passed = flip(far, 2)
-        by_y = add_low(by_y, passed)
-    else:
-        passed = flip(far, 4)
-        by_x = add_low(by_x, passed)
-    from_x, from_y = flip(by_x, 2), flip(by_y, 4)
-    total = (
-        own.astype(jnp.float32) + from_x.astype(jnp.float32) + from_y.astype(jnp.float32)
-    ).astype(own.dtype)
+def far_scatter(part):
     for mask in reversed(far_bits()):
-        half = total.shape[1] // 2
-        total = add_low(total[:, :half], flip(total[:, half:], mask))
-    size = lax.axis_size("tensor")
-    total = total.reshape(size, total.shape[0] // size, total.shape[1])
-    return (total, (received, passed, from_x, from_y))
+        half = part.shape[1] // 2
+        part = add_low(part[:, :half], flip(part[:, half:], mask))
+    return part
 
 
 def to_relative(rows, back=False):
@@ -185,8 +189,8 @@
     return lax.dot_general(left, right, (dims, ((), ())), preferred_element_type=jnp.float32)
 
 
-def wide(pieces, rows):
-    return jnp.concatenate([piece[0, rows, :] for piece in pieces], axis=1)
+def wide(pieces, rows, slab=0):
+    return jnp.concatenate([piece[slab, rows, :] for piece in pieces], axis=1)
 
 
 def relative(order, ref, rows):
@@ -226,7 +230,7 @@
     return pl.BlockSpec(array.shape, lambda *_: (0,) * len(array.shape))
 
 
-def run(kernel, name, operands, outs, scratch, flops, after=()):
+def run(kernel, name, operands, outs, scratch, flops, after=(), steps=None):
     order, operands = operands[0], operands[1:]
     specs = [spec if spec is not None else whole_spec(array) for array, spec in operands]
     out_specs = [
@@ -235,36 +239,123 @@
     ]
     moved = sum(array.size * array.dtype.itemsize for array, _ in operands)
     moved += sum(math.prod(shape) * jnp.dtype(dtype).itemsize for shape, dtype, _ in outs)
-    kept = len(operands)
+    kept, made = len(operands), len(outs)
 
     def body(order_ref, *refs):
-        kernel(order_ref, *refs[:kept], *refs[kept + len(after) :])
+        refs = refs[:kept] + refs[kept + len(after) :]
+        token = refs[kept + made]
+        token[...] = jnp.zeros_like(token)
+        kernel(order_ref, *refs[: kept + made], *refs[kept + made + 1 :])
 
     return pl.pallas_call(
         body,
         grid_spec=pltpu.PrefetchScalarGridSpec(
             num_scalar_prefetch=1,
-            grid=(lax.axis_size("tensor"),),
+            grid=(steps or lax.axis_size("tensor"),),
             in_specs=specs + [pl.BlockSpec(memory_space=pl.ANY)] * len(after),
-            out_specs=out_specs,
+            out_specs=out_specs + [pl.BlockSpec((8, LANES), lambda *_: (0, 0))],
             scratch_shapes=scratch,
         ),
-        out_shape=[jax.ShapeDtypeStruct(shape, dtype) for shape, dtype, _ in outs],
+        out_shape=[jax.ShapeDtypeStruct(shape, dtype) for shape, dtype, _ in outs]
+        + [jax.ShapeDtypeStruct((8, LANES), jnp.int32)],
         compiler_params=pltpu.CompilerParams(
             dimension_semantics=("arbitrary",), vmem_limit_bytes=VMEM_BYTES
         ),
-        cost_estimate=pl.CostEstimate(flops=flops, bytes_accessed=moved, transcendentals=0),
+        cost_estimate=pl.CostEstimate(
+            flops=COST_FACTOR * flops, bytes_accessed=moved, transcendentals=0
+        ),
         name=name,
     )(order, *[array for array, _ in operands], *after)
 
 
-def slabs(piece, rows, first=0):
-    return (piece, pl.BlockSpec((1, rows, LANES), lambda n, *_: (n, first, 0)))
-
-
-def lead(array):
-    shape = (1,) + array.shape[1:]
-    return (array, pl.BlockSpec(shape, lambda n, *_: (n,) + (0,) * (len(shape) - 1)))
+def held_back(value, after):
+    def body(value_ref, *refs):
+        refs[-1][...] = value_ref[...]
+
+    return pl.pallas_call(
+        body,
+        in_specs=[pl.BlockSpec(memory_space=pltpu.VMEM)]
+        + [pl.BlockSpec(memory_space=pl.ANY)] * len(after),
+        out_specs=pl.BlockSpec(memory_space=pltpu.VMEM),
+        out_shape=jax.ShapeDtypeStruct(value.shape, value.dtype),
+        name="held_back",
+    )(value, *after)
+
+
+def blend(name, jobs, after):
+    halves = 2
+    operands, specs, out_specs, shapes, counts, cut = [], [], [], [], [], []
+    for terms in jobs:
+        rows, lanes = terms[0][0].shape[-2:]
+        small = rows % (16 * halves) != 0 or rows < 512
+        height = rows if small else rows // halves
+        for term in terms:
+            operands.append(term[0])
+            if len(term) == 1:
+                specs.append(pl.BlockSpec((height, lanes), lambda i, s=small: (0 if s else i, 0)))
+            else:
+                specs.append(
+                    pl.BlockSpec(
+                        (None, height, lanes),
+                        lambda i, s=small, n=term[1]: (n, 0 if s else i, 0),
+                    )
+                )
+        out_specs.append(pl.BlockSpec((height, lanes), lambda i, s=small: (0 if s else i, 0)))
+        shapes.append(jax.ShapeDtypeStruct((rows, lanes), jnp.bfloat16))
+        counts.append(len(terms))
+        cut.append(small)
+
+    def body(*refs):
+        ins = refs[: len(operands)]
+        outs = refs[len(operands) + len(after) :]
+        outs[-1][...] = jnp.zeros_like(outs[-1])
+        first = 0
+        for n, count in enumerate(counts):
+            terms = ins[first : first + count]
+            first += count
+
+            def add(out=outs[n], terms=terms):
+                out[...] = sum(
+                    (term[...].astype(jnp.float32) for term in terms[1:]),
+                    terms[0][...].astype(jnp.float32),
+                ).astype(jnp.bfloat16)
+
+            pl.when((pl.program_id(0) == 0) | (not cut[n]))(add)
+
+    *sums, token = pl.pallas_call(
+        body,
+        grid=(halves,),
+        in_specs=specs + [pl.BlockSpec(memory_space=pl.ANY)] * len(after),
+        out_specs=out_specs + [pl.BlockSpec((8, LANES), lambda i: (0, 0))],
+        out_shape=shapes + [jax.ShapeDtypeStruct((8, LANES), jnp.int32)],
+        compiler_params=pltpu.CompilerParams(
+            dimension_semantics=("arbitrary",), vmem_limit_bytes=VMEM_BYTES
+        ),
+        name=name,
+    )(*operands, *after)
+    return (sums, token)
+
+
+ALL, ODD, EVEN, SECOND, OWN = (0, 1), (1, 2), (0, 2), (2, 1), (0, 1)
+
+
+def slabs(piece, rows, part=ALL, first=0, count=1):
+    return (
+        piece,
+        pl.BlockSpec((count, rows, LANES), lambda n, *_: (part[0] + part[1] * n, first, 0)),
+    )
+
+
+def lead(array, part=ALL, count=1):
+    shape = (count,) + array.shape[1:]
+    return (
+        array,
+        pl.BlockSpec(shape, lambda n, *_: (part[0] + part[1] * n,) + (0,) * (len(shape) - 1)),
+    )
+
+
+def turned_block(array, rows, part=ALL):
+    return (array, pl.BlockSpec((rows, array.shape[1]), lambda n, *_: (part[0] + part[1] * n, 0)))
 
 
 def lead_out(shape, dtype):
@@ -286,7 +377,7 @@
 
 
 def heads_kernel(order, hidden, before, after, gains, cosine, sine, *refs):
-    pieces, (q_out, k_out, v_out, rows_out, rows_wide) = refs[:PIECES], refs[PIECES:]
+    pieces, (q_out, k_out, v_out, rows_wide) = refs[:PIECES], refs[PIECES:]
     row_count = hidden.shape[0]
     gain = gains[0:1, :]
 
@@ -301,7 +392,6 @@
 
         def one(rows):
             values = norm_rows(hidden, rows, 0)
-            rows_out[rows, :] = values
             rows_wide[pl.ds(pl.multiple_of(rows.start + HALF, HALF), HALF), :] = values
 
         row_steps(row_count, HALF, one)
@@ -315,7 +405,7 @@
 
     inner = slice(HALF, HALF + row_count)
     scale = HEAD_DIM ** (-0.5)
-    front, back = turned(dot(rows_out[...], wide(pieces, slice(0, width)), NT), inner)
+    front, back = turned(dot(rows_wide[inner, :], wide(pieces, slice(0, width)), NT), inner)
     q_out[0, :, :LANES] = (front.astype(jnp.bfloat16) * scale).astype(jnp.bfloat16)
     q_out[0, :, LANES:] = (back.astype(jnp.bfloat16) * scale).astype(jnp.bfloat16)
     front, back = turned(
@@ -456,18 +546,20 @@
     store_pieces(grads, slice(count, 2 * count), dot(up_out[...], rows_two[...], NN))
 
 
-def middle_grad_kernel(order, middle, cot, gains, gate_grad, up_grad, *refs):
-    pieces, (grad_middle, grad_low, gain_out, total) = refs[:PIECES], refs[PIECES:]
+def middle_grad_kernel(order, middle, cot, gains, *refs):
+    sides, pieces, refs = refs[:4], refs[4 : 4 + PIECES], refs[4 + PIECES :]
+    grad_middle, grad_low, gain_out, total = refs
     step = pl.program_id(0)
-    count = gate_grad.shape[0]
+    count = sides[0].shape[0]
 
     @pl.when(step == 0)
     def _():
         total[...] = jnp.zeros_like(total)
         gain_out[...] = jnp.zeros_like(gain_out)
 
-    total[...] += dot(gate_grad[...], wide(pieces, slice(0, count)), TN)
-    total[...] += dot(up_grad[...], wide(pieces, slice(count, 2 * count)), TN)
+    for n, side in enumerate(sides):
+        rows = slice((n % 2) * count, (n % 2 + 1) * count)
+        total[...] += dot(side[...], wide(pieces, rows, n // 2), TN)
 
     @pl.when(step == pl.num_programs(0) - 1)
     def _():
@@ -482,11 +574,15 @@
         row_steps(middle.shape[0], HALF, one)
 
 
-def attend_grad_kernel(order, bias, cosine, sine, grad_low, q_in, k_in, v_in, logs, *refs):
-    pieces, (grads, edges, grad_keys, grad_values, grad_out) = refs[:PIECES], refs[PIECES:]
+def attend_grad_kernel(
+    order, bias, cosine, sine, grad_low, rows_wide, q_in, k_in, v_in, attended, logs, *refs
+):
+    pieces, refs = refs[:PIECES], refs[PIECES:]
+    weight_grads, (query_out, pair_out, grad_keys, grad_values, grad_out) = refs[:5], refs[5:]
     turned, plain = head_masks()
     row_count = grad_low.shape[0]
     low = jnp.bfloat16
+    width = 2 * LANES
     grad_out[...] = dot(grad_low[...], wide(pieces, slice(None)), NT).astype(low)
     grad_keys[...] = jnp.zeros_like(grad_keys)
     grad_values[...] = jnp.zeros_like(grad_values)
@@ -503,9 +599,9 @@
         grad_rows = grad_out[rows, :]
         masked = bias[n]
         log_rows = logs[0, rows, :]
-        grad_query = jnp.zeros((BLOCK, 2 * LANES), jnp.float32)
-        grad_key = jnp.zeros((BLOCK + 2 * HALF, 2 * LANES), jnp.float32)
-        grad_value = jnp.zeros((BLOCK + 2 * HALF, 2 * LANES), jnp.float32)
+        grad_query = jnp.zeros((BLOCK, width), jnp.float32)
+        grad_key = jnp.zeros((BLOCK + 2 * HALF, width), jnp.float32)
+        grad_value = jnp.zeros((BLOCK + 2 * HALF, width), jnp.float32)
         for h in range(4):
             query_head, grad_head = queries * turned[h], grad_rows * plain[h]
             scores = dot(query_head, keys, NT) + masked
@@ -518,30 +614,28 @@
             grad_value = grad_value + dot(probs.astype(low), grad_head, TN)
         place = pl.ds(pl.multiple_of(n * BLOCK + HALF, HALF), BLOCK)
         front, rear = back(grad_query * HEAD_DIM ** (-0.5), place)
-        grads[0, 0, rows, :LANES] = front.astype(low)
-        grads[0, 0, rows, LANES:] = rear.astype(low)
+        query_out[0, rows, :LANES] = front.astype(low)
+        query_out[0, rows, LANES:] = rear.astype(low)
         grad_keys[span, :] += grad_key
         grad_values[span, :] += grad_value
         return carried
 
     lax.fori_loop(0, bias.shape[0], block, 0)
+    front, rear = back(grad_keys[...], slice(None))
+    pair_out[0, 0, :, :LANES] = front.astype(low)
+    pair_out[0, 0, :, LANES:] = rear.astype(low)
+    pair_out[0, 1] = grad_values[...].astype(low)
     inner = slice(HALF, HALF + row_count)
-    for rows, out in (
-        (inner, lambda n: grads.at[0, 1 + n]),
-        (slice(0, HALF), lambda n: edges.at[0, 0, n]),
-        (slice(HALF + row_count, None), lambda n: edges.at[0, 1, n]),
-    ):
-        front, rear = back(grad_keys[rows, :], rows)
-        out(0)[:, :LANES] = front.astype(low)
-        out(0)[:, LANES:] = rear.astype(low)
-        out(1)[...] = grad_values[rows, :].astype(low)
-
-
-def heads_grad_kernel(
-    order, hidden, gains, gain_two, grad_middle, grad_low, rows_one, attended, grads, before, after, *refs
-):
-    pieces, outs = refs[:PIECES], refs[PIECES : PIECES + 5]
-    grad_input, mixed, total, gain_one = refs[PIECES + 5 :]
+    store_pieces(weight_grads, slice(0, width), dot(query_out[0], rows_wide[inner, :], TN))
+    for c in range(2):
+        rows = slice((1 + c) * width, (2 + c) * width)
+        store_pieces(weight_grads, rows, dot(pair_out[0, c], rows_wide[...], TN))
+    store_pieces(weight_grads, slice(3 * width, 4 * width), dot(attended[0], grad_low[...], TN))
+
+
+def input_grad_kernel(order, hidden, gains, grad_middle, *refs):
+    own, second, odd, (before, after), refs = refs[:2], refs[2:4], refs[4:6], refs[6:8], refs[8:]
+    pieces, (grad_input, gain_out, mixed, total) = refs[:PIECES], refs[PIECES:]
     step = pl.program_id(0)
     row_count = hidden.shape[0]
     width = 2 * LANES
@@ -550,22 +644,23 @@
     @pl.when(step == 0)
     def _():
         total[...] = jnp.zeros_like(total)
-        gain_one[...] = jnp.zeros_like(gain_one)
-
-    def add_low(left, right):
+        gain_out[...] = jnp.zeros_like(gain_out)
+
+    def sum_low(left, right):
         return (left.astype(jnp.float32) + right.astype(jnp.float32)).astype(jnp.bfloat16)
 
-    mixed[...] = grads[0]
-    for c in range(2):
-        mixed[1 + c, 0:HALF, :] = add_low(grads[0, 1 + c, 0:HALF, :], before[0, c])
-        mixed[1 + c, last:, :] = add_low(grads[0, 1 + c, last:, :], after[0, c])
-    for c in range(3):
-        rows = slice(c * width, (c + 1) * width)
-        total[...] += dot(mixed[c], wide(pieces, rows), NN)
-        store_pieces(outs, rows, dot(mixed[c], rows_one[...], TN))
-    store_pieces(outs, slice(3 * width, 4 * width), dot(attended[0], grad_low[...], TN))
-    tail = slice(4 * width, 4 * width + SLAB_PAD)
-    store_pieces(outs, tail, jnp.zeros((SLAB_PAD, PIECES * LANES), jnp.float32))
+    def add(slab, queries, pairs):
+        total[...] += dot(queries[0], wide(pieces, slice(0, width), slab), NN)
+        for c in range(2):
+            mixed[...] = pairs[0, c, HALF : HALF + row_count, :]
+            mixed[0:HALF, :] = sum_low(mixed[0:HALF, :], before[slab, c])
+            mixed[last:, :] = sum_low(mixed[last:, :], after[slab, c])
+            rows = slice((1 + c) * width, (2 + c) * width)
+            total[...] += dot(mixed[...], wide(pieces, rows, slab), NN)
+
+    pl.when(step == 0)(functools.partial(add, 0, *own))
+    pl.when(step == 1)(functools.partial(add, 0, *second))
+    add(1, *odd)
 
     @pl.when(step == pl.num_programs(0) - 1)
     def _():
@@ -576,14 +671,9 @@
             for n in range(PIECES):
                 lanes = pl.ds(pl.multiple_of(order[n] * LANES, LANES), LANES)
                 grad_input[rows, lanes] = result[:, n * LANES : (n + 1) * LANES]
-            gain_one[0:1, :] += jnp.sum(grad * hat, axis=0, keepdims=True)
+            gain_out[0:1, :] += jnp.sum(grad * hat, axis=0, keepdims=True)
 
         row_steps(row_count, HALF, one)
-        both = jnp.concatenate(
-            [gain_one[0:1, :], gain_two[0:1, :], jnp.zeros((SLAB_PAD - 2, PIECES * LANES), jnp.float32)],
-            axis=0,
-        )
-        store_pieces(outs, tail, both)
 
 
 def local(
@@ -639,20 +729,23 @@
     in_slab = w_in.astype(low).reshape(chunk, 2 * hidden_wide).T
     down_slab = w_down.astype(low).T
     if dp_size == PIECES:
-        place = jnp.array([0, 2, 4, 6, 1, 3, 5, 7], jnp.int32)
-        order = lax.axis_index("dp").astype(jnp.int32) ^ place
+        apart = jnp.array([0, 2, 4, 6, 1, 3, 5, 7], jnp.int32)
+        order = lax.axis_index("dp").astype(jnp.int32) ^ apart
         hidden, cot_in = hidden_in, cotangent
     else:
         order = jnp.arange(PIECES, dtype=jnp.int32)
         hidden, cot_in = to_relative(hidden_in), to_relative(cotangent)
 
     edges = (shift(hidden[-HALF:], 1), shift(hidden[:HALF], -1))
-    heads_pieces, heads_line = gather(heads_slab, True)
-    in_pieces, in_line = gather(in_slab, False)
-    down_pieces, down_line = gather(down_slab, True)
+    place = lax.axis_index("tensor").astype(jnp.int32)
+    place_rows = jnp.full((8, LANES), place)
+    heads_near = gather_near(heads_slab, place)
+    heads_pieces = gather_far(heads_near, True)
+    line_token = held_back(place_rows * 0, heads_near[:1])
+    in_near = gather_near(
+        tied(in_slab, line_token), held_back(place_rows, heads_pieces[3:4])[0, 0]
+    )
     heads_pieces = [piece.reshape(size, -1, LANES) for piece in heads_pieces]
-    in_pieces = [piece.reshape(size, -1, LANES) for piece in in_pieces]
-    down_pieces = [piece.reshape(size, -1, LANES) for piece in down_pieces]
     gains = jnp.concatenate(
         [piece[0, head_rows : head_rows + 8] for piece in heads_pieces], axis=1
     ).astype(full)
@@ -671,36 +764,42 @@
     turned_spec = pl.BlockSpec((hidden_wide, row_count), lambda n, *_: (n, 0))
     matmul = 2 * row_count * D
 
-    queries, keys, values, rows_one = run(
+    queries, keys, values, rows_wide, token = run(
         heads_kernel,
         "heads",
         [order, (hidden, None), (edges[0], None), (edges[1], None), (gains, None)]
         + [(cosine, None), (sine, None)]
         + [slabs(piece, 3 * head_wide) for piece in heads_pieces],
         [lead_out(head_block, low), lead_out(wide_block, low), lead_out(wide_block, low)]
-        + [(tokens, low, None)],
-        [pltpu.VMEM((wide_count, D), low)],
+        + [((wide_count, D), low, None)],
+        [],
         3 * matmul * D,
-        after=(in_line, down_line),
-    )
-    attended, logs = run(
+        after=in_near[:1],
+    )
+    in_pieces = gather_far(in_near, False, token)
+    attended, logs, token = run(
         attend_kernel,
         "attend",
         [order, (bias, None), lead(queries), lead(keys), lead(values)],
         [lead_out(head_block, low), lead_out((size, row_count, LANES), full)],
         [],
         2 * matmul * D,
-    )
-    middle, rows_two = run(
+        after=in_near[1:],
+    )
+    down_near = gather_near(tied(down_slab, line_token), place + token[0, 0])
+    middle, rows_two, proj_token = run(
         proj_kernel,
         "proj",
         [order, (hidden, None), (gains, None), lead(attended)]
-        + [slabs(piece, head_wide, 3) for piece in heads_pieces],
+        + [slabs(piece, head_wide, first=3) for piece in heads_pieces],
         [(tokens, full, None), (tokens, low, None)],
         [],
         matmul * D,
-    )
-    active, gate_side, up_side = run(
+        after=in_pieces[3:4],
+    )
+    in_pieces = [piece.reshape(size, -1, LANES) for piece in in_pieces]
+    _, proj_token = blend("arrived", [], (proj_token, *down_near[1:]))
+    active, gate_side, up_side, token = run(
         gate_kernel,
         "gate",
         [order, (rows_two, None)] + [slabs(piece, 2 * hidden_wide) for piece in in_pieces],
@@ -711,98 +810,212 @@
             pltpu.VMEM((hidden_wide, row_count), full),
         ],
         2 * matmul * FF,
-    )
-
-    *down_own, down_partner, cot = run(
+        after=(proj_token,),
+    )
+    down_pieces = gather_far(down_near, True, proj_token, token)
+
+    *down_own, down_partner, cot, token = run(
         down_grad_kernel,
         "down_grad",
-        [order, (cot_in, None), (active, turned_spec)],
+        [order, (cot_in, None), turned_block(active, hidden_wide)],
         piece_outs(size, hidden_wide) + [(tokens, low, None)],
         [],
         matmul * FF,
-    )
-    flat = lambda part: part.reshape(-1, LANES)
-    flat_four = lambda part: part.reshape(4, -1, LANES)
-    down_total, down_steps = scatter([flat(p) for p in down_own], flat_four(down_partner), True)
-    *in_own, in_partner, gate_grad, up_grad = run(
-        in_grad_kernel,
-        "in_grad",
-        [order, (cot, None), (rows_two, None), (gate_side, turned_spec), (up_side, turned_spec)]
-        + [slabs(piece, hidden_wide) for piece in down_pieces],
-        piece_outs(size, 2 * hidden_wide) + [(turned, low, turned_spec)] * 2,
-        [pltpu.VMEM((D, row_count), low), pltpu.VMEM((hidden_wide, row_count), full)],
-        3 * matmul * FF,
-    )
-    in_total, in_steps = scatter([flat(p) for p in in_own], flat_four(in_partner), False)
-    grad_middle, grad_low, gain_two = run(
+        after=down_pieces[3:4],
+    )
+    down_pieces = [piece.reshape(size, -1, LANES) for piece in down_pieces]
+
+    half = size // 2
+    half_turned = (half * hidden_wide, row_count)
+
+    def core_hop(outs):
+        own = [part.reshape(-1, LANES) for part in outs[:4]]
+        return (own, flip(outs[4].reshape(4, -1, LANES), 1))
+
+    def core_sums(own, received):
+        return [[(part,), (received, n)] for n, part in enumerate(own)]
+
+    def near_sums(own, arrived, entries):
+        terms = [part.reshape(entries, -1, LANES) for part in (own, *arrived)]
+        return [[(term, n) for term in terms] for n in range(entries)]
+
+    def line_sums(to_after, to_before, arrived):
+        return [[(to_after,), (arrived[0],)], [(to_before,), (arrived[1],)]]
+
+    down_core = core_hop([*down_own, down_partner])
+
+    def in_grad(part, name, after):
+        return run(
+            in_grad_kernel,
+            name,
+            [order, (cot, None), (rows_two, None)]
+            + [turned_block(gate_side, hidden_wide, part), turned_block(up_side, hidden_wide, part)]
+            + [slabs(piece, hidden_wide, part) for piece in down_pieces],
+            piece_outs(half, 2 * hidden_wide) + [(half_turned, low, turned_spec)] * 2,
+            [pltpu.VMEM((D, row_count), low), pltpu.VMEM((hidden_wide, row_count), full)],
+            3 * matmul * FF // 2,
+            after=after,
+            steps=half,
+        )
+
+    *odd_outs, odd_gate, odd_up, token = in_grad(ODD, "in_grad_odd", ())
+    odd_core = core_hop(odd_outs)
+    down_sums, token = blend("sums_one", core_sums(*down_core), (token,))
+    down_far = flip(down_sums[3], 2)
+    *even_outs, even_gate, even_up, token = in_grad(EVEN, "in_grad_even", (token,))
+    even_core = core_hop(even_outs)
+    (*odd_sums, down_y), token = blend(
+        "sums_two", core_sums(*odd_core) + [[(down_sums[2],), (down_far,)]], (token,)
+    )
+    odd_far = flip(odd_sums[3], 4)
+    down_near = (flip(down_sums[1], 2), flip(down_y, 4))
+    grad_middle, grad_low, gain_two, token = run(
         middle_grad_kernel,
         "middle_grad",
         [order, (middle, None), (cot, None), (gains, None)]
-        + [(gate_grad, turned_spec), (up_grad, turned_spec)]
-        + [slabs(piece, 2 * hidden_wide) for piece in in_pieces],
+        + [turned_block(side, hidden_wide) for side in (even_gate, even_up, odd_gate, odd_up)]
+        + [slabs(piece, 2 * hidden_wide, count=2) for piece in in_pieces],
         [(tokens, full, None), (tokens, low, None), ((8, D), full, None)],
         [pltpu.VMEM(tokens, full)],
         2 * matmul * FF,
-        after=down_steps[:1],
-    )
-    grads, edge_grads = run(
-        attend_grad_kernel,
-        "attend_grad",
-        [order, (bias, None), (cosine, None), (sine, None), (grad_low, None)]
-        + [lead(queries), lead(keys), lead(values), lead(logs)]
-        + [slabs(piece, head_wide, 3) for piece in heads_pieces],
-        [
-            lead_out((size, 3, row_count, head_wide), low),
-            lead_out((size, 2, 2, HALF, head_wide), low),
-        ],
-        [
-            pltpu.VMEM((wide_count, head_wide), full),
-            pltpu.VMEM((wide_count, head_wide), full),
-            pltpu.VMEM((row_count, head_wide), low),
-        ],
-        5 * matmul * D,
-        after=(down_steps[1], in_steps[0]),
-    )
-    grads_before = jnp.roll(shift(edge_grads[:, 1], 1), 1, axis=0)
-    grads_after = jnp.roll(shift(edge_grads[:, 0], -1), -1, axis=0)
-    *heads_own, heads_partner, grad_input = run(
-        heads_grad_kernel,
-        "heads_grad",
-        [order, (hidden, None), (gains, None), (gain_two, None), (grad_middle, None)]
-        + [(grad_low, None), (rows_one, None), lead(attended), lead(grads)]
-        + [lead(grads_before), lead(grads_after)]
-        + [slabs(piece, 3 * head_wide) for piece in heads_pieces],
-        piece_outs(size, slab_rows) + [(tokens, full, None)],
-        [
-            pltpu.VMEM((3, row_count, head_wide), low),
-            pltpu.VMEM(tokens, full),
-            pltpu.VMEM((8, D), full),
-        ],
-        7 * matmul * D,
-        after=down_steps[2:] + in_steps[1:2],
-    )
-    heads_total, heads_steps = scatter([flat(p) for p in heads_own], flat_four(heads_partner), True)
-    (hidden_out,) = run(
+        after=(token,),
+        steps=half,
+    )
+    sums, token = blend(
+        "sums_three",
+        core_sums(*even_core)
+        + [[(odd_sums[1],), (odd_far,)]]
+        + near_sums(down_sums[0], down_near, size),
+        (token,),
+    )
+    even_sums, odd_x, down_parts = sums[:4], sums[4], [far_scatter(part) for part in sums[5:]]
+    even_far = flip(even_sums[3], 4)
+    odd_near = (flip(odd_x, 2), flip(odd_sums[2], 4))
+    down_line = line_hop(down_parts[1], down_parts[3], 3)
+
+    def attend_grad(part, count, name, after):
+        return run(
+            attend_grad_kernel,
+            name,
+            [order, (bias, None), (cosine, None), (sine, None), (grad_low, None), (rows_wide, None)]
+            + [lead(array, part) for array in (queries, keys, values, attended, logs)]
+            + [slabs(piece, head_wide, part, first=3) for piece in heads_pieces],
+            piece_outs(count, head_rows)
+            + [
+                lead_out((count, row_count, head_wide), low),
+                lead_out((count, 2, wide_count, head_wide), low),
+            ],
+            [
+                pltpu.VMEM((wide_count, head_wide), full),
+                pltpu.VMEM((wide_count, head_wide), full),
+                pltpu.VMEM((row_count, head_wide), low),
+            ],
+            3 * count * matmul * D,
+            after=after,
+            steps=count,
+        )
+
+    *odd_outs, odd_queries, odd_pairs, token = attend_grad(ODD, half, "attend_grad_odd", (token,))
+    heads_odd_core = core_hop(odd_outs)
+    sums, token = blend(
+        "sums_four",
+        [[(even_sums[1],), (even_far,)]]
+        + near_sums(odd_sums[0], odd_near, half)
+        + line_sums(down_parts[2], down_parts[2], down_line),
+        (token,),
+    )
+    even_near = (flip(sums[0], 2), flip(even_sums[2], 4))
+    odd_parts = [far_scatter(part) for part in sums[1:3]]
+    down_line = line_hop(sums[3], sums[4], 2)
+    *second_outs, second_queries, second_pairs, token = attend_grad(
+        SECOND, 1, "attend_grad_second", (token,)
+    )
+    heads_second_core = core_hop(second_outs)
+    sums, token = blend(
+        "sums_five",
+        core_sums(*heads_odd_core)
+        + near_sums(even_sums[0], even_near, half)
+        + line_sums(down_parts[3], down_parts[1], down_line),
+        (token,),
+    )
+    heads_odd_sums, even_parts = sums[:4], [far_scatter(part) for part in sums[4:6]]
+    heads_odd_far = flip(heads_odd_sums[3], 2)
+    down_line = line_hop(sums[6], sums[7], 1)
+    in_line = line_hop(odd_parts[0], odd_parts[1], 3)
+    *own_outs, own_queries, own_pairs, token = attend_grad(OWN, 1, "attend_grad_own", (token,))
+    heads_own_core = core_hop(own_outs)
+    sums, token = blend(
+        "sums_six",
+        core_sums(*heads_second_core)
+        + [[(heads_odd_sums[2],), (heads_odd_far,)]]
+        + line_sums(even_parts[1], even_parts[1], in_line),
+        (token, *down_line),
+    )
+    heads_second_sums = sums[:4]
+    heads_second_far = flip(heads_second_sums[3], 4)
+    heads_odd_near = (flip(heads_odd_sums[1], 2), flip(sums[4], 4))
+    in_line = line_hop(sums[5], sums[6], 2)
+    pairs = [own_pairs[0], odd_pairs[0], second_pairs[0], odd_pairs[1]]
+    edge_after = jnp.stack([pair[:, -HALF:] for pair in pairs[-1:] + pairs[:-1]])
+    edge_before = jnp.stack([pair[:, :HALF] for pair in pairs[1:] + pairs[:1]])
+    edges = (shift(edge_after, 1), shift(edge_before, -1))
+    hidden_out, token = run(
         down_kernel,
         "down",
-        [order, (middle, None), (active, turned_spec)]
+        [order, (middle, None), turned_block(active, hidden_wide)]
         + [slabs(piece, hidden_wide) for piece in down_pieces],
         [(tokens, low, None)],
         [pltpu.VMEM(tokens, full)],
         matmul * FF,
-        after=heads_steps[:1],
-    )
+        after=(token,),
+    )
+    sums, token = blend(
+        "sums_seven",
+        core_sums(*heads_own_core)
+        + [[(heads_second_sums[1],), (heads_second_far,)]]
+        + near_sums(heads_odd_sums[0], heads_odd_near, half)
+        + line_sums(odd_parts[1], odd_parts[0], in_line),
+        (token,),
+    )
+    heads_own_sums, heads_odd_parts = sums[:4], [far_scatter(part) for part in sums[5:7]]
+    heads_own_far = flip(heads_own_sums[3], 2)
+    heads_second_near = (flip(sums[4], 2), flip(heads_second_sums[2], 4))
+    in_line = line_hop(sums[7], sums[8], 1)
+    heads_line = line_hop(heads_odd_parts[0], heads_odd_parts[1], 3)
+    grad_input, gain_one, token = run(
+        input_grad_kernel,
+        "input_grad",
+        [order, (hidden, None), (gains, None), (grad_middle, None)]
+        + [(own_queries, None), (own_pairs, None), (second_queries, None), (second_pairs, None)]
+        + [lead(odd_queries), lead(odd_pairs)]
+        + [lead(array, count=2) for array in edges]
+        + [slabs(piece, 3 * head_wide, count=2) for piece in heads_pieces],
+        [(tokens, full, None), ((8, D), full, None)],
+        [pltpu.VMEM((row_count, head_wide), low), pltpu.VMEM(tokens, full)],
+        3 * matmul * D,
+        after=(token,),
+        steps=half,
+    )
+    sums, token = blend(
+        "sums_eight",
+        near_sums(heads_second_sums[0], heads_second_near, 1)
+        + [[(heads_own_sums[2],), (heads_own_far,)]],
+        (token, *heads_line),
+    )
+    heads_second_part = far_scatter(sums[0])
+    heads_own_near = (flip(heads_own_sums[1], 2), flip(sums[1], 4))
+    heads_line = line_hop(*[add_low(heads_second_part, part) for part in heads_line], 2)
+    heads_line = line_hop(
+        add_low(heads_odd_parts[1], heads_line[0]), add_low(heads_odd_parts[0], heads_line[1]), 1
+    )
+    heads_own_part = far_scatter(line_end(heads_own_sums[0], heads_own_near).astype(low))
+    gain_sum = gain_scatter(tied(jnp.concatenate([gain_one[:1], gain_two[:1]]), token))
     if dp_size != PIECES:
         hidden_out, grad_input = to_relative(hidden_out, True), to_relative(grad_input, True)
 
-    down_sum = line_scatter(down_total).T
-    in_sum = line_scatter(in_total).T.reshape(w_in.shape)
-    gain_sum = heads_total[size - 1, head_rows : head_rows + 2].astype(full)
-    for mask in (1 << n for n in range(size.bit_length() - 1)):
-        gain_sum = gain_sum + lax.ppermute(
-            gain_sum, "tensor", [(n, n ^ mask) for n in range(size)]
-        )
-    heads_sum = line_scatter(heads_total[:, :head_rows]).T
+    down_sum = line_end(down_parts[0], down_line).T
+    in_sum = line_end(even_parts[0], in_line).T.reshape(w_in.shape)
+    heads_sum = line_end(heads_own_part, heads_line).T
     qkv_sum = jnp.concatenate(
         [
             heads_first(heads_sum[:, : 2 * head_wide]),

time: 548 us -> 565 us (1.031)
  waiting for transfers between devices: 156 us -> 95 us
  Pallas kernels: 202 us -> 252 us
  local copies, waits for them, and re-layouts: 17 us -> 45 us
  other arithmetic: 30.9 us -> 24.7 us
  between operations: 2.62 us -> 8.29 us
    ppermute x33 -> x48, waiting for transfers between devices: 115 us -> 56.7 us  [flip(): lax.ppermute(rows, 'dp', [(n, n ^ mask) for n in range(lax.axis_size('dp'...]
    pallas_call x0 -> x11, Pallas kernels: none -> 31.2 us  [the longest x9 28.7 us: blend(): pl.pallas_call(body, grid=(halves,), in_specs=specs + [pl.BlockSpec(memor...]
    pallas_call x10 -> x13, Pallas kernels: 202 us -> 221 us  [run(): pl.pallas_call(body, grid_spec=pltpu.PrefetchScalarGridSpec(num_scalar_pr...]
    unnamed x129 -> x157, local copies, waits for them, and re-layouts: 14.5 us -> 30.3 us
    ppermute x33 -> x48, starting transfers between devices: 24.8 us -> 35.4 us  [flip(): lax.ppermute(rows, 'dp', [(n, n ^ mask) for n in range(lax.axis_size('dp'...]
    convert_element_type x11 -> x0, other arithmetic: 9.54 us -> none  [the longest x3 6.05 us: scatter(): total = (own.astype(jnp.float32) + from_x.astype(jnp.float32) + from_y.as...]
    ppermute x4, waiting for transfers between devices: 8.95 us -> 0.01 us  [shift(): return lax.ppermute(rows, 'tensor', pairs)]
    select_n x0 -> x6, other arithmetic: none -> 7.2 us  [tied(): jnp.where(token[0, 0] == 0, values, 0.0 * values)]
  transfers between devices with their start and end apart: 75 -> 90, of which waited for: 19 -> 17; matrix products, arithmetic and copies ran while one was open for 7% -> 7% of each run, Pallas kernels for 28% -> 45%
where the time goes in v4:
time: 565 us; the launch traced here: 559 us
  Pallas kernels  252 us (45%)
  starting transfers between devices  134 us (24%)
  waiting for transfers between devices  95 us (17%)
  local copies, waits for them, and re-layouts  45 us (8%)
  other arithmetic  24.7 us (4%)
  between operations  8.29 us (1%)
    pallas_call x13, Pallas kernels, run(): pl.pallas_call(body, grid_spec=pltpu.PrefetchScalarGridSpec(num_scalar_pr...  221 us
    ppermute x48, waiting for transfers between devices, flip(): lax.ppermute(rows, 'dp', [(n, n ^ mask) for n in range(lax.axis_size('dp'...  56.7 us
    ppermute x9, starting transfers between devices, line_hop(): lax.ppermute(to_after, 'tensor', [(n, n + 1) for n in range(size - step)])  45 us
    ppermute x48, starting transfers between devices, flip(): lax.ppermute(rows, 'dp', [(n, n ^ mask) for n in range(lax.axis_size('dp'...  35.4 us
    ppermute x9, waiting for transfers between devices, line_gather(): lax.ppermute(from_after[-1], 'tensor', [(n, n - 1) for n in range(1, size...  31.5 us
    unnamed x157, local copies, waits for them, and re-layouts  30.3 us
    pallas_call x9, Pallas kernels, blend(): pl.pallas_call(body, grid=(halves,), in_specs=specs + [pl.BlockSpec(memor...  28.7 us
    ppermute x9, starting transfers between devices, line_gather(): lax.ppermute(from_before[-1], 'tensor', [(n, n + 1) for n in range(step -...  17.7 us
  transfers between devices with their start and end apart: 90, of which 17 were waited for; matrix products, arithmetic and copies ran while one was open for 7% of the time, Pallas kernels for 45%

profile of v4, /device:TPU:0, one launch (start us, length us, event | category | flops | bytes accessed | tf_op | source)
XLA Modules:
  0.0 559.3 jit_solution(14133905711363613472)
XLA Ops:
  2.6 4.9 collective-permute-start
  9.5 3.7 collective-permute-done
  13.9 3.5 collective-permute-done.1
  19.8 6.5 %collective-permute-done.2 = bf16[1040,128]{1,0:T(8,128)(2,1)S(1)} collective-permute-done((bf16[1040,128]{1,0:T(8,128)(2,1)S(1)}, bf16[1040,128]{1,0:T(8,128)(2,1)S(1)}, u32[]{:S(2)}, u32[]{:S(2)}) %collective-permute-start.2) | collective-permute-done | bytes 266272 | tf_op jit(solution)/shard_map/ppermute | solution.py:86
  27.7 6.9 %collective-permute-done.3 = bf16[1040,128]{1,0:T(8,128)(2,1)S(1)} collective-permute-done((bf16[1040,128]{1,0:T(8,128)(2,1)S(1)}, bf16[1040,128]{1,0:T(8,128)(2,1)S(1)}, u32[]{:S(2)}, u32[]{:S(2)}) %collective-permute-start.3) | collective-permute-done | bytes 266272 | tf_op jit(solution)/shard_map/ppermute | solution.py:86
  37.3 1.6 fusion.21
  39.1 1.6 collective-permute-start.7
  46.0 12.3 %collective-permute-done.6 = bf16[4160,128]{1,0:T(8,128)(2,1)} collective-permute-done((bf16[4160,128]{1,0:T(8,128)(2,1)}, bf16[4160,128]{1,0:T(8,128)(2,1)}, u32[]{:S(2)}, u32[]{:S(2)}) %collective-permute-start.6) | collective-permute-done | bytes 1064992 | tf_op jit(solution)/shard_map/ppermute | solution.py:124
  58.2 1.5 collective-permute-start.8
  63.7 8.8 %collective-permute-done.16 = bf16[1312,128]{1,0:T(8,128)(2,1)S(1)} collective-permute-done((bf16[1312,128]{1,0:T(8,128)(2,1)S(1)}, bf16[1312,128]{1,0:T(8,128)(2,1)S(1)}, u32[]{:S(2)}, u32[]{:S(2)}) %collective-permute-start.16) | collective-permute-done | bytes 335904 | tf_op jit(solution)/shard_map/ppermute | solution.py:86
  74.5 5.2 collective-permute-start.28
  81.8 2.4 collective-permute-done.8.refs_0_
  94.7 4.6 collective-permute-start.13
  103.2 5.9 %collective-permute-done.30 = bf16[656,128]{1,0:T(8,128)(2,1)} collective-permute-done((bf16[656,128]{1,0:T(8,128)(2,1)S(1)}, bf16[656,128]{1,0:T(8,128)(2,1)}, u32[]{:S(2)}, u32[]{:S(2)}) %collective-permute-start.30) | collective-permute-done | bytes 167968 | tf_op jit(solution)/shard_map/ppermute | solution.py:86
  113.9 1.6 collective-permute-start.22
  115.5 13.7 %heads.1 = (bf16[4,768,256]{2,1,0:T(8,128)(2,1)}, bf16[4,896,256]{2,1,0:T(8,128)(2,1)}, bf16[4,896,256]{2,1,0:T(8,128)(2,1)}, bf16[896,1024]{1,0:T(8,128)(2,1)}, s32[8,128]{1,0:T(8,128)S(1)}) custom-call(s32[8]{0:T(128)S(1)} %broadcast_xor_fusion.order_ref, bf16[768,1024]{1,0:T(8,128)(2,1)} %refs_0_.7, bf16[64,1024]{1,0:T(8,128)(2,1)S(1)} %collective-permute-done.13.refs_1_, ...), custom_call_target="tpu_custom_call" | custom-call | flops 483183820800 | bytes 18382848 | tf_op jit(solution)/shard_map/heads/pallas_call | solution.py:250
  130.3 14.5 %collective-permute-done.22.refs_5_ = bf16[5248,128]{1,0:T(8,128)(2,1)} collective-permute-done((bf16[5248,128]{1,0:T(8,128)(2,1)}, bf16[5248,128]{1,0:T(8,128)(2,1)}, u32[]{:S(2)}, u32[]{:S(2)}) %collective-permute-start.22) | collective-permute-done | bytes 1343520 | tf_op jit(solution)/shard_map/ppermute | solution.py:124
  144.8 2.5 multiply_select_fusion
  148.8 19.7 %attend.1 = (bf16[4,768,256]{2,1,0:T(8,128)(2,1)}, f32[4,768,128]{2,1,0:T(8,128)}, s32[8,128]{1,0:T(8,128)S(1)}) custom-call(s32[8]{0:T(128)S(1)} %broadcast_xor_fusion.order_ref, f32[6,128,256]{2,1,0:T(8,128)S(1)} %and_select_fusion.refs_0_, bf16[4,768,256]{2,1,0:T(8,128)(2,1)} %get-tuple-element.144.refs_1_.refs_5_, ...), custom_call_target="tpu_custom_call" | custom-call | flops 322122547200 | bytes 9175040 | tf_op jit(solution)/shard_map/attend/pallas_call | solution.py:250
  174.9 16.8 %collective-permute-done.34.refs_1_ = bf16[2624,128]{1,0:T(8,128)(2,1)} collective-permute-done((bf16[2624,128]{1,0:T(8,128)(2,1)}, bf16[2624,128]{1,0:T(8,128)(2,1)}, u32[]{:S(2)}, u32[]{:S(2)}) %collective-permute-start.34) | collective-permute-done | bytes 671776 | tf_op jit(solution)/shard_map/ppermute | solution.py:124
  192.2 10.6 %proj.1 = (f32[768,1024]{1,0:T(8,128)}, bf16[768,1024]{1,0:T(8,128)(2,1)}, s32[8,128]{1,0:T(8,128)S(1)}) custom-call(s32[8]{0:T(128)S(1)} %broadcast_xor_fusion.order_ref, bf16[768,1024]{1,0:T(8,128)(2,1)} %refs_0_.7, f32[8,1024]{1,0:T(8,128)S(1)} %copy-done.30, bf16[4,768,256]{2,1,0:T(8,128)(2,1)} %get-tuple-element.147.refs_2_.refs_8_, ...), custom_call_target="tpu_custom_call" | custom-call | flops 161061273600 | bytes 16416768 | tf_op jit(solution)/shard_map/proj/pallas_call | solution.py:250
  204.1 2.0 multiply_select_fusion.2
  206.6 1.5 collective-permute-start.36
  208.1 20.5 %gate.1 = (bf16[2624,768]{1,0:T(8,128)(2,1)}, bf16[2624,768]{1,0:T(8,128)(2,1)}, bf16[2624,768]{1,0:T(8,128)(2,1)}, s32[8,128]{1,0:T(8,128)S(1)}) custom-call(s32[8]{0:T(128)S(1)} %broadcast_xor_fusion.order_ref, bf16[768,1024]{1,0:T(8,128)(2,1)} %get-tuple-element.150.refs_0_.refs_1_, bf16[4,1312,128]{2,1,0:T(8,128)(2,1)} %pad_maximum_fusion.refs_1_.refs_7_, ...), custom_call_target="tpu_custom_call" | custom-call | flops 825439027200 | bytes 24412160 | tf_op jit(solution)/shard_map/gate/pallas_call | solution.py:250
  229.8 2.0 multiply_select_fusion.1.refs_2_
  231.9 9.4 %down_grad.1 = (bf16[4,656,128]{2,1,0:T(8,128)(2,1)S(1)}, bf16[4,656,128]{2,1,0:T(8,128)(2,1)S(1)}, bf16[4,656,128]{2,1,0:T(8,128)(2,1)S(1)}, bf16[4,656,128]{2,...) custom-call(s32[8]{0:T(128)S(1)} %broadcast_xor_fusion.order_ref, ...), custom_call_target="tpu_custom_call" | custom-call | flops 412719513600 | bytes 12550144 | tf_op jit(solution)/shard_map/down_grad/pallas_call | solution.py:250
  244.3 16.4 %in_grad_odd.1 = (bf16[2,1312,128]{2,1,0:T(8,128)(2,1)S(1)}, bf16[2,1312,128]{2,1,0:T(8,128)(2,1)S(1)}, bf16[2,1312,128]{2,1,0:T(8,128)(2,1)S(1)}, bf16[2,1312,1...) custom-call(s32[8]{0:T(128)S(1)} %broadcast_xor_fusion.order_ref, ...), custom_call_target="tpu_custom_call" | custom-call | flops 619079270400 | bytes 25985024 | tf_op jit(solution)/shard_map/in_grad_odd/pallas_call | solution.py:250
  263.4 3.6 sums_one.1
  270.2 16.6 %in_grad_even.1 = (bf16[2,1312,128]{2,1,0:T(8,128)(2,1)S(1)}, bf16[2,1312,128]{2,1,0:T(8,128)(2,1)S(1)}, bf16[2,1312,128]{2,1,0:T(8,128)(2,1)S(1)}, bf16[2,1312,...) custom-call(s32[8]{0:T(128)S(1)} %broadcast_xor_fusion.order_ref, ...), custom_call_target="tpu_custom_call" | custom-call | flops 619079270400 | bytes 25985024 | tf_op jit(solution)/shard_map/in_grad_even/pallas_call | solution.py:250
  290.1 4.1 sums_two.1
  296.4 1.5 collective-permute-start.47
  298.4 23.6 %middle_grad.1 = (f32[768,1024]{1,0:T(8,128)}, bf16[768,1024]{1,0:T(8,128)(2,1)}, f32[8,1024]{1,0:T(8,128)S(1)}, s32[8,128]{1,0:T(8,128)S(1)}) custom-call(s32[8]{0:T(128)S(1)} %broadcast_xor_fusion.order_ref, f32[768,1024]{1,0:T(8,128)} %get-tuple-element.149.refs_0_, bf16[768,1024]{1,0:T(8,128)(2,1)} %get-tuple-element.155.refs_0_.refs_1_, ...), custom_call_target="tpu_custom_call" | custom-call | flops 825439027200 | bytes 28311552 | tf_op jit(solution)/shard_map/middle_grad/pallas_call | solution.py:250
  322.6 5.9 %collective-permute-done.47 = bf16[2624,128]{1,0:T(8,128)(2,1)} collective-permute-done((bf16[2624,128]{1,0:T(8,128)(2,1)}, bf16[2624,128]{1,0:T(8,128)(2,1)}, u32[]{:S(2)}, u32[]{:S(2)}) %collective-permute-start.47) | collective-permute-done | bytes 671776 | tf_op jit(solution)/shard_map/ppermute | solution.py:124
  328.6 5.0 sums_three.1
  337.2 5.3 collective-permute-start.51
  342.6 1.6 collective-permute-start.56
  344.1 29.3 %attend_grad_odd.1 = (bf16[2,1024,128]{2,1,0:T(8,128)(2,1)S(1)}, bf16[2,1024,128]{2,1,0:T(8,128)(2,1)S(1)}, bf16[2,1024,128]{2,1,0:T(8,128)(2,1)}, bf16[2,1024,1...) custom-call(s32[8]{0:T(128)S(1)} %broadcast_xor_fusion.order_ref, ...), custom_call_target="tpu_custom_call" | custom-call | flops 966367641600 | bytes 28835840 | tf_op jit(solution)/shard_map/attend_grad_odd/pallas_call | solution.py:250
  373.4 2.0 slice_bitcast_fusion.1
  377.4 3.3 sums_four.1
  381.3 2.0 collective-permute-start.57
  383.2 9.5 %collective-permute-start.60 = (bf16[1312,128]{1,0:T(8,128)(2,1)}, bf16[1312,128]{1,0:T(8,128)(2,1)}, u32[]{:S(2)}, u32[]{:S(2)}) collective-permute-start(bf16[1312,128]{1,0:T(8,128)(2,1)} %get-tuple-element.222.refs_18_), channel_id=1, source_target_pairs={{0,1},{4,5},{8,9},{12,13},{16,17},{20,21},{24,25},{28,29}} | collective-permute-start | bytes 1007624 | tf_op jit(solution)/shard_map/ppermute | solution.py:104
  394.2 16.5 %attend_grad_second.1 = (bf16[1,1024,128]{2,1,0:T(8,128)(2,1)S(1)}, bf16[1,1024,128]{2,1,0:T(8,128)(2,1)S(1)}, bf16[1,1024,128]{2,1,0:T(8,128)(2,1)S(1)}, bf16[1...) custom-call(s32[8]{0:T(128)S(1)} %broadcast_xor_fusion.order_ref, ...), custom_call_target="tpu_custom_call" | custom-call | flops 483183820800 | bytes 25427968 | tf_op jit(solution)/shard_map/attend_grad_second/pallas_call | solution.py:250
  412.1 1.5 slice_bitcast_fusion.5
  413.7 4.3 sums_five.1
  420.3 6.2 %collective-permute-start.62 = (bf16[656,128]{1,0:T(8,128)(2,1)}, bf16[656,128]{1,0:T(8,128)(2,1)}, u32[]{:S(2)}, u32[]{:S(2)}) collective-permute-start(bf16[656,128]{1,0:T(8,128)(2,1)} %get-tuple-element.226), channel_id=1, source_target_pairs={{0,1},{1,2},{2,3},{4,5},{5,6},{6,7},{8,9},{9,10},{10,11},{12,13},{... | collective-permute-start | bytes 503816 | tf_op jit(solution)/shard_map/ppermute | solution.py:104
  428.4 16.7 %attend_grad_own.1 = (bf16[1,1024,128]{2,1,0:T(8,128)(2,1)S(1)}, bf16[1,1024,128]{2,1,0:T(8,128)(2,1)S(1)}, bf16[1,1024,128]{2,1,0:T(8,128)(2,1)S(1)}, bf16[1,10...) custom-call(s32[8]{0:T(128)S(1)} %broadcast_xor_fusion.order_ref, ...), custom_call_target="tpu_custom_call" | custom-call | flops 483183820800 | bytes 25427968 | tf_op jit(solution)/shard_map/attend_grad_own/pallas_call | solution.py:250
  448.0 3.2 sums_six.1
  452.4 4.6 collective-permute-start.70
  458.6 2.6 collective-permute-start.64
  463.4 1.6 collective-permute-start.69
  467.0 11.3 %down.1 = (bf16[768,1024]{1,0:T(8,128)(2,1)}, s32[8,128]{1,0:T(8,128)S(1)}) custom-call(s32[8]{0:T(128)S(1)} %broadcast_xor_fusion.order_ref, f32[768,1024]{1,0:T(8,128)} %get-tuple-element.149.refs_0_, bf16[2624,768]{1,0:T(8,128)(2,1)} %get-tuple-element.153.refs_1_, bf16[4,656,128]{2,1,0:T(8,128)(2,1)} %pad_maximum_fusion.2.refs_4_.refs_2_, ...), custom_call_target="tpu_custom_call" | custom-call | flops 412719513600 | bytes 14123008 | tf_op jit(solution)/shard_map/down/pallas_call | solution.py:250
  478.4 1.5 collective-permute-start.74
  479.9 3.8 sums_seven.1
  483.7 1.6 collective-permute-start.73
  485.8 4.9 collective-permute-start.76
  492.0 16.6 %input_grad.1 = (f32[768,1024]{1,0:T(8,128)}, f32[8,1024]{1,0:T(8,128)S(1)}, s32[8,128]{1,0:T(8,128)S(1)}) custom-call(s32[8]{0:T(128)S(1)} %broadcast_xor_fusion.order_ref, bf16[768,1024]{1,0:T(8,128)(2,1)} %refs_0_.7, f32[8,1024]{1,0:T(8,128)S(1)} %copy-done.31, f32[768,1024]{1,0:T(8,128)} %get-tuple-element.230.refs_2_, ...), custom_call_target="tpu_custom_call" | custom-call | flops 483183820800 | bytes 22216704 | tf_op jit(solution)/shard_map/input_grad/pallas_call | solution.py:250
  513.2 3.0 collective-permute-done.86
  519.8 2.4 multiply_subtract_fusion.2
  525.0 4.6 collective-permute-start.83
  529.6 4.2 collective-permute-start.89
  535.8 3.3 collective-permute-start.79
  544.1 4.6 collective-permute-start.80
  548.7 1.6 multiply_subtract_fusion
  550.3 2.2 collective-permute-done.80
  (383 shorter events, 114.3 us)
Async XLA Ops:
  35.8 22.5 %collective-permute-start.6 = (bf16[4160,128]{1,0:T(8,128)(2,1)}, bf16[4160,128]{1,0:T(8,128)(2,1)}, u32[]{:S(2)}, u32[]{:S(2)}) collective-permute-start(bf16[4160,128]{1,0:T(8,128)(2,1)} %bitcast.10.refs_0_), channel_id=1, source_target_pairs={{0,8},{4,12},{8,0},{12,4},{16,24},{20,28},{24,16},{28,20},{1,9},{5... | collective-permute-start | bytes 3194888 | tf_op jit(solution)/shard_map/ppermute | solution.py:124
  39.1 40.6 %collective-permute-start.7 = (bf16[4160,128]{1,0:T(8,128)(2,1)}, bf16[4160,128]{1,0:T(8,128)(2,1)}, u32[]{:S(2)}, u32[]{:S(2)}) collective-permute-start(bf16[4160,128]{1,0:T(8,128)(2,1)} %bitcast.10.refs_0_), channel_id=1, source_target_pairs={{0,16},{4,20},{8,24},{12,28},{16,0},{20,4},{24,8},{28,12},{1,17},{... | collective-permute-start | bytes 3194888 | tf_op jit(solution)/shard_map/ppermute | solution.py:124
  44.5 17.8 %collective-permute-start.15 = (bf16[1312,128]{1,0:T(8,128)(2,1)S(1)}, bf16[1312,128]{1,0:T(8,128)(2,1)S(1)}, u32[]{:S(2)}, u32[]{:S(2)}) collective-permute-start(bf16[1312,128]{1,0:T(8,128)(2,1)S(1)} %multiply_select_fusion.3), channel_id=1, source_target_pairs={{0,1},{1,2},{2,3},{4,5},{5,6},{6,7},{8,9},{9,10},{10,11},{12,13},{... | collective-permute-start | bytes 1007624 | tf_op jit(solution)/shard_map/ppermute | solution.py:83
  58.2 26.0 %collective-permute-start.8 = (bf16[4160,128]{1,0:T(8,128)(2,1)}, bf16[4160,128]{1,0:T(8,128)(2,1)}, u32[]{:S(2)}, u32[]{:S(2)}) collective-permute-start(bf16[4160,128]{1,0:T(8,128)(2,1)} %collective-permute-done.6), channel_id=1, source_target_pairs={{0,16},{4,20},{8,24},{12,28},{16,0},{20,4},{24,8},{28,12},{1,17},{... | collective-permute-start | bytes 3194888 | tf_op jit(solution)/shard_map/ppermute | solution.py:124
  60.2 29.6 %collective-permute-start.9 = (bf16[4160,128]{1,0:T(8,128)(2,1)}, bf16[4160,128]{1,0:T(8,128)(2,1)}, u32[]{:S(2)}, u32[]{:S(2)}) collective-permute-start(bf16[4160,128]{1,0:T(8,128)(2,1)} %bitcast.10.refs_0_), channel_id=1, source_target_pairs={{0,4},{4,0},{8,12},{12,8},{16,20},{20,16},{24,28},{28,24},{1,5},{5... | collective-permute-start | bytes 3194888 | tf_op jit(solution)/shard_map/ppermute | solution.py:124
  72.5 15.5 %collective-permute-start.17 = (bf16[1312,128]{1,0:T(8,128)(2,1)S(1)}, bf16[1312,128]{1,0:T(8,128)(2,1)S(1)}, u32[]{:S(2)}, u32[]{:S(2)}) collective-permute-start(bf16[1312,128]{1,0:T(8,128)(2,1)S(1)} %collective-permute-done.16), channel_id=1, source_target_pairs={{1,0},{2,1},{5,4},{6,5},{9,8},{10,9},{13,12},{14,13},{17,16},{18,1... | collective-permute-start | bytes 1007624 | tf_op jit(solution)/shard_map/ppermute | solution.py:86
  74.5 20.2 %collective-permute-start.28 = (bf16[656,128]{1,0:T(8,128)(2,1)}, bf16[656,128]{1,0:T(8,128)(2,1)}, u32[]{:S(2)}, u32[]{:S(2)}) collective-permute-start(bf16[656,128]{1,0:T(8,128)(2,1)} %multiply_select_fusion.4), channel_id=1, source_target_pairs={{0,1},{1,2},{2,3},{4,5},{5,6},{6,7},{8,9},{9,10},{10,11},{12,13},{... | collective-permute-start | bytes 503816 | tf_op jit(solution)/shard_map/ppermute | solution.py:83
  88.0 12.6 %collective-permute-start.11 = (bf16[4160,128]{1,0:T(8,128)(2,1)}, bf16[4160,128]{1,0:T(8,128)(2,1)S(1)}, u32[]{:S(2)}, u32[]{:S(2)}) collective-permute-start(bf16[4160,128]{1,0:T(8,128)(2,1)} %collective-permute-done.7), channel_id=1, source_target_pairs={{0,4},{4,0},{8,12},{12,8},{16,20},{20,16},{24,28},{28,24},{1,5},{5... | collective-permute-start | bytes 3194888 | tf_op jit(solution)/shard_map/ppermute | solution.py:124
  91.9 18.6 %collective-permute-start.18 = (bf16[1312,128]{1,0:T(8,128)(2,1)S(1)}, bf16[1312,128]{1,0:T(8,128)(2,1)S(1)}, u32[]{:S(2)}, u32[]{:S(2)}) collective-permute-start(bf16[1312,128]{1,0:T(8,128)(2,1)S(1)} %collective-permute-done.17), channel_id=1, source_target_pairs={{1,0},{5,4},{9,8},{13,12},{17,16},{21,20},{25,24},{29,28}} | collective-permute-start | bytes 1007624 | tf_op jit(solution)/shard_map/ppermute | solution.py:86
  93.2 20.0 %collective-permute-start.12 = (bf16[4160,128]{1,0:T(8,128)(2,1)}, bf16[4160,128]{1,0:T(8,128)(2,1)S(1)}, u32[]{:S(2)}, u32[]{:S(2)}) collective-permute-start(bf16[4160,128]{1,0:T(8,128)(2,1)} %collective-permute-done.8.refs_0_), channel_id=1, source_target_pairs={{0,4},{4,0},{8,12},{12,8},{16,20},{20,16},{24,28},{28,24},{1,5},{5... | collective-permute-start | bytes 3194888 | tf_op jit(solution)/shard_map/ppermute | solution.py:124
  94.7 19.2 %collective-permute-start.13 = (bf16[64,1024]{1,0:T(8,128)(2,1)S(1)}, bf16[64,1024]{1,0:T(8,128)(2,1)S(1)}, u32[]{:S(2)}, u32[]{:S(2)}) collective-permute-start(bf16[64,1024]{1,0:T(8,128)(2,1)S(1)} %copy-done.57), channel_id=1, source_target_pairs={{0,1},{1,2},{2,3},{4,5},{5,6},{6,7},{8,9},{9,10},{10,11},{12,13},{... | collective-permute-start | bytes 393224 | tf_op jit(solution)/shard_map/ppermute | solution.py:180
  101.9 13.5 %collective-permute-start.14 = (bf16[64,1024]{1,0:T(8,128)(2,1)S(1)}, bf16[64,1024]{1,0:T(8,128)(2,1)S(1)}, u32[]{:S(2)}, u32[]{:S(2)}) collective-permute-start(bf16[64,1024]{1,0:T(8,128)(2,1)S(1)} %get-tuple-element.339), channel_id=1, source_target_pairs={{1,0},{2,1},{3,2},{5,4},{6,5},{7,6},{9,8},{10,9},{11,10},{13,12},{... | collective-permute-start | bytes 393224 | tf_op jit(solution)/shard_map/ppermute | solution.py:180
  109.1 61.5 %collective-permute-start.33 = (bf16[656,128]{1,0:T(8,128)(2,1)}, bf16[656,128]{1,0:T(8,128)(2,1)}, u32[]{:S(2)}, u32[]{:S(2)}) collective-permute-start(bf16[656,128]{1,0:T(8,128)(2,1)} %collective-permute-done.32), channel_id=1, source_target_pairs={{2,3},{6,7},{10,11},{14,15},{18,19},{22,23},{26,27},{30,31}} | collective-permute-start | bytes 503816 | tf_op jit(solution)/shard_map/ppermute | solution.py:83
  110.4 60.3 %collective-permute-start.31 = (bf16[656,128]{1,0:T(8,128)(2,1)}, bf16[656,128]{1,0:T(8,128)(2,1)}, u32[]{:S(2)}, u32[]{:S(2)}) collective-permute-start(bf16[656,128]{1,0:T(8,128)(2,1)} %collective-permute-done.30), channel_id=1, source_target_pairs={{1,0},{5,4},{9,8},{13,12},{17,16},{21,20},{25,24},{29,28}} | collective-permute-start | bytes 503816 | tf_op jit(solution)/shard_map/ppermute | solution.py:86
  113.3 35.6 %collective-permute-start.21 = (bf16[5248,128]{1,0:T(8,128)(2,1)}, bf16[5248,128]{1,0:T(8,128)(2,1)}, u32[]{:S(2)}, u32[]{:S(2)}) collective-permute-start(bf16[5248,128]{1,0:T(8,128)(2,1)} %bitcast.49.refs_14_), channel_id=1, source_target_pairs={{0,8},{4,12},{8,0},{12,4},{16,24},{20,28},{24,16},{28,20},{1,9},{5... | collective-permute-start | bytes 4030472 | tf_op jit(solution)/shard_map/ppermute | solution.py:124
  113.9 31.0 %collective-permute-start.22 = (bf16[5248,128]{1,0:T(8,128)(2,1)}, bf16[5248,128]{1,0:T(8,128)(2,1)}, u32[]{:S(2)}, u32[]{:S(2)}) collective-permute-start(bf16[5248,128]{1,0:T(8,128)(2,1)} %bitcast.49.refs_14_), channel_id=1, source_target_pairs={{0,16},{4,20},{8,24},{12,28},{16,0},{20,4},{24,8},{28,12},{1,17},{... | collective-permute-start | bytes 4030472 | tf_op jit(solution)/shard_map/ppermute | solution.py:124
  147.3 44.4 %collective-permute-start.23 = (bf16[5248,128]{1,0:T(8,128)(2,1)}, bf16[5248,128]{1,0:T(8,128)(2,1)}, u32[]{:S(2)}, u32[]{:S(2)}) collective-permute-start(bf16[5248,128]{1,0:T(8,128)(2,1)} %multiply_select_fusion), channel_id=1, source_target_pairs={{0,8},{4,12},{8,0},{12,4},{16,24},{20,28},{24,16},{28,20},{1,9},{5... | collective-permute-start | bytes 4030472 | tf_op jit(solution)/shard_map/ppermute | solution.py:124
  172.6 19.1 %collective-permute-start.34 = (bf16[2624,128]{1,0:T(8,128)(2,1)}, bf16[2624,128]{1,0:T(8,128)(2,1)}, u32[]{:S(2)}, u32[]{:S(2)}) collective-permute-start(bf16[2624,128]{1,0:T(8,128)(2,1)} %bitcast.64), channel_id=1, source_target_pairs={{0,8},{4,12},{8,0},{12,4},{16,24},{20,28},{24,16},{28,20},{1,9},{5... | collective-permute-start | bytes 2015240 | tf_op jit(solution)/shard_map/ppermute | solution.py:124
  173.1 32.9 %collective-permute-start.24 = (bf16[5248,128]{1,0:T(8,128)(2,1)}, bf16[5248,128]{1,0:T(8,128)(2,1)}, u32[]{:S(2)}, u32[]{:S(2)}) collective-permute-start(bf16[5248,128]{1,0:T(8,128)(2,1)} %bitcast.49.refs_14_), channel_id=1, source_target_pairs={{0,4},{4,0},{8,12},{12,8},{16,20},{20,16},{24,28},{28,24},{1,5},{5... | collective-permute-start | bytes 4030472 | tf_op jit(solution)/shard_map/ppermute | solution.py:124
  173.1 29.6 %collective-permute-start.35 = (bf16[2624,128]{1,0:T(8,128)(2,1)}, bf16[2624,128]{1,0:T(8,128)(2,1)}, u32[]{:S(2)}, u32[]{:S(2)}) collective-permute-start(bf16[2624,128]{1,0:T(8,128)(2,1)} %bitcast.64), channel_id=1, source_target_pairs={{0,16},{4,20},{8,24},{12,28},{16,0},{20,4},{24,8},{28,12},{1,17},{... | collective-permute-start | bytes 2015240 | tf_op jit(solution)/shard_map/ppermute | solution.py:124
  174.7 31.9 %collective-permute-start.25 = (bf16[5248,128]{1,0:T(8,128)(2,1)}, bf16[5248,128]{1,0:T(8,128)(2,1)}, u32[]{:S(2)}, u32[]{:S(2)}) collective-permute-start(bf16[5248,128]{1,0:T(8,128)(2,1)} %collective-permute-done.21.refs_4_), channel_id=1, source_target_pairs={{0,4},{4,0},{8,12},{12,8},{16,20},{20,16},{24,28},{28,24},{1,5},{5... | collective-permute-start | bytes 4030472 | tf_op jit(solution)/shard_map/ppermute | solution.py:124
  191.7 14.9 %collective-permute-start.26 = (bf16[5248,128]{1,0:T(8,128)(2,1)}, bf16[5248,128]{1,0:T(8,128)(2,1)}, u32[]{:S(2)}, u32[]{:S(2)}) collective-permute-start(bf16[5248,128]{1,0:T(8,128)(2,1)} %collective-permute-done.22.refs_5_), channel_id=1, source_target_pairs={{0,4},{4,0},{8,12},{12,8},{16,20},{20,16},{24,28},{28,24},{1,5},{5... | collective-permute-start | bytes 4030472 | tf_op jit(solution)/shard_map/ppermute | solution.py:124
  191.7 16.4 %collective-permute-start.27 = (bf16[5248,128]{1,0:T(8,128)(2,1)}, bf16[5248,128]{1,0:T(8,128)(2,1)}, u32[]{:S(2)}, u32[]{:S(2)}) collective-permute-start(bf16[5248,128]{1,0:T(8,128)(2,1)} %collective-permute-done.23.refs_11_), channel_id=1, source_target_pairs={{0,4},{4,0},{8,12},{12,8},{16,20},{20,16},{24,28},{28,24},{1,5},{5... | collective-permute-start | bytes 4030472 | tf_op jit(solution)/shard_map/ppermute | solution.py:124
  202.8 41.5 %collective-permute-start.37 = (bf16[2624,128]{1,0:T(8,128)(2,1)}, bf16[2624,128]{1,0:T(8,128)(2,1)}, u32[]{:S(2)}, u32[]{:S(2)}) collective-permute-start(bf16[2624,128]{1,0:T(8,128)(2,1)} %bitcast.64), channel_id=1, source_target_pairs={{0,4},{4,0},{8,12},{12,8},{16,20},{20,16},{24,28},{28,24},{1,5},{5... | collective-permute-start | bytes 2015240 | tf_op jit(solution)/shard_map/ppermute | solution.py:124
  206.0 38.2 %collective-permute-start.38 = (bf16[2624,128]{1,0:T(8,128)(2,1)}, bf16[2624,128]{1,0:T(8,128)(2,1)}, u32[]{:S(2)}, u32[]{:S(2)}) collective-permute-start(bf16[2624,128]{1,0:T(8,128)(2,1)} %collective-permute-done.34.refs_1_), channel_id=1, source_target_pairs={{0,4},{4,0},{8,12},{12,8},{16,20},{20,16},{24,28},{28,24},{1,5},{5... | collective-permute-start | bytes 2015240 | tf_op jit(solution)/shard_map/ppermute | solution.py:124
  206.5 37.8 %collective-permute-start.39 = (bf16[2624,128]{1,0:T(8,128)(2,1)}, bf16[2624,128]{1,0:T(8,128)(2,1)}, u32[]{:S(2)}, u32[]{:S(2)}) collective-permute-start(bf16[2624,128]{1,0:T(8,128)(2,1)} %collective-permute-done.35.refs_2_), channel_id=1, source_target_pairs={{0,4},{4,0},{8,12},{12,8},{16,20},{20,16},{24,28},{28,24},{1,5},{5... | collective-permute-start | bytes 2015240 | tf_op jit(solution)/shard_map/ppermute | solution.py:124
  206.6 23.2 %collective-permute-start.36 = (bf16[2624,128]{1,0:T(8,128)(2,1)}, bf16[2624,128]{1,0:T(8,128)(2,1)}, u32[]{:S(2)}, u32[]{:S(2)}) collective-permute-start(bf16[2624,128]{1,0:T(8,128)(2,1)} %multiply_select_fusion.2), channel_id=1, source_target_pairs={{0,16},{4,20},{8,24},{12,28},{16,0},{20,4},{24,8},{28,12},{1,17},{... | collective-permute-start | bytes 2015240 | tf_op jit(solution)/shard_map/ppermute | solution.py:124
  231.8 12.5 %collective-permute-start.40 = (bf16[2624,128]{1,0:T(8,128)(2,1)}, bf16[2624,128]{1,0:T(8,128)(2,1)}, u32[]{:S(2)}, u32[]{:S(2)}) collective-permute-start(bf16[2624,128]{1,0:T(8,128)(2,1)} %multiply_select_fusion.1.refs_2_), channel_id=1, source_target_pairs={{0,4},{4,0},{8,12},{12,8},{16,20},{20,16},{24,28},{28,24},{1,5},{5... | collective-permute-start | bytes 2015240 | tf_op jit(solution)/shard_map/ppermute | solution.py:124
  243.9 19.5 %collective-permute-start.41 = (bf16[4,2624,128]{2,1,0:T(8,128)(2,1)}, bf16[4,2624,128]{2,1,0:T(8,128)(2,1)}, u32[]{:S(2)}, u32[]{:S(2)}) collective-permute-start(bf16[4,2624,128]{2,1,0:T(8,128)(2,1)} %bitcast.275), channel_id=1, source_target_pairs={{0,4},{4,0},{8,12},{12,8},{16,20},{20,16},{24,28},{28,24},{1,5},{5... | collective-permute-start | bytes 8060936 | tf_op jit(solution)/shard_map/ppermute | solution.py:124
  263.3 26.8 %collective-permute-start.42 = (bf16[4,2624,128]{2,1,0:T(8,128)(2,1)}, bf16[4,2624,128]{2,1,0:T(8,128)(2,1)}, u32[]{:S(2)}, u32[]{:S(2)}) collective-permute-start(bf16[4,2624,128]{2,1,0:T(8,128)(2,1)} %bitcast.274), channel_id=1, source_target_pairs={{0,4},{4,0},{8,12},{12,8},{16,20},{20,16},{24,28},{28,24},{1,5},{5... | collective-permute-start | bytes 8060936 | tf_op jit(solution)/shard_map/ppermute | solution.py:124
  268.7 21.4 %collective-permute-start.43 = (bf16[2624,128]{1,0:T(8,128)(2,1)}, bf16[2624,128]{1,0:T(8,128)(2,1)}, u32[]{:S(2)}, u32[]{:S(2)}) collective-permute-start(bf16[2624,128]{1,0:T(8,128)(2,1)} %get-tuple-element.175), channel_id=1, source_target_pairs={{0,8},{4,12},{8,0},{12,4},{16,24},{20,28},{24,16},{28,20},{1,9},{5... | collective-permute-start | bytes 2015240 | tf_op jit(solution)/shard_map/ppermute | solution.py:124
  289.5 39.1 %collective-permute-start.44 = (bf16[4,2624,128]{2,1,0:T(8,128)(2,1)}, bf16[4,2624,128]{2,1,0:T(8,128)(2,1)}, u32[]{:S(2)}, u32[]{:S(2)}) collective-permute-start(bf16[4,2624,128]{2,1,0:T(8,128)(2,1)} %bitcast.273), channel_id=1, source_target_pairs={{0,4},{4,0},{8,12},{12,8},{16,20},{20,16},{24,28},{28,24},{1,5},{5... | collective-permute-start | bytes 8060936 | tf_op jit(solution)/shard_map/ppermute | solution.py:124
  289.5 33.1 %collective-permute-start.46 = (bf16[2624,128]{1,0:T(8,128)(2,1)}, bf16[2624,128]{1,0:T(8,128)(2,1)}, u32[]{:S(2)}, u32[]{:S(2)}) collective-permute-start(bf16[2624,128]{1,0:T(8,128)(2,1)} %get-tuple-element.189), channel_id=1, source_target_pairs={{0,8},{4,12},{8,0},{12,4},{16,24},{20,28},{24,16},{28,20},{1,9},{5... | collective-permute-start | bytes 2015240 | tf_op jit(solution)/shard_map/ppermute | solution.py:124
  295.9 26.7 %collective-permute-start.45 = (bf16[2624,128]{1,0:T(8,128)(2,1)}, bf16[2624,128]{1,0:T(8,128)(2,1)}, u32[]{:S(2)}, u32[]{:S(2)}) collective-permute-start(bf16[2624,128]{1,0:T(8,128)(2,1)} %get-tuple-element.187), channel_id=1, source_target_pairs={{0,16},{4,20},{8,24},{12,28},{16,0},{20,4},{24,8},{28,12},{1,17},{... | collective-permute-start | bytes 2015240 | tf_op jit(solution)/shard_map/ppermute | solution.py:124
  296.4 32.2 %collective-permute-start.47 = (bf16[2624,128]{1,0:T(8,128)(2,1)}, bf16[2624,128]{1,0:T(8,128)(2,1)}, u32[]{:S(2)}, u32[]{:S(2)}) collective-permute-start(bf16[2624,128]{1,0:T(8,128)(2,1)} %get-tuple-element.190), channel_id=1, source_target_pairs={{0,16},{4,20},{8,24},{12,28},{16,0},{20,4},{24,8},{28,12},{1,17},{... | collective-permute-start | bytes 2015240 | tf_op jit(solution)/shard_map/ppermute | solution.py:124
  297.9 78.1 %collective-permute-start.50 = (bf16[2624,128]{1,0:T(8,128)(2,1)}, bf16[2624,128]{1,0:T(8,128)(2,1)}, u32[]{:S(2)}, u32[]{:S(2)}) collective-permute-start(bf16[2624,128]{1,0:T(8,128)(2,1)} %get-tuple-element.196), channel_id=1, source_target_pairs={{0,16},{4,20},{8,24},{12,28},{16,0},{20,4},{24,8},{28,12},{1,17},{... | collective-permute-start | bytes 2015240 | tf_op jit(solution)/shard_map/ppermute | solution.py:124
  335.3 42.1 %collective-permute-start.48 = (bf16[2624,128]{1,0:T(8,128)(2,1)}, bf16[2624,128]{1,0:T(8,128)(2,1)}, u32[]{:S(2)}, u32[]{:S(2)}) collective-permute-start(bf16[2624,128]{1,0:T(8,128)(2,1)} %get-tuple-element.193), channel_id=1, source_target_pairs={{0,16},{4,20},{8,24},{12,28},{16,0},{20,4},{24,8},{28,12},{1,17},{... | collective-permute-start | bytes 2015240 | tf_op jit(solution)/shard_map/ppermute | solution.py:124
  335.8 41.7 %collective-permute-start.49 = (bf16[2624,128]{1,0:T(8,128)(2,1)}, bf16[2624,128]{1,0:T(8,128)(2,1)}, u32[]{:S(2)}, u32[]{:S(2)}) collective-permute-start(bf16[2624,128]{1,0:T(8,128)(2,1)} %get-tuple-element.195), channel_id=1, source_target_pairs={{0,8},{4,12},{8,0},{12,4},{16,24},{20,28},{24,16},{28,20},{1,9},{5... | collective-permute-start | bytes 2015240 | tf_op jit(solution)/shard_map/ppermute | solution.py:124
  337.2 40.1 %collective-permute-start.51 = (bf16[656,128]{1,0:T(8,128)(2,1)}, bf16[656,128]{1,0:T(8,128)(2,1)}, u32[]{:S(2)}, u32[]{:S(2)}) collective-permute-start(bf16[656,128]{1,0:T(8,128)(2,1)} %get-tuple-element.198.refs_16_), channel_id=1, source_target_pairs={{0,1},{4,5},{8,9},{12,13},{16,17},{20,21},{24,25},{28,29}} | collective-permute-start | bytes 503816 | tf_op jit(solution)/shard_map/ppermute | solution.py:104
  342.6 50.2 %collective-permute-start.56 = (bf16[2624,128]{1,0:T(8,128)(2,1)}, bf16[2624,128]{1,0:T(8,128)(2,1)}, u32[]{:S(2)}, u32[]{:S(2)}) collective-permute-start(bf16[2624,128]{1,0:T(8,128)(2,1)} %get-tuple-element.215), channel_id=1, source_target_pairs={{0,16},{4,20},{8,24},{12,28},{16,0},{20,4},{24,8},{28,12},{1,17},{... | collective-permute-start | bytes 2015240 | tf_op jit(solution)/shard_map/ppermute | solution.py:124
  377.4 36.3 %collective-permute-start.54 = (bf16[4,2048,128]{2,1,0:T(8,128)(2,1)}, bf16[4,2048,128]{2,1,0:T(8,128)(2,1)}, u32[]{:S(2)}, u32[]{:S(2)}) collective-permute-start(bf16[4,2048,128]{2,1,0:T(8,128)(2,1)} %bitcast.101), channel_id=1, source_target_pairs={{0,4},{4,0},{8,12},{12,8},{16,20},{20,16},{24,28},{28,24},{1,5},{5... | collective-permute-start | bytes 6291464 | tf_op jit(solution)/shard_map/ppermute | solution.py:124
  380.7 33.0 %collective-permute-start.55 = (bf16[2624,128]{1,0:T(8,128)(2,1)}, bf16[2624,128]{1,0:T(8,128)(2,1)}, u32[]{:S(2)}, u32[]{:S(2)}) collective-permute-start(bf16[2624,128]{1,0:T(8,128)(2,1)} %get-tuple-element.214), channel_id=1, source_target_pairs={{0,8},{4,12},{8,0},{12,4},{16,24},{20,28},{24,16},{28,20},{1,9},{5... | collective-permute-start | bytes 2015240 | tf_op jit(solution)/shard_map/ppermute | solution.py:124
  381.3 30.2 %collective-permute-start.57 = (bf16[656,128]{1,0:T(8,128)(2,1)}, bf16[656,128]{1,0:T(8,128)(2,1)}, u32[]{:S(2)}, u32[]{:S(2)}) collective-permute-start(bf16[656,128]{1,0:T(8,128)(2,1)} %get-tuple-element.216), channel_id=1, source_target_pairs={{0,1},{1,2},{4,5},{5,6},{8,9},{9,10},{12,13},{13,14},{16,17},{17,1... | collective-permute-start | bytes 503816 | tf_op jit(solution)/shard_map/ppermute | solution.py:104
  383.2 43.3 %collective-permute-start.60 = (bf16[1312,128]{1,0:T(8,128)(2,1)}, bf16[1312,128]{1,0:T(8,128)(2,1)}, u32[]{:S(2)}, u32[]{:S(2)}) collective-permute-start(bf16[1312,128]{1,0:T(8,128)(2,1)} %get-tuple-element.222.refs_18_), channel_id=1, source_target_pairs={{0,1},{4,5},{8,9},{12,13},{16,17},{20,21},{24,25},{28,29}} | collective-permute-start | bytes 1007624 | tf_op jit(solution)/shard_map/ppermute | solution.py:104
  392.8 35.0 %collective-permute-start.61 = (bf16[1312,128]{1,0:T(8,128)(2,1)}, bf16[1312,128]{1,0:T(8,128)(2,1)}, u32[]{:S(2)}, u32[]{:S(2)}) collective-permute-start(bf16[1312,128]{1,0:T(8,128)(2,1)} %get-tuple-element.223.refs_16_), channel_id=1, source_target_pairs={{3,2},{7,6},{11,10},{15,14},{19,18},{23,22},{27,26},{31,30}} | collective-permute-start | bytes 1007624 | tf_op jit(solution)/shard_map/ppermute | solution.py:105
  413.7 34.3 %collective-permute-start.53 = (bf16[4,1024,128]{2,1,0:T(8,128)(2,1)}, bf16[4,1024,128]{2,1,0:T(8,128)(2,1)}, u32[]{:S(2)}, u32[]{:S(2)}) collective-permute-start(bf16[4,1024,128]{2,1,0:T(8,128)(2,1)} %bitcast.276), channel_id=1, source_target_pairs={{0,4},{4,0},{8,12},{12,8},{16,20},{20,16},{24,28},{28,24},{1,5},{5... | collective-permute-start | bytes 3145736 | tf_op jit(solution)/shard_map/ppermute | solution.py:124
  418.8 29.2 %collective-permute-start.59 = (bf16[2048,128]{1,0:T(8,128)(2,1)}, bf16[2048,128]{1,0:T(8,128)(2,1)}, u32[]{:S(2)}, u32[]{:S(2)}) collective-permute-start(bf16[2048,128]{1,0:T(8,128)(2,1)} %get-tuple-element.220), channel_id=1, source_target_pairs={{0,8},{4,12},{8,0},{12,4},{16,24},{20,28},{24,16},{28,20},{1,9},{5... | collective-permute-start | bytes 1572872 | tf_op jit(solution)/shard_map/ppermute | solution.py:124
  420.3 27.7 %collective-permute-start.62 = (bf16[656,128]{1,0:T(8,128)(2,1)}, bf16[656,128]{1,0:T(8,128)(2,1)}, u32[]{:S(2)}, u32[]{:S(2)}) collective-permute-start(bf16[656,128]{1,0:T(8,128)(2,1)} %get-tuple-element.226), channel_id=1, source_target_pairs={{0,1},{1,2},{2,3},{4,5},{5,6},{6,7},{8,9},{9,10},{10,11},{12,13},{... | collective-permute-start | bytes 503816 | tf_op jit(solution)/shard_map/ppermute | solution.py:104
  426.5 21.4 %collective-permute-start.63 = (bf16[656,128]{1,0:T(8,128)(2,1)}, bf16[656,128]{1,0:T(8,128)(2,1)}, u32[]{:S(2)}, u32[]{:S(2)}) collective-permute-start(bf16[656,128]{1,0:T(8,128)(2,1)} %get-tuple-element.227), channel_id=1, source_target_pairs={{1,0},{2,1},{3,2},{5,4},{6,5},{7,6},{9,8},{10,9},{11,10},{13,12},{... | collective-permute-start | bytes 503816 | tf_op jit(solution)/shard_map/ppermute | solution.py:105
  427.8 35.5 %collective-permute-start.68 = (bf16[2048,128]{1,0:T(8,128)(2,1)}, bf16[2048,128]{1,0:T(8,128)(2,1)}, u32[]{:S(2)}, u32[]{:S(2)}) collective-permute-start(bf16[2048,128]{1,0:T(8,128)(2,1)} %get-tuple-element.245), channel_id=1, source_target_pairs={{0,8},{4,12},{8,0},{12,4},{16,24},{20,28},{24,16},{28,20},{1,9},{5... | collective-permute-start | bytes 1572872 | tf_op jit(solution)/shard_map/ppermute | solution.py:124
  452.4 13.2 %collective-permute-start.70 = (bf16[1312,128]{1,0:T(8,128)(2,1)}, bf16[1312,128]{1,0:T(8,128)(2,1)S(1)}, u32[]{:S(2)}, u32[]{:S(2)}) collective-permute-start(bf16[1312,128]{1,0:T(8,128)(2,1)} %get-tuple-element.247), channel_id=1, source_target_pairs={{0,1},{1,2},{4,5},{5,6},{8,9},{9,10},{12,13},{13,14},{16,17},{17,1... | collective-permute-start | bytes 1007624 | tf_op jit(solution)/shard_map/ppermute | solution.py:104
  458.6 27.1 %collective-permute-start.64 = (bf16[4,2,64,256]{3,2,1,0:T(8,128)(2,1)}, bf16[4,2,64,256]{3,2,1,0:T(8,128)(2,1)}, u32[]{:S(2)}, u32[]{:S(2)}) collective-permute-start(bf16[4,2,64,256]{3,2,1,0:T(8,128)(2,1)} %pad_maximum_fusion.4), channel_id=1, source_target_pairs={{0,1},{1,2},{2,3},{4,5},{5,6},{6,7},{8,9},{9,10},{10,11},{12,13},{... | collective-permute-start | bytes 786440 | tf_op jit(solution)/shard_map/ppermute | solution.py:180
  462.0 28.6 %collective-permute-start.65 = (bf16[4,2,64,256]{3,2,1,0:T(8,128)(2,1)}, bf16[4,2,64,256]{3,2,1,0:T(8,128)(2,1)}, u32[]{:S(2)}, u32[]{:S(2)}) collective-permute-start(bf16[4,2,64,256]{3,2,1,0:T(8,128)(2,1)} %pad_maximum_fusion.5), channel_id=1, source_target_pairs={{1,0},{2,1},{3,2},{5,4},{6,5},{7,6},{9,8},{10,9},{11,10},{13,12},{... | collective-permute-start | bytes 786440 | tf_op jit(solution)/shard_map/ppermute | solution.py:180
  463.3 16.6 %collective-permute-start.66 = (bf16[4,1024,128]{2,1,0:T(8,128)(2,1)}, bf16[4,1024,128]{2,1,0:T(8,128)(2,1)}, u32[]{:S(2)}, u32[]{:S(2)}) collective-permute-start(bf16[4,1024,128]{2,1,0:T(8,128)(2,1)} %bitcast.121), channel_id=1, source_target_pairs={{0,4},{4,0},{8,12},{12,8},{16,20},{20,16},{24,28},{28,24},{1,5},{5... | collective-permute-start | bytes 3145736 | tf_op jit(solution)/shard_map/ppermute | solution.py:124
  463.4 16.5 %collective-permute-start.69 = (bf16[2048,128]{1,0:T(8,128)(2,1)}, bf16[2048,128]{1,0:T(8,128)(2,1)}, u32[]{:S(2)}, u32[]{:S(2)}) collective-permute-start(bf16[2048,128]{1,0:T(8,128)(2,1)} %get-tuple-element.246), channel_id=1, source_target_pairs={{0,16},{4,20},{8,24},{12,28},{16,0},{20,4},{24,8},{28,12},{1,17},{... | collective-permute-start | bytes 1572872 | tf_op jit(solution)/shard_map/ppermute | solution.py:124
  465.6 12.8 %collective-permute-start.71 = (bf16[1312,128]{1,0:T(8,128)(2,1)}, bf16[1312,128]{1,0:T(8,128)(2,1)}, u32[]{:S(2)}, u32[]{:S(2)}) collective-permute-start(bf16[1312,128]{1,0:T(8,128)(2,1)} %get-tuple-element.248), channel_id=1, source_target_pairs={{2,1},{3,2},{6,5},{7,6},{10,9},{11,10},{14,13},{15,14},{18,17},{19... | collective-permute-start | bytes 1007624 | tf_op jit(solution)/shard_map/ppermute | solution.py:105
  478.4 30.3 %collective-permute-start.74 = (bf16[1024,128]{1,0:T(8,128)(2,1)}, bf16[1024,128]{1,0:T(8,128)(2,1)}, u32[]{:S(2)}, u32[]{:S(2)}) collective-permute-start(bf16[1024,128]{1,0:T(8,128)(2,1)} %get-tuple-element.256), channel_id=1, source_target_pairs={{0,16},{4,20},{8,24},{12,28},{16,0},{20,4},{24,8},{28,12},{1,17},{... | collective-permute-start | bytes 786440 | tf_op jit(solution)/shard_map/ppermute | solution.py:124
  483.7 25.0 %collective-permute-start.73 = (bf16[1024,128]{1,0:T(8,128)(2,1)}, bf16[1024,128]{1,0:T(8,128)(2,1)}, u32[]{:S(2)}, u32[]{:S(2)}) collective-permute-start(bf16[1024,128]{1,0:T(8,128)(2,1)} %get-tuple-element.255), channel_id=1, source_target_pairs={{0,8},{4,12},{8,0},{12,4},{16,24},{20,28},{24,16},{28,20},{1,9},{5... | collective-permute-start | bytes 786440 | tf_op jit(solution)/shard_map/ppermute | solution.py:124
  485.3 23.4 %collective-permute-start.75 = (bf16[1024,128]{1,0:T(8,128)(2,1)}, bf16[1024,128]{1,0:T(8,128)(2,1)}, u32[]{:S(2)}, u32[]{:S(2)}) collective-permute-start(bf16[1024,128]{1,0:T(8,128)(2,1)} %get-tuple-element.258), channel_id=1, source_target_pairs={{0,8},{4,12},{8,0},{12,4},{16,24},{20,28},{24,16},{28,20},{1,9},{5... | collective-permute-start | bytes 786440 | tf_op jit(solution)/shard_map/ppermute | solution.py:124
  485.8 22.9 %collective-permute-start.76 = (bf16[1024,128]{1,0:T(8,128)(2,1)}, bf16[1024,128]{1,0:T(8,128)(2,1)}, u32[]{:S(2)}, u32[]{:S(2)}) collective-permute-start(bf16[1024,128]{1,0:T(8,128)(2,1)} %get-tuple-element.260), channel_id=1, source_target_pairs={{0,1},{4,5},{8,9},{12,13},{16,17},{20,21},{24,25},{28,29}} | collective-permute-start | bytes 786440 | tf_op jit(solution)/shard_map/ppermute | solution.py:104
  490.7 18.0 %collective-permute-start.77 = (bf16[1024,128]{1,0:T(8,128)(2,1)}, bf16[1024,128]{1,0:T(8,128)(2,1)}, u32[]{:S(2)}, u32[]{:S(2)}) collective-permute-start(bf16[1024,128]{1,0:T(8,128)(2,1)} %get-tuple-element.261), channel_id=1, source_target_pairs={{3,2},{7,6},{11,10},{15,14},{19,18},{23,22},{27,26},{31,30}} | collective-permute-start | bytes 786440 | tf_op jit(solution)/shard_map/ppermute | solution.py:105
  522.2 28.1 %collective-permute-start.72 = (bf16[1024,128]{1,0:T(8,128)(2,1)S(1)}, bf16[1024,128]{1,0:T(8,128)(2,1)S(1)}, u32[]{:S(2)}, u32[]{:S(2)}) collective-permute-start(bf16[1024,128]{1,0:T(8,128)(2,1)S(1)} %get-tuple-element.253), channel_id=1, source_target_pairs={{0,8},{4,12},{8,0},{12,4},{16,24},{20,28},{24,16},{28,20},{1,9},{5... | collective-permute-start | bytes 786440 | tf_op jit(solution)/shard_map/ppermute | solution.py:124
  523.7 16.1 %collective-permute-start.84 = (bf16[1312,128]{1,0:T(8,128)(2,1)S(1)}, bf16[1312,128]{1,0:T(8,128)(2,1)S(1)}, u32[]{:S(2)}, u32[]{:S(2)}) collective-permute-start(bf16[1312,128]{1,0:T(8,128)(2,1)S(1)} %copy-done.66), channel_id=1, source_target_pairs={{1,0},{2,1},{3,2},{5,4},{6,5},{7,6},{9,8},{10,9},{11,10},{13,12},{... | collective-permute-start | bytes 1007624 | tf_op jit(solution)/shard_map/ppermute | solution.py:105
  525.0 15.3 %collective-permute-start.83 = (bf16[1312,128]{1,0:T(8,128)(2,1)S(1)}, bf16[1312,128]{1,0:T(8,128)(2,1)S(1)}, u32[]{:S(2)}, u32[]{:S(2)}) collective-permute-start(bf16[1312,128]{1,0:T(8,128)(2,1)S(1)} %copy-done.65), channel_id=1, source_target_pairs={{0,1},{1,2},{2,3},{4,5},{5,6},{6,7},{8,9},{9,10},{10,11},{12,13},{... | collective-permute-start | bytes 1007624 | tf_op jit(solution)/shard_map/ppermute | solution.py:104
  (95 other events, 1070.8 us)

commit v5 on v4

--- a/solution.py
+++ b/solution.py
@@ -30,7 +30,7 @@
 PIECES = 8
 SLAB_PAD = 16
 VMEM_BYTES = 52 * 1024 * 1024
-COST_FACTOR = 100
+COST_FACTOR = 1e-3
 
 
 def layout(lengths, token_index, group_rows):
@@ -137,10 +137,11 @@
     return (piece, flip(piece, 2), flip(piece, 4))
 
 
-def gather_far(near, x_first, token=None, core_token=None):
+def gather_far(near):
     piece, by_x, by_y = near
-    far = flip(tied(by_x, token), 4) if x_first else flip(tied(by_y, token), 2)
-    mine = [piece, by_x, by_y, tied(far, core_token)]
+    half = piece.shape[0] // 2
+    far = jnp.concatenate([flip(by_x[:half], 4), flip(by_y[half:], 2)])
+    mine = [piece, by_x, by_y, far]
     return mine + [flip(part, 1) for part in mine]
 
 
@@ -153,6 +154,26 @@
         half = part.shape[1] // 2
         part = add_low(part[:, :half], flip(part[:, half:], mask))
     return part
+
+
+def gather_dp(piece):
+    if lax.axis_size("dp") == PIECES:
+        return lax.all_gather(piece, "dp", axis=0)
+    flat = piece.reshape(-1, piece.shape[-1])
+    for mask in far_bits():
+        flat = jnp.concatenate([flat, flip(flat, mask)], axis=1)
+    pieces = gather_far((flat, flip(flat, 2), flip(flat, 4)))
+    return jnp.stack(pieces).reshape((PIECES,) + piece.shape[:-1] + (LANES,))
+
+
+def scatter_dp(grads):
+    if lax.axis_size("dp") == PIECES:
+        return lax.psum_scatter(grads, "dp", scatter_dimension=0, tiled=False)
+    flat = grads.reshape(PIECES, -1, LANES)
+    own, by_x, by_y, far = add_low(flat[:4], flip(flat[4:], 1))
+    by_y = add_low(by_y, flip(far, 2))
+    total = add_low(add_low(own, flip(by_x, 2)), flip(by_y, 4))
+    return far_scatter(total).reshape(grads.shape[1:3] + (-1,))
 
 
 def to_relative(rows, back=False):
@@ -262,7 +283,7 @@
             dimension_semantics=("arbitrary",), vmem_limit_bytes=VMEM_BYTES
         ),
         cost_estimate=pl.CostEstimate(
-            flops=COST_FACTOR * flops, bytes_accessed=moved, transcendentals=0
+            flops=int(COST_FACTOR * flops), bytes_accessed=LANES, transcendentals=0
         ),
         name=name,
     )(order, *[array for array, _ in operands], *after)
@@ -336,7 +357,7 @@
     return (sums, token)
 
 
-ALL, ODD, EVEN, SECOND, OWN = (0, 1), (1, 2), (0, 2), (2, 1), (0, 1)
+ALL, ODD, EVEN = (0, 1), (1, 2), (0, 2)
 
 
 def slabs(piece, rows, part=ALL, first=0, count=1):
@@ -344,6 +365,33 @@
         piece,
         pl.BlockSpec((count, rows, LANES), lambda n, *_: (part[0] + part[1] * n, first, 0)),
     )
+
+
+def gathered(array, rows, part=ALL, count=1):
+    return [
+        (
+            array,
+            pl.BlockSpec(
+                (None, count, rows, LANES),
+                lambda n, order, p=p: (order[p], part[0] + part[1] * n, 0, 0),
+            ),
+        )
+        for p in range(PIECES)
+    ]
+
+
+def gathered_out(parts, rows):
+    return (
+        (PIECES, parts, rows, LANES),
+        jnp.bfloat16,
+        pl.BlockSpec((PIECES, 1, rows, LANES), lambda n, *_: (0, n, 0, 0)),
+    )
+
+
+def store_gathered(order, ref, rows, values):
+    values = values.astype(jnp.bfloat16)
+    for n in range(PIECES):
+        ref[order[n], 0, rows, :] = values[:, n * LANES : (n + 1) * LANES]
 
 
 def lead(array, part=ALL, count=1):
@@ -513,7 +561,7 @@
 
 
 def down_grad_kernel(order, cotangent, active, *refs):
-    pieces, (cot_out,) = refs[:5], refs[5:]
+    grads, cot_out = refs
 
     @pl.when(pl.program_id(0) == 0)
     def _():
@@ -522,12 +570,11 @@
 
         row_steps(cotangent.shape[0], HALF, one)
 
-    store_pieces(pieces, slice(None), dot(active[...], cot_out[...], NN))
+    store_gathered(order, grads, slice(None), dot(active[...], cot_out[...], NN))
 
 
 def in_grad_kernel(order, cot, rows_two, gate_side, up_side, *refs):
-    pieces, grads = refs[:PIECES], refs[PIECES : PIECES + 5]
-    gate_out, up_out, cot_turned, grad_active = refs[PIECES + 5 :]
+    pieces, (grads, gate_out, up_out, cot_turned, grad_active) = refs[:PIECES], refs[PIECES:]
 
     @pl.when(pl.program_id(0) == 0)
     def _():
@@ -542,12 +589,12 @@
         up_out[rows, :] = (grad * up_side[rows, :].astype(jnp.float32)).astype(jnp.bfloat16)
 
     row_steps(count, 16, one)
-    store_pieces(grads, slice(0, count), dot(gate_out[...], rows_two[...], NN))
-    store_pieces(grads, slice(count, 2 * count), dot(up_out[...], rows_two[...], NN))
+    store_gathered(order, grads, slice(0, count), dot(gate_out[...], rows_two[...], NN))
+    store_gathered(order, grads, slice(count, 2 * count), dot(up_out[...], rows_two[...], NN))
 
 
 def middle_grad_kernel(order, middle, cot, gains, *refs):
-    sides, pieces, refs = refs[:4], refs[4 : 4 + PIECES], refs[4 + PIECES :]
+    sides, pieces, refs = refs[:2], refs[2 : 2 + PIECES], refs[2 + PIECES :]
     grad_middle, grad_low, gain_out, total = refs
     step = pl.program_id(0)
     count = sides[0].shape[0]
@@ -558,8 +605,7 @@
         gain_out[...] = jnp.zeros_like(gain_out)
 
     for n, side in enumerate(sides):
-        rows = slice((n % 2) * count, (n % 2 + 1) * count)
-        total[...] += dot(side[...], wide(pieces, rows, n // 2), TN)
+        total[...] += dot(side[...], wide(pieces, slice(n * count, (n + 1) * count)), TN)
 
     @pl.when(step == pl.num_programs(0) - 1)
     def _():
@@ -634,7 +680,7 @@
 
 
 def input_grad_kernel(order, hidden, gains, grad_middle, *refs):
-    own, second, odd, (before, after), refs = refs[:2], refs[2:4], refs[4:6], refs[6:8], refs[8:]
+    even, odd, (before, after), refs = refs[:2], refs[2:4], refs[4:6], refs[6:]
     pieces, (grad_input, gain_out, mixed, total) = refs[:PIECES], refs[PIECES:]
     step = pl.program_id(0)
     row_count = hidden.shape[0]
@@ -658,8 +704,7 @@
             rows = slice((1 + c) * width, (2 + c) * width)
             total[...] += dot(mixed[...], wide(pieces, rows, slab), NN)
 
-    pl.when(step == 0)(functools.partial(add, 0, *own))
-    pl.when(step == 1)(functools.partial(add, 0, *second))
+    add(0, *even)
     add(1, *odd)
 
     @pl.when(step == pl.num_programs(0) - 1)
@@ -726,8 +771,9 @@
             jnp.pad(norm_gains.astype(low), ((0, SLAB_PAD - 2), (0, 0))),
         ]
     )
-    in_slab = w_in.astype(low).reshape(chunk, 2 * hidden_wide).T
-    down_slab = w_down.astype(low).T
+    ffn_slab = jnp.concatenate(
+        [w_in.astype(low).reshape(chunk, 2 * hidden_wide), w_down.astype(low)], axis=1
+    ).T
     if dp_size == PIECES:
         apart = jnp.array([0, 2, 4, 6, 1, 3, 5, 7], jnp.int32)
         order = lax.axis_index("dp").astype(jnp.int32) ^ apart
@@ -740,12 +786,10 @@
     place = lax.axis_index("tensor").astype(jnp.int32)
     place_rows = jnp.full((8, LANES), place)
     heads_near = gather_near(heads_slab, place)
-    heads_pieces = gather_far(heads_near, True)
     line_token = held_back(place_rows * 0, heads_near[:1])
-    in_near = gather_near(
-        tied(in_slab, line_token), held_back(place_rows, heads_pieces[3:4])[0, 0]
-    )
-    heads_pieces = [piece.reshape(size, -1, LANES) for piece in heads_pieces]
+    ffn_line = line_gather(tied(ffn_slab, line_token), place)
+    in_all = gather_dp(ffn_line[:, : 2 * hidden_wide])
+    heads_pieces = [piece.reshape(size, -1, LANES) for piece in gather_far(heads_near)]
     gains = jnp.concatenate(
         [piece[0, head_rows : head_rows + 8] for piece in heads_pieces], axis=1
     ).astype(full)
@@ -774,9 +818,8 @@
         + [((wide_count, D), low, None)],
         [],
         3 * matmul * D,
-        after=in_near[:1],
-    )
-    in_pieces = gather_far(in_near, False, token)
+    )
+    down_all = gather_dp(tied(ffn_line[:, 2 * hidden_wide :], token))
     attended, logs, token = run(
         attend_kernel,
         "attend",
@@ -784,10 +827,8 @@
         [lead_out(head_block, low), lead_out((size, row_count, LANES), full)],
         [],
         2 * matmul * D,
-        after=in_near[1:],
-    )
-    down_near = gather_near(tied(down_slab, line_token), place + token[0, 0])
-    middle, rows_two, proj_token = run(
+    )
+    middle, rows_two, token = run(
         proj_kernel,
         "proj",
         [order, (hidden, None), (gains, None), lead(attended)]
@@ -795,14 +836,11 @@
         [(tokens, full, None), (tokens, low, None)],
         [],
         matmul * D,
-        after=in_pieces[3:4],
-    )
-    in_pieces = [piece.reshape(size, -1, LANES) for piece in in_pieces]
-    _, proj_token = blend("arrived", [], (proj_token, *down_near[1:]))
+    )
     active, gate_side, up_side, token = run(
         gate_kernel,
         "gate",
-        [order, (rows_two, None)] + [slabs(piece, 2 * hidden_wide) for piece in in_pieces],
+        [order, (rows_two, None)] + gathered(in_all, 2 * hidden_wide),
         [(turned, low, turned_spec)] * 3,
         [
             pltpu.VMEM((D, row_count), low),
@@ -810,88 +848,66 @@
             pltpu.VMEM((hidden_wide, row_count), full),
         ],
         2 * matmul * FF,
-        after=(proj_token,),
-    )
-    down_pieces = gather_far(down_near, True, proj_token, token)
-
-    *down_own, down_partner, cot, token = run(
+    )
+
+    down_grads, cot, token = run(
         down_grad_kernel,
         "down_grad",
         [order, (cot_in, None), turned_block(active, hidden_wide)],
-        piece_outs(size, hidden_wide) + [(tokens, low, None)],
+        [gathered_out(size, hidden_wide), (tokens, low, None)],
         [],
         matmul * FF,
-        after=down_pieces[3:4],
-    )
-    down_pieces = [piece.reshape(size, -1, LANES) for piece in down_pieces]
-
+    )
+    down_sum = scatter_dp(down_grads)
     half = size // 2
-    half_turned = (half * hidden_wide, row_count)
-
-    def core_hop(outs):
-        own = [part.reshape(-1, LANES) for part in outs[:4]]
-        return (own, flip(outs[4].reshape(4, -1, LANES), 1))
-
-    def core_sums(own, received):
-        return [[(part,), (received, n)] for n, part in enumerate(own)]
-
-    def near_sums(own, arrived, entries):
-        terms = [part.reshape(entries, -1, LANES) for part in (own, *arrived)]
-        return [[(term, n) for term in terms] for n in range(entries)]
-
-    def line_sums(to_after, to_before, arrived):
-        return [[(to_after,), (arrived[0],)], [(to_before,), (arrived[1],)]]
-
-    down_core = core_hop([*down_own, down_partner])
-
-    def in_grad(part, name, after):
-        return run(
-            in_grad_kernel,
-            name,
-            [order, (cot, None), (rows_two, None)]
-            + [turned_block(gate_side, hidden_wide, part), turned_block(up_side, hidden_wide, part)]
-            + [slabs(piece, hidden_wide, part) for piece in down_pieces],
-            piece_outs(half, 2 * hidden_wide) + [(half_turned, low, turned_spec)] * 2,
-            [pltpu.VMEM((D, row_count), low), pltpu.VMEM((hidden_wide, row_count), full)],
-            3 * matmul * FF // 2,
-            after=after,
-            steps=half,
-        )
-
-    *odd_outs, odd_gate, odd_up, token = in_grad(ODD, "in_grad_odd", ())
-    odd_core = core_hop(odd_outs)
-    down_sums, token = blend("sums_one", core_sums(*down_core), (token,))
-    down_far = flip(down_sums[3], 2)
-    *even_outs, even_gate, even_up, token = in_grad(EVEN, "in_grad_even", (token,))
-    even_core = core_hop(even_outs)
-    (*odd_sums, down_y), token = blend(
-        "sums_two", core_sums(*odd_core) + [[(down_sums[2],), (down_far,)]], (token,)
-    )
-    odd_far = flip(odd_sums[3], 4)
-    down_near = (flip(down_sums[1], 2), flip(down_y, 4))
+    in_grads, gate_grad, up_grad, token = run(
+        in_grad_kernel,
+        "in_grad",
+        [order, (cot, None), (rows_two, None)]
+        + [turned_block(gate_side, hidden_wide), turned_block(up_side, hidden_wide)]
+        + gathered(down_all, hidden_wide),
+        [gathered_out(size, 2 * hidden_wide)] + [(turned, low, turned_spec)] * 2,
+        [pltpu.VMEM((D, row_count), low), pltpu.VMEM((hidden_wide, row_count), full)],
+        3 * matmul * FF,
+    )
+    in_sum = scatter_dp(in_grads)
     grad_middle, grad_low, gain_two, token = run(
         middle_grad_kernel,
         "middle_grad",
         [order, (middle, None), (cot, None), (gains, None)]
-        + [turned_block(side, hidden_wide) for side in (even_gate, even_up, odd_gate, odd_up)]
-        + [slabs(piece, 2 * hidden_wide, count=2) for piece in in_pieces],
+        + [turned_block(side, hidden_wide) for side in (gate_grad, up_grad)]
+        + gathered(in_all, 2 * hidden_wide),
         [(tokens, full, None), (tokens, low, None), ((8, D), full, None)],
         [pltpu.VMEM(tokens, full)],
         2 * matmul * FF,
-        after=(token,),
-        steps=half,
-    )
-    sums, token = blend(
-        "sums_three",
-        core_sums(*even_core)
-        + [[(odd_sums[1],), (odd_far,)]]
-        + near_sums(down_sums[0], down_near, size),
-        (token,),
-    )
-    even_sums, odd_x, down_parts = sums[:4], sums[4], [far_scatter(part) for part in sums[5:]]
-    even_far = flip(even_sums[3], 4)
-    odd_near = (flip(odd_x, 2), flip(odd_sums[2], 4))
-    down_line = line_hop(down_parts[1], down_parts[3], 3)
+    )
+
+    def core_hop(outs):
+        return (outs[:4], flip(outs[4], 1))
+
+    def core_sums(own, received):
+        entries = own[0].shape[0]
+        received = received.reshape((-1,) + received.shape[2:])
+        return [
+            [(part, e), (received, n * entries + e)]
+            for n, part in enumerate(own)
+            for e in range(entries)
+        ]
+
+    def far_hop(sums):
+        return (flip(sums[6], 2), flip(sums[7], 4))
+
+    def far_sums(sums, arrived):
+        return [[(sums[4],), (arrived[0],)], [(sums[3],), (arrived[1],)]]
+
+    def near_hop(sums, added):
+        return (flip(sums[2], 2), flip(added[0], 4), flip(added[1], 2), flip(sums[5], 4))
+
+    def near_sums(sums, arrived):
+        return [
+            [(sums[0],), (arrived[0],), (arrived[1],)],
+            [(sums[1],), (arrived[2],), (arrived[3],)],
+        ]
 
     def attend_grad(part, count, name, after):
         return run(
@@ -915,47 +931,15 @@
             steps=count,
         )
 
-    *odd_outs, odd_queries, odd_pairs, token = attend_grad(ODD, half, "attend_grad_odd", (token,))
-    heads_odd_core = core_hop(odd_outs)
-    sums, token = blend(
-        "sums_four",
-        [[(even_sums[1],), (even_far,)]]
-        + near_sums(odd_sums[0], odd_near, half)
-        + line_sums(down_parts[2], down_parts[2], down_line),
-        (token,),
-    )
-    even_near = (flip(sums[0], 2), flip(even_sums[2], 4))
-    odd_parts = [far_scatter(part) for part in sums[1:3]]
-    down_line = line_hop(sums[3], sums[4], 2)
-    *second_outs, second_queries, second_pairs, token = attend_grad(
-        SECOND, 1, "attend_grad_second", (token,)
-    )
-    heads_second_core = core_hop(second_outs)
-    sums, token = blend(
-        "sums_five",
-        core_sums(*heads_odd_core)
-        + near_sums(even_sums[0], even_near, half)
-        + line_sums(down_parts[3], down_parts[1], down_line),
-        (token,),
-    )
-    heads_odd_sums, even_parts = sums[:4], [far_scatter(part) for part in sums[4:6]]
-    heads_odd_far = flip(heads_odd_sums[3], 2)
-    down_line = line_hop(sums[6], sums[7], 1)
-    in_line = line_hop(odd_parts[0], odd_parts[1], 3)
-    *own_outs, own_queries, own_pairs, token = attend_grad(OWN, 1, "attend_grad_own", (token,))
-    heads_own_core = core_hop(own_outs)
-    sums, token = blend(
-        "sums_six",
-        core_sums(*heads_second_core)
-        + [[(heads_odd_sums[2],), (heads_odd_far,)]]
-        + line_sums(even_parts[1], even_parts[1], in_line),
-        (token, *down_line),
-    )
-    heads_second_sums = sums[:4]
-    heads_second_far = flip(heads_second_sums[3], 4)
-    heads_odd_near = (flip(heads_odd_sums[1], 2), flip(sums[4], 4))
-    in_line = line_hop(sums[5], sums[6], 2)
-    pairs = [own_pairs[0], odd_pairs[0], second_pairs[0], odd_pairs[1]]
+    *odd_outs, odd_queries, odd_pairs, token = attend_grad(ODD, half, "attend_grad_odd", ())
+    odd_core = core_hop(odd_outs)
+    *even_outs, even_queries, even_pairs, token = attend_grad(
+        EVEN, half, "attend_grad_even", (token,)
+    )
+    even_core = core_hop(even_outs)
+    odd, token = blend("sums_one", core_sums(*odd_core), (token,))
+    odd_far = far_hop(odd)
+    pairs = [even_pairs[0], odd_pairs[0], even_pairs[1], odd_pairs[1]]
     edge_after = jnp.stack([pair[:, -HALF:] for pair in pairs[-1:] + pairs[:-1]])
     edge_before = jnp.stack([pair[:, :HALF] for pair in pairs[1:] + pairs[:1]])
     edges = (shift(edge_after, 1), shift(edge_before, -1))
@@ -963,31 +947,24 @@
         down_kernel,
         "down",
         [order, (middle, None), turned_block(active, hidden_wide)]
-        + [slabs(piece, hidden_wide) for piece in down_pieces],
+        + gathered(down_all, hidden_wide),
         [(tokens, low, None)],
         [pltpu.VMEM(tokens, full)],
         matmul * FF,
         after=(token,),
     )
-    sums, token = blend(
-        "sums_seven",
-        core_sums(*heads_own_core)
-        + [[(heads_second_sums[1],), (heads_second_far,)]]
-        + near_sums(heads_odd_sums[0], heads_odd_near, half)
-        + line_sums(odd_parts[1], odd_parts[0], in_line),
-        (token,),
-    )
-    heads_own_sums, heads_odd_parts = sums[:4], [far_scatter(part) for part in sums[5:7]]
-    heads_own_far = flip(heads_own_sums[3], 2)
-    heads_second_near = (flip(sums[4], 2), flip(heads_second_sums[2], 4))
-    in_line = line_hop(sums[7], sums[8], 1)
-    heads_line = line_hop(heads_odd_parts[0], heads_odd_parts[1], 3)
+    (*even, odd_y, odd_x), token = blend(
+        "sums_two", core_sums(*even_core) + far_sums(odd, odd_far), (token,)
+    )
+    even_far = far_hop(even)
+    odd_near = near_hop(odd, (odd_y, odd_x))
+    ffn_parts = tied(jnp.concatenate([in_sum, down_sum], axis=1), token)
+    ffn_arrived = line_hop(ffn_parts[1], ffn_parts[size - 1], size - 1)
     grad_input, gain_one, token = run(
         input_grad_kernel,
         "input_grad",
         [order, (hidden, None), (gains, None), (grad_middle, None)]
-        + [(own_queries, None), (own_pairs, None), (second_queries, None), (second_pairs, None)]
-        + [lead(odd_queries), lead(odd_pairs)]
+        + [lead(array) for array in (even_queries, even_pairs, odd_queries, odd_pairs)]
         + [lead(array, count=2) for array in edges]
         + [slabs(piece, 3 * head_wide, count=2) for piece in heads_pieces],
         [(tokens, full, None), ((8, D), full, None)],
@@ -996,26 +973,38 @@
         after=(token,),
         steps=half,
     )
-    sums, token = blend(
-        "sums_eight",
-        near_sums(heads_second_sums[0], heads_second_near, 1)
-        + [[(heads_own_sums[2],), (heads_own_far,)]],
-        (token, *heads_line),
-    )
-    heads_second_part = far_scatter(sums[0])
-    heads_own_near = (flip(heads_own_sums[1], 2), flip(sums[1], 4))
-    heads_line = line_hop(*[add_low(heads_second_part, part) for part in heads_line], 2)
-    heads_line = line_hop(
-        add_low(heads_odd_parts[1], heads_line[0]), add_low(heads_odd_parts[0], heads_line[1]), 1
-    )
-    heads_own_part = far_scatter(line_end(heads_own_sums[0], heads_own_near).astype(low))
-    gain_sum = gain_scatter(tied(jnp.concatenate([gain_one[:1], gain_two[:1]]), token))
+    (*odd_parts, even_y, even_x), token = blend(
+        "sums_three",
+        near_sums(odd, odd_near) + far_sums(even, even_far),
+        (token, *ffn_arrived),
+    )
+    even_near = near_hop(even, (even_y, even_x))
+    odd_parts = [far_scatter(part) for part in odd_parts]
+
+    def line_round(parts, step, arrived=None):
+        to_after, to_before = parts[size - step], parts[step]
+        if arrived is not None:
+            to_after, to_before = add_low(to_after, arrived[0]), add_low(to_before, arrived[1])
+        return line_hop(to_after, to_before, step)
+
+    ffn_arrived = line_round(ffn_parts, 2, ffn_arrived)
+    three_token = token
+    even_parts, token = blend("sums_four", near_sums(even, even_near), (token, *ffn_arrived))
+    ffn_total = line_end(ffn_parts[0], line_round(ffn_parts, 1, ffn_arrived))
+    even_parts = [far_scatter(part) for part in even_parts]
+    heads_parts = [even_parts[0], odd_parts[0], even_parts[1], odd_parts[1]]
+    heads_arrived = None
+    for step in range(size - 1, 0, -1):
+        heads_arrived = line_round(heads_parts, step, heads_arrived)
+    heads_total = line_end(heads_parts[0], heads_arrived)
+    gain_sum = gain_scatter(tied(jnp.concatenate([gain_one[:1], gain_two[:1]]), three_token))
     if dp_size != PIECES:
         hidden_out, grad_input = to_relative(hidden_out, True), to_relative(grad_input, True)
 
-    down_sum = line_end(down_parts[0], down_line).T
-    in_sum = line_end(even_parts[0], in_line).T.reshape(w_in.shape)
-    heads_sum = line_end(heads_own_part, heads_line).T
+    ffn_total = ffn_total.T
+    in_sum = ffn_total[:, : 2 * hidden_wide].reshape(w_in.shape)
+    down_sum = ffn_total[:, 2 * hidden_wide :]
+    heads_sum = heads_total.T
     qkv_sum = jnp.concatenate(
         [
             heads_first(heads_sum[:, : 2 * head_wide]),

time: 565 us -> 508 us (0.90)
  starting transfers between devices: 134 us -> 85.9 us
  Pallas kernels: 252 us -> 219 us
  waiting for transfers between devices: 95 us -> 120 us
  between operations: 8.29 us -> 18.4 us
  other arithmetic: 24.7 us -> 16.8 us
  local copies, waits for them, and re-layouts: 45 us -> 38 us
    ppermute x9 -> x6, starting transfers between devices: 45 us -> 25 us  [line_hop(): lax.ppermute(to_after, 'tensor', [(n, n + 1) for n in range(size - step)])]
    pallas_call x9 -> x4, Pallas kernels: 28.7 us -> 10 us  [blend(): pl.pallas_call(body, grid=(halves,), in_specs=specs + [pl.BlockSpec(memor...]
    ppermute x48 -> x25, starting transfers between devices: 35.4 us -> 20.6 us  [flip(): lax.ppermute(rows, 'dp', [(n, n ^ mask) for n in range(lax.axis_size('dp'...]
    pallas_call x13 -> x11, Pallas kernels: 221 us -> 208 us  [run(): pl.pallas_call(body, grid_spec=pltpu.PrefetchScalarGridSpec(num_scalar_pr...]
    ppermute x9 -> x6, waiting for transfers between devices: 31.5 us -> 41.8 us  [line_gather(): lax.ppermute(from_after[-1], 'tensor', [(n, n - 1) for n in range(1, size...]
    ppermute x2, waiting for transfers between devices: 0.01 us -> 6.62 us  [gain_scatter(): lax.ppermute(gains, 'tensor', [(n, n ^ mask) for n in range(size)])]
    ppermute x9 -> x6, starting transfers between devices: 17.7 us -> 12.4 us  [line_gather(): lax.ppermute(from_before[-1], 'tensor', [(n, n + 1) for n in range(step -...]
    unnamed x157 -> x156, local copies, waits for them, and re-layouts: 30.3 us -> 25.2 us
  transfers between devices with their start and end apart: 90 -> 59, of which waited for: 17 -> 17; matrix products, arithmetic and copies ran while one was open for 7% -> 6% of each run, Pallas kernels for 45% -> 43%
where the time goes in v5:
time: 508 us; the launch traced here: 499 us
  Pallas kernels  219 us (43%)
  waiting for transfers between devices  120 us (24%)
  starting transfers between devices  85.9 us (17%)
  local copies, waits for them, and re-layouts  38 us (7%)
  between operations  18.4 us (4%)
  other arithmetic  16.8 us (3%)
    pallas_call x11, Pallas kernels, run(): pl.pallas_call(body, grid_spec=pltpu.PrefetchScalarGridSpec(num_scalar_pr...  208 us
    ppermute x25, waiting for transfers between devices, flip(): lax.ppermute(rows, 'dp', [(n, n ^ mask) for n in range(lax.axis_size('dp'...  57 us
    ppermute x6, waiting for transfers between devices, line_gather(): lax.ppermute(from_after[-1], 'tensor', [(n, n - 1) for n in range(1, size...  41.8 us
    unnamed x156, local copies, waits for them, and re-layouts  25.2 us
    ppermute x6, starting transfers between devices, line_hop(): lax.ppermute(to_after, 'tensor', [(n, n + 1) for n in range(size - step)])  25 us
    ppermute x25, starting transfers between devices, flip(): lax.ppermute(rows, 'dp', [(n, n ^ mask) for n in range(lax.axis_size('dp'...  20.6 us
    ppermute x6, starting transfers between devices, line_gather(): lax.ppermute(from_before[-1], 'tensor', [(n, n + 1) for n in range(step -...  12.4 us
    ppermute x4, starting transfers between devices, shift(): return lax.ppermute(rows, 'tensor', pairs)  11.7 us
  transfers between devices with their start and end apart: 59, of which 17 were waited for; matrix products, arithmetic and copies ran while one was open for 6% of the time, Pallas kernels for 43%

profile of v5, /device:TPU:0, one launch (start us, length us, event | category | flops | bytes accessed | tf_op | source)
XLA Modules:
  0.0 498.7 jit_solution(371061721497007152)
XLA Ops:
  8.8 5.1 %collective-permute-start = (bf16[1040,128]{1,0:T(8,128)(2,1)S(1)}, bf16[1040,128]{1,0:T(8,128)(2,1)S(1)}, u32[]{:S(2)}, u32[]{:S(2)}) collective-permute-start(bf16[1040,128]{1,0:T(8,128)(2,1)S(1)} %get-tuple-element.257), channel_id=1, source_target_pairs={{0,1},{1,2},{2,3},{4,5},{5,6},{6,7},{8,9},{9,10},{10,11},{12,13},{... | collective-permute-start | bytes 798728 | tf_op jit(solution)/shard_map/ppermute | solution.py:83
  13.9 1.3 collective-permute-start.1
  15.2 4.3 collective-permute-done
  20.2 3.5 collective-permute-done.1
  25.7 6.9 %collective-permute-done.2 = bf16[1040,128]{1,0:T(8,128)(2,1)S(1)} collective-permute-done((bf16[1040,128]{1,0:T(8,128)(2,1)S(1)}, bf16[1040,128]{1,0:T(8,128)(2,1)S(1)}, u32[]{:S(2)}, u32[]{:S(2)}) %collective-permute-start.2) | collective-permute-done | bytes 266272 | tf_op jit(solution)/shard_map/ppermute | solution.py:86
  34.0 6.9 %collective-permute-done.3 = bf16[1040,128]{1,0:T(8,128)(2,1)S(1)} collective-permute-done((bf16[1040,128]{1,0:T(8,128)(2,1)S(1)}, bf16[1040,128]{1,0:T(8,128)(2,1)S(1)}, u32[]{:S(2)}, u32[]{:S(2)}) %collective-permute-start.3) | collective-permute-done | bytes 266272 | tf_op jit(solution)/shard_map/ppermute | solution.py:86
  46.0 1.3 collective-permute-start.17
  47.3 4.6 collective-permute-start.16
  51.8 6.1 %collective-permute-done.17 = bf16[1968,128]{1,0:T(8,128)(2,1)S(1)} collective-permute-done((bf16[1968,128]{1,0:T(8,128)(2,1)S(1)}, bf16[1968,128]{1,0:T(8,128)(2,1)S(1)}, u32[]{:S(2)}, u32[]{:S(2)}) %collective-permute-start.17) | collective-permute-done | bytes 503840 | tf_op jit(solution)/shard_map/ppermute | solution.py:86
  60.0 9.7 %collective-permute-done.18 = bf16[1968,128]{1,0:T(8,128)(2,1)S(1)} collective-permute-done((bf16[1968,128]{1,0:T(8,128)(2,1)S(1)}, bf16[1968,128]{1,0:T(8,128)(2,1)S(1)}, u32[]{:S(2)}, u32[]{:S(2)}) %collective-permute-start.18) | collective-permute-done | bytes 503840 | tf_op jit(solution)/shard_map/ppermute | solution.py:86
  71.7 8.8 %collective-permute-done.19 = bf16[1968,128]{1,0:T(8,128)(2,1)S(1)} collective-permute-done((bf16[1968,128]{1,0:T(8,128)(2,1)S(1)}, bf16[1968,128]{1,0:T(8,128)(2,1)S(1)}, u32[]{:S(2)}, u32[]{:S(2)}) %collective-permute-start.19) | collective-permute-done | bytes 503840 | tf_op jit(solution)/shard_map/ppermute | solution.py:86
  82.8 1.8 fusion.23
  85.8 1.6 collective-permute-start.6
  87.7 1.6 collective-permute-start.7
  89.8 29.7 %collective-permute-done.6 = bf16[4160,128]{1,0:T(8,128)(2,1)S(1)} collective-permute-done((bf16[4160,128]{1,0:T(8,128)(2,1)S(1)}, bf16[4160,128]{1,0:T(8,128)(2,1)S(1)}, u32[]{:S(2)}, u32[]{:S(2)}) %collective-permute-start.6) | collective-permute-done | bytes 1064992 | tf_op jit(solution)/shard_map/ppermute | solution.py:124
  120.4 1.5 collective-permute-start.8
  124.9 2.0 collective-permute-done.7
  128.6 10.5 %collective-permute-done.8 = bf16[2080,128]{1,0:T(8,128)(2,1)} collective-permute-done((bf16[2080,128]{1,0:T(8,128)(2,1)}, bf16[2080,128]{1,0:T(8,128)(2,1)}, u32[]{:S(2)}, u32[]{:S(2)}) %collective-permute-start.8) | collective-permute-done | bytes 532512 | tf_op jit(solution)/shard_map/ppermute | solution.py:124
  140.2 12.8 %collective-permute-done.9 = bf16[2080,128]{1,0:T(8,128)(2,1)S(1)} collective-permute-done((bf16[2080,128]{1,0:T(8,128)(2,1)S(1)}, bf16[2080,128]{1,0:T(8,128)(2,1)S(1)}, u32[]{:S(2)}, u32[]{:S(2)}) %collective-permute-start.9) | collective-permute-done | bytes 532512 | tf_op jit(solution)/shard_map/ppermute | solution.py:124
  153.9 4.9 collective-permute-start.14
  159.0 3.2 collective-permute-done.14.refs_1_
  162.2 13.8 %heads.1 = (bf16[4,768,256]{2,1,0:T(8,128)(2,1)}, bf16[4,896,256]{2,1,0:T(8,128)(2,1)}, bf16[4,896,256]{2,1,0:T(8,128)(2,1)}, bf16[896,1024]{1,0:T(8,128)(2,1)}, s32[8,128]{1,0:T(8,128)S(1)}) custom-call(s32[8]{0:T(128)S(1)} %broadcast_xor_fusion.order_ref, bf16[768,1024]{1,0:T(8,128)(2,1)} %refs_0_.7, bf16[64,1024]{1,0:T(8,128)(2,1)S(1)} %collective-permute-done.14.refs_1_, ...), custom_call_target="tpu_custom_call" | custom-call | flops 4831838 | bytes 128 | tf_op jit(solution)/shard_map/heads/pallas_call | solution.py:271
  178.7 19.7 %attend.1 = (bf16[4,768,256]{2,1,0:T(8,128)(2,1)}, f32[4,768,128]{2,1,0:T(8,128)}, s32[8,128]{1,0:T(8,128)}) custom-call(s32[8]{0:T(128)S(1)} %broadcast_xor_fusion.order_ref, f32[6,128,256]{2,1,0:T(8,128)S(1)} %and_select_fusion.refs_0_, bf16[4,768,256]{2,1,0:T(8,128)(2,1)} %get-tuple-element.85.refs_1_.refs_5_, ...), custom_call_target="tpu_custom_call" | custom-call | flops 3221225 | bytes 128 | tf_op jit(solution)/shard_map/attend/pallas_call | solution.py:271
  198.4 10.5 %proj.1 = (f32[768,1024]{1,0:T(8,128)}, bf16[768,1024]{1,0:T(8,128)(2,1)}, s32[8,128]{1,0:T(8,128)}) custom-call(s32[8]{0:T(128)S(1)} %broadcast_xor_fusion.order_ref, bf16[768,1024]{1,0:T(8,128)(2,1)} %refs_0_.7, f32[8,1024]{1,0:T(8,128)S(1)} %convert_element_type.134.refs_3_.refs_1_.refs_2_, bf16[4,768,256]{2,1,0:T(8,128)(2,1)} %get-tuple-element.88.refs_2_.refs_8_, ...), custom_call_target="tpu_custom_call" | custom-call | flops 1610612 | bytes 128 | tf_op jit(solution)/shard_map/proj/pallas_call | solution.py:271
  209.0 1.4 copy-done.4
  210.4 19.8 %gate.1 = (bf16[2624,768]{1,0:T(8,128)(2,1)}, bf16[2624,768]{1,0:T(8,128)(2,1)}, bf16[2624,768]{1,0:T(8,128)(2,1)}, s32[8,128]{1,0:T(8,128)}) custom-call(s32[8]{0:T(128)S(1)} %broadcast_xor_fusion.order_ref, bf16[768,1024]{1,0:T(8,128)(2,1)S(1)} %copy-done.4, bf16[8,4,1312,128]{3,2,1,0:T(8,128)(2,1)} %bitcast.155, bf16[8,4,1312,128]{3,2,1,0:T(8,128)(2,1)} %bitcast.156, ...), custom_call_target="tpu_custom_call" | custom-call | flops 8254390 | bytes 128 | tf_op jit(solution)/shard_map/gate/pallas_call | solution.py:271
  230.2 9.6 %down_grad.1 = (bf16[8,4,656,128]{3,2,1,0:T(8,128)(2,1)}, bf16[768,1024]{1,0:T(8,128)(2,1)S(1)}, s32[8,128]{1,0:T(8,128)}) custom-call(s32[8]{0:T(128)S(1)} %broadcast_xor_fusion.order_ref, bf16[768,1024]{1,0:T(8,128)(2,1)} %refs_0_.6, bf16[2624,768]{1,0:T(8,128)(2,1)} %get-tuple-element.91.refs_1_), custom_call_target="tpu_custom_call" | custom-call | flops 4127195 | bytes 128 | tf_op jit(solution)/shard_map/down_grad/pallas_call | solution.py:271
  240.9 27.2 %in_grad.1 = (bf16[8,4,1312,128]{3,2,1,0:T(8,128)(2,1)}, bf16[2624,768]{1,0:T(8,128)(2,1)}, bf16[2624,768]{1,0:T(8,128)(2,1)}, s32[8,128]{1,0:T(8,128)}) custom-call(s32[8]{0:T(128)S(1)} %broadcast_xor_fusion.order_ref, bf16[768,1024]{1,0:T(8,128)(2,1)S(1)} %get-tuple-element.93.refs_0_.refs_1_, bf16[768,1024]{1,0:T(8,128)(2,1)} %get-tuple-element.90.refs_0_.refs_1_, ...), custom_call_target="tpu_custom_call" | custom-call | flops 12381585 | bytes 128 | tf_op jit(solution)/shard_map/in_grad/pallas_call | solution.py:271
  268.1 21.5 %middle_grad.1 = (f32[768,1024]{1,0:T(8,128)}, bf16[768,1024]{1,0:T(8,128)(2,1)S(1)}, f32[8,1024]{1,0:T(8,128)S(1)}, s32[8,128]{1,0:T(8,128)}) custom-call(s32[8]{0:T(128)S(1)} %broadcast_xor_fusion.order_ref, f32[768,1024]{1,0:T(8,128)} %get-tuple-element.89.refs_0_, bf16[768,1024]{1,0:T(8,128)(2,1)} %copy-done.3, ...), custom_call_target="tpu_custom_call" | custom-call | flops 8254390 | bytes 128 | tf_op jit(solution)/shard_map/middle_grad/pallas_call | solution.py:271
  290.8 28.9 %attend_grad_odd.1 = (bf16[2,1024,128]{2,1,0:T(8,128)(2,1)S(1)}, bf16[2,1024,128]{2,1,0:T(8,128)(2,1)S(1)}, bf16[2,1024,128]{2,1,0:T(8,128)(2,1)}, bf16[2,1024,1...) custom-call(s32[8]{0:T(128)S(1)} %broadcast_xor_fusion.order_ref, ...), custom_call_target="tpu_custom_call" | custom-call | flops 9663676 | bytes 128 | tf_op jit(solution)/shard_map/attend_grad_odd/pallas_call | solution.py:271
  320.5 29.1 %attend_grad_even.1 = (bf16[2,1024,128]{2,1,0:T(8,128)(2,1)S(1)}, bf16[2,1024,128]{2,1,0:T(8,128)(2,1)S(1)}, bf16[2,1024,128]{2,1,0:T(8,128)(2,1)}, bf16[2,1024,...) custom-call(s32[8]{0:T(128)S(1)} %broadcast_xor_fusion.order_ref, ...), custom_call_target="tpu_custom_call" | custom-call | flops 9663676 | bytes 128 | tf_op jit(solution)/shard_map/attend_grad_even/pallas_call | solution.py:271
  350.2 1.7 slice_bitcast_fusion.2
  353.7 3.1 sums_one.1
  359.8 4.2 collective-permute-start.23
  366.0 11.6 %down.1 = (bf16[768,1024]{1,0:T(8,128)(2,1)}, s32[8,128]{1,0:T(8,128)S(1)}) custom-call(s32[8]{0:T(128)S(1)} %broadcast_xor_fusion.order_ref, f32[768,1024]{1,0:T(8,128)} %get-tuple-element.89.refs_0_, bf16[2624,768]{1,0:T(8,128)(2,1)} %get-tuple-element.91.refs_1_, bf16[8,4,656,128]{3,2,1,0:T(8,128)(2,1)} %bitcast.179, bf16[8,4,656,128]{3,2,1,0:T(8,128)(2,1)} %bitcast.180, ...), custom_call_target="tpu_custom_call" | custom-call | flops 4127195 | bytes 128 | tf_op jit(solution)/shard_map/down/pallas_call | solution.py:271
  378.3 1.7 collective-permute-start.32
  380.8 3.5 sums_two.1
  387.1 2.1 multiply_select_fusion
  390.2 4.7 collective-permute-start.35
  394.9 1.5 collective-permute-start.31
  397.0 1.8 collective-permute-start.34
  398.8 16.3 %input_grad.1 = (f32[768,1024]{1,0:T(8,128)}, f32[8,1024]{1,0:T(8,128)S(1)}, s32[8,128]{1,0:T(8,128)S(1)}) custom-call(s32[8]{0:T(128)S(1)} %broadcast_xor_fusion.order_ref, bf16[768,1024]{1,0:T(8,128)(2,1)} %refs_0_.7, f32[8,1024]{1,0:T(8,128)S(1)} %convert_element_type.134.refs_3_.refs_1_.refs_2_, f32[768,1024]{1,0:T(8,128)} %get-tuple-element.110.refs_2_, ...), custom_call_target="tpu_custom_call" | custom-call | flops 4831838 | bytes 128 | tf_op jit(solution)/shard_map/input_grad/pallas_call | solution.py:271
  416.3 1.7 sums_three.1
  420.7 1.5 collective-permute-start.28
  422.7 1.5 collective-permute-start.37
  424.9 2.4 fusion.1
  429.0 2.1 collective-permute-start.40
  431.1 1.7 collective-permute-start.53
  432.8 1.5 collective-permute-start.38
  434.2 6.6 %collective-permute-done.53 = f32[2,128]{1,0:T(2,128)S(1)} collective-permute-done((f32[2,128]{1,0:T(2,128)S(1)}, f32[2,128]{1,0:T(2,128)S(1)}, u32[]{:S(2)}, u32[]{:S(2)}) %collective-permute-start.53) | collective-permute-done | bytes 1056 | tf_op jit(solution)/shard_map/ppermute | solution.py:119
  440.9 1.4 collective-permute-start.45
  442.2 5.1 %collective-permute-start.42 = (bf16[1024,128]{1,0:T(8,128)(2,1)S(1)}, bf16[1024,128]{1,0:T(8,128)(2,1)}, u32[]{:S(2)}, u32[]{:S(2)}) collective-permute-start(bf16[1024,128]{1,0:T(8,128)(2,1)S(1)} %get-tuple-element.150), channel_id=1, source_target_pairs={{0,1},{4,5},{8,9},{12,13},{16,17},{20,21},{24,25},{28,29}} | collective-permute-start | bytes 786440 | tf_op jit(solution)/shard_map/ppermute | solution.py:104
  448.4 1.9 copy.105
  450.3 1.9 copy.107
  453.1 1.8 sums_four.1
  456.1 1.7 collective-permute-start.43
  458.5 1.3 add_convert_fusion.1
  459.8 6.2 %collective-permute-start.48 = (bf16[1968,128]{1,0:T(8,128)(2,1)S(1)}, bf16[1968,128]{1,0:T(8,128)(2,1)S(1)}, u32[]{:S(2)}, u32[]{:S(2)}) collective-permute-start(bf16[1968,128]{1,0:T(8,128)(2,1)S(1)} %get-tuple-element.236), channel_id=1, source_target_pairs={{0,1},{1,2},{2,3},{4,5},{5,6},{6,7},{8,9},{9,10},{10,11},{12,13},{... | collective-permute-start | bytes 1511432 | tf_op jit(solution)/shard_map/ppermute | solution.py:104
  466.0 1.3 collective-permute-start.49
  468.0 5.2 %collective-permute-start.44 = (bf16[1024,128]{1,0:T(8,128)(2,1)S(1)}, bf16[1024,128]{1,0:T(8,128)(2,1)S(1)}, u32[]{:S(2)}, u32[]{:S(2)}) collective-permute-start(bf16[1024,128]{1,0:T(8,128)(2,1)S(1)} %add_convert_fusion.3), channel_id=1, source_target_pairs={{0,1},{1,2},{2,3},{4,5},{5,6},{6,7},{8,9},{9,10},{10,11},{12,13},{... | collective-permute-start | bytes 786440 | tf_op jit(solution)/shard_map/ppermute | solution.py:104
  473.3 1.4 collective-permute-start.47
  474.7 2.6 collective-permute-done.48
  477.3 4.7 collective-permute-done.49
  482.3 1.6 multiply_subtract_fusion
  (316 shorter events, 61.8 us)
Async XLA Ops:
  7.2 201.8 %all-gather.5.cloned.1.call-start = ((), (), s32[]{:S(2)}) async-start(), calls=%async_computation.4 | async-start | bytes 12091392 | tf_op jit(solution)/shard_map/all_gather | solution.py:161
  8.8 32.2 %copy-start.47 = (bf16[1,1040,128]{2,1,0:T(8,128)(2,1)}, bf16[1,1040,128]{2,1,0:T(8,128)(2,1)S(1)}, u32[]{:S(2)}) copy-start(bf16[1,1040,128]{2,1,0:T(8,128)(2,1)S(1)} %get-tuple-element.258) | copy-start | bytes 798724
  8.8 10.7 %collective-permute-start = (bf16[1040,128]{1,0:T(8,128)(2,1)S(1)}, bf16[1040,128]{1,0:T(8,128)(2,1)S(1)}, u32[]{:S(2)}, u32[]{:S(2)}) collective-permute-start(bf16[1040,128]{1,0:T(8,128)(2,1)S(1)} %get-tuple-element.257), channel_id=1, source_target_pairs={{0,1},{1,2},{2,3},{4,5},{5,6},{6,7},{8,9},{9,10},{10,11},{12,13},{... | collective-permute-start | bytes 798728 | tf_op jit(solution)/shard_map/ppermute | solution.py:83
  13.9 9.7 %collective-permute-start.1 = (bf16[1040,128]{1,0:T(8,128)(2,1)S(1)}, bf16[1040,128]{1,0:T(8,128)(2,1)S(1)}, u32[]{:S(2)}, u32[]{:S(2)}) collective-permute-start(bf16[1040,128]{1,0:T(8,128)(2,1)S(1)} %get-tuple-element.257), channel_id=1, source_target_pairs={{1,0},{2,1},{3,2},{5,4},{6,5},{7,6},{9,8},{10,9},{11,10},{13,12},{... | collective-permute-start | bytes 798728 | tf_op jit(solution)/shard_map/ppermute | solution.py:86
  19.5 5.5 %collective-permute-start.4 = (bf16[1040,128]{1,0:T(8,128)(2,1)S(1)}, bf16[1040,128]{1,0:T(8,128)(2,1)S(1)}, u32[]{:S(2)}, u32[]{:S(2)}) collective-permute-start(bf16[1040,128]{1,0:T(8,128)(2,1)S(1)} %collective-permute-done), channel_id=1, source_target_pairs={{1,2},{2,3},{5,6},{6,7},{9,10},{10,11},{13,14},{14,15},{17,18},{18... | collective-permute-start | bytes 798728 | tf_op jit(solution)/shard_map/ppermute | solution.py:83
  23.6 9.0 %collective-permute-start.2 = (bf16[1040,128]{1,0:T(8,128)(2,1)S(1)}, bf16[1040,128]{1,0:T(8,128)(2,1)S(1)}, u32[]{:S(2)}, u32[]{:S(2)}) collective-permute-start(bf16[1040,128]{1,0:T(8,128)(2,1)S(1)} %collective-permute-done.1), channel_id=1, source_target_pairs={{1,0},{2,1},{5,4},{6,5},{9,8},{10,9},{13,12},{14,13},{17,16},{18,1... | collective-permute-start | bytes 798728 | tf_op jit(solution)/shard_map/ppermute | solution.py:86
  25.1 8.9 %collective-permute-start.5 = (bf16[1040,128]{1,0:T(8,128)(2,1)S(1)}, bf16[1040,128]{1,0:T(8,128)(2,1)S(1)}, u32[]{:S(2)}, u32[]{:S(2)}) collective-permute-start(bf16[1040,128]{1,0:T(8,128)(2,1)S(1)} %collective-permute-done.4), channel_id=1, source_target_pairs={{2,3},{6,7},{10,11},{14,15},{18,19},{22,23},{26,27},{30,31}} | collective-permute-start | bytes 798728 | tf_op jit(solution)/shard_map/ppermute | solution.py:83
  32.6 8.3 %collective-permute-start.3 = (bf16[1040,128]{1,0:T(8,128)(2,1)S(1)}, bf16[1040,128]{1,0:T(8,128)(2,1)S(1)}, u32[]{:S(2)}, u32[]{:S(2)}) collective-permute-start(bf16[1040,128]{1,0:T(8,128)(2,1)S(1)} %collective-permute-done.2), channel_id=1, source_target_pairs={{1,0},{5,4},{9,8},{13,12},{17,16},{21,20},{25,24},{29,28}} | collective-permute-start | bytes 798728 | tf_op jit(solution)/shard_map/ppermute | solution.py:86
  46.0 34.7 %copy-start.27 = (bf16[1968,128]{1,0:T(8,128)(2,1)}, bf16[1968,128]{1,0:T(8,128)(2,1)S(1)}, u32[]{:S(2)}) copy-start(bf16[1968,128]{1,0:T(8,128)(2,1)S(1)} %multiply_select_fusion.2) | copy-start | bytes 1511428
  46.0 12.0 %collective-permute-start.17 = (bf16[1968,128]{1,0:T(8,128)(2,1)S(1)}, bf16[1968,128]{1,0:T(8,128)(2,1)S(1)}, u32[]{:S(2)}, u32[]{:S(2)}) collective-permute-start(bf16[1968,128]{1,0:T(8,128)(2,1)S(1)} %multiply_select_fusion.2), channel_id=1, source_target_pairs={{1,0},{2,1},{3,2},{5,4},{6,5},{7,6},{9,8},{10,9},{11,10},{13,12},{... | collective-permute-start | bytes 1511432 | tf_op jit(solution)/shard_map/ppermute | solution.py:86
  47.3 12.0 %collective-permute-start.16 = (bf16[1968,128]{1,0:T(8,128)(2,1)S(1)}, bf16[1968,128]{1,0:T(8,128)(2,1)S(1)}, u32[]{:S(2)}, u32[]{:S(2)}) collective-permute-start(bf16[1968,128]{1,0:T(8,128)(2,1)S(1)} %multiply_select_fusion.2), channel_id=1, source_target_pairs={{0,1},{1,2},{2,3},{4,5},{5,6},{6,7},{8,9},{9,10},{10,11},{12,13},{... | collective-permute-start | bytes 1511432 | tf_op jit(solution)/shard_map/ppermute | solution.py:83
  58.0 11.7 %collective-permute-start.18 = (bf16[1968,128]{1,0:T(8,128)(2,1)S(1)}, bf16[1968,128]{1,0:T(8,128)(2,1)S(1)}, u32[]{:S(2)}, u32[]{:S(2)}) collective-permute-start(bf16[1968,128]{1,0:T(8,128)(2,1)S(1)} %collective-permute-done.17), channel_id=1, source_target_pairs={{1,0},{2,1},{5,4},{6,5},{9,8},{10,9},{13,12},{14,13},{17,16},{18,1... | collective-permute-start | bytes 1511432 | tf_op jit(solution)/shard_map/ppermute | solution.py:86
  59.3 11.6 %collective-permute-start.20 = (bf16[1968,128]{1,0:T(8,128)(2,1)S(1)}, bf16[1968,128]{1,0:T(8,128)(2,1)S(1)}, u32[]{:S(2)}, u32[]{:S(2)}) collective-permute-start(bf16[1968,128]{1,0:T(8,128)(2,1)S(1)} %collective-permute-done.16), channel_id=1, source_target_pairs={{1,2},{2,3},{5,6},{6,7},{9,10},{10,11},{13,14},{14,15},{17,18},{18... | collective-permute-start | bytes 1511432 | tf_op jit(solution)/shard_map/ppermute | solution.py:83
  69.6 10.8 %collective-permute-start.19 = (bf16[1968,128]{1,0:T(8,128)(2,1)S(1)}, bf16[1968,128]{1,0:T(8,128)(2,1)S(1)}, u32[]{:S(2)}, u32[]{:S(2)}) collective-permute-start(bf16[1968,128]{1,0:T(8,128)(2,1)S(1)} %collective-permute-done.18), channel_id=1, source_target_pairs={{1,0},{5,4},{9,8},{13,12},{17,16},{21,20},{25,24},{29,28}} | collective-permute-start | bytes 1511432 | tf_op jit(solution)/shard_map/ppermute | solution.py:86
  70.9 9.6 %collective-permute-start.21 = (bf16[1968,128]{1,0:T(8,128)(2,1)S(1)}, bf16[1968,128]{1,0:T(8,128)(2,1)S(1)}, u32[]{:S(2)}, u32[]{:S(2)}) collective-permute-start(bf16[1968,128]{1,0:T(8,128)(2,1)S(1)} %collective-permute-done.20), channel_id=1, source_target_pairs={{2,3},{6,7},{10,11},{14,15},{18,19},{22,23},{26,27},{30,31}} | collective-permute-start | bytes 1511432 | tf_op jit(solution)/shard_map/ppermute | solution.py:83
  82.7 39.3 %copy-start.67 = (s32[8]{0:T(128)S(1)}, s32[8]{0:T(128)}, u32[]{:S(2)}) copy-start(s32[8]{0:T(128)} %constant.59.clone) | copy-start | bytes 100
  82.7 157.3 %all-gather.7.cloned.1.call-start = ((), (), s32[]{:S(2)}) async-start(), calls=%async_computation.5 | async-start | bytes 6045696 | tf_op jit(solution)/shard_map/all_gather | solution.py:161
  84.5 74.4 %collective-permute-start.15 = (bf16[64,1024]{1,0:T(8,128)(2,1)}, bf16[64,1024]{1,0:T(8,128)(2,1)S(1)}, u32[]{:S(2)}, u32[]{:S(2)}) collective-permute-start(bf16[64,1024]{1,0:T(8,128)(2,1)} %get-tuple-element.246), channel_id=1, source_target_pairs={{1,0},{2,1},{3,2},{5,4},{6,5},{7,6},{9,8},{10,9},{11,10},{13,12},{... | collective-permute-start | bytes 393224 | tf_op jit(solution)/shard_map/ppermute | solution.py:201
  85.8 33.7 %collective-permute-start.6 = (bf16[4160,128]{1,0:T(8,128)(2,1)S(1)}, bf16[4160,128]{1,0:T(8,128)(2,1)S(1)}, u32[]{:S(2)}, u32[]{:S(2)}) collective-permute-start(bf16[4160,128]{1,0:T(8,128)(2,1)S(1)} %bitcast.152), channel_id=1, source_target_pairs={{0,8},{4,12},{8,0},{12,4},{16,24},{20,28},{24,16},{28,20},{1,9},{5... | collective-permute-start | bytes 3194888 | tf_op jit(solution)/shard_map/ppermute | solution.py:124
  87.7 39.2 %collective-permute-start.7 = (bf16[4160,128]{1,0:T(8,128)(2,1)S(1)}, bf16[4160,128]{1,0:T(8,128)(2,1)}, u32[]{:S(2)}, u32[]{:S(2)}) collective-permute-start(bf16[4160,128]{1,0:T(8,128)(2,1)S(1)} %bitcast.153), channel_id=1, source_target_pairs={{0,16},{4,20},{8,24},{12,28},{16,0},{20,4},{24,8},{28,12},{1,17},{... | collective-permute-start | bytes 3194888 | tf_op jit(solution)/shard_map/ppermute | solution.py:124
  120.4 18.7 %collective-permute-start.8 = (bf16[2080,128]{1,0:T(8,128)(2,1)}, bf16[2080,128]{1,0:T(8,128)(2,1)}, u32[]{:S(2)}, u32[]{:S(2)}) collective-permute-start(bf16[2080,128]{1,0:T(8,128)(2,1)} %slice.234), channel_id=1, source_target_pairs={{0,16},{4,20},{8,24},{12,28},{16,0},{20,4},{24,8},{28,12},{1,17},{... | collective-permute-start | bytes 1597448 | tf_op jit(solution)/shard_map/ppermute | solution.py:124
  124.9 29.0 %collective-permute-start.10 = (bf16[4160,128]{1,0:T(8,128)(2,1)S(1)}, bf16[4160,128]{1,0:T(8,128)(2,1)S(1)}, u32[]{:S(2)}, u32[]{:S(2)}) collective-permute-start(bf16[4160,128]{1,0:T(8,128)(2,1)S(1)} %bitcast.154), channel_id=1, source_target_pairs={{0,4},{4,0},{8,12},{12,8},{16,20},{20,16},{24,28},{28,24},{1,5},{5... | collective-permute-start | bytes 3194888 | tf_op jit(solution)/shard_map/ppermute | solution.py:124
  128.0 25.0 %collective-permute-start.9 = (bf16[2080,128]{1,0:T(8,128)(2,1)S(1)}, bf16[2080,128]{1,0:T(8,128)(2,1)S(1)}, u32[]{:S(2)}, u32[]{:S(2)}) collective-permute-start(bf16[2080,128]{1,0:T(8,128)(2,1)S(1)} %slice.235), channel_id=1, source_target_pairs={{0,8},{4,12},{8,0},{12,4},{16,24},{20,28},{24,16},{28,20},{1,9},{5... | collective-permute-start | bytes 1597448 | tf_op jit(solution)/shard_map/ppermute | solution.py:124
  128.6 30.3 %collective-permute-start.12 = (bf16[4160,128]{1,0:T(8,128)(2,1)}, bf16[4160,128]{1,0:T(8,128)(2,1)S(1)}, u32[]{:S(2)}, u32[]{:S(2)}) collective-permute-start(bf16[4160,128]{1,0:T(8,128)(2,1)} %collective-permute-done.7), channel_id=1, source_target_pairs={{0,4},{4,0},{8,12},{12,8},{16,20},{20,16},{24,28},{28,24},{1,5},{5... | collective-permute-start | bytes 3194888 | tf_op jit(solution)/shard_map/ppermute | solution.py:124
  139.1 19.7 %collective-permute-start.11 = (bf16[4160,128]{1,0:T(8,128)(2,1)S(1)}, bf16[4160,128]{1,0:T(8,128)(2,1)S(1)}, u32[]{:S(2)}, u32[]{:S(2)}) collective-permute-start(bf16[4160,128]{1,0:T(8,128)(2,1)S(1)} %collective-permute-done.6), channel_id=1, source_target_pairs={{0,4},{4,0},{8,12},{12,8},{16,20},{20,16},{24,28},{28,24},{1,5},{5... | collective-permute-start | bytes 3194888 | tf_op jit(solution)/shard_map/ppermute | solution.py:124
  153.1 5.8 %collective-permute-start.13 = (bf16[4160,128]{1,0:T(8,128)(2,1)S(1)}, bf16[4160,128]{1,0:T(8,128)(2,1)S(1)}, u32[]{:S(2)}, u32[]{:S(2)}) collective-permute-start(bf16[4160,128]{1,0:T(8,128)(2,1)S(1)} %constant_dynamic-update-slice_fusion), channel_id=1, source_target_pairs={{0,4},{4,0},{8,12},{12,8},{16,20},{20,16},{24,28},{28,24},{1,5},{5... | collective-permute-start | bytes 3194888 | tf_op jit(solution)/shard_map/ppermute | solution.py:124
  153.9 8.3 %collective-permute-start.14 = (bf16[64,1024]{1,0:T(8,128)(2,1)S(1)}, bf16[64,1024]{1,0:T(8,128)(2,1)S(1)}, u32[]{:S(2)}, u32[]{:S(2)}) collective-permute-start(bf16[64,1024]{1,0:T(8,128)(2,1)S(1)} %copy-done.60), channel_id=1, source_target_pairs={{0,1},{1,2},{2,3},{4,5},{5,6},{6,7},{8,9},{9,10},{10,11},{12,13},{... | collective-permute-start | bytes 393224 | tf_op jit(solution)/shard_map/ppermute | solution.py:201
  178.2 208.9 %reduce-scatter.5.cloned.1.call-start = ((), (), s32[]{:S(2)}) async-start(), calls=%async_computation.3 | async-start | bytes 6045696 | tf_op jit(solution)/shard_map/reduce_scatter | solution.py:171
  239.8 147.3 %reduce-scatter.3.cloned.1.call-start = ((), (), s32[]{:S(2)}) async-start(), calls=%async_computation.2 | async-start | bytes 12091392 | tf_op jit(solution)/shard_map/reduce_scatter | solution.py:171
  320.5 31.9 %collective-permute-start.22 = (bf16[4,2,1024,128]{3,2,1,0:T(8,128)(2,1)}, bf16[4,2,1024,128]{3,2,1,0:T(8,128)(2,1)S(1)}, u32[]{:S(2)}, u32[]{:S(2)}) collective-permute-start(bf16[4,2,1024,128]{3,2,1,0:T(8,128)(2,1)} %get-tuple-element.102), channel_id=1, source_target_pairs={{0,4},{4,0},{8,12},{12,8},{16,20},{20,16},{24,28},{28,24},{1,5},{5... | collective-permute-start | bytes 6291464 | tf_op jit(solution)/shard_map/ppermute | solution.py:124
  349.6 28.1 %collective-permute-start.25 = (bf16[4,2,1024,128]{3,2,1,0:T(8,128)(2,1)}, bf16[4,2,1024,128]{3,2,1,0:T(8,128)(2,1)S(1)}, u32[]{:S(2)}, u32[]{:S(2)}) collective-permute-start(bf16[4,2,1024,128]{3,2,1,0:T(8,128)(2,1)} %get-tuple-element.116), channel_id=1, source_target_pairs={{0,4},{4,0},{8,12},{12,8},{16,20},{20,16},{24,28},{28,24},{1,5},{5... | collective-permute-start | bytes 6291464 | tf_op jit(solution)/shard_map/ppermute | solution.py:124
  356.8 21.5 %collective-permute-start.26 = (bf16[1024,128]{1,0:T(8,128)(2,1)S(1)}, bf16[1024,128]{1,0:T(8,128)(2,1)S(1)}, u32[]{:S(2)}, u32[]{:S(2)}) collective-permute-start(bf16[1024,128]{1,0:T(8,128)(2,1)S(1)} %get-tuple-element.121), channel_id=1, source_target_pairs={{0,8},{4,12},{8,0},{12,4},{16,24},{20,28},{24,16},{28,20},{1,9},{5... | collective-permute-start | bytes 786440 | tf_op jit(solution)/shard_map/ppermute | solution.py:124
  357.9 22.2 %collective-permute-start.27 = (bf16[1024,128]{1,0:T(8,128)(2,1)}, bf16[1024,128]{1,0:T(8,128)(2,1)S(1)}, u32[]{:S(2)}, u32[]{:S(2)}) collective-permute-start(bf16[1024,128]{1,0:T(8,128)(2,1)} %get-tuple-element.123), channel_id=1, source_target_pairs={{0,16},{4,20},{8,24},{12,28},{16,0},{20,4},{24,8},{28,12},{1,17},{... | collective-permute-start | bytes 786440 | tf_op jit(solution)/shard_map/ppermute | solution.py:124
  359.8 29.6 %collective-permute-start.23 = (bf16[4,2,64,256]{3,2,1,0:T(8,128)(2,1)}, bf16[4,2,64,256]{3,2,1,0:T(8,128)(2,1)S(1)}, u32[]{:S(2)}, u32[]{:S(2)}) collective-permute-start(bf16[4,2,64,256]{3,2,1,0:T(8,128)(2,1)} %pad_maximum_fusion.3), channel_id=1, source_target_pairs={{0,1},{1,2},{2,3},{4,5},{5,6},{6,7},{8,9},{9,10},{10,11},{12,13},{... | collective-permute-start | bytes 786440 | tf_op jit(solution)/shard_map/ppermute | solution.py:201
  364.7 25.4 %collective-permute-start.24 = (bf16[4,2,64,256]{3,2,1,0:T(8,128)(2,1)}, bf16[4,2,64,256]{3,2,1,0:T(8,128)(2,1)S(1)}, u32[]{:S(2)}, u32[]{:S(2)}) collective-permute-start(bf16[4,2,64,256]{3,2,1,0:T(8,128)(2,1)} %pad_maximum_fusion.4), channel_id=1, source_target_pairs={{1,0},{2,1},{3,2},{5,4},{6,5},{7,6},{9,8},{10,9},{11,10},{13,12},{... | collective-permute-start | bytes 786440 | tf_op jit(solution)/shard_map/ppermute | solution.py:201
  377.7 17.2 %collective-permute-start.29 = (bf16[1024,128]{1,0:T(8,128)(2,1)S(1)}, bf16[1024,128]{1,0:T(8,128)(2,1)S(1)}, u32[]{:S(2)}, u32[]{:S(2)}) collective-permute-start(bf16[1024,128]{1,0:T(8,128)(2,1)S(1)} %get-tuple-element.130), channel_id=1, source_target_pairs={{0,8},{4,12},{8,0},{12,4},{16,24},{20,28},{24,16},{28,20},{1,9},{5... | collective-permute-start | bytes 786440 | tf_op jit(solution)/shard_map/ppermute | solution.py:124
  378.3 18.2 %collective-permute-start.32 = (bf16[1024,128]{1,0:T(8,128)(2,1)S(1)}, bf16[1024,128]{1,0:T(8,128)(2,1)}, u32[]{:S(2)}, u32[]{:S(2)}) collective-permute-start(bf16[1024,128]{1,0:T(8,128)(2,1)S(1)} %get-tuple-element.134), channel_id=1, source_target_pairs={{0,16},{4,20},{8,24},{12,28},{16,0},{20,4},{24,8},{28,12},{1,17},{... | collective-permute-start | bytes 786440 | tf_op jit(solution)/shard_map/ppermute | solution.py:124
  386.8 10.2 %collective-permute-start.30 = (bf16[1024,128]{1,0:T(8,128)(2,1)}, bf16[1024,128]{1,0:T(8,128)(2,1)S(1)}, u32[]{:S(2)}, u32[]{:S(2)}) collective-permute-start(bf16[1024,128]{1,0:T(8,128)(2,1)} %get-tuple-element.131), channel_id=1, source_target_pairs={{0,16},{4,20},{8,24},{12,28},{16,0},{20,4},{24,8},{28,12},{1,17},{... | collective-permute-start | bytes 786440 | tf_op jit(solution)/shard_map/ppermute | solution.py:124
  389.2 35.6 %copy-start.24 = (bf16[4,1968,128]{2,1,0:T(8,128)(2,1)}, bf16[4,1968,128]{2,1,0:T(8,128)(2,1)S(1)}, u32[]{:S(2)}) copy-start(bf16[4,1968,128]{2,1,0:T(8,128)(2,1)S(1)} %multiply_select_fusion) | copy-start | bytes 6045700
  389.3 25.8 %collective-permute-start.36 = (bf16[1968,128]{1,0:T(8,128)(2,1)S(1)}, bf16[1968,128]{1,0:T(8,128)(2,1)S(1)}, u32[]{:S(2)}, u32[]{:S(2)}) collective-permute-start(bf16[1968,128]{1,0:T(8,128)(2,1)S(1)} %get-tuple-element.240), channel_id=1, source_target_pairs={{3,2},{7,6},{11,10},{15,14},{19,18},{23,22},{27,26},{31,30}} | collective-permute-start | bytes 1511432 | tf_op jit(solution)/shard_map/ppermute | solution.py:105
  390.2 25.0 %collective-permute-start.35 = (bf16[1968,128]{1,0:T(8,128)(2,1)S(1)}, bf16[1968,128]{1,0:T(8,128)(2,1)S(1)}, u32[]{:S(2)}, u32[]{:S(2)}) collective-permute-start(bf16[1968,128]{1,0:T(8,128)(2,1)S(1)} %get-tuple-element.241), channel_id=1, source_target_pairs={{0,1},{4,5},{8,9},{12,13},{16,17},{20,21},{24,25},{28,29}} | collective-permute-start | bytes 1511432 | tf_op jit(solution)/shard_map/ppermute | solution.py:104
  394.9 20.2 %collective-permute-start.31 = (bf16[1024,128]{1,0:T(8,128)(2,1)S(1)}, bf16[1024,128]{1,0:T(8,128)(2,1)S(1)}, u32[]{:S(2)}, u32[]{:S(2)}) collective-permute-start(bf16[1024,128]{1,0:T(8,128)(2,1)S(1)} %copy-done.65), channel_id=1, source_target_pairs={{0,8},{4,12},{8,0},{12,4},{16,24},{20,28},{24,16},{28,20},{1,9},{5... | collective-permute-start | bytes 786440 | tf_op jit(solution)/shard_map/ppermute | solution.py:124
  396.5 18.6 %collective-permute-start.33 = (bf16[1024,128]{1,0:T(8,128)(2,1)S(1)}, bf16[1024,128]{1,0:T(8,128)(2,1)S(1)}, u32[]{:S(2)}, u32[]{:S(2)}) collective-permute-start(bf16[1024,128]{1,0:T(8,128)(2,1)S(1)} %get-tuple-element.136), channel_id=1, source_target_pairs={{0,8},{4,12},{8,0},{12,4},{16,24},{20,28},{24,16},{28,20},{1,9},{5... | collective-permute-start | bytes 786440 | tf_op jit(solution)/shard_map/ppermute | solution.py:124
  397.0 18.1 %collective-permute-start.34 = (bf16[1024,128]{1,0:T(8,128)(2,1)S(1)}, bf16[1024,128]{1,0:T(8,128)(2,1)S(1)}, u32[]{:S(2)}, u32[]{:S(2)}) collective-permute-start(bf16[1024,128]{1,0:T(8,128)(2,1)S(1)} %copy-done.64), channel_id=1, source_target_pairs={{0,16},{4,20},{8,24},{12,28},{16,0},{20,4},{24,8},{28,12},{1,17},{... | collective-permute-start | bytes 786440 | tf_op jit(solution)/shard_map/ppermute | solution.py:124
  418.0 29.3 %copy-start.59 = (f32[128,256]{1,0:T(8,128)S(1)}, f32[128,256]{1,0:T(8,128)}, u32[]{:S(2)}) copy-start(f32[128,256]{1,0:T(8,128)} %param.29) | copy-start | bytes 393220
  419.2 1.2 collective-permute-start.50
  420.5 3.7 collective-permute-start.51
  420.7 10.3 %collective-permute-start.28 = (bf16[1024,128]{1,0:T(8,128)(2,1)S(1)}, bf16[1024,128]{1,0:T(8,128)(2,1)S(1)}, u32[]{:S(2)}, u32[]{:S(2)}) collective-permute-start(bf16[1024,128]{1,0:T(8,128)(2,1)S(1)} %get-tuple-element.128), channel_id=1, source_target_pairs={{0,8},{4,12},{8,0},{12,4},{16,24},{20,28},{24,16},{28,20},{1,9},{5... | collective-permute-start | bytes 786440 | tf_op jit(solution)/shard_map/ppermute | solution.py:124
  422.2 10.6 %collective-permute-start.39 = (bf16[1024,128]{1,0:T(8,128)(2,1)S(1)}, bf16[1024,128]{1,0:T(8,128)(2,1)S(1)}, u32[]{:S(2)}, u32[]{:S(2)}) collective-permute-start(bf16[1024,128]{1,0:T(8,128)(2,1)S(1)} %get-tuple-element.145), channel_id=1, source_target_pairs={{0,16},{4,20},{8,24},{12,28},{16,0},{20,4},{24,8},{28,12},{1,17},{... | collective-permute-start | bytes 786440 | tf_op jit(solution)/shard_map/ppermute | solution.py:124
  422.7 19.5 %collective-permute-start.37 = (bf16[1024,128]{1,0:T(8,128)(2,1)S(1)}, bf16[1024,128]{1,0:T(8,128)(2,1)S(1)}, u32[]{:S(2)}, u32[]{:S(2)}) collective-permute-start(bf16[1024,128]{1,0:T(8,128)(2,1)S(1)} %get-tuple-element.142), channel_id=1, source_target_pairs={{0,16},{4,20},{8,24},{12,28},{16,0},{20,4},{24,8},{28,12},{1,17},{... | collective-permute-start | bytes 786440 | tf_op jit(solution)/shard_map/ppermute | solution.py:124
  424.2 4.8 collective-permute-start.52
  427.2 25.0 %collective-permute-start.41 = (bf16[1968,128]{1,0:T(8,128)(2,1)}, bf16[1968,128]{1,0:T(8,128)(2,1)S(1)}, u32[]{:S(2)}, u32[]{:S(2)}) collective-permute-start(bf16[1968,128]{1,0:T(8,128)(2,1)} %get-tuple-element.238), channel_id=1, source_target_pairs={{2,1},{3,2},{6,5},{7,6},{10,9},{11,10},{14,13},{15,14},{18,17},{19... | collective-permute-start | bytes 1511432 | tf_op jit(solution)/shard_map/ppermute | solution.py:105
  429.0 23.3 %collective-permute-start.40 = (bf16[1968,128]{1,0:T(8,128)(2,1)}, bf16[1968,128]{1,0:T(8,128)(2,1)}, u32[]{:S(2)}, u32[]{:S(2)}) collective-permute-start(bf16[1968,128]{1,0:T(8,128)(2,1)} %get-tuple-element.239), channel_id=1, source_target_pairs={{0,1},{1,2},{4,5},{5,6},{8,9},{9,10},{12,13},{13,14},{16,17},{17,1... | collective-permute-start | bytes 1511432 | tf_op jit(solution)/shard_map/ppermute | solution.py:104
  431.1 9.8 %collective-permute-start.53 = (f32[2,128]{1,0:T(2,128)S(1)}, f32[2,128]{1,0:T(2,128)S(1)}, u32[]{:S(2)}, u32[]{:S(2)}) collective-permute-start(f32[2,128]{1,0:T(2,128)S(1)} %slice_add_fusion.2), channel_id=1, source_target_pairs={{0,1},{1,0},{2,3},{3,2},{4,5},{5,4},{6,7},{7,6},{8,9},{9,8},{10,11... | collective-permute-start | bytes 3080 | tf_op jit(solution)/shard_map/ppermute | solution.py:119
  432.8 19.5 %collective-permute-start.38 = (bf16[1024,128]{1,0:T(8,128)(2,1)S(1)}, bf16[1024,128]{1,0:T(8,128)(2,1)S(1)}, u32[]{:S(2)}, u32[]{:S(2)}) collective-permute-start(bf16[1024,128]{1,0:T(8,128)(2,1)S(1)} %get-tuple-element.144), channel_id=1, source_target_pairs={{0,8},{4,12},{8,0},{12,4},{16,24},{20,28},{24,16},{28,20},{1,9},{5... | collective-permute-start | bytes 786440 | tf_op jit(solution)/shard_map/ppermute | solution.py:124
  440.9 14.0 %collective-permute-start.45 = (bf16[1024,128]{1,0:T(8,128)(2,1)S(1)}, bf16[1024,128]{1,0:T(8,128)(2,1)}, u32[]{:S(2)}, u32[]{:S(2)}) collective-permute-start(bf16[1024,128]{1,0:T(8,128)(2,1)S(1)} %get-tuple-element.148), channel_id=1, source_target_pairs={{3,2},{7,6},{11,10},{15,14},{19,18},{23,22},{27,26},{31,30}} | collective-permute-start | bytes 786440 | tf_op jit(solution)/shard_map/ppermute | solution.py:105
  442.2 12.6 %collective-permute-start.42 = (bf16[1024,128]{1,0:T(8,128)(2,1)S(1)}, bf16[1024,128]{1,0:T(8,128)(2,1)}, u32[]{:S(2)}, u32[]{:S(2)}) collective-permute-start(bf16[1024,128]{1,0:T(8,128)(2,1)S(1)} %get-tuple-element.150), channel_id=1, source_target_pairs={{0,1},{4,5},{8,9},{12,13},{16,17},{20,21},{24,25},{28,29}} | collective-permute-start | bytes 786440 | tf_op jit(solution)/shard_map/ppermute | solution.py:104
  452.3 15.1 %collective-permute-start.54 = (f32[2,128]{1,0:T(2,128)S(1)}, f32[2,128]{1,0:T(2,128)S(1)}, u32[]{:S(2)}, u32[]{:S(2)}) collective-permute-start(f32[2,128]{1,0:T(2,128)S(1)} %add.196), channel_id=1, source_target_pairs={{0,2},{1,3},{2,0},{3,1},{4,6},{5,7},{6,4},{7,5},{8,10},{9,11},{10,... | collective-permute-start | bytes 3080 | tf_op jit(solution)/shard_map/ppermute | solution.py:119
  456.1 11.9 %collective-permute-start.43 = (bf16[1024,128]{1,0:T(8,128)(2,1)S(1)}, bf16[1024,128]{1,0:T(8,128)(2,1)S(1)}, u32[]{:S(2)}, u32[]{:S(2)}) collective-permute-start(bf16[1024,128]{1,0:T(8,128)(2,1)S(1)} %get-tuple-element.259), channel_id=1, source_target_pairs={{0,1},{1,2},{4,5},{5,6},{8,9},{9,10},{12,13},{13,14},{16,17},{17,1... | collective-permute-start | bytes 786440 | tf_op jit(solution)/shard_map/ppermute | solution.py:104
  457.8 15.4 %collective-permute-start.46 = (bf16[1024,128]{1,0:T(8,128)(2,1)S(1)}, bf16[1024,128]{1,0:T(8,128)(2,1)S(1)}, u32[]{:S(2)}, u32[]{:S(2)}) collective-permute-start(bf16[1024,128]{1,0:T(8,128)(2,1)S(1)} %get-tuple-element.260), channel_id=1, source_target_pairs={{2,1},{3,2},{6,5},{7,6},{10,9},{11,10},{14,13},{15,14},{18,17},{19... | collective-permute-start | bytes 786440 | tf_op jit(solution)/shard_map/ppermute | solution.py:105
  459.8 17.5 %collective-permute-start.48 = (bf16[1968,128]{1,0:T(8,128)(2,1)S(1)}, bf16[1968,128]{1,0:T(8,128)(2,1)S(1)}, u32[]{:S(2)}, u32[]{:S(2)}) collective-permute-start(bf16[1968,128]{1,0:T(8,128)(2,1)S(1)} %get-tuple-element.236), channel_id=1, source_target_pairs={{0,1},{1,2},{2,3},{4,5},{5,6},{6,7},{8,9},{9,10},{10,11},{12,13},{... | collective-permute-start | bytes 1511432 | tf_op jit(solution)/shard_map/ppermute | solution.py:104
  466.0 16.0 %collective-permute-start.49 = (bf16[1968,128]{1,0:T(8,128)(2,1)S(1)}, bf16[1968,128]{1,0:T(8,128)(2,1)S(1)}, u32[]{:S(2)}, u32[]{:S(2)}) collective-permute-start(bf16[1968,128]{1,0:T(8,128)(2,1)S(1)} %get-tuple-element.237), channel_id=1, source_target_pairs={{1,0},{2,1},{3,2},{5,4},{6,5},{7,6},{9,8},{10,9},{11,10},{13,12},{... | collective-permute-start | bytes 1511432 | tf_op jit(solution)/shard_map/ppermute | solution.py:105
  468.0 17.1 %collective-permute-start.44 = (bf16[1024,128]{1,0:T(8,128)(2,1)S(1)}, bf16[1024,128]{1,0:T(8,128)(2,1)S(1)}, u32[]{:S(2)}, u32[]{:S(2)}) collective-permute-start(bf16[1024,128]{1,0:T(8,128)(2,1)S(1)} %add_convert_fusion.3), channel_id=1, source_target_pairs={{0,1},{1,2},{2,3},{4,5},{5,6},{6,7},{8,9},{9,10},{10,11},{12,13},{... | collective-permute-start | bytes 786440 | tf_op jit(solution)/shard_map/ppermute | solution.py:104
  473.3 11.8 %collective-permute-start.47 = (bf16[1024,128]{1,0:T(8,128)(2,1)S(1)}, bf16[1024,128]{1,0:T(8,128)(2,1)S(1)}, u32[]{:S(2)}, u32[]{:S(2)}) collective-permute-start(bf16[1024,128]{1,0:T(8,128)(2,1)S(1)} %add_convert_fusion.2), channel_id=1, source_target_pairs={{1,0},{2,1},{3,2},{5,4},{6,5},{7,6},{9,8},{10,9},{11,10},{13,12},{... | collective-permute-start | bytes 786440 | tf_op jit(solution)/shard_map/ppermute | solution.py:105
  (63 other events, 460.8 us)
Sparse Core Ops, SparseCore 0:
  82.8 88.1 all-gather.4
  178.3 40.8 all-gather.6
  239.9 56.7 reduce-scatter.4
  300.1 83.8 reduce-scatter.2

commit v6 on v5

--- a/solution.py
+++ b/solution.py
@@ -98,6 +98,14 @@
     return values if token is None else jnp.where(token[0, 0] == 0, values, 0.0 * values)
 
 
+def gather_hop(from_before, from_after, step):
+    size = lax.axis_size("tensor")
+    return (
+        lax.ppermute(from_before, "tensor", [(n, n + 1) for n in range(step - 1, size - 1)]),
+        lax.ppermute(from_after, "tensor", [(n, n - 1) for n in range(1, size - step + 1)]),
+    )
+
+
 def line_hop(to_after, to_before, step):
     size = lax.axis_size("tensor")
     return (
@@ -111,13 +119,16 @@
 
 
 def gain_scatter(gains):
+    steps = []
     for mask in [1, 4, 2] + far_bits()[::-1]:
         half = gains.shape[1] // 2
-        gains = gains[:, :half] + flip(gains[:, half:], mask)
+        steps.append(flip(gains[:, half:], mask))
+        gains = gains[:, :half] + steps[-1]
     size = lax.axis_size("tensor")
     for mask in (1 << n for n in range(size.bit_length() - 1)):
-        gains = gains + lax.ppermute(gains, "tensor", [(n, n ^ mask) for n in range(size)])
-    return gains
+        steps.append(lax.ppermute(gains, "tensor", [(n, n ^ mask) for n in range(size)]))
+        gains = gains + steps[-1]
+    return (gains, steps)
 
 
 def flip(rows, mask):
@@ -137,10 +148,17 @@
     return (piece, flip(piece, 2), flip(piece, 4))
 
 
-def gather_far(near):
+def gather_far_hop(near, token=None):
     piece, by_x, by_y = near
     half = piece.shape[0] // 2
-    far = jnp.concatenate([flip(by_x[:half], 4), flip(by_y[half:], 2)])
+    return (flip(tied(by_x[:half], token), 4), flip(tied(by_y[half:], token), 2))
+
+
+def gather_far(near, arrived=None, token=None):
+    piece, by_x, by_y = near
+    if arrived is None:
+        arrived = gather_far_hop(near)
+    far = tied(jnp.concatenate(arrived), token)
     mine = [piece, by_x, by_y, far]
     return mine + [flip(part, 1) for part in mine]
 
@@ -384,7 +402,7 @@
     return (
         (PIECES, parts, rows, LANES),
         jnp.bfloat16,
-        pl.BlockSpec((PIECES, 1, rows, LANES), lambda n, *_: (0, n, 0, 0)),
+        pl.BlockSpec((PIECES, 1, rows, LANES), lambda n, order: (0, order[PIECES + n], 0, 0)),
     )
 
 
@@ -782,14 +800,31 @@
         order = jnp.arange(PIECES, dtype=jnp.int32)
         hidden, cot_in = to_relative(hidden_in), to_relative(cotangent)
 
+    place = lax.axis_index("tensor").astype(jnp.int32)
+    owners = (place + size - jnp.arange(size, dtype=jnp.int32)) % size
+    order = jnp.concatenate([order, owners])
     edges = (shift(hidden[-HALF:], 1), shift(hidden[:HALF], -1))
-    place = lax.axis_index("tensor").astype(jnp.int32)
-    place_rows = jnp.full((8, LANES), place)
+    zeros = jnp.zeros((8, LANES), jnp.int32)
     heads_near = gather_near(heads_slab, place)
-    line_token = held_back(place_rows * 0, heads_near[:1])
-    ffn_line = line_gather(tied(ffn_slab, line_token), place)
+    ffn_slab = tied(ffn_slab, held_back(zeros, heads_near[:1]))
+    first = gather_hop(ffn_slab, ffn_slab, 1)
+    token = held_back(zeros, (*heads_near[1:], *first))
+    heads_far = gather_far_hop(heads_near, token)
+    second = gather_hop(tied(first[0], token), tied(first[1], token), 2)
+    token = held_back(zeros, (*heads_far, *second))
+    third = gather_hop(tied(second[0], token), tied(second[1], token), 3)
+    ffn_line = jnp.stack(
+        [
+            ffn_slab,
+            jnp.where(place >= 1, first[0], third[1]),
+            jnp.where(place >= 2, second[0], second[1]),
+            jnp.where(place >= 3, third[0], first[1]),
+        ]
+    )
     in_all = gather_dp(ffn_line[:, : 2 * hidden_wide])
-    heads_pieces = [piece.reshape(size, -1, LANES) for piece in gather_far(heads_near)]
+    heads_pieces = [
+        piece.reshape(size, -1, LANES) for piece in gather_far(heads_near, heads_far, token)
+    ]
     gains = jnp.concatenate(
         [piece[0, head_rows : head_rows + 8] for piece in heads_pieces], axis=1
     ).astype(full)
@@ -858,7 +893,8 @@
         [],
         matmul * FF,
     )
-    down_sum = scatter_dp(down_grads)
+    down_line = scatter_dp(down_grads)
+    down_sum = lax.psum_scatter(down_line, "tensor", scatter_dimension=0, tiled=False)
     half = size // 2
     in_grads, gate_grad, up_grad, token = run(
         in_grad_kernel,
@@ -870,7 +906,8 @@
         [pltpu.VMEM((D, row_count), low), pltpu.VMEM((hidden_wide, row_count), full)],
         3 * matmul * FF,
     )
-    in_sum = scatter_dp(in_grads)
+    in_line = scatter_dp(in_grads)
+    in_sum = lax.psum_scatter(in_line, "tensor", scatter_dimension=0, tiled=False)
     grad_middle, grad_low, gain_two, token = run(
         middle_grad_kernel,
         "middle_grad",
@@ -934,7 +971,7 @@
     *odd_outs, odd_queries, odd_pairs, token = attend_grad(ODD, half, "attend_grad_odd", ())
     odd_core = core_hop(odd_outs)
     *even_outs, even_queries, even_pairs, token = attend_grad(
-        EVEN, half, "attend_grad_even", (token,)
+        EVEN, half, "attend_grad_even", (token, down_line)
     )
     even_core = core_hop(even_outs)
     odd, token = blend("sums_one", core_sums(*odd_core), (token,))
@@ -943,23 +980,6 @@
     edge_after = jnp.stack([pair[:, -HALF:] for pair in pairs[-1:] + pairs[:-1]])
     edge_before = jnp.stack([pair[:, :HALF] for pair in pairs[1:] + pairs[:1]])
     edges = (shift(edge_after, 1), shift(edge_before, -1))
-    hidden_out, token = run(
-        down_kernel,
-        "down",
-        [order, (middle, None), turned_block(active, hidden_wide)]
-        + gathered(down_all, hidden_wide),
-        [(tokens, low, None)],
-        [pltpu.VMEM(tokens, full)],
-        matmul * FF,
-        after=(token,),
-    )
-    (*even, odd_y, odd_x), token = blend(
-        "sums_two", core_sums(*even_core) + far_sums(odd, odd_far), (token,)
-    )
-    even_far = far_hop(even)
-    odd_near = near_hop(odd, (odd_y, odd_x))
-    ffn_parts = tied(jnp.concatenate([in_sum, down_sum], axis=1), token)
-    ffn_arrived = line_hop(ffn_parts[1], ffn_parts[size - 1], size - 1)
     grad_input, gain_one, token = run(
         input_grad_kernel,
         "input_grad",
@@ -973,10 +993,26 @@
         after=(token,),
         steps=half,
     )
+    (*even, odd_y, odd_x), token = blend(
+        "sums_two", core_sums(*even_core) + far_sums(odd, odd_far), (token, in_line)
+    )
+    even_far = far_hop(even)
+    odd_near = near_hop(odd, (odd_y, odd_x))
+    gain_sum, gain_steps = gain_scatter(tied(jnp.concatenate([gain_one[:1], gain_two[:1]]), token))
+    hidden_out, token = run(
+        down_kernel,
+        "down",
+        [order, (middle, None), turned_block(active, hidden_wide)]
+        + gathered(down_all, hidden_wide),
+        [(tokens, low, None)],
+        [pltpu.VMEM(tokens, full)],
+        matmul * FF,
+        after=(token,),
+    )
     (*odd_parts, even_y, even_x), token = blend(
         "sums_three",
         near_sums(odd, odd_near) + far_sums(even, even_far),
-        (token, *ffn_arrived),
+        (token, down_sum, gain_steps[1]),
     )
     even_near = near_hop(even, (even_y, even_x))
     odd_parts = [far_scatter(part) for part in odd_parts]
@@ -987,23 +1023,18 @@
             to_after, to_before = add_low(to_after, arrived[0]), add_low(to_before, arrived[1])
         return line_hop(to_after, to_before, step)
 
-    ffn_arrived = line_round(ffn_parts, 2, ffn_arrived)
-    three_token = token
-    even_parts, token = blend("sums_four", near_sums(even, even_near), (token, *ffn_arrived))
-    ffn_total = line_end(ffn_parts[0], line_round(ffn_parts, 1, ffn_arrived))
+    even_parts, token = blend("sums_four", near_sums(even, even_near), (token, in_sum, gain_steps[3]))
     even_parts = [far_scatter(part) for part in even_parts]
     heads_parts = [even_parts[0], odd_parts[0], even_parts[1], odd_parts[1]]
     heads_arrived = None
     for step in range(size - 1, 0, -1):
         heads_arrived = line_round(heads_parts, step, heads_arrived)
     heads_total = line_end(heads_parts[0], heads_arrived)
-    gain_sum = gain_scatter(tied(jnp.concatenate([gain_one[:1], gain_two[:1]]), three_token))
     if dp_size != PIECES:
         hidden_out, grad_input = to_relative(hidden_out, True), to_relative(grad_input, True)
 
-    ffn_total = ffn_total.T
-    in_sum = ffn_total[:, : 2 * hidden_wide].reshape(w_in.shape)
-    down_sum = ffn_total[:, 2 * hidden_wide :]
+    in_sum = in_sum.astype(full).T.reshape(w_in.shape)
+    down_sum = down_sum.astype(full).T
     heads_sum = heads_total.T
     qkv_sum = jnp.concatenate(
         [

time: 508 us -> 491 us (0.967)
  starting transfers between devices: 85.9 us -> 70.1 us
    ppermute x25, waiting for transfers between devices: 57 us -> 7.8 us  [flip(): lax.ppermute(rows, 'dp', [(n, n ^ mask) for n in range(lax.axis_size('dp'...]
    reduce_scatter x2, waiting for transfers between devices: 0.01 us -> 36 us  [scatter_dp(): return lax.psum_scatter(grads, 'dp', scatter_dimension=0, tiled=False)]
    ppermute x0 -> x6, waiting for transfers between devices: none -> 25 us  [the longest x3 23.8 us: gather_hop(): lax.ppermute(from_after, 'tensor', [(n, n - 1) for n in range(1, size - s...]
    ppermute x6 -> x3, waiting for transfers between devices: 41.8 us -> 17.4 us  [line_gather(): lax.ppermute(from_after[-1], 'tensor', [(n, n - 1) for n in range(1, size...]
    ppermute x6 -> x3, starting transfers between devices: 25 us -> 12 us  [line_hop(): lax.ppermute(to_after, 'tensor', [(n, n + 1) for n in range(size - step)])]
    all_gather x2, waiting for transfers between devices: 0.04 us -> 11 us  [gather_dp(): return lax.all_gather(piece, 'dp', axis=0)]
    ppermute x0 -> x6, starting transfers between devices: none -> 9.97 us  [the longest x3 6.1 us: gather_hop(): lax.ppermute(from_before, 'tensor', [(n, n + 1) for n in range(step - 1,...]
    ppermute x4, waiting for transfers between devices: 3.2 us -> 10.4 us  [shift(): return lax.ppermute(rows, 'tensor', pairs)]
  transfers between devices with their start and end apart: 59 -> 55, of which waited for: 17 -> 22; matrix products, arithmetic and copies ran while one was open for 6% -> 4% of each run, Pallas kernels for 43% -> 46%
where the time goes in v6:
time: 491 us; the launch traced here: 484 us
  Pallas kernels  223 us (45%)
  waiting for transfers between devices  121 us (25%)
  starting transfers between devices  70.1 us (14%)
  local copies, waits for them, and re-layouts  36.2 us (7%)
  between operations  19.3 us (4%)
  other arithmetic  13.7 us (3%)
    pallas_call x11, Pallas kernels, run(): pl.pallas_call(body, grid_spec=pltpu.PrefetchScalarGridSpec(num_scalar_pr...  209 us
    reduce_scatter x2, waiting for transfers between devices, scatter_dp(): return lax.psum_scatter(grads, 'dp', scatter_dimension=0, tiled=False)  36 us
    unnamed x170, local copies, waits for them, and re-layouts  25.2 us
    ppermute x3, waiting for transfers between devices, gather_hop(): lax.ppermute(from_after, 'tensor', [(n, n - 1) for n in range(1, size - s...  23.8 us
    ppermute x25, starting transfers between devices, flip(): lax.ppermute(rows, 'dp', [(n, n ^ mask) for n in range(lax.axis_size('dp'...  22.4 us
    ppermute x3, waiting for transfers between devices, line_gather(): lax.ppermute(from_after[-1], 'tensor', [(n, n - 1) for n in range(1, size...  17.4 us
    ppermute x3, starting transfers between devices, line_hop(): lax.ppermute(to_after, 'tensor', [(n, n + 1) for n in range(size - step)])  12 us
    all_gather x2, waiting for transfers between devices, gather_dp(): return lax.all_gather(piece, 'dp', axis=0)  11 us
  transfers between devices with their start and end apart: 55, of which 22 were waited for; matrix products, arithmetic and copies ran while one was open for 4% of the time, Pallas kernels for 46%

profile of v6, /device:TPU:0, one launch (start us, length us, event | category | flops | bytes accessed | tf_op | source)
XLA Modules:
  0.0 483.9 jit_solution(2899468949180305780)
XLA Ops:
  9.2 4.9 %collective-permute-start = (bf16[1040,128]{1,0:T(8,128)(2,1)S(1)}, bf16[1040,128]{1,0:T(8,128)(2,1)S(1)}, u32[]{:S(2)}, u32[]{:S(2)}) collective-permute-start(bf16[1040,128]{1,0:T(8,128)(2,1)S(1)} %get-tuple-element.254), channel_id=1, source_target_pairs={{0,1},{1,2},{2,3},{4,5},{5,6},{6,7},{8,9},{9,10},{10,11},{12,13},{... | collective-permute-start | bytes 798728 | tf_op jit(solution)/shard_map/ppermute | solution.py:83
  14.1 1.3 collective-permute-start.1
  15.4 4.3 collective-permute-done
  20.4 3.5 collective-permute-done.1
  23.9 1.3 collective-permute-start.2
  25.9 7.0 %collective-permute-done.2 = bf16[1040,128]{1,0:T(8,128)(2,1)S(1)} collective-permute-done((bf16[1040,128]{1,0:T(8,128)(2,1)S(1)}, bf16[1040,128]{1,0:T(8,128)(2,1)S(1)}, u32[]{:S(2)}, u32[]{:S(2)}) %collective-permute-start.2) | collective-permute-done | bytes 266272 | tf_op jit(solution)/shard_map/ppermute | solution.py:86
  32.9 1.3 collective-permute-start.3
  34.3 6.9 %collective-permute-done.3 = bf16[1040,128]{1,0:T(8,128)(2,1)S(1)} collective-permute-done((bf16[1040,128]{1,0:T(8,128)(2,1)S(1)}, bf16[1040,128]{1,0:T(8,128)(2,1)S(1)}, u32[]{:S(2)}, u32[]{:S(2)}) %collective-permute-start.3) | collective-permute-done | bytes 266272 | tf_op jit(solution)/shard_map/ppermute | solution.py:86
  41.4 1.6 collective-permute-start.7
  43.0 1.5 collective-permute-start.6
  45.8 1.3 held_back.3
  50.0 1.3 collective-permute-start.9
  51.3 4.6 collective-permute-start.8
  55.9 5.6 %collective-permute-done.9.refs_3_ = bf16[1968,128]{1,0:T(8,128)(2,1)S(1)} collective-permute-done((bf16[1968,128]{1,0:T(8,128)(2,1)S(1)}, bf16[1968,128]{1,0:T(8,128)(2,1)S(1)}, u32[]{:S(2)}, u32[]{:S(2)}) %collective-permute-start.9) | collective-permute-done | bytes 503840 | tf_op jit(solution)/shard_map/ppermute | solution.py:105
  65.9 1.3 held_back.4
  67.1 1.3 slice.166
  72.0 1.4 collective-permute-start.10
  73.4 1.6 collective-permute-start.11
  75.0 1.3 collective-permute-start.13
  76.3 9.5 %collective-permute-done.13.refs_3_ = bf16[1968,128]{1,0:T(8,128)(2,1)S(1)} collective-permute-done((bf16[1968,128]{1,0:T(8,128)(2,1)S(1)}, bf16[1968,128]{1,0:T(8,128)(2,1)S(1)}, u32[]{:S(2)}, u32[]{:S(2)}) %collective-permute-start.13) | collective-permute-done | bytes 503840 | tf_op jit(solution)/shard_map/ppermute | solution.py:105
  88.3 1.3 held_back.5
  91.4 1.3 multiply_select_fusion.6
  92.8 1.3 collective-permute-start.20
  94.9 8.7 %collective-permute-done.20 = bf16[1968,128]{1,0:T(8,128)(2,1)S(1)} collective-permute-done((bf16[1968,128]{1,0:T(8,128)(2,1)S(1)}, bf16[1968,128]{1,0:T(8,128)(2,1)S(1)}, u32[]{:S(2)}, u32[]{:S(2)}) %collective-permute-start.20) | collective-permute-done | bytes 503840 | tf_op jit(solution)/shard_map/ppermute | solution.py:105
  105.8 1.6 fusion.22
  107.5 1.3 collective-permute-start.19
  116.0 4.5 collective-permute-start.18
  120.7 2.7 collective-permute-done.18.refs_1_
  123.5 13.9 %heads.1 = (bf16[4,768,256]{2,1,0:T(8,128)(2,1)}, bf16[4,896,256]{2,1,0:T(8,128)(2,1)}, bf16[4,896,256]{2,1,0:T(8,128)(2,1)}, bf16[896,1024]{1,0:T(8,128)(2,1)}, s32[8,128]{1,0:T(8,128)S(1)}) custom-call(s32[12]{0:T(128)S(1)} %pad_add_fusion.order_ref, bf16[768,1024]{1,0:T(8,128)(2,1)} %refs_0_.7, bf16[64,1024]{1,0:T(8,128)(2,1)S(1)} %collective-permute-done.18.refs_1_, ...), custom_call_target="tpu_custom_call" | custom-call | flops 4831838 | bytes 128 | tf_op jit(solution)/shard_map/heads/pallas_call | solution.py:289
  140.3 19.8 %attend.1 = (bf16[4,768,256]{2,1,0:T(8,128)(2,1)}, f32[4,768,128]{2,1,0:T(8,128)}, s32[8,128]{1,0:T(8,128)}) custom-call(s32[12]{0:T(128)S(1)} %pad_add_fusion.order_ref, f32[6,128,256]{2,1,0:T(8,128)S(1)} %and_select_fusion.refs_0_, bf16[4,768,256]{2,1,0:T(8,128)(2,1)} %get-tuple-element.85.refs_1_.refs_5_, ...), custom_call_target="tpu_custom_call" | custom-call | flops 3221225 | bytes 128 | tf_op jit(solution)/shard_map/attend/pallas_call | solution.py:289
  160.1 10.5 %proj.1 = (f32[768,1024]{1,0:T(8,128)}, bf16[768,1024]{1,0:T(8,128)(2,1)}, s32[8,128]{1,0:T(8,128)}) custom-call(s32[12]{0:T(128)S(1)} %pad_add_fusion.order_ref, bf16[768,1024]{1,0:T(8,128)(2,1)} %refs_0_.7, f32[8,1024]{1,0:T(8,128)S(1)} %convert_element_type.89.refs_3_.refs_1_.refs_2_, bf16[4,768,256]{2,1,0:T(8,128)(2,1)} %get-tuple-element.88.refs_2_.refs_8_, ...), custom_call_target="tpu_custom_call" | custom-call | flops 1610612 | bytes 128 | tf_op jit(solution)/shard_map/proj/pallas_call | solution.py:289
  170.6 1.4 copy-done.6
  172.0 19.8 %gate.1 = (bf16[2624,768]{1,0:T(8,128)(2,1)}, bf16[2624,768]{1,0:T(8,128)(2,1)}, bf16[2624,768]{1,0:T(8,128)(2,1)}, s32[8,128]{1,0:T(8,128)}) custom-call(s32[12]{0:T(128)S(1)} %pad_add_fusion.order_ref, bf16[768,1024]{1,0:T(8,128)(2,1)S(1)} %copy-done.6, bf16[8,4,1312,128]{3,2,1,0:T(8,128)(2,1)} %bitcast.151, bf16[8,4,1312,128]{3,2,1,0:T(8,128)(2,1)} %bitcast.152, ...), custom_call_target="tpu_custom_call" | custom-call | flops 8254390 | bytes 128 | tf_op jit(solution)/shard_map/gate/pallas_call | solution.py:289
  191.8 9.7 %down_grad.1 = (bf16[8,4,656,128]{3,2,1,0:T(8,128)(2,1)}, bf16[768,1024]{1,0:T(8,128)(2,1)S(1)}, s32[8,128]{1,0:T(8,128)}) custom-call(s32[12]{0:T(128)S(1)} %pad_add_fusion.order_ref, bf16[768,1024]{1,0:T(8,128)(2,1)} %refs_0_.6, bf16[2624,768]{1,0:T(8,128)(2,1)} %get-tuple-element.91.refs_1_), custom_call_target="tpu_custom_call" | custom-call | flops 4127195 | bytes 128 | tf_op jit(solution)/shard_map/down_grad/pallas_call | solution.py:289
  201.6 11.0 %all-gather.7.cloned.1.call-done = bf16[32,656,128]{2,1,0:T(8,128)(2,1)} async-done(((bf16[4,656,128]{2,1,0:T(8,128)(2,1)}), bf16[32,656,128]{2,1,0:T(8,128)(2,1)}) %all-gather.7.cloned.1.call-update) | async-done | bytes 5373968 | tf_op jit(solution)/shard_map/all_gather | solution.py:179
  212.6 27.6 %in_grad.1 = (bf16[8,4,1312,128]{3,2,1,0:T(8,128)(2,1)}, bf16[2624,768]{1,0:T(8,128)(2,1)}, bf16[2624,768]{1,0:T(8,128)(2,1)}, s32[8,128]{1,0:T(8,128)}) custom-call(s32[12]{0:T(128)S(1)} %pad_add_fusion.order_ref, bf16[768,1024]{1,0:T(8,128)(2,1)S(1)} %get-tuple-element.93.refs_0_.refs_1_, bf16[768,1024]{1,0:T(8,128)(2,1)} %get-tuple-element.90.refs_0_.refs_1_, ...), custom_call_target="tpu_custom_call" | custom-call | flops 12381585 | bytes 128 | tf_op jit(solution)/shard_map/in_grad/pallas_call | solution.py:289
  240.2 33.0 %reduce-scatter.5.cloned.1.call-done = bf16[1,4,656,128]{3,2,1,0:T(8,128)(2,1)} async-done(((bf16[8,4,656,128]{3,2,1,0:T(8,128)(2,1)}), bf16[1,4,656,128]{3,2,1,0:T(8,128)(2,1)}) %reduce-scatter.5.cloned.1.call-update) | async-done | bytes 671760 | tf_op jit(solution)/shard_map/reduce_scatter | solution.py:189
  273.5 22.1 %middle_grad.1 = (f32[768,1024]{1,0:T(8,128)}, bf16[768,1024]{1,0:T(8,128)(2,1)S(1)}, f32[8,1024]{1,0:T(8,128)S(1)}, s32[8,128]{1,0:T(8,128)}) custom-call(s32[12]{0:T(128)S(1)} %pad_add_fusion.order_ref, f32[768,1024]{1,0:T(8,128)} %get-tuple-element.89.refs_0_, bf16[768,1024]{1,0:T(8,128)(2,1)} %copy-done.4, ...), custom_call_target="tpu_custom_call" | custom-call | flops 8254390 | bytes 128 | tf_op jit(solution)/shard_map/middle_grad/pallas_call | solution.py:289
  296.7 28.9 %attend_grad_odd.1 = (bf16[2,1024,128]{2,1,0:T(8,128)(2,1)S(1)}, bf16[2,1024,128]{2,1,0:T(8,128)(2,1)S(1)}, bf16[2,1024,128]{2,1,0:T(8,128)(2,1)}, bf16[2,1024,1...) custom-call(s32[12]{0:T(128)S(1)} %pad_add_fusion.order_ref, ...), custom_call_target="tpu_custom_call" | custom-call | flops 9663676 | bytes 128 | tf_op jit(solution)/shard_map/attend_grad_odd/pallas_call | solution.py:289
  326.4 29.1 %attend_grad_even.1 = (bf16[2,1024,128]{2,1,0:T(8,128)(2,1)S(1)}, bf16[2,1024,128]{2,1,0:T(8,128)(2,1)S(1)}, bf16[2,1024,128]{2,1,0:T(8,128)(2,1)}, bf16[2,1024,...) custom-call(s32[12]{0:T(128)S(1)} %pad_add_fusion.order_ref, ...), custom_call_target="tpu_custom_call" | custom-call | flops 9663676 | bytes 128 | tf_op jit(solution)/shard_map/attend_grad_even/pallas_call | solution.py:289
  356.5 3.0 reduce-scatter.7.cloned.1.call-done
  359.7 3.4 collective-permute-start.26
  363.2 1.5 collective-permute-start.27
  364.7 3.2 sums_one.1
  369.3 1.3 collective-permute-start.24
  371.3 7.6 %collective-permute-done.27.refs_8_ = bf16[4,2,64,256]{3,2,1,0:T(8,128)(2,1)S(1)} collective-permute-done((bf16[4,2,64,256]{3,2,1,0:T(8,128)(2,1)S(1)}, bf16[4,2,64,256]{3,2,1,0:T(8,128)(2,1)S(1)}, u32[]{:S(2)}, u32[]{:S(2)}) %collective-permute-start.27) | collective-permute-done | bytes 262176 | tf_op jit(solution)/shard_map/ppermute | solution.py:219
  379.0 16.4 %input_grad.1 = (f32[768,1024]{1,0:T(8,128)}, f32[8,1024]{1,0:T(8,128)S(1)}, s32[8,128]{1,0:T(8,128)S(1)}) custom-call(s32[12]{0:T(128)S(1)} %pad_add_fusion.order_ref, bf16[768,1024]{1,0:T(8,128)(2,1)} %refs_0_.7, f32[8,1024]{1,0:T(8,128)S(1)} %convert_element_type.89.refs_3_.refs_1_.refs_2_, f32[768,1024]{1,0:T(8,128)} %get-tuple-element.118.refs_2_, ...), custom_call_target="tpu_custom_call" | custom-call | flops 4831838 | bytes 128 | tf_op jit(solution)/shard_map/input_grad/pallas_call | solution.py:289
  396.2 3.5 sums_two.1
  404.9 2.0 collective-permute-start.32
  408.8 4.0 collective-permute-done.40
  414.1 1.6 collective-permute-start.33
  420.8 11.5 %down.1 = (bf16[768,1024]{1,0:T(8,128)(2,1)}, s32[8,128]{1,0:T(8,128)S(1)}) custom-call(s32[12]{0:T(128)S(1)} %pad_add_fusion.order_ref, f32[768,1024]{1,0:T(8,128)} %get-tuple-element.89.refs_0_, bf16[2624,768]{1,0:T(8,128)(2,1)} %get-tuple-element.91.refs_1_, bf16[8,4,656,128]{3,2,1,0:T(8,128)(2,1)} %bitcast.175, bf16[8,4,656,128]{3,2,1,0:T(8,128)(2,1)} %bitcast.176, ...), custom_call_target="tpu_custom_call" | custom-call | flops 4127195 | bytes 128 | tf_op jit(solution)/shard_map/down/pallas_call | solution.py:289
  432.3 1.7 collective-permute-start.39
  435.0 1.8 sums_three.1
  437.4 1.4 collective-permute-start.38
  438.9 1.4 collective-permute-start.45
  440.2 3.0 collective-permute-start.42
  445.1 1.7 sums_four.1
  448.3 4.5 collective-permute-start.43
  453.6 3.8 collective-permute-done.43
  457.4 4.4 collective-permute-start.44
  461.9 1.3 collective-permute-start.47
  463.2 1.6 multiply_subtract_fusion
  465.7 4.5 collective-permute-done.47
  (328 shorter events, 62.5 us)
Async XLA Ops:
  7.2 163.4 %all-gather.5.cloned.1.call-start = ((), (), s32[]{:S(2)}) async-start(), calls=%async_computation.8 | async-start | bytes 12091392 | tf_op jit(solution)/shard_map/all_gather | solution.py:179
  8.7 25.6 %copy-start.53 = (f32[128,256]{0,1:T(8,128)}, f32[128,256]{0,1:T(8,128)S(1)}, u32[]{:S(2)}) copy-start(f32[128,256]{0,1:T(8,128)S(1)} %copy.98) | copy-start | bytes 393220
  9.2 32.2 %copy-start.55 = (bf16[1,1040,128]{2,1,0:T(8,128)(2,1)}, bf16[1,1040,128]{2,1,0:T(8,128)(2,1)S(1)}, u32[]{:S(2)}) copy-start(bf16[1,1040,128]{2,1,0:T(8,128)(2,1)S(1)} %get-tuple-element.255) | copy-start | bytes 798724
  9.2 10.6 %collective-permute-start = (bf16[1040,128]{1,0:T(8,128)(2,1)S(1)}, bf16[1040,128]{1,0:T(8,128)(2,1)S(1)}, u32[]{:S(2)}, u32[]{:S(2)}) collective-permute-start(bf16[1040,128]{1,0:T(8,128)(2,1)S(1)} %get-tuple-element.254), channel_id=1, source_target_pairs={{0,1},{1,2},{2,3},{4,5},{5,6},{6,7},{8,9},{9,10},{10,11},{12,13},{... | collective-permute-start | bytes 798728 | tf_op jit(solution)/shard_map/ppermute | solution.py:83
  14.1 9.7 %collective-permute-start.1 = (bf16[1040,128]{1,0:T(8,128)(2,1)S(1)}, bf16[1040,128]{1,0:T(8,128)(2,1)S(1)}, u32[]{:S(2)}, u32[]{:S(2)}) collective-permute-start(bf16[1040,128]{1,0:T(8,128)(2,1)S(1)} %get-tuple-element.254), channel_id=1, source_target_pairs={{1,0},{2,1},{3,2},{5,4},{6,5},{7,6},{9,8},{10,9},{11,10},{13,12},{... | collective-permute-start | bytes 798728 | tf_op jit(solution)/shard_map/ppermute | solution.py:86
  19.8 5.4 %collective-permute-start.4 = (bf16[1040,128]{1,0:T(8,128)(2,1)S(1)}, bf16[1040,128]{1,0:T(8,128)(2,1)S(1)}, u32[]{:S(2)}, u32[]{:S(2)}) collective-permute-start(bf16[1040,128]{1,0:T(8,128)(2,1)S(1)} %collective-permute-done), channel_id=1, source_target_pairs={{1,2},{2,3},{5,6},{6,7},{9,10},{10,11},{13,14},{14,15},{17,18},{18... | collective-permute-start | bytes 798728 | tf_op jit(solution)/shard_map/ppermute | solution.py:83
  23.9 9.0 %collective-permute-start.2 = (bf16[1040,128]{1,0:T(8,128)(2,1)S(1)}, bf16[1040,128]{1,0:T(8,128)(2,1)S(1)}, u32[]{:S(2)}, u32[]{:S(2)}) collective-permute-start(bf16[1040,128]{1,0:T(8,128)(2,1)S(1)} %collective-permute-done.1), channel_id=1, source_target_pairs={{1,0},{2,1},{5,4},{6,5},{9,8},{10,9},{13,12},{14,13},{17,16},{18,1... | collective-permute-start | bytes 798728 | tf_op jit(solution)/shard_map/ppermute | solution.py:86
  25.2 9.0 %collective-permute-start.5 = (bf16[1040,128]{1,0:T(8,128)(2,1)S(1)}, bf16[1040,128]{1,0:T(8,128)(2,1)S(1)}, u32[]{:S(2)}, u32[]{:S(2)}) collective-permute-start(bf16[1040,128]{1,0:T(8,128)(2,1)S(1)} %collective-permute-done.4), channel_id=1, source_target_pairs={{2,3},{6,7},{10,11},{14,15},{18,19},{22,23},{26,27},{30,31}} | collective-permute-start | bytes 798728 | tf_op jit(solution)/shard_map/ppermute | solution.py:83
  32.9 8.3 %collective-permute-start.3 = (bf16[1040,128]{1,0:T(8,128)(2,1)S(1)}, bf16[1040,128]{1,0:T(8,128)(2,1)S(1)}, u32[]{:S(2)}, u32[]{:S(2)}) collective-permute-start(bf16[1040,128]{1,0:T(8,128)(2,1)S(1)} %collective-permute-done.2), channel_id=1, source_target_pairs={{1,0},{5,4},{9,8},{13,12},{17,16},{21,20},{25,24},{29,28}} | collective-permute-start | bytes 798728 | tf_op jit(solution)/shard_map/ppermute | solution.py:86
  41.4 22.2 %collective-permute-start.7 = (bf16[4160,128]{1,0:T(8,128)(2,1)S(1)}, bf16[4160,128]{1,0:T(8,128)(2,1)S(1)}, u32[]{:S(2)}, u32[]{:S(2)}) collective-permute-start(bf16[4160,128]{1,0:T(8,128)(2,1)S(1)} %bitcast.146), channel_id=1, source_target_pairs={{0,16},{4,20},{8,24},{12,28},{16,0},{20,4},{24,8},{28,12},{1,17},{... | collective-permute-start | bytes 3194888 | tf_op jit(solution)/shard_map/ppermute | solution.py:135
  43.0 21.9 %collective-permute-start.6 = (bf16[4160,128]{1,0:T(8,128)(2,1)S(1)}, bf16[4160,128]{1,0:T(8,128)(2,1)S(1)}, u32[]{:S(2)}, u32[]{:S(2)}) collective-permute-start(bf16[4160,128]{1,0:T(8,128)(2,1)S(1)} %bitcast.147), channel_id=1, source_target_pairs={{0,8},{4,12},{8,0},{12,4},{16,24},{20,28},{24,16},{28,20},{1,9},{5... | collective-permute-start | bytes 3194888 | tf_op jit(solution)/shard_map/ppermute | solution.py:135
  50.0 11.5 %collective-permute-start.9 = (bf16[1968,128]{1,0:T(8,128)(2,1)S(1)}, bf16[1968,128]{1,0:T(8,128)(2,1)S(1)}, u32[]{:S(2)}, u32[]{:S(2)}) collective-permute-start(bf16[1968,128]{1,0:T(8,128)(2,1)S(1)} %multiply_select_fusion.9), channel_id=1, source_target_pairs={{1,0},{2,1},{3,2},{5,4},{6,5},{7,6},{9,8},{10,9},{11,10},{13,12},{... | collective-permute-start | bytes 1511432 | tf_op jit(solution)/shard_map/ppermute | solution.py:105
  51.3 11.3 %collective-permute-start.8 = (bf16[1968,128]{1,0:T(8,128)(2,1)S(1)}, bf16[1968,128]{1,0:T(8,128)(2,1)S(1)}, u32[]{:S(2)}, u32[]{:S(2)}) collective-permute-start(bf16[1968,128]{1,0:T(8,128)(2,1)S(1)} %multiply_select_fusion.9), channel_id=1, source_target_pairs={{0,1},{1,2},{2,3},{4,5},{5,6},{6,7},{8,9},{9,10},{10,11},{12,13},{... | collective-permute-start | bytes 1511432 | tf_op jit(solution)/shard_map/ppermute | solution.py:104
  70.2 6.1 %collective-permute-start.12 = (bf16[1968,128]{1,0:T(8,128)(2,1)S(1)}, bf16[1968,128]{1,0:T(8,128)(2,1)S(1)}, u32[]{:S(2)}, u32[]{:S(2)}) collective-permute-start(bf16[1968,128]{1,0:T(8,128)(2,1)S(1)} %multiply_select_fusion.8), channel_id=1, source_target_pairs={{1,2},{2,3},{5,6},{6,7},{9,10},{10,11},{13,14},{14,15},{17,18},{18... | collective-permute-start | bytes 1511432 | tf_op jit(solution)/shard_map/ppermute | solution.py:104
  72.0 13.9 %collective-permute-start.10 = (bf16[2080,128]{1,0:T(8,128)(2,1)S(1)}, bf16[2080,128]{1,0:T(8,128)(2,1)S(1)}, u32[]{:S(2)}, u32[]{:S(2)}) collective-permute-start(bf16[2080,128]{1,0:T(8,128)(2,1)S(1)} %multiply_select_fusion.4), channel_id=1, source_target_pairs={{0,16},{4,20},{8,24},{12,28},{16,0},{20,4},{24,8},{28,12},{1,17},{... | collective-permute-start | bytes 1597448 | tf_op jit(solution)/shard_map/ppermute | solution.py:135
  73.4 13.2 %collective-permute-start.11 = (bf16[2080,128]{1,0:T(8,128)(2,1)S(1)}, bf16[2080,128]{1,0:T(8,128)(2,1)S(1)}, u32[]{:S(2)}, u32[]{:S(2)}) collective-permute-start(bf16[2080,128]{1,0:T(8,128)(2,1)S(1)} %multiply_select_fusion.3), channel_id=1, source_target_pairs={{0,8},{4,12},{8,0},{12,4},{16,24},{20,28},{24,16},{28,20},{1,9},{5... | collective-permute-start | bytes 1597448 | tf_op jit(solution)/shard_map/ppermute | solution.py:135
  75.0 10.9 %collective-permute-start.13 = (bf16[1968,128]{1,0:T(8,128)(2,1)S(1)}, bf16[1968,128]{1,0:T(8,128)(2,1)S(1)}, u32[]{:S(2)}, u32[]{:S(2)}) collective-permute-start(bf16[1968,128]{1,0:T(8,128)(2,1)S(1)} %multiply_select_fusion.7), channel_id=1, source_target_pairs={{1,0},{2,1},{5,4},{6,5},{9,8},{10,9},{13,12},{14,13},{17,16},{18,1... | collective-permute-start | bytes 1511432 | tf_op jit(solution)/shard_map/ppermute | solution.py:105
  92.8 10.9 %collective-permute-start.20 = (bf16[1968,128]{1,0:T(8,128)(2,1)S(1)}, bf16[1968,128]{1,0:T(8,128)(2,1)S(1)}, u32[]{:S(2)}, u32[]{:S(2)}) collective-permute-start(bf16[1968,128]{1,0:T(8,128)(2,1)S(1)} %get-tuple-element.251), channel_id=1, source_target_pairs={{1,0},{5,4},{9,8},{13,12},{17,16},{21,20},{25,24},{29,28}} | collective-permute-start | bytes 1511432 | tf_op jit(solution)/shard_map/ppermute | solution.py:105
  94.1 9.6 %collective-permute-start.21 = (bf16[1968,128]{1,0:T(8,128)(2,1)S(1)}, bf16[1968,128]{1,0:T(8,128)(2,1)S(1)}, u32[]{:S(2)}, u32[]{:S(2)}) collective-permute-start(bf16[1968,128]{1,0:T(8,128)(2,1)S(1)} %get-tuple-element.253), channel_id=1, source_target_pairs={{2,3},{6,7},{10,11},{14,15},{18,19},{22,23},{26,27},{30,31}} | collective-permute-start | bytes 1511432 | tf_op jit(solution)/shard_map/ppermute | solution.py:104
  105.8 106.8 %all-gather.7.cloned.1.call-start = ((), (), s32[]{:S(2)}) async-start(), calls=%async_computation.9 | async-start | bytes 6045696 | tf_op jit(solution)/shard_map/all_gather | solution.py:179
  107.5 13.2 %collective-permute-start.19 = (bf16[64,1024]{1,0:T(8,128)(2,1)}, bf16[64,1024]{1,0:T(8,128)(2,1)S(1)}, u32[]{:S(2)}, u32[]{:S(2)}) collective-permute-start(bf16[64,1024]{1,0:T(8,128)(2,1)} %get-tuple-element.240), channel_id=1, source_target_pairs={{1,0},{2,1},{3,2},{5,4},{6,5},{7,6},{9,8},{10,9},{11,10},{13,12},{... | collective-permute-start | bytes 393224 | tf_op jit(solution)/shard_map/ppermute | solution.py:219
  112.9 3.1 collective-permute-start.14
  112.9 7.7 %collective-permute-start.16 = (bf16[4160,128]{1,0:T(8,128)(2,1)S(1)}, bf16[4160,128]{1,0:T(8,128)(2,1)S(1)}, u32[]{:S(2)}, u32[]{:S(2)}) collective-permute-start(bf16[4160,128]{1,0:T(8,128)(2,1)S(1)} %copy-done.19), channel_id=1, source_target_pairs={{0,4},{4,0},{8,12},{12,8},{16,20},{20,16},{24,28},{28,24},{1,5},{5... | collective-permute-start | bytes 3194888 | tf_op jit(solution)/shard_map/ppermute | solution.py:135
  113.4 7.1 %collective-permute-start.15 = (bf16[4160,128]{1,0:T(8,128)(2,1)}, bf16[4160,128]{1,0:T(8,128)(2,1)S(1)}, u32[]{:S(2)}, u32[]{:S(2)}) collective-permute-start(bf16[4160,128]{1,0:T(8,128)(2,1)} %copy-done.20), channel_id=1, source_target_pairs={{0,4},{4,0},{8,12},{12,8},{16,20},{20,16},{24,28},{28,24},{1,5},{5... | collective-permute-start | bytes 3194888 | tf_op jit(solution)/shard_map/ppermute | solution.py:135
  115.3 5.3 %collective-permute-start.17 = (bf16[4160,128]{1,0:T(8,128)(2,1)S(1)}, bf16[4160,128]{1,0:T(8,128)(2,1)S(1)}, u32[]{:S(2)}, u32[]{:S(2)}) collective-permute-start(bf16[4160,128]{1,0:T(8,128)(2,1)S(1)} %multiply_select_fusion), channel_id=1, source_target_pairs={{0,4},{4,0},{8,12},{12,8},{16,20},{20,16},{24,28},{28,24},{1,5},{5... | collective-permute-start | bytes 3194888 | tf_op jit(solution)/shard_map/ppermute | solution.py:135
  116.0 7.4 %collective-permute-start.18 = (bf16[64,1024]{1,0:T(8,128)(2,1)S(1)}, bf16[64,1024]{1,0:T(8,128)(2,1)S(1)}, u32[]{:S(2)}, u32[]{:S(2)}) collective-permute-start(bf16[64,1024]{1,0:T(8,128)(2,1)S(1)} %get-tuple-element.241), channel_id=1, source_target_pairs={{0,1},{1,2},{2,3},{4,5},{5,6},{6,7},{8,9},{9,10},{10,11},{12,13},{... | collective-permute-start | bytes 393224 | tf_op jit(solution)/shard_map/ppermute | solution.py:219
  139.6 133.6 %reduce-scatter.5.cloned.1.call-start = ((), (), s32[]{:S(2)}) async-start(), calls=%async_computation.4 | async-start | bytes 6045696 | tf_op jit(solution)/shard_map/reduce_scatter | solution.py:189
  140.3 19.8 %copy-start.3 = (f32[6,128,256]{2,1,0:T(8,128)}, f32[6,128,256]{2,1,0:T(8,128)S(1)}, u32[]{:S(2)}) copy-start(f32[6,128,256]{2,1,0:T(8,128)S(1)} %and_select_fusion.refs_0_) | copy-start | bytes 2359300
  201.5 157.9 %reduce-scatter.7.cloned.1.call-start = ((), (), s32[]{:S(2)}) async-start(), calls=%async_computation.5 | async-start | bytes 12091392 | tf_op jit(solution)/shard_map/reduce_scatter | solution.py:189
  240.2 193.8 %reduce-scatter.9.cloned.1.call-start = ((), (), s32[]{:S(2)}) async-start(), calls=%async_computation.6 | async-start | bytes 839680 | tf_op jit(solution)/shard_map/reduce_scatter | solution.py:897
  273.3 171.8 %reduce-scatter.11.cloned.1.call-start = ((), (), s32[]{:S(2)}) async-start(), calls=%async_computation.7 | async-start | bytes 1679360 | tf_op jit(solution)/shard_map/reduce_scatter | solution.py:910
  326.4 29.1 %copy-start.9 = (bf16[2,1024,128]{2,1,0:T(8,128)(2,1)}, bf16[2,1024,128]{2,1,0:T(8,128)(2,1)S(1)}, u32[]{:S(2)}) copy-start(bf16[2,1024,128]{2,1,0:T(8,128)(2,1)S(1)} %get-tuple-element.108.refs_0_.refs_2_) | copy-start | bytes 1572868
  326.4 38.3 %collective-permute-start.23 = (bf16[4,2,1024,128]{3,2,1,0:T(8,128)(2,1)}, bf16[4,2,1024,128]{3,2,1,0:T(8,128)(2,1)}, u32[]{:S(2)}, u32[]{:S(2)}) collective-permute-start(bf16[4,2,1024,128]{3,2,1,0:T(8,128)(2,1)} %get-tuple-element.109), channel_id=1, source_target_pairs={{0,4},{4,0},{8,12},{12,8},{16,20},{20,16},{24,28},{28,24},{1,5},{5... | collective-permute-start | bytes 6291464 | tf_op jit(solution)/shard_map/ppermute | solution.py:135
  326.4 29.5 %copy-start.26 = (bf16[2,2,896,256]{3,2,1,0:T(8,128)(2,1)S(1)}, bf16[2,2,896,256]{3,2,1,0:T(8,128)(2,1)}, u32[]{:S(2)}) copy-start(bf16[2,2,896,256]{3,2,1,0:T(8,128)(2,1)} %get-tuple-element.122.refs_6_) | copy-start | bytes 5505028
  355.5 40.0 %collective-permute-start.22 = (bf16[4,2,1024,128]{3,2,1,0:T(8,128)(2,1)}, bf16[4,2,1024,128]{3,2,1,0:T(8,128)(2,1)}, u32[]{:S(2)}, u32[]{:S(2)}) collective-permute-start(bf16[4,2,1024,128]{3,2,1,0:T(8,128)(2,1)} %get-tuple-element.104), channel_id=1, source_target_pairs={{0,4},{4,0},{8,12},{12,8},{16,20},{20,16},{24,28},{28,24},{1,5},{5... | collective-permute-start | bytes 6291464 | tf_op jit(solution)/shard_map/ppermute | solution.py:135
  359.7 11.7 %collective-permute-start.26 = (bf16[4,2,64,256]{3,2,1,0:T(8,128)(2,1)S(1)}, bf16[4,2,64,256]{3,2,1,0:T(8,128)(2,1)S(1)}, u32[]{:S(2)}, u32[]{:S(2)}) collective-permute-start(bf16[4,2,64,256]{3,2,1,0:T(8,128)(2,1)S(1)} %pad_maximum_fusion.3), channel_id=1, source_target_pairs={{0,1},{1,2},{2,3},{4,5},{5,6},{6,7},{8,9},{9,10},{10,11},{12,13},{... | collective-permute-start | bytes 786440 | tf_op jit(solution)/shard_map/ppermute | solution.py:219
  363.2 15.8 %collective-permute-start.27 = (bf16[4,2,64,256]{3,2,1,0:T(8,128)(2,1)S(1)}, bf16[4,2,64,256]{3,2,1,0:T(8,128)(2,1)S(1)}, u32[]{:S(2)}, u32[]{:S(2)}) collective-permute-start(bf16[4,2,64,256]{3,2,1,0:T(8,128)(2,1)S(1)} %pad_maximum_fusion.4), channel_id=1, source_target_pairs={{1,0},{2,1},{3,2},{5,4},{6,5},{7,6},{9,8},{10,9},{11,10},{13,12},{... | collective-permute-start | bytes 786440 | tf_op jit(solution)/shard_map/ppermute | solution.py:219
  369.3 26.1 %copy-start.15 = (bf16[1024,128]{1,0:T(8,128)(2,1)}, bf16[1024,128]{1,0:T(8,128)(2,1)S(1)}, u32[]{:S(2)}) copy-start(bf16[1024,128]{1,0:T(8,128)(2,1)S(1)} %get-tuple-element.134.refs_3_) | copy-start | bytes 786436
  369.3 26.1 %collective-permute-start.24 = (bf16[1024,128]{1,0:T(8,128)(2,1)S(1)}, bf16[1024,128]{1,0:T(8,128)(2,1)S(1)}, u32[]{:S(2)}, u32[]{:S(2)}) collective-permute-start(bf16[1024,128]{1,0:T(8,128)(2,1)S(1)} %get-tuple-element.115), channel_id=1, source_target_pairs={{0,8},{4,12},{8,0},{12,4},{16,24},{20,28},{24,16},{28,20},{1,9},{5... | collective-permute-start | bytes 786440 | tf_op jit(solution)/shard_map/ppermute | solution.py:135
  370.6 24.8 %collective-permute-start.25 = (bf16[1024,128]{1,0:T(8,128)(2,1)}, bf16[1024,128]{1,0:T(8,128)(2,1)S(1)}, u32[]{:S(2)}, u32[]{:S(2)}) collective-permute-start(bf16[1024,128]{1,0:T(8,128)(2,1)} %get-tuple-element.117), channel_id=1, source_target_pairs={{0,16},{4,20},{8,24},{12,28},{16,0},{20,4},{24,8},{28,12},{1,17},{... | collective-permute-start | bytes 786440 | tf_op jit(solution)/shard_map/ppermute | solution.py:135
  396.2 21.5 %copy-start.68 = (f32[128,256]{1,0:T(8,128)S(1)}, f32[128,256]{1,0:T(8,128)}, u32[]{:S(2)}) copy-start(f32[128,256]{1,0:T(8,128)} %param.29) | copy-start | bytes 393220
  396.2 22.3 %copy-start.69 = (f32[128,256]{1,0:T(8,128)S(1)}, f32[128,256]{1,0:T(8,128)}, u32[]{:S(2)}) copy-start(f32[128,256]{1,0:T(8,128)} %param.30) | copy-start | bytes 393220
  396.2 23.1 %copy-start.60 = (f32[128,3,256]{2,0,1:T(8,128)S(1)}, f32[128,3,256]{2,0,1:T(8,128)}, u32[]{:S(2)}) copy-start(f32[128,3,256]{2,0,1:T(8,128)} %param.27) | copy-start | bytes 1179652
  402.4 1.2 collective-permute-start.35
  403.6 3.6 collective-permute-start.36
  404.7 9.4 %collective-permute-start.29 = (bf16[1024,128]{1,0:T(8,128)(2,1)S(1)}, bf16[1024,128]{1,0:T(8,128)(2,1)S(1)}, u32[]{:S(2)}, u32[]{:S(2)}) collective-permute-start(bf16[1024,128]{1,0:T(8,128)(2,1)S(1)} %get-tuple-element.132), channel_id=1, source_target_pairs={{0,8},{4,12},{8,0},{12,4},{16,24},{20,28},{24,16},{28,20},{1,9},{5... | collective-permute-start | bytes 786440 | tf_op jit(solution)/shard_map/ppermute | solution.py:135
  404.9 10.8 %collective-permute-start.32 = (bf16[1024,128]{1,0:T(8,128)(2,1)S(1)}, bf16[1024,128]{1,0:T(8,128)(2,1)S(1)}, u32[]{:S(2)}, u32[]{:S(2)}) collective-permute-start(bf16[1024,128]{1,0:T(8,128)(2,1)S(1)} %get-tuple-element.136), channel_id=1, source_target_pairs={{0,16},{4,20},{8,24},{12,28},{16,0},{20,4},{24,8},{28,12},{1,17},{... | collective-permute-start | bytes 786440 | tf_op jit(solution)/shard_map/ppermute | solution.py:135
  407.2 5.7 %collective-permute-start.40 = (f32[2,128]{1,0:T(2,128)S(1)}, f32[2,128]{1,0:T(2,128)S(1)}, u32[]{:S(2)}, u32[]{:S(2)}) collective-permute-start(f32[2,128]{1,0:T(2,128)S(1)} %slice.237), channel_id=1, source_target_pairs={{0,8},{4,12},{8,0},{12,4},{16,24},{20,28},{24,16},{28,20},{1,9},{5... | collective-permute-start | bytes 3080 | tf_op jit(solution)/shard_map/ppermute | solution.py:135
  408.4 12.3 %collective-permute-start.30 = (bf16[1024,128]{1,0:T(8,128)(2,1)}, bf16[1024,128]{1,0:T(8,128)(2,1)S(1)}, u32[]{:S(2)}, u32[]{:S(2)}) collective-permute-start(bf16[1024,128]{1,0:T(8,128)(2,1)} %get-tuple-element.133), channel_id=1, source_target_pairs={{0,16},{4,20},{8,24},{12,28},{16,0},{20,4},{24,8},{28,12},{1,17},{... | collective-permute-start | bytes 786440 | tf_op jit(solution)/shard_map/ppermute | solution.py:135
  412.9 3.7 collective-permute-start.41
  413.6 18.7 %collective-permute-start.31 = (bf16[1024,128]{1,0:T(8,128)(2,1)}, bf16[1024,128]{1,0:T(8,128)(2,1)S(1)}, u32[]{:S(2)}, u32[]{:S(2)}) collective-permute-start(bf16[1024,128]{1,0:T(8,128)(2,1)} %get-tuple-element.135), channel_id=1, source_target_pairs={{0,8},{4,12},{8,0},{12,4},{16,24},{20,28},{24,16},{28,20},{1,9},{5... | collective-permute-start | bytes 786440 | tf_op jit(solution)/shard_map/ppermute | solution.py:135
  414.1 19.9 %collective-permute-start.33 = (bf16[1024,128]{1,0:T(8,128)(2,1)S(1)}, bf16[1024,128]{1,0:T(8,128)(2,1)}, u32[]{:S(2)}, u32[]{:S(2)}) collective-permute-start(bf16[1024,128]{1,0:T(8,128)(2,1)S(1)} %get-tuple-element.138), channel_id=1, source_target_pairs={{0,8},{4,12},{8,0},{12,4},{16,24},{20,28},{24,16},{28,20},{1,9},{5... | collective-permute-start | bytes 786440 | tf_op jit(solution)/shard_map/ppermute | solution.py:135
  415.7 18.4 %collective-permute-start.34 = (bf16[1024,128]{1,0:T(8,128)(2,1)}, bf16[1024,128]{1,0:T(8,128)(2,1)}, u32[]{:S(2)}, u32[]{:S(2)}) collective-permute-start(bf16[1024,128]{1,0:T(8,128)(2,1)} %get-tuple-element.140), channel_id=1, source_target_pairs={{0,16},{4,20},{8,24},{12,28},{16,0},{20,4},{24,8},{28,12},{1,17},{... | collective-permute-start | bytes 786440 | tf_op jit(solution)/shard_map/ppermute | solution.py:135
  416.5 23.7 %collective-permute-start.28 = (bf16[1024,128]{1,0:T(8,128)(2,1)S(1)}, bf16[1024,128]{1,0:T(8,128)(2,1)S(1)}, u32[]{:S(2)}, u32[]{:S(2)}) collective-permute-start(bf16[1024,128]{1,0:T(8,128)(2,1)S(1)} %get-tuple-element.130), channel_id=1, source_target_pairs={{0,8},{4,12},{8,0},{12,4},{16,24},{20,28},{24,16},{28,20},{1,9},{5... | collective-permute-start | bytes 786440 | tf_op jit(solution)/shard_map/ppermute | solution.py:135
  420.7 18.2 %collective-permute-start.48 = (f32[2,128]{1,0:T(2,128)S(1)}, f32[2,128]{1,0:T(2,128)S(1)}, u32[]{:S(2)}, u32[]{:S(2)}) collective-permute-start(f32[2,128]{1,0:T(2,128)S(1)} %add.187), channel_id=1, source_target_pairs={{0,2},{1,3},{2,0},{3,1},{4,6},{5,7},{6,4},{7,5},{8,10},{9,11},{10,... | collective-permute-start | bytes 3080 | tf_op jit(solution)/shard_map/ppermute | solution.py:129
  432.3 12.7 %collective-permute-start.39 = (bf16[1024,128]{1,0:T(8,128)(2,1)S(1)}, bf16[1024,128]{1,0:T(8,128)(2,1)}, u32[]{:S(2)}, u32[]{:S(2)}) collective-permute-start(bf16[1024,128]{1,0:T(8,128)(2,1)S(1)} %get-tuple-element.147), channel_id=1, source_target_pairs={{0,16},{4,20},{8,24},{12,28},{16,0},{20,4},{24,8},{28,12},{1,17},{... | collective-permute-start | bytes 786440 | tf_op jit(solution)/shard_map/ppermute | solution.py:135
  436.8 8.3 %collective-permute-start.37 = (bf16[1024,128]{1,0:T(8,128)(2,1)S(1)}, bf16[1024,128]{1,0:T(8,128)(2,1)S(1)}, u32[]{:S(2)}, u32[]{:S(2)}) collective-permute-start(bf16[1024,128]{1,0:T(8,128)(2,1)S(1)} %get-tuple-element.144), channel_id=1, source_target_pairs={{0,16},{4,20},{8,24},{12,28},{16,0},{20,4},{24,8},{28,12},{1,17},{... | collective-permute-start | bytes 786440 | tf_op jit(solution)/shard_map/ppermute | solution.py:135
  437.4 7.6 %collective-permute-start.38 = (bf16[1024,128]{1,0:T(8,128)(2,1)S(1)}, bf16[1024,128]{1,0:T(8,128)(2,1)S(1)}, u32[]{:S(2)}, u32[]{:S(2)}) collective-permute-start(bf16[1024,128]{1,0:T(8,128)(2,1)S(1)} %get-tuple-element.146), channel_id=1, source_target_pairs={{0,8},{4,12},{8,0},{12,4},{16,24},{20,28},{24,16},{28,20},{1,9},{5... | collective-permute-start | bytes 786440 | tf_op jit(solution)/shard_map/ppermute | solution.py:135
  438.9 7.9 %collective-permute-start.45 = (bf16[1024,128]{1,0:T(8,128)(2,1)S(1)}, bf16[1024,128]{1,0:T(8,128)(2,1)}, u32[]{:S(2)}, u32[]{:S(2)}) collective-permute-start(bf16[1024,128]{1,0:T(8,128)(2,1)S(1)} %get-tuple-element.150), channel_id=1, source_target_pairs={{3,2},{7,6},{11,10},{15,14},{19,18},{23,22},{27,26},{31,30}} | collective-permute-start | bytes 786440 | tf_op jit(solution)/shard_map/ppermute | solution.py:113
  440.2 6.9 %collective-permute-start.42 = (bf16[1024,128]{1,0:T(8,128)(2,1)S(1)}, bf16[1024,128]{1,0:T(8,128)(2,1)S(1)}, u32[]{:S(2)}, u32[]{:S(2)}) collective-permute-start(bf16[1024,128]{1,0:T(8,128)(2,1)S(1)} %get-tuple-element.152), channel_id=1, source_target_pairs={{0,1},{4,5},{8,9},{12,13},{16,17},{20,21},{24,25},{28,29}} | collective-permute-start | bytes 786440 | tf_op jit(solution)/shard_map/ppermute | solution.py:112
  448.3 9.1 %collective-permute-start.43 = (bf16[1024,128]{1,0:T(8,128)(2,1)S(1)}, bf16[1024,128]{1,0:T(8,128)(2,1)S(1)}, u32[]{:S(2)}, u32[]{:S(2)}) collective-permute-start(bf16[1024,128]{1,0:T(8,128)(2,1)S(1)} %get-tuple-element.256), channel_id=1, source_target_pairs={{0,1},{1,2},{4,5},{5,6},{8,9},{9,10},{12,13},{13,14},{16,17},{17,1... | collective-permute-start | bytes 786440 | tf_op jit(solution)/shard_map/ppermute | solution.py:112
  452.8 9.0 %collective-permute-start.46 = (bf16[1024,128]{1,0:T(8,128)(2,1)S(1)}, bf16[1024,128]{1,0:T(8,128)(2,1)S(1)}, u32[]{:S(2)}, u32[]{:S(2)}) collective-permute-start(bf16[1024,128]{1,0:T(8,128)(2,1)S(1)} %get-tuple-element.257), channel_id=1, source_target_pairs={{2,1},{3,2},{6,5},{7,6},{10,9},{11,10},{14,13},{15,14},{18,17},{19... | collective-permute-start | bytes 786440 | tf_op jit(solution)/shard_map/ppermute | solution.py:113
  457.4 8.3 %collective-permute-start.44 = (bf16[1024,128]{1,0:T(8,128)(2,1)S(1)}, bf16[1024,128]{1,0:T(8,128)(2,1)S(1)}, u32[]{:S(2)}, u32[]{:S(2)}) collective-permute-start(bf16[1024,128]{1,0:T(8,128)(2,1)S(1)} %add_convert_fusion.1), channel_id=1, source_target_pairs={{0,1},{1,2},{2,3},{4,5},{5,6},{6,7},{8,9},{9,10},{10,11},{12,13},{... | collective-permute-start | bytes 786440 | tf_op jit(solution)/shard_map/ppermute | solution.py:112
  461.9 8.3 %collective-permute-start.47 = (bf16[1024,128]{1,0:T(8,128)(2,1)S(1)}, bf16[1024,128]{1,0:T(8,128)(2,1)S(1)}, u32[]{:S(2)}, u32[]{:S(2)}) collective-permute-start(bf16[1024,128]{1,0:T(8,128)(2,1)S(1)} %add_convert_fusion), channel_id=1, source_target_pairs={{1,0},{2,1},{3,2},{5,4},{6,5},{7,6},{9,8},{10,9},{11,10},{13,12},{... | collective-permute-start | bytes 786440 | tf_op jit(solution)/shard_map/ppermute | solution.py:113
  (66 other events, 380.4 us)
Sparse Core Ops, SparseCore 0:
  105.9 62.4 all-gather.4
  170.9 41.6 all-gather.6
  216.0 57.1 reduce-scatter.4
  276.6 82.7 reduce-scatter.6
  361.7 24.5 reduce-scatter.8
  388.5 30.4 reduce-scatter.10
